TPU v7x, 32 devices: a whole 2x2x4 slice. The times are simulated.
32 devices in a mesh: dp: 2 (over x), expert: 16 (over z, y, core).
Axes of the slice: x: 2, y: 2, z: 4, core: 2. Of those that a mesh axis runs over, the one named last changes fastest.
Arguments:
- tokens: bfloat16 [4096, 5120], P(('dp', 'expert')), may hold values from -6 to 6
- cotangent: bfloat16 [4096, 5120], P(('dp', 'expert')), may hold values from -2 to 2
- picks: int32 [32, 16, 4], P(('dp', 'expert')), may hold values from 0 to 127, as said below
- gates: float32 [32, 16, 4], P(('dp', 'expert')), may hold values from 0.05 to 1
- w_gate: bfloat16 [16, 5120, 768], P('expert', 'dp'), may hold values from -0.078125 to 0.078125
- w_up: bfloat16 [16, 5120, 768], P('expert', 'dp'), may hold values from -0.078125 to 0.078125
- w_down: bfloat16 [16, 768, 5120], P('expert', None, 'dp'), may hold values from -0.21875 to 0.21875
Outputs:
- mixed: bfloat16 [4096, 5120], P(('dp', 'expert'))
- token_grad: bfloat16 [4096, 5120], P(('dp', 'expert'))
- gate_grad: float32 [32, 16, 4], P(('dp', 'expert'))
- grad_w_gate: bfloat16 [16, 5120, 768], P('expert', 'dp')
- grad_w_up: bfloat16 [16, 5120, 768], P('expert', 'dp')
- grad_w_down: bfloat16 [16, 768, 5120], P('expert', None, 'dp')
Inputs may be any that keep to these rules, and one draw needn't show every extreme that they name: picks[d, e] holds 4 distinct token indices of device d; every expert takes exactly 4 tokens from every device.
All inputs are finite; a program needn't handle non-finite values.
Results may differ from a plain program's by a relative error of at most 0.02.
Values may be sent and summed in bfloat16 or wider, within the bound.
No kernel may reach another device: no remote copies, remote signals or barrier semaphores. Data moves between devices by JAX's collectives and lax.ppermute only.
A program may use at most 64 MiB of HBM per device.

v0:
```python
import jax
import jax.numpy as jnp
from jax import lax
from jax.sharding import PartitionSpec as P


def contract_rows(left, right):
    return lax.dot_general(
        left, right, (((0,), (0,)), ((), ())), preferred_element_type=jnp.float32
    )


def contract_cols(left, right):
    return lax.dot_general(
        left, right, (((1,), (1,)), ((), ())), preferred_element_type=jnp.float32
    )


def rounded(values):
    return lax.optimization_barrier(values.astype(jnp.bfloat16)).astype(jnp.float32)


def swiglu_grads(column_sums, hidden_units):
    gate_sum = column_sums[:, :hidden_units]
    up_sum = column_sums[:, hidden_units : 2 * hidden_units]
    back_sum = column_sums[:, 2 * hidden_units :]
    sigmoid_gate = jax.nn.sigmoid(gate_sum)
    silu_gate = gate_sum * sigmoid_gate
    hidden = (silu_gate * up_sum).astype(jnp.bfloat16)
    grad_up = (back_sum * silu_gate).astype(jnp.bfloat16)
    grad_gate = (back_sum * up_sum * sigmoid_gate * (1.0 + gate_sum * (1.0 - sigmoid_gate))).astype(
        jnp.bfloat16
    )
    return (hidden, grad_gate, grad_up)


def body(tokens, cotangent, picks, gates, w_gate, w_up, w_down):
    expert_count = picks.shape[1]
    slot_count = picks.shape[2]
    model_width = tokens.shape[1]
    chosen = picks[0].reshape(-1)
    scales = gates[0].reshape(-1)
    token_rows = jnp.take(tokens, chosen, axis=0)
    grad_rows = jnp.take(cotangent, chosen, axis=0)
    scaled_grad = (scales[:, None] * grad_rows.astype(jnp.float32)).astype(jnp.bfloat16)
    outgoing = (
        token_rows.reshape(expert_count, slot_count, model_width),
        scaled_grad.reshape(expert_count, slot_count, model_width),
    )
    arrived_in, arrived_up = (
        lax.all_to_all(
            lax.all_to_all(outgoing[0], "dp", split_axis=2, concat_axis=1, tiled=True),
            "expert",
            split_axis=0,
            concat_axis=0,
            tiled=True,
        ),
        lax.all_to_all(
            lax.all_to_all(outgoing[1], "dp", split_axis=2, concat_axis=1, tiled=True),
            "expert",
            split_axis=0,
            concat_axis=0,
            tiled=True,
        ),
    )
    arrived_shape = arrived_in.shape
    row_count = arrived_shape[0] * arrived_shape[1]
    slice_width = arrived_shape[2]
    inputs = arrived_in.reshape(row_count, slice_width)
    upstream = arrived_up.reshape(row_count, slice_width)
    gate_mat = w_gate[0]
    up_mat = w_up[0]
    down_mat = w_down[0]
    hidden_units = gate_mat.shape[1]
    terms = jnp.concatenate(
        [
            rounded(jnp.dot(inputs, gate_mat, preferred_element_type=jnp.float32)),
            rounded(jnp.dot(inputs, up_mat, preferred_element_type=jnp.float32)),
            rounded(contract_cols(upstream, down_mat)),
        ],
        axis=1,
    )
    shares = lax.psum_scatter(
        terms.astype(jnp.bfloat16), "dp", scatter_dimension=0, tiled=True
    ).astype(jnp.float32)
    own_hidden, own_grad_gate, own_grad_up = swiglu_grads(shares, hidden_units)
    hidden, grad_gate, grad_up = (
        lax.all_gather(own_hidden, "dp", axis=0, tiled=True),
        lax.all_gather(own_grad_gate, "dp", axis=0, tiled=True),
        lax.all_gather(own_grad_up, "dp", axis=0, tiled=True),
    )
    expert_out = jnp.dot(hidden, down_mat, preferred_element_type=jnp.float32).astype(jnp.bfloat16)
    input_grad = (contract_cols(grad_gate, gate_mat) + contract_cols(grad_up, up_mat)).astype(
        jnp.bfloat16
    )
    grad_down = contract_rows(hidden, upstream).astype(jnp.bfloat16)[None]
    grad_gate_w = contract_rows(inputs, grad_gate).astype(jnp.bfloat16)[None]
    grad_up_w = contract_rows(inputs, grad_up).astype(jnp.bfloat16)[None]
    back_out, back_grad = (
        lax.all_to_all(
            lax.all_to_all(
                expert_out.reshape(arrived_shape), "dp", split_axis=1, concat_axis=2, tiled=True
            ),
            "expert",
            split_axis=0,
            concat_axis=0,
            tiled=True,
        ),
        lax.all_to_all(
            lax.all_to_all(
                input_grad.reshape(arrived_shape), "dp", split_axis=1, concat_axis=2, tiled=True
            ),
            "expert",
            split_axis=0,
            concat_axis=0,
            tiled=True,
        ),
    )
    back_out = back_out.reshape(expert_count * slot_count, model_width)
    back_grad = back_grad.reshape(expert_count * slot_count, model_width)
    positions = jnp.arange(tokens.shape[0], dtype=jnp.int32)
    select = chosen[:, None] == positions[None, :]
    weighted = jnp.where(select, scales[:, None], jnp.float32(0.0))
    out_float = back_out.astype(jnp.float32)
    mixed = lax.dot_general(
        weighted,
        out_float,
        (((0,), (0,)), ((), ())),
        precision=lax.Precision.HIGHEST,
        preferred_element_type=jnp.float32,
    ).astype(jnp.bfloat16)
    token_grad = contract_rows(select.astype(jnp.bfloat16), back_grad).astype(jnp.bfloat16)
    gate_grad = jnp.sum(grad_rows.astype(jnp.float32) * out_float, axis=1).reshape(
        1, expert_count, slot_count
    )
    return (mixed, token_grad, gate_grad, grad_gate_w, grad_up_w, grad_down)


def solution(mesh):
    return jax.shard_map(
        body,
        mesh=mesh,
        in_specs=(
            P(("dp", "expert"), None),
            P(("dp", "expert"), None),
            P(("dp", "expert"), None, None),
            P(("dp", "expert"), None, None),
            P("expert", "dp", None),
            P("expert", "dp", None),
            P("expert", None, "dp"),
        ),
        out_specs=(
            P(("dp", "expert"), None),
            P(("dp", "expert"), None),
            P(("dp", "expert"), None, None),
            P("expert", "dp", None),
            P("expert", "dp", None),
            P("expert", None, "dp"),
        ),
        check_vma=False,
    )
```

profile of v0, /device:TPU:0, one launch (start us, length us, event | category | flops | bytes accessed | tf_op | source)
XLA Modules:
  0.0 225.9 jit_solution(14843492705610957919)
XLA Ops:
  9.8 5.1 %copy.75 = bf16[16,4,5120]{0,1,2:T(4,128)(2,1)} copy(bf16[16,4,5120]{2,1,0:T(4,128)(2,1)S(1)} %reshape.46) | data formatting | bytes 1310720 | tf_op jit(solution)/shard_map/reshape | solution.py:47
  14.9 8.0 %reshape.79 = bf16[2,2,81920]{2,1,0:T(2,128)(2,1)} reshape(bf16[5120,4,16]{2,1,0:T(4,128)(2,1)} %bitcast.82) | data formatting | bytes 1310720
  22.9 4.3 %all-to-all-start = ((bf16[2,2,81920]{2,1,0:T(2,128)(2,1)}), bf16[2,2,81920]{2,1,0:T(2,128)(2,1)S(1)}, u32[]{:S(2)}, u32[]{:S(2)}) async-start(bf16[2,2,81920]{2,1,0:T(2,128)(2,1)} %reshape.79), calls=%async_computation | async-start | bytes 1310720 | tf_op jit(solution)/shard_map/all_to_all | solution.py:52
  28.8 5.1 %copy.79 = bf16[16,4,5120]{0,1,2:T(4,128)(2,1)} copy(bf16[16,4,5120]{2,1,0:T(4,128)(2,1)S(1)} %reshape.48) | data formatting | bytes 1310720 | tf_op jit(solution)/shard_map/reshape | solution.py:48
  33.9 7.9 %reshape.77 = bf16[2,2,81920]{2,1,0:T(2,128)(2,1)} reshape(bf16[5120,4,16]{2,1,0:T(4,128)(2,1)} %bitcast.83) | data formatting | bytes 1310720
  45.3 5.4 %reshape.80 = bf16[5120,4,16]{2,1,0:T(4,128)(2,1)} reshape(bf16[2,2,81920]{2,1,0:T(2,128)(2,1)S(1)} %all-to-all-done) | data formatting | bytes 1310720
  50.7 7.6 %copy.89 = bf16[16,4,2,2560]{3,2,0,1:T(2,128)(2,1)S(1)} copy(bf16[16,4,2,2560]{0,1,3,2:T(4,128)(2,1)} %bitcast.84) | data formatting | bytes 1310720 | tf_op jit(solution)/shard_map/all_to_all | solution.py:52
  59.6 6.7 %all-to-all-start.1 = ((bf16[16,8,2560]{2,1,0:T(8,128)(2,1)}), bf16[16,8,2560]{2,1,0:T(8,128)(2,1)S(1)}, u32[]{:S(2)}, u32[]{:S(2)}) async-start(bf16[16,8,2560]{2,1,0:T(8,128)(2,1)} %copy.78), calls=%async_computation.1 | async-start | bytes 1310720 | tf_op jit(solution)/shard_map/all_to_all | solution.py:51
  66.4 5.4 %reshape.78 = bf16[5120,4,16]{2,1,0:T(4,128)(2,1)} reshape(bf16[2,2,81920]{2,1,0:T(2,128)(2,1)S(1)} %all-to-all-done.2) | data formatting | bytes 1310720
  71.8 7.6 %copy.90 = bf16[16,4,2,2560]{3,2,0,1:T(2,128)(2,1)S(1)} copy(bf16[16,4,2,2560]{0,1,3,2:T(4,128)(2,1)} %bitcast.85) | data formatting | bytes 1310720 | tf_op jit(solution)/shard_map/all_to_all | solution.py:59
  83.0 4.8 %all-to-all-start.3 = ((bf16[16,8,2560]{2,1,0:T(8,128)(2,1)}), bf16[16,8,2560]{2,1,0:T(8,128)(2,1)S(1)}, u32[]{:S(2)}, u32[]{:S(2)}) async-start(bf16[16,8,2560]{2,1,0:T(8,128)(2,1)} %copy.82), calls=%async_computation.3 | async-start | bytes 1310720 | tf_op jit(solution)/shard_map/all_to_all | solution.py:58
  90.6 13.8 %all-to-all-done.3 = bf16[16,8,2560]{2,1,0:T(8,128)(2,1)S(1)} async-done(((bf16[16,8,2560]{2,1,0:T(8,128)(2,1)}), bf16[16,8,2560]{2,1,0:T(8,128)(2,1)S(1)}, u32[]{:S(2)}, u32[]{:S(2)}) %all-to-all-start.3) | async-done | bytes 655392 | tf_op jit(solution)/shard_map/all_to_all | solution.py:58
  104.3 3.6 %fusion.38 = bf16[128,768]{1,0:T(8,128)(2,1)S(1)} fusion(bf16[1,768,2560]{2,1,0:T(8,128)(2,1)} %param.15, bf16[16,8,2560]{2,1,0:T(8,128)(2,1)S(1)} %all-to-all-done.3), kind=kOutput, calls=%fused_computation.33 | convolution fusion | flops 503414784 | bytes 4784128 | tf_op jit(solution)/shard_map/dot_general | solution.py:14
  109.6 16.0 %reduce-scatter.2.cloned.1.call-done = bf16[64,2304]{1,0:T(8,128)(2,1)} async-done(((bf16[128,2304]{1,0:T(8,128)(2,1)}), bf16[64,2304]{1,0:T(8,128)(2,1)}) %reduce-scatter.2.cloned.1.call-update) | async-done | bytes 294928 | tf_op jit(solution)/shard_map/reduce_scatter | solution.py:83
  126.8 5.3 %all_gather.11 = bf16[128,768]{1,0:T(8,128)(2,1)S(1)} all-gather(bf16[64,768]{1,0:T(8,128)(2,1)S(1)} %get-tuple-element.51), channel_id=1, replica_groups=mesh['dp'=2,'expert'=16] {'dp'}, dimensions={0}, use_global_device_ids=true | all-gather | bytes 294912 | tf_op jit(solution)/shard_map/all_gather | solution.py:90
  132.1 4.5 %fusion.7 = f32[128,2560]{1,0:T(8,128)} fusion(bf16[128,768]{1,0:T(8,128)(2,1)S(1)} %all_gather.11, bf16[1,2560,768]{2,1,0:T(8,128)(2,1)} %param.14), kind=kOutput, calls=%fused_computation.14 | convolution fusion | flops 503316480 | bytes 5439488 | tf_op jit(solution)/shard_map/dot_general | solution.py:14
  136.7 5.3 %all_gather.10 = bf16[128,768]{1,0:T(8,128)(2,1)S(1)} all-gather(bf16[64,768]{1,0:T(8,128)(2,1)S(1)} %get-tuple-element.49), channel_id=1, replica_groups=mesh['dp'=2,'expert'=16] {'dp'}, dimensions={0}, use_global_device_ids=true | all-gather | bytes 294912 | tf_op jit(solution)/shard_map/all_gather | solution.py:89
  142.0 5.3 %all_gather.9 = bf16[128,768]{1,0:T(8,128)(2,1)S(1)} all-gather(bf16[64,768]{1,0:T(8,128)(2,1)S(1)} %get-tuple-element.50), channel_id=1, replica_groups=mesh['dp'=2,'expert'=16] {'dp'}, dimensions={0}, use_global_device_ids=true | all-gather | bytes 294912 | tf_op jit(solution)/shard_map/all_gather | solution.py:88
  152.5 3.9 %fusion.24 = bf16[16,8,2560]{2,1,0:T(8,128)(2,1)S(1)} fusion(f32[128,2560]{1,0:T(8,128)} %fusion.7, bf16[128,768]{1,0:T(8,128)(2,1)S(1)} %all_gather.10, bf16[1,2560,768]{2,1,0:T(8,128)(2,1)} %param.13), kind=kOutput, calls=%fused_computation.25 | convolution fusion | flops 503971840 | bytes 6094848 | tf_op jit(solution)/shard_map/dot_general | solution.py:14
  159.7 4.3 %all-to-all-start.6 = ((bf16[16,8,2560]{2,0,1:T(8,128)(2,1)}), bf16[16,8,2560]{2,0,1:T(8,128)(2,1)}, u32[]{:S(2)}, u32[]{:S(2)}) async-start(bf16[16,8,2560]{2,0,1:T(8,128)(2,1)} %copy.85), calls=%async_computation.7 | async-start | bytes 1310720 | tf_op jit(solution)/shard_map/all_to_all | solution.py:110
  171.4 5.6 %all-to-all-start.5 = ((bf16[16,4,5120]{2,1,0:T(4,128)(2,1)}), bf16[16,4,5120]{2,1,0:T(4,128)(2,1)S(1)}, u32[]{:S(2)}, u32[]{:S(2)}) async-start(bf16[16,4,5120]{2,1,0:T(4,128)(2,1)} %all_to_all.77), calls=%async_computation.6 | async-start | bytes 1310720 | tf_op jit(solution)/shard_map/all_to_all | solution.py:100
  185.0 8.6 %all-to-all-done.5 = bf16[16,4,5120]{2,1,0:T(4,128)(2,1)S(1)} async-done(((bf16[16,4,5120]{2,1,0:T(4,128)(2,1)}), bf16[16,4,5120]{2,1,0:T(4,128)(2,1)S(1)}, u32[]{:S(2)}, u32[]{:S(2)}) %all-to-all-start.5) | async-done | bytes 655392 | tf_op jit(solution)/shard_map/all_to_all | solution.py:100
  193.6 4.8 %all-to-all-start.7 = ((bf16[16,4,5120]{2,1,0:T(4,128)(2,1)}), bf16[16,4,5120]{2,1,0:T(4,128)(2,1)}, u32[]{:S(2)}, u32[]{:S(2)}) async-start(bf16[16,4,5120]{2,1,0:T(4,128)(2,1)} %copy.87), calls=%async_computation.8 | async-start | bytes 1310720 | tf_op jit(solution)/shard_map/all_to_all | solution.py:109
  210.7 4.4 %all-to-all-done.7 = bf16[16,4,5120]{2,1,0:T(4,128)(2,1)} async-done(((bf16[16,4,5120]{2,1,0:T(4,128)(2,1)}), bf16[16,4,5120]{2,1,0:T(4,128)(2,1)}, u32[]{:S(2)}, u32[]{:S(2)}) %all-to-all-start.7) | async-done | bytes 655392 | tf_op jit(solution)/shard_map/all_to_all | solution.py:109
  (61 shorter events, 58.3 us)
Async XLA Ops:
  7.2 1.3 copy-start
  14.9 12.3 %copy-start.2 = (bf16[128,5120]{1,0:T(8,128)(2,1)S(1)}, bf16[128,5120]{1,0:T(8,128)(2,1)}, u32[]{:S(2)}) copy-start(bf16[128,5120]{1,0:T(8,128)(2,1)} %param.10) | copy-start | bytes 3932164
  22.9 5.3 %copy-start.5 = (f32[1,16,4]{1,2,0:T(4,128)S(1)}, f32[1,16,4]{1,2,0:T(4,128)}, u32[]{:S(2)}) copy-start(f32[1,16,4]{1,2,0:T(4,128)} %param.12) | copy-start | bytes 772
  22.9 18.9 %all-to-all-start = ((bf16[2,2,81920]{2,1,0:T(2,128)(2,1)}), bf16[2,2,81920]{2,1,0:T(2,128)(2,1)S(1)}, u32[]{:S(2)}, u32[]{:S(2)}) async-start(bf16[2,2,81920]{2,1,0:T(2,128)(2,1)} %reshape.79), calls=%async_computation | async-start | bytes 1310720 | tf_op jit(solution)/shard_map/all_to_all | solution.py:52
  41.8 17.9 %all-to-all-start.2 = ((bf16[2,2,81920]{2,1,0:T(2,128)(2,1)}), bf16[2,2,81920]{2,1,0:T(2,128)(2,1)S(1)}, u32[]{:S(2)}, u32[]{:S(2)}) async-start(bf16[2,2,81920]{2,1,0:T(2,128)(2,1)} %reshape.77), calls=%async_computation.2 | async-start | bytes 1310720 | tf_op jit(solution)/shard_map/all_to_all | solution.py:59
  59.6 23.3 %all-to-all-start.1 = ((bf16[16,8,2560]{2,1,0:T(8,128)(2,1)}), bf16[16,8,2560]{2,1,0:T(8,128)(2,1)S(1)}, u32[]{:S(2)}, u32[]{:S(2)}) async-start(bf16[16,8,2560]{2,1,0:T(8,128)(2,1)} %copy.78), calls=%async_computation.1 | async-start | bytes 1310720 | tf_op jit(solution)/shard_map/all_to_all | solution.py:51
  83.0 21.4 %all-to-all-start.3 = ((bf16[16,8,2560]{2,1,0:T(8,128)(2,1)}), bf16[16,8,2560]{2,1,0:T(8,128)(2,1)S(1)}, u32[]{:S(2)}, u32[]{:S(2)}) async-start(bf16[16,8,2560]{2,1,0:T(8,128)(2,1)} %copy.82), calls=%async_computation.3 | async-start | bytes 1310720 | tf_op jit(solution)/shard_map/all_to_all | solution.py:58
  87.7 37.8 %reduce-scatter.2.cloned.1.call-start = ((), (), s32[]{:S(2)}) async-start(), calls=%async_computation.9 | async-start | bytes 884736 | tf_op jit(solution)/shard_map/reduce_scatter | solution.py:83
  104.3 3.6 %copy-start.4 = (bf16[1,2560,768]{2,1,0:T(8,128)(2,1)S(1)}, bf16[1,2560,768]{2,1,0:T(8,128)(2,1)}, u32[]{:S(2)}) copy-start(bf16[1,2560,768]{2,1,0:T(8,128)(2,1)} %param.13) | copy-start | bytes 11796484
  125.6 21.7 %copy-start.3 = (bf16[1,768,2560]{2,1,0:T(8,128)(2,1)S(1)}, bf16[1,768,2560]{2,1,0:T(8,128)(2,1)}, u32[]{:S(2)}) copy-start(bf16[1,768,2560]{2,1,0:T(8,128)(2,1)} %param.15) | copy-start | bytes 11796484
  149.0 10.8 %all-to-all-start.4 = ((bf16[16,8,2560]{2,0,1:T(8,128)(2,1)}), bf16[16,8,2560]{2,0,1:T(8,128)(2,1)S(1)}, u32[]{:S(2)}, u32[]{:S(2)}) async-start(bf16[16,8,2560]{2,0,1:T(8,128)(2,1)} %copy.83), calls=%async_computation.5 | async-start | bytes 1310720 | tf_op jit(solution)/shard_map/all_to_all | solution.py:101
  159.7 11.6 %all-to-all-start.6 = ((bf16[16,8,2560]{2,0,1:T(8,128)(2,1)}), bf16[16,8,2560]{2,0,1:T(8,128)(2,1)}, u32[]{:S(2)}, u32[]{:S(2)}) async-start(bf16[16,8,2560]{2,0,1:T(8,128)(2,1)} %copy.85), calls=%async_computation.7 | async-start | bytes 1310720 | tf_op jit(solution)/shard_map/all_to_all | solution.py:110
  171.4 22.2 %all-to-all-start.5 = ((bf16[16,4,5120]{2,1,0:T(4,128)(2,1)}), bf16[16,4,5120]{2,1,0:T(4,128)(2,1)S(1)}, u32[]{:S(2)}, u32[]{:S(2)}) async-start(bf16[16,4,5120]{2,1,0:T(4,128)(2,1)} %all_to_all.77), calls=%async_computation.6 | async-start | bytes 1310720 | tf_op jit(solution)/shard_map/all_to_all | solution.py:100
  193.6 21.5 %all-to-all-start.7 = ((bf16[16,4,5120]{2,1,0:T(4,128)(2,1)}), bf16[16,4,5120]{2,1,0:T(4,128)(2,1)}, u32[]{:S(2)}, u32[]{:S(2)}) async-start(bf16[16,4,5120]{2,1,0:T(4,128)(2,1)} %copy.87), calls=%async_computation.8 | async-start | bytes 1310720 | tf_op jit(solution)/shard_map/all_to_all | solution.py:109
  204.7 14.3 %copy-start.1 = (bf16[128,5120]{1,0:T(8,128)(2,1)S(1)}, bf16[128,5120]{1,0:T(8,128)(2,1)}, u32[]{:S(2)}) copy-start(bf16[128,5120]{1,0:T(8,128)(2,1)} %param.9) | copy-start | bytes 3932164
Sparse Core Ops, SparseCore 0:
  109.7 15.8 reduce-scatter.1
where the time goes:
time: 227 us; the launch traced here: 226 us
  local copies, waits for them, and re-layouts  75.5 us (33%)
  waiting for transfers between devices  50.1 us (22%)
  starting transfers between devices  37.6 us (17%)
  matrix products  29.7 us (13%)
  blocking collectives  15.9 us (7%)
  between operations  14.3 us (6%)
  other arithmetic  2.87 us (1%)
    unnamed x19, local copies, waits for them, and re-layouts  28.6 us
    reduce_scatter x1, waiting for transfers between devices, body(): lax.psum_scatter(terms.astype(jnp.bfloat16), 'dp', scatter_dimension=0, t...  16 us
    all_to_all x1, waiting for transfers between devices, body(): lax.all_to_all(lax.all_to_all(outgoing[1], 'dp', split_axis=2, concat_axi...  13.8 us
    dot_general x3, matrix products, contract_cols(): lax.dot_general(left, right, (((1,), (1,)), ((), ())), preferred_element_...  12.1 us
    dot_general x4, matrix products, contract_rows(): lax.dot_general(left, right, (((0,), (0,)), ((), ())), preferred_element_...  11.1 us
    all_to_all x3, local copies, waits for them, and re-layouts, body(): lax.all_to_all(outgoing[1], 'dp', split_axis=2, concat_axis=1, tiled=True)  8.91 us
    all_to_all x3, local copies, waits for them, and re-layouts, body(): lax.all_to_all(outgoing[0], 'dp', split_axis=2, concat_axis=1, tiled=True)  8.91 us
    all_to_all x1, waiting for transfers between devices, body(): lax.all_to_all(lax.all_to_all(expert_out.reshape(arrived_shape), 'dp', sp...  8.62 us
  transfers between devices with their start and end apart: 9, of which 7 were waited for; matrix products, arithmetic and copies ran while one was open for 31% of the time, Pallas kernels for 0%

commit v1 on v0

v1 whole, which is shorter than its diff:
```python
import functools

import jax
import jax.numpy as jnp
from jax import lax
from jax.experimental import pallas as pl
from jax.experimental.pallas import tpu as pltpu
from jax.sharding import PartitionSpec as P

F32 = jnp.float32
BF16 = jnp.bfloat16
MIB = 1024 * 1024


def dot(left, right, dims=((1,), (0,)), precision=None):
    return lax.dot_general(left, right, (dims, ((), ())), precision=precision, preferred_element_type=F32)


def exact_dot(left, right, dims=((1,), (0,))):
    return dot(left, right, dims, lax.Precision.HIGHEST)


def iota(shape, axis):
    return lax.broadcasted_iota(jnp.int32, shape, axis)


def block_of(width, limit):
    best = 128
    for size in range(128, limit + 1, 128):
        if width % size == 0:
            best = size
    return best


def params(mib):
    return pltpu.CompilerParams(vmem_limit_bytes=mib * MIB)


def spread(values, slots):
    experts = values.shape[0]
    rows = experts * slots * 2
    owner = (iota((rows, experts), 0) // (2 * slots) == iota((rows, experts), 1)).astype(F32)
    wide = exact_dot(owner, values)
    mine = iota((rows, slots), 0) % slots == iota((rows, slots), 1)
    return jnp.sum(jnp.where(mine, wide, 0.0), axis=1, keepdims=True)


def second_half(shape, slots):
    return iota(shape, 0) % (2 * slots) >= slots


def pack_kernel(slots, picks_ref, gates_ref, tokens_ref, cot_ref, out_ref):
    count = tokens_ref.shape[0]
    rows = out_ref.shape[0]
    chosen = spread(picks_ref[0].astype(F32), slots).astype(jnp.int32)
    scale = spread(gates_ref[0], slots)
    late = second_half((rows, count), slots)
    hit = chosen == iota((rows, count), 1)
    from_tokens = jnp.where(hit & ~late, 1.0, 0.0).astype(BF16)
    from_cot = jnp.where(hit & late, 1.0, 0.0).astype(BF16)
    picked = dot(from_tokens, tokens_ref[...]) + dot(from_cot, cot_ref[...])
    factor = jnp.where(second_half((rows, 1), slots), scale, 1.0)
    out_ref[...] = (picked * factor).astype(BF16)


def pack(tokens, cotangent, picks, gates, n_dp):
    experts, slots = picks.shape[1:]
    count, width = tokens.shape
    rows = experts * slots * 2
    part = width // n_dp
    cols = block_of(part, 1280)
    steps = part // cols
    return pl.pallas_call(
        functools.partial(pack_kernel, slots),
        grid=(n_dp, steps),
        in_specs=[
            pl.BlockSpec((1, experts, slots), lambda k, b: (0, 0, 0)),
            pl.BlockSpec((1, experts, slots), lambda k, b: (0, 0, 0)),
            pl.BlockSpec((count, cols), lambda k, b: (0, k * steps + b)),
            pl.BlockSpec((count, cols), lambda k, b: (0, k * steps + b)),
        ],
        out_specs=pl.BlockSpec((rows, cols), lambda k, b: (k, b)),
        out_shape=jax.ShapeDtypeStruct((n_dp * rows, part), BF16),
        compiler_params=params(16),
        name="pack_rows",
    )(picks, gates, tokens, cotangent)


def split_rows(packed, slots, late):
    total = packed.shape[0]
    group = min(total, 256)
    kept = group // 2
    source = iota((kept, group), 0) // slots * (2 * slots) + iota((kept, group), 0) % slots + late * slots
    take = jnp.where(source == iota((kept, group), 1), 1.0, 0.0).astype(BF16)
    parts = [dot(take, packed[g : g + group]).astype(BF16) for g in range(0, total, group)]
    return parts[0] if len(parts) == 1 else jnp.concatenate(parts, axis=0)


def merge_rows(first, second, slots):
    shown = first if first is not None else second
    total = shown.shape[0]
    kept = min(total, 128)
    group = 2 * kept
    result = []
    for g in range(0, total, kept):
        acc = None
        for late, value in enumerate((first, second)):
            if value is None:
                continue
            source = iota((group, kept), 1) // slots * (2 * slots) + iota((group, kept), 1) % slots + late * slots
            put = jnp.where(source == iota((group, kept), 0), 1.0, 0.0).astype(BF16)
            term = dot(put, value[g : g + kept])
            acc = term if acc is None else acc + term
        result.append(acc.astype(BF16))
    return result[0] if len(result) == 1 else jnp.concatenate(result, axis=0)


def terms_kernel(slots, packed_ref, gate_ref, up_ref, down_ref, out_ref, acc_ref):
    hidden = gate_ref.shape[2]
    step = pl.program_id(0)
    packed = packed_ref[...]
    rows_in = split_rows(packed, slots, 0)
    rows_up = split_rows(packed, slots, 1)

    @pl.when(step == 0)
    def _():
        acc_ref[...] = jnp.zeros_like(acc_ref)

    acc_ref[:, :hidden] += dot(rows_in, gate_ref[0])
    acc_ref[:, hidden : 2 * hidden] += dot(rows_in, up_ref[0])
    acc_ref[:, 2 * hidden :] += dot(rows_up, down_ref[0], ((1,), (1,)))

    @pl.when(step == pl.num_programs(0) - 1)
    def _():
        out_ref[...] = acc_ref[...].astype(BF16)


def terms(packed, w_gate, w_up, w_down, slots):
    total, part = packed.shape
    hidden = w_gate.shape[2]
    cols = block_of(part, 640)
    rows = total // 2
    return pl.pallas_call(
        functools.partial(terms_kernel, slots),
        grid=(part // cols,),
        in_specs=[
            pl.BlockSpec((total, cols), lambda b: (0, b)),
            pl.BlockSpec((1, cols, hidden), lambda b: (0, b, 0)),
            pl.BlockSpec((1, cols, hidden), lambda b: (0, b, 0)),
            pl.BlockSpec((1, hidden, cols), lambda b: (0, 0, b)),
        ],
        out_specs=pl.BlockSpec((rows, 3 * hidden), lambda b: (0, 0)),
        out_shape=jax.ShapeDtypeStruct((rows, 3 * hidden), BF16),
        scratch_shapes=[pltpu.VMEM((rows, 3 * hidden), F32)],
        compiler_params=params(48),
        cost_estimate=pl.CostEstimate(
            flops=2 * rows * part * 3 * hidden, bytes_accessed=6 * part * hidden, transcendentals=0
        ),
        name="partial_products",
    )(packed, w_gate, w_up, w_down)


def results_kernel(slots, count, *refs):
    term_refs = refs[:count]
    gate_ref, up_ref, down_ref, out_ref, acts_ref, own_ref = refs[count:]
    hidden = gate_ref.shape[2]

    @pl.when(pl.program_id(0) == 0)
    def _():
        total = term_refs[0][...].astype(F32)
        for ref in term_refs[1:]:
            total = total + ref[...].astype(F32)
        gate_sum = total[:, :hidden]
        up_sum = total[:, hidden : 2 * hidden]
        back_sum = total[:, 2 * hidden :]
        sig = jax.nn.sigmoid(gate_sum)
        silu = gate_sum * sig
        act = (silu * up_sum).astype(BF16)
        grad_up = (back_sum * silu).astype(BF16)
        grad_gate = (back_sum * up_sum * sig * (1.0 + gate_sum * (1.0 - sig))).astype(BF16)
        own_ref[:, :hidden] = act
        own_ref[:, hidden : 2 * hidden] = grad_gate
        own_ref[:, 2 * hidden :] = grad_up
        acts_ref[:, :hidden] = merge_rows(None, act, slots)
        acts_ref[:, hidden : 2 * hidden] = merge_rows(grad_gate, None, slots)
        acts_ref[:, 2 * hidden :] = merge_rows(grad_up, None, slots)

    out = dot(own_ref[:, :hidden], down_ref[0]).astype(BF16)
    grad = (
        dot(own_ref[:, hidden : 2 * hidden], gate_ref[0], ((1,), (1,)))
        + dot(own_ref[:, 2 * hidden :], up_ref[0], ((1,), (1,)))
    ).astype(BF16)
    out_ref[...] = merge_rows(out, grad, slots)


def results(shares, w_gate, w_up, w_down, slots):
    rows = shares[0].shape[0]
    part, hidden = w_gate.shape[1:]
    cols = block_of(part, 640)
    whole = pl.BlockSpec((rows, 3 * hidden), lambda b: (0, 0))
    return pl.pallas_call(
        functools.partial(results_kernel, slots, len(shares)),
        grid=(part // cols,),
        in_specs=[whole] * len(shares)
        + [
            pl.BlockSpec((1, cols, hidden), lambda b: (0, b, 0)),
            pl.BlockSpec((1, cols, hidden), lambda b: (0, b, 0)),
            pl.BlockSpec((1, hidden, cols), lambda b: (0, 0, b)),
        ],
        out_specs=[
            pl.BlockSpec((2 * rows, cols), lambda b: (0, b)),
            pl.BlockSpec((2 * rows, 3 * hidden), lambda b: (0, 0)),
        ],
        out_shape=[
            jax.ShapeDtypeStruct((2 * rows, part), BF16),
            jax.ShapeDtypeStruct((2 * rows, 3 * hidden), BF16),
        ],
        scratch_shapes=[pltpu.VMEM((rows, 3 * hidden), BF16)],
        compiler_params=params(48),
        cost_estimate=pl.CostEstimate(
            flops=2 * rows * part * 3 * hidden, bytes_accessed=6 * part * hidden, transcendentals=rows * hidden
        ),
        name="expert_rows",
    )(*shares, w_gate, w_up, w_down)


def weights_kernel(packed_ref, acts_ref, gate_ref, up_ref, down_ref):
    hidden = gate_ref.shape[2]
    packed = packed_ref[...]
    gate_ref[0] = dot(packed, acts_ref[:, hidden : 2 * hidden], ((0,), (0,))).astype(BF16)
    up_ref[0] = dot(packed, acts_ref[:, 2 * hidden :], ((0,), (0,))).astype(BF16)
    down_ref[0] = dot(acts_ref[:, :hidden], packed, ((0,), (0,))).astype(BF16)


def weight_grads(packed, acts):
    total, part = packed.shape
    hidden = acts.shape[1] // 3
    cols = block_of(part, 640)
    return pl.pallas_call(
        weights_kernel,
        grid=(part // cols,),
        in_specs=[
            pl.BlockSpec((total, cols), lambda b: (0, b)),
            pl.BlockSpec((total, 3 * hidden), lambda b: (0, 0)),
        ],
        out_specs=[
            pl.BlockSpec((1, cols, hidden), lambda b: (0, b, 0)),
            pl.BlockSpec((1, cols, hidden), lambda b: (0, b, 0)),
            pl.BlockSpec((1, hidden, cols), lambda b: (0, 0, b)),
        ],
        out_shape=[
            jax.ShapeDtypeStruct((1, part, hidden), BF16),
            jax.ShapeDtypeStruct((1, part, hidden), BF16),
            jax.ShapeDtypeStruct((1, hidden, part), BF16),
        ],
        compiler_params=params(48),
        cost_estimate=pl.CostEstimate(
            flops=2 * total * part * 3 * hidden, bytes_accessed=6 * part * hidden, transcendentals=0
        ),
        name="weight_grads",
    )(packed, acts)


def combine_kernel(slots, picks_ref, gates_ref, back_ref, cot_ref, mixed_ref, grad_ref, gate_grad_ref, acc_ref):
    count = cot_ref.shape[0]
    rows = back_ref.shape[0]
    experts = picks_ref.shape[1]
    first = (pl.program_id(0) == 0) & (pl.program_id(1) == 0)
    last = (pl.program_id(0) == pl.num_programs(0) - 1) & (pl.program_id(1) == pl.num_programs(1) - 1)
    chosen = spread(picks_ref[0].astype(F32), slots).astype(jnp.int32)
    scale = spread(gates_ref[0], slots)
    late = second_half((rows, count), slots)
    hit = chosen == iota((rows, count), 1)
    back = back_ref[...]
    ones = jnp.where(hit & late, 1.0, 0.0).astype(BF16)
    rest = jnp.where(hit & ~late, scale, 0.0)
    mixed = None
    for _ in range(3):
        piece = rest.astype(BF16)
        rest = rest - piece.astype(F32)
        term = dot(piece, back, ((0,), (0,)))
        mixed = term if mixed is None else mixed + term
    mixed_ref[...] = mixed.astype(BF16)
    grad_ref[...] = dot(ones, back, ((0,), (0,))).astype(BF16)

    @pl.when(first)
    def _():
        acc_ref[...] = jnp.zeros_like(acc_ref)

    acc_ref[...] += dot(back, cot_ref[...], ((1,), (1,)))

    @pl.when(last)
    def _():
        values = jnp.sum(jnp.where(hit & ~late, acc_ref[...], 0.0), axis=1, keepdims=True)
        mine = iota((rows, slots), 0) % slots == iota((rows, slots), 1)
        owner = (iota((rows, experts), 0) // (2 * slots) == iota((rows, experts), 1)).astype(F32)
        gate_grad_ref[0] = exact_dot(owner, jnp.where(mine, values, 0.0), ((0,), (0,)))


def combine(back, cotangent, picks, gates, n_dp):
    experts, slots = picks.shape[1:]
    count, width = cotangent.shape
    rows = experts * slots * 2
    part = width // n_dp
    cols = block_of(part, 1280)
    steps = part // cols
    return pl.pallas_call(
        functools.partial(combine_kernel, slots),
        grid=(n_dp, steps),
        in_specs=[
            pl.BlockSpec((1, experts, slots), lambda k, b: (0, 0, 0)),
            pl.BlockSpec((1, experts, slots), lambda k, b: (0, 0, 0)),
            pl.BlockSpec((rows, cols), lambda k, b: (k, b)),
            pl.BlockSpec((count, cols), lambda k, b: (0, k * steps + b)),
        ],
        out_specs=[
            pl.BlockSpec((count, cols), lambda k, b: (0, k * steps + b)),
            pl.BlockSpec((count, cols), lambda k, b: (0, k * steps + b)),
            pl.BlockSpec((1, experts, slots), lambda k, b: (0, 0, 0)),
        ],
        out_shape=[
            jax.ShapeDtypeStruct((count, width), BF16),
            jax.ShapeDtypeStruct((count, width), BF16),
            jax.ShapeDtypeStruct((1, experts, slots), F32),
        ],
        scratch_shapes=[pltpu.VMEM((rows, count), F32)],
        compiler_params=params(16),
        name="combine_rows",
    )(picks, gates, back, cotangent)


def body(n_dp, tokens, cotangent, picks, gates, w_gate, w_up, w_down):
    slots = picks.shape[2]
    everyone = ("dp", "expert")
    outgoing = pack(tokens, cotangent, picks, gates, n_dp)
    packed = lax.all_to_all(outgoing, everyone, split_axis=0, concat_axis=0, tiled=True)
    own = terms(packed, w_gate, w_up, w_down, slots)
    shares = [own] + [
        lax.ppermute(own, "dp", [(i, (i + shift) % n_dp) for i in range(n_dp)]) for shift in range(1, n_dp)
    ]
    if n_dp > 2:
        shares = [functools.reduce(jnp.add, [share.astype(F32) for share in shares])]
    returning, acts = results(shares, w_gate, w_up, w_down, slots)
    back = lax.all_to_all(returning, everyone, split_axis=0, concat_axis=0, tiled=True)
    grad_gate_w, grad_up_w, grad_down = weight_grads(packed, acts)
    mixed, token_grad, gate_grad = combine(back, cotangent, picks, gates, n_dp)
    return mixed, token_grad, gate_grad, grad_gate_w, grad_up_w, grad_down


def solution(mesh):
    rows = P(("dp", "expert"), None)
    lists = P(("dp", "expert"), None, None)
    tall = P("expert", "dp", None)
    wide = P("expert", None, "dp")
    return jax.shard_map(
        functools.partial(body, mesh.shape["dp"]),
        mesh=mesh,
        in_specs=(rows, rows, lists, lists, tall, tall, wide),
        out_specs=(rows, rows, lists, tall, tall, wide),
        check_vma=False,
    )
```

time: 227 us -> 123 us (0.54)
  local copies, waits for them, and re-layouts: 75.5 us -> 8.4 us
  starting transfers between devices: 37.6 us -> 3.75 us
  Pallas kernels: 0 us -> 30.9 us
  matrix products: 29.7 us -> 0 us
  blocking collectives: 15.9 us -> 39.9 us
  between operations: 14.3 us -> 0.68 us
  waiting for transfers between devices: 50.1 us -> 38.7 us
  other arithmetic: 2.87 us -> 0 us
    all_to_all x0 -> x1, blocking collectives: none -> 39.9 us  [body(): lax.all_to_all(outgoing, everyone, split_axis=0, concat_axis=0, tiled=True)]
    all_to_all x8 -> x1, starting transfers between devices: 37.6 us -> 2.67 us  [body(): lax.all_to_all(returning, everyone, split_axis=0, concat_axis=0, tiled=True)]
    pallas_call x0 -> x5, Pallas kernels: none -> 30.9 us  [the longest x1 9.52 us: results(): pl.pallas_call(functools.partial(results_kernel, slots, len(shares)), gri...]
    all_to_all x11 -> x0, local copies, waits for them, and re-layouts: 30.4 us -> none  [the longest x3 8.91 us: body(): lax.all_to_all(outgoing[1], 'dp', split_axis=2, concat_axis=1, tiled=True)]
    dot_general x11 -> x0, matrix products: 29.7 us -> none  [the longest x3 12.1 us: contract_cols(): lax.dot_general(left, right, (((1,), (1,)), ((), ())), preferred_element_...]
    unnamed x19, local copies, waits for them, and re-layouts: 28.6 us -> 8.4 us
    reduce_scatter x1 -> x0, waiting for transfers between devices: 16 us -> none  [body(): lax.psum_scatter(terms.astype(jnp.bfloat16), 'dp', scatter_dimension=0, t...]
    all_gather x3 -> x0, blocking collectives: 15.9 us -> none  [the longest x1 5.29 us: body(): lax.all_gather(own_grad_up, 'dp', axis=0, tiled=True)]
  transfers between devices with their start and end apart: 9 -> 2, of which waited for: 7 -> 2; matrix products, arithmetic and copies ran while one was open for 31% -> 0% of each run, Pallas kernels for 0% -> 5%
where the time goes in v1:
time: 123 us; the launch traced here: 122 us
  blocking collectives  39.9 us (32%)
  waiting for transfers between devices  38.7 us (31%)
  Pallas kernels  30.9 us (25%)
  local copies, waits for them, and re-layouts  8.4 us (7%)
  starting transfers between devices  3.75 us (3%)
    all_to_all x1, blocking collectives, body(): lax.all_to_all(outgoing, everyone, split_axis=0, concat_axis=0, tiled=True)  39.9 us
    all_to_all x1, waiting for transfers between devices, body(): lax.all_to_all(returning, everyone, split_axis=0, concat_axis=0, tiled=True)  24.3 us
    ppermute x1, waiting for transfers between devices, body(): lax.ppermute(own, 'dp', [(i, (i + shift) % n_dp) for i in range(n_dp)])  14.4 us
    pallas_call x1, Pallas kernels, results(): pl.pallas_call(functools.partial(results_kernel, slots, len(shares)), gri...  9.52 us
    unnamed x19, local copies, waits for them, and re-layouts  8.4 us
    pallas_call x1, Pallas kernels, terms(): pl.pallas_call(functools.partial(terms_kernel, slots), grid=(part // cols...  6.9 us
    pallas_call x1, Pallas kernels, combine(): pl.pallas_call(functools.partial(combine_kernel, slots), grid=(n_dp, step...  5.88 us
    pallas_call x1, Pallas kernels, weight_grads(): pl.pallas_call(weights_kernel, grid=(part // cols,), in_specs=[pl.BlockSp...  5.87 us
  transfers between devices with their start and end apart: 2, of which 2 were waited for; matrix products, arithmetic and copies ran while one was open for 0% of the time, Pallas kernels for 5%

profile of v1, /device:TPU:0, one launch (start us, length us, event | category | flops | bytes accessed | tf_op | source)
XLA Modules:
  0.0 122.3 jit_solution(17576009517059434883)
XLA Ops:
  0.6 0.8 copy.15.picks_ref
  1.4 0.8 copy.16.gates_ref
  2.1 0.0 copy-start.1
  2.2 1.3 %copy-done.1 = bf16[128,5120]{1,0:T(8,128)(2,1)S(1)} copy-done((bf16[128,5120]{1,0:T(8,128)(2,1)S(1)}, bf16[128,5120]{1,0:T(8,128)(2,1)}, u32[]{:S(2)}) %copy-start.1) | copy-done | bytes 1310744
  3.5 0.0 copy-start.5
  3.5 1.3 %copy-done.5 = bf16[128,5120]{1,0:T(8,128)(2,1)S(1)} copy-done((bf16[128,5120]{1,0:T(8,128)(2,1)S(1)}, bf16[128,5120]{1,0:T(8,128)(2,1)}, u32[]{:S(2)}) %copy-start.5) | copy-done | bytes 1310744
  4.8 2.7 %pack_rows.1 = bf16[256,2560]{1,0:T(8,128)(2,1)S(1)} custom-call(s32[1,16,4]{2,1,0:T(8,128)S(1)} %copy.15.picks_ref, f32[1,16,4]{2,1,0:T(8,128)S(1)} %copy.16.gates_ref, bf16[128,5120]{1,0:T(8,128)(2,1)S(1)} %copy-done.5, bf16[128,5120]{1,0:T(8,128)(2,1)S(1)} %copy-done.1), custom_call_target="tpu_custom_call" | custom-call | tf_op jit(solution)/shard_map/pack_rows/pallas_call | solution.py:73
  7.5 39.9 %all_to_all.22 = bf16[32,8,2560]{2,1,0:T(8,128)(2,1)S(1)} all-to-all(bf16[32,8,2560]{2,1,0:T(8,128)(2,1)S(1)} %bitcast.5), channel_id=1, replica_groups=mesh['dp'=2,'expert'=16] {'dp','expert'}, dimensions={0} | all-to-all | bytes 2621440 | tf_op jit(solution)/shard_map/all_to_all | solution.py:336
  47.4 0.0 copy-done
  47.4 6.9 %partial_products.1.refs_0_ = bf16[128,2304]{1,0:T(8,128)(2,1)S(1)} custom-call(bf16[256,2560]{1,0:T(8,128)(2,1)S(1)} %bitcast.6, bf16[1,2560,768]{2,1,0:T(8,128)(2,1)S(1)} %copy-done, bf16[1,2560,768]{2,1,0:T(8,128)(2,1)} %refs_3_.1, bf16[1,768,2560]{2,1,0:T(8,128)(2,1)} %refs_4_.1), custom_call_target="tpu_custom_call" | custom-call | flops 1509949440 | bytes 11796480 | tf_op jit(solution)/shard_map/partial_products/pallas_call | solution.py:143
  54.3 0.0 copy-done.3
  54.3 1.1 collective-permute-start
  55.4 14.4 %collective-permute-done.refs_1_ = bf16[128,2304]{1,0:T(8,128)(2,1)S(1)} collective-permute-done((bf16[128,2304]{1,0:T(8,128)(2,1)S(1)}, bf16[128,2304]{1,0:T(8,128)(2,1)S(1)}, u32[]{:S(2)}, u32[]{:S(2)}) %collective-permute-start) | collective-permute-done | bytes 589856 | tf_op jit(solution)/shard_map/ppermute | solution.py:339
  69.8 9.5 %expert_rows.1 = (bf16[256,2560]{1,0:T(8,128)(2,1)}, bf16[256,2304]{1,0:T(8,128)(2,1)S(1)}) custom-call(bf16[128,2304]{1,0:T(8,128)(2,1)S(1)} %partial_products.1.refs_0_, bf16[128,2304]{1,0:T(8,128)(2,1)S(1)} %collective-permute-done.refs_1_, bf16[1,2560,768]{2,1,0:T(8,128)(2,1)} %refs_2_.1, bf16[1,2560,768]{2,1,0:T(8,128)(2,1)} %refs_3_.1, ...), custom_call_target="tpu_custom_call" | custom-call | flops 1509949440 | bytes 11796480 | tf_op jit(solution)/shard_map/expert_rows/pallas_call | solution.py:201
  79.3 1.0 copy-done.6
  80.3 2.7 %all-to-all-start.1 = ((bf16[32,8,2560]{2,1,0:T(8,128)(2,1)}), bf16[32,8,2560]{2,1,0:T(8,128)(2,1)S(1)}, u32[]{:S(2)}, u32[]{:S(2)}) async-start(bf16[32,8,2560]{2,1,0:T(8,128)(2,1)} %bitcast.2), calls=%async_computation.1 | async-start | bytes 2621440 | tf_op jit(solution)/shard_map/all_to_all | solution.py:344
  83.0 0.0 copy-start.4
  83.0 1.3 %copy-done.4 = bf16[32,8,2560]{2,1,0:T(8,128)(2,1)S(1)} copy-done((bf16[32,8,2560]{2,1,0:T(8,128)(2,1)S(1)}, bf16[32,8,2560]{2,1,0:T(8,128)(2,1)}, u32[]{:S(2)}) %copy-start.4) | copy-done | bytes 1310744
  84.3 1.3 %copy-done.7 = bf16[256,2304]{1,0:T(8,128)(2,1)S(1)} copy-done((bf16[256,2304]{1,0:T(8,128)(2,1)S(1)}, bf16[256,2304]{1,0:T(8,128)(2,1)}, u32[]{:S(2)}) %copy-start.7) | copy-done | bytes 1179672
  85.6 5.9 %weight_grads.1 = (bf16[1,2560,768]{2,1,0:T(8,128)(2,1)}, bf16[1,2560,768]{2,1,0:T(8,128)(2,1)}, bf16[1,768,2560]{2,1,0:T(8,128)(2,1)}) custom-call(bf16[256,2560]{1,0:T(8,128)(2,1)S(1)} %bitcast.7, bf16[256,2304]{1,0:T(8,128)(2,1)S(1)} %copy-done.7), custom_call_target="tpu_custom_call" | custom-call | flops 3019898880 | bytes 11796480 | tf_op jit(solution)/shard_map/weight_grads/pallas_call | solution.py:239
  91.5 24.3 %all-to-all-done.1 = bf16[32,8,2560]{2,1,0:T(8,128)(2,1)S(1)} async-done(((bf16[32,8,2560]{2,1,0:T(8,128)(2,1)}), bf16[32,8,2560]{2,1,0:T(8,128)(2,1)S(1)}, u32[]{:S(2)}, u32[]{:S(2)}) %all-to-all-start.1) | async-done | bytes 1310752 | tf_op jit(solution)/shard_map/all_to_all | solution.py:344
  115.8 0.0 copy-done.2
  115.8 5.9 %combine_rows.1 = (bf16[128,5120]{1,0:T(8,128)(2,1)}, bf16[128,5120]{1,0:T(8,128)(2,1)}, f32[1,16,4]{2,1,0:T(8,128)S(1)}) custom-call(s32[1,16,4]{2,1,0:T(8,128)S(1)} %copy.15.picks_ref, f32[1,16,4]{2,1,0:T(8,128)S(1)} %copy.16.gates_ref, bf16[256,2560]{1,0:T(8,128)(2,1)S(1)} %bitcast.4, bf16[128,5120]{1,0:T(8,128)(2,1)S(1)} %copy-done.2), custom_call_target="tpu_custom_call" | custom-call | tf_op jit(solution)/shard_map/combine_rows/pallas_call | solution.py:307
  121.6 0.7 copy.17
  (5 shorter events, 0.0 us)
Async XLA Ops:
  2.1 1.3 %copy-start.1 = (bf16[128,5120]{1,0:T(8,128)(2,1)S(1)}, bf16[128,5120]{1,0:T(8,128)(2,1)}, u32[]{:S(2)}) copy-start(bf16[128,5120]{1,0:T(8,128)(2,1)} %cot_ref.3) | copy-start | bytes 3932164
  3.5 1.3 %copy-start.5 = (bf16[128,5120]{1,0:T(8,128)(2,1)S(1)}, bf16[128,5120]{1,0:T(8,128)(2,1)}, u32[]{:S(2)}) copy-start(bf16[128,5120]{1,0:T(8,128)(2,1)} %tokens_ref.1) | copy-start | bytes 3932164
  4.8 42.6 %copy-start = (bf16[1,2560,768]{2,1,0:T(8,128)(2,1)S(1)}, bf16[1,2560,768]{2,1,0:T(8,128)(2,1)}, u32[]{:S(2)}) copy-start(bf16[1,2560,768]{2,1,0:T(8,128)(2,1)} %refs_2_.1) | copy-start | bytes 11796484
  47.4 6.9 %copy-start.3 = (bf16[32,8,2560]{2,1,0:T(8,128)(2,1)}, bf16[32,8,2560]{2,1,0:T(8,128)(2,1)S(1)}, u32[]{:S(2)}) copy-start(bf16[32,8,2560]{2,1,0:T(8,128)(2,1)S(1)} %all_to_all.22) | copy-start | bytes 3932164
  54.3 15.5 %collective-permute-start = (bf16[128,2304]{1,0:T(8,128)(2,1)S(1)}, bf16[128,2304]{1,0:T(8,128)(2,1)S(1)}, u32[]{:S(2)}, u32[]{:S(2)}) collective-permute-start(bf16[128,2304]{1,0:T(8,128)(2,1)S(1)} %partial_products.1.refs_0_), channel_id=1, source_target_pairs={{0,16},{16,0},{1,17},{17,1},{2,18},{18,2},{3,19},{19,3},{4,20},{20... | collective-permute-start | bytes 1769480 | tf_op jit(solution)/shard_map/ppermute | solution.py:339
  79.3 1.0 copy-start.6
  80.3 35.4 %all-to-all-start.1 = ((bf16[32,8,2560]{2,1,0:T(8,128)(2,1)}), bf16[32,8,2560]{2,1,0:T(8,128)(2,1)S(1)}, u32[]{:S(2)}, u32[]{:S(2)}) async-start(bf16[32,8,2560]{2,1,0:T(8,128)(2,1)} %bitcast.2), calls=%async_computation.1 | async-start | bytes 2621440 | tf_op jit(solution)/shard_map/all_to_all | solution.py:344
  83.0 1.3 %copy-start.4 = (bf16[32,8,2560]{2,1,0:T(8,128)(2,1)S(1)}, bf16[32,8,2560]{2,1,0:T(8,128)(2,1)}, u32[]{:S(2)}) copy-start(bf16[32,8,2560]{2,1,0:T(8,128)(2,1)} %copy-done.3) | copy-start | bytes 3932164
  84.3 1.3 %copy-start.7 = (bf16[256,2304]{1,0:T(8,128)(2,1)S(1)}, bf16[256,2304]{1,0:T(8,128)(2,1)}, u32[]{:S(2)}) copy-start(bf16[256,2304]{1,0:T(8,128)(2,1)} %copy-done.6) | copy-start | bytes 3538948
  85.6 30.2 %copy-start.2 = (bf16[128,5120]{1,0:T(8,128)(2,1)S(1)}, bf16[128,5120]{1,0:T(8,128)(2,1)}, u32[]{:S(2)}) copy-start(bf16[128,5120]{1,0:T(8,128)(2,1)} %cot_ref.3) | copy-start | bytes 3932164

commit v2 on v0

v2 whole, which is shorter than its diff:
```python
import functools

import jax
import jax.numpy as jnp
from jax import lax
from jax.experimental import pallas as pl
from jax.experimental.pallas import tpu as pltpu
from jax.sharding import PartitionSpec as P

F32 = jnp.float32
BF16 = jnp.bfloat16
MIB = 1024 * 1024
EVERYONE = ("dp", "expert")


def dot(left, right, dims=((1,), (0,)), precision=None):
    return lax.dot_general(left, right, (dims, ((), ())), precision=precision, preferred_element_type=F32)


def exact_dot(left, right, dims=((1,), (0,))):
    return dot(left, right, dims, lax.Precision.HIGHEST)


def iota(shape, axis):
    return lax.broadcasted_iota(jnp.int32, shape, axis)


def one_hot(condition):
    return jnp.where(condition, 1.0, 0.0).astype(BF16)


def vmem():
    return pl.BlockSpec(memory_space=pltpu.VMEM)


def hbm():
    return pl.BlockSpec(memory_space=pltpu.HBM)


def in_hbm(value):
    return pltpu.with_memory_space_constraint(value, pltpu.HBM)


def shape_of(*sizes, dtype=BF16):
    return jax.ShapeDtypeStruct(sizes, dtype)


def params(mib=24):
    return pltpu.CompilerParams(vmem_limit_bytes=mib * MIB)


def cost(flops, moved):
    return pl.CostEstimate(flops=flops, bytes_accessed=moved, transcendentals=0)


def block_of(width, limit):
    best = 128
    for size in range(128, limit + 1, 128):
        if width % size == 0:
            best = size
    return best


def spread_column(values, blocks):
    slots, experts = values.shape
    rows = experts * blocks * slots
    owner = (iota((rows, experts), 0) // (blocks * slots) == iota((rows, experts), 1)).astype(F32)
    wide = exact_dot(owner, values, ((1,), (1,)))
    mine = iota((rows, slots), 0) % slots == iota((rows, slots), 1)
    return jnp.sum(jnp.where(mine, wide, 0.0), axis=1, keepdims=True)


def spread_row(values, blocks):
    slots, experts = values.shape
    rows = experts * blocks * slots
    owner = (iota((experts, rows), 1) // (blocks * slots) == iota((experts, rows), 0)).astype(F32)
    wide = exact_dot(values, owner)
    mine = iota((slots, rows), 1) % slots == iota((slots, rows), 0)
    return jnp.sum(jnp.where(mine, wide, 0.0), axis=0, keepdims=True)


def send_kernel(halves, blocks, scaled, *refs):
    count = 2 if scaled else 1
    lists, source_ref, out_ref = refs[:count], refs[count], refs[count + 1]
    held_ref, sems, list_sems = refs[count + 2 : count + 5]
    list_refs = refs[count + 5 :]
    rows, cols = out_ref.shape
    rows = rows // halves
    tokens = source_ref.shape[0]
    list_copies = [
        pltpu.make_async_copy(ref, target, list_sems.at[i]) for i, (ref, target) in enumerate(zip(lists, list_refs))
    ]
    copies = []
    for copy in list_copies:
        copy.start()
    for half in range(halves):
        for block in range(blocks):
            place = half * blocks + block
            copies.append(
                pltpu.make_async_copy(
                    source_ref.at[:, place * cols : (place + 1) * cols],
                    held_ref.at[half, block * tokens : (block + 1) * tokens],
                    sems.at[half, block],
                )
            )
            copies[-1].start()
    for copy in list_copies:
        copy.wait()
    slots = list_refs[0].shape[0]
    chosen = spread_column(list_refs[0][...].astype(F32), blocks).astype(jnp.int32)
    target = chosen + iota((rows, 1), 0) % (blocks * slots) // slots * tokens
    take = one_hot(target == iota((rows, blocks * tokens), 1))
    scale = spread_column(list_refs[1][...], blocks) if scaled else None
    for half in range(halves):
        for block in range(blocks):
            copies[half * blocks + block].wait()
        picked = dot(take, held_ref[half])
        if scaled:
            picked = picked * scale
        out_ref[half * rows : (half + 1) * rows] = picked.astype(BF16)


def send_rows(source, lists, halves, blocks):
    slots, experts = lists[0].shape
    tokens, width = source.shape
    cols = width // (halves * blocks)
    rows = halves * experts * blocks * slots
    return pl.pallas_call(
        functools.partial(send_kernel, halves, blocks, len(lists) == 2),
        in_specs=[hbm()] * (len(lists) + 1),
        out_specs=vmem(),
        out_shape=shape_of(rows, cols),
        scratch_shapes=[
            pltpu.VMEM((halves, blocks * tokens, cols), BF16),
            pltpu.SemaphoreType.DMA((halves, blocks)),
            pltpu.SemaphoreType.DMA((2,)),
        ]
        + [pltpu.VMEM((slots, experts), value.dtype) for value in lists],
        compiler_params=params(16),
        cost_estimate=cost(2 * rows * cols * tokens * blocks, 2 * tokens * width + 2 * rows * cols),
        name="send_rows",
    )(*[in_hbm(value) for value in lists], in_hbm(source))


def sort_matrix(rows, blocks, slots, back):
    a = iota((rows, rows), 1 if back else 0)
    b = iota((rows, rows), 0 if back else 1)
    group = rows // blocks
    return one_hot(a % group // slots * (blocks * slots) + a // group * slots + a % slots == b)


def sort_rows(messages_ref, rows_ref, slots):
    blocks, total = rows_ref.shape[:2]
    if blocks == 1:
        rows_ref[0] = messages_ref[...]
        return
    size = min(blocks * total, 256)
    group = size // blocks
    order = sort_matrix(size, blocks, slots, False)
    for part in range(total // group):
        ordered = dot(order, messages_ref[part * size : (part + 1) * size]).astype(BF16)
        for block in range(blocks):
            rows_ref[block, part * group : (part + 1) * group] = ordered[block * group : (block + 1) * group]


def unsort_rows(made, out_ref, slots):
    blocks, total = len(made), made[0].shape[0]
    if blocks == 1:
        out_ref[...] = made[0]
        return
    size = min(blocks * total, 256)
    group = size // blocks
    order = sort_matrix(size, blocks, slots, True)
    for part in range(total // group):
        stacked = jnp.concatenate([value[part * group : (part + 1) * group] for value in made], axis=0)
        out_ref[part * size : (part + 1) * size] = dot(order, stacked).astype(BF16)


def spans(ref, blocks):
    cols = ref // blocks
    return [slice(block * cols, (block + 1) * cols) for block in range(blocks)]


def added(terms):
    return functools.reduce(jnp.add, terms)


def in_sums_kernel(slots, messages_ref, gate_ref, up_ref, out_ref, rows_ref):
    blocks = rows_ref.shape[0]
    part, hidden = gate_ref.shape[1:]
    sort_rows(messages_ref, rows_ref, slots)
    for place, ref in enumerate((gate_ref, up_ref)):
        total = added([dot(rows_ref[b], ref[0, span, :]) for b, span in enumerate(spans(part, blocks))])
        out_ref[:, place * hidden : (place + 1) * hidden] = total.astype(BF16)


def in_sums(messages, w_gate, w_up, blocks, slots):
    part, hidden = w_gate.shape[1:]
    rows = messages.shape[0] // blocks
    return pl.pallas_call(
        functools.partial(in_sums_kernel, slots),
        in_specs=[vmem()] * 3,
        out_specs=[vmem()] * 2,
        out_shape=[shape_of(rows, 2 * hidden), shape_of(blocks, rows, part // blocks)],
        compiler_params=params(),
        cost_estimate=cost(4 * rows * part * hidden, 4 * part * hidden),
        name="gate_up_sums",
    )(messages, w_gate, w_up)


def up_sums_kernel(slots, messages_ref, down_ref, out_ref, rows_ref):
    blocks = rows_ref.shape[0]
    part = down_ref.shape[2]
    sort_rows(messages_ref, rows_ref, slots)
    total = added(
        [dot(rows_ref[b], down_ref[0, :, span], ((1,), (1,))) for b, span in enumerate(spans(part, blocks))]
    )
    out_ref[...] = total.astype(BF16)


def up_sums(messages, w_down, blocks, slots):
    hidden, part = w_down.shape[1:]
    rows = messages.shape[0] // blocks
    return pl.pallas_call(
        functools.partial(up_sums_kernel, slots),
        in_specs=[vmem()] * 2,
        out_specs=[vmem()] * 2,
        out_shape=[shape_of(rows, hidden), shape_of(blocks, rows, part // blocks)],
        compiler_params=params(),
        cost_estimate=cost(2 * rows * part * hidden, 2 * part * hidden),
        name="back_sums",
    )(messages, w_down)


def row_parts(total):
    size = min(total, 128)
    return [slice(start, start + size) for start in range(0, total, size)]


def summed(refs, rows, span):
    return added([ref[rows, span].astype(F32) for ref in refs])


def out_rows_kernel(slots, blocks, count, *refs):
    shares, (down_ref, act_ref, out_ref) = refs[:count], refs[count:]
    hidden, part = down_ref.shape[1:]
    for rows in row_parts(act_ref.shape[0]):
        gate_sum = summed(shares, rows, slice(0, hidden))
        up_sum = summed(shares, rows, slice(hidden, 2 * hidden))
        act_ref[rows] = (gate_sum * jax.nn.sigmoid(gate_sum) * up_sum).astype(BF16)
    unsort_rows([dot(act_ref[...], down_ref[0, :, span]).astype(BF16) for span in spans(part, blocks)], out_ref, slots)


def out_rows(shares, w_down, blocks, slots):
    hidden, part = w_down.shape[1:]
    rows = shares[0].shape[0]
    return pl.pallas_call(
        functools.partial(out_rows_kernel, slots, blocks, len(shares)),
        in_specs=[vmem()] * (len(shares) + 1),
        out_specs=[vmem()] * 2,
        out_shape=[shape_of(rows, hidden), shape_of(blocks * rows, part // blocks)],
        compiler_params=params(),
        cost_estimate=cost(2 * rows * part * hidden, 2 * part * hidden),
        name="output_rows",
    )(*shares, w_down)


def grad_rows_kernel(slots, blocks, count, *refs):
    shares, backs = refs[:count], refs[count : 2 * count]
    gate_ref, up_ref, act_ref, out_ref = refs[2 * count :]
    part, hidden = gate_ref.shape[1:]
    for rows in row_parts(act_ref.shape[0]):
        gate_sum = summed(shares, rows, slice(0, hidden))
        up_sum = summed(shares, rows, slice(hidden, 2 * hidden))
        back_sum = summed(backs, rows, slice(0, hidden))
        sig = jax.nn.sigmoid(gate_sum)
        act_ref[rows, :hidden] = (back_sum * up_sum * sig * (1.0 + gate_sum * (1.0 - sig))).astype(BF16)
        act_ref[rows, hidden:] = (back_sum * (gate_sum * sig)).astype(BF16)
    made = []
    for span in spans(part, blocks):
        total = dot(act_ref[:, :hidden], gate_ref[0, span, :], ((1,), (1,)))
        total = total + dot(act_ref[:, hidden:], up_ref[0, span, :], ((1,), (1,)))
        made.append(total.astype(BF16))
    unsort_rows(made, out_ref, slots)


def grad_rows(shares, backs, w_gate, w_up, blocks, slots):
    part, hidden = w_gate.shape[1:]
    rows = shares[0].shape[0]
    return pl.pallas_call(
        functools.partial(grad_rows_kernel, slots, blocks, len(shares)),
        in_specs=[vmem()] * (2 * len(shares) + 2),
        out_specs=[vmem()] * 2,
        out_shape=[shape_of(rows, 2 * hidden), shape_of(blocks * rows, part // blocks)],
        compiler_params=params(32),
        cost_estimate=cost(4 * rows * part * hidden, 4 * part * hidden),
        name="gradient_rows",
    )(*shares, *backs, w_gate, w_up)


def weights_kernel(rows_in_ref, rows_up_ref, act_ref, grad_act_ref, gate_ref, up_ref, down_ref):
    hidden = gate_ref.shape[2]
    rows_in = rows_in_ref[0]
    gate_ref[0] = dot(rows_in, grad_act_ref[:, :hidden], ((0,), (0,))).astype(BF16)
    up_ref[0] = dot(rows_in, grad_act_ref[:, hidden:], ((0,), (0,))).astype(BF16)
    down_ref[0] = dot(act_ref[...], rows_up_ref[0], ((0,), (0,))).astype(BF16)


def weight_grads(rows_in, rows_up, act, grad_act):
    blocks, total, width = rows_in.shape
    part = blocks * width
    hidden = act.shape[1]
    cols = block_of(width, 640)
    steps = width // cols
    chunk = pl.BlockSpec((1, total, cols), lambda k, b: (k, 0, b))
    tall = pl.BlockSpec((1, cols, hidden), lambda k, b: (0, k * steps + b, 0))
    return pl.pallas_call(
        weights_kernel,
        grid=(blocks, steps),
        in_specs=[
            chunk,
            chunk,
            pl.BlockSpec((total, hidden), lambda k, b: (0, 0)),
            pl.BlockSpec((total, 2 * hidden), lambda k, b: (0, 0)),
        ],
        out_specs=[tall, tall, pl.BlockSpec((1, hidden, cols), lambda k, b: (0, 0, k * steps + b))],
        out_shape=[shape_of(1, part, hidden), shape_of(1, part, hidden), shape_of(1, hidden, part)],
        compiler_params=params(),
        cost_estimate=cost(6 * total * part * hidden, 6 * part * hidden),
        name="weight_grads",
    )(rows_in, rows_up, act, grad_act)


def put_columns(held_ref, target_ref, sems, half, block):
    blocks, _, cols = held_ref.shape[1:]
    place = half * blocks + block
    copy = pltpu.make_async_copy(
        held_ref.at[half, block], target_ref.at[:, place * cols : (place + 1) * cols], sems.at[half, block]
    )
    copy.start()
    return copy


def mixed_kernel(picks_ref, gates_ref, cot_ref, back_ref, mixed_ref, gate_grad_ref, put_ref, held_ref, sems):
    slots, experts = picks_ref.shape
    halves, blocks, tokens, cols = held_ref.shape
    rows = experts * blocks * slots
    hit = spread_row(picks_ref[...].astype(F32), blocks).astype(jnp.int32) == iota((tokens, rows), 0)
    scale = spread_row(gates_ref[...], blocks)
    of_block = iota((tokens, rows), 1) % (blocks * slots) // slots
    copies = []
    products = None
    for block in range(blocks):
        inside = hit & (of_block == block)
        put_ref[block] = one_hot(inside)
        rest = jnp.where(inside, scale, 0.0)
        pieces = []
        for _ in range(3):
            pieces.append(rest.astype(BF16))
            rest = rest - pieces[-1].astype(F32)
        for half in range(halves):
            back = back_ref[half * rows : (half + 1) * rows]
            held_ref[half, block] = added([dot(piece, back) for piece in pieces]).astype(BF16)
            copies.append(put_columns(held_ref, mixed_ref, sems, half, block))
            place = half * blocks + block
            product = dot(cot_ref[:, place * cols : (place + 1) * cols], back, ((1,), (1,)))
            product = jnp.where(inside, product, 0.0)
            products = product if products is None else products + product
    values = jnp.sum(products, axis=0, keepdims=True)
    mine = iota((slots, rows), 1) % slots == iota((slots, rows), 0)
    owner = (iota((rows, experts), 0) // (blocks * slots) == iota((rows, experts), 1)).astype(F32)
    gate_grad_ref[...] = exact_dot(jnp.where(mine, values, 0.0), owner)
    for copy in copies:
        copy.wait()


def mix_rows(back, cotangent, picks, gates, halves, blocks):
    slots, experts = picks.shape
    tokens, width = cotangent.shape
    cols = width // (halves * blocks)
    rows = experts * blocks * slots
    return pl.pallas_call(
        mixed_kernel,
        in_specs=[vmem()] * 4,
        out_specs=[hbm(), vmem(), vmem()],
        out_shape=[shape_of(tokens, width), shape_of(slots, experts, dtype=F32), shape_of(blocks, tokens, rows)],
        scratch_shapes=[pltpu.VMEM((halves, blocks, tokens, cols), BF16), pltpu.SemaphoreType.DMA((halves, blocks))],
        compiler_params=params(16),
        cost_estimate=cost(8 * rows * tokens * width, 4 * tokens * width),
        name="mixed_rows",
    )(picks, gates, cotangent, back)


def token_grad_kernel(put_ref, back_ref, grad_ref, held_ref, sems):
    halves, blocks = held_ref.shape[:2]
    rows = back_ref.shape[0] // halves
    copies = []
    for half in range(halves):
        for block in range(blocks):
            back = back_ref[half * rows : (half + 1) * rows]
            held_ref[half, block] = dot(put_ref[block], back).astype(BF16)
            copies.append(put_columns(held_ref, grad_ref, sems, half, block))
    for copy in copies:
        copy.wait()


def token_grads(back, put, halves):
    blocks, tokens, rows = put.shape
    cols = back.shape[1]
    width = halves * blocks * cols
    return pl.pallas_call(
        token_grad_kernel,
        in_specs=[vmem()] * 2,
        out_specs=hbm(),
        out_shape=shape_of(tokens, width),
        scratch_shapes=[pltpu.VMEM((halves, blocks, tokens, cols), BF16), pltpu.SemaphoreType.DMA((halves, blocks))],
        compiler_params=params(16),
        cost_estimate=cost(2 * rows * tokens * width, 2 * tokens * width),
        name="token_grads",
    )(put, back)


def scatter(messages):
    return lax.all_to_all(messages, EVERYONE, split_axis=0, concat_axis=0, tiled=True)


def dp_shares(own, halves):
    shares = [own] + [
        lax.ppermute(own, "dp", [(i, (i + shift) % halves) for i in range(halves)]) for shift in range(1, halves)
    ]
    return shares if halves <= 2 else [added([share.astype(F32) for share in shares])]


def body(halves, tokens, cotangent, picks, gates, w_gate, w_up, w_down):
    slots = picks.shape[2]
    blocks = 2 if tokens.shape[1] // halves % 256 == 0 else 1
    picks_t = picks[0].T
    gates_t = gates[0].T
    arrived_in = scatter(send_rows(tokens, (picks_t,), halves, blocks))
    arrived_up = scatter(send_rows(cotangent, (picks_t, gates_t), halves, blocks))
    own_sums, rows_in = in_sums(arrived_in, w_gate, w_up, blocks, slots)
    shares = dp_shares(own_sums, halves)
    act, outputs = out_rows(shares, w_down, blocks, slots)
    back_out = scatter(outputs)
    own_back, rows_up = up_sums(arrived_up, w_down, blocks, slots)
    backs = dp_shares(own_back, halves)
    grad_act, gradients = grad_rows(shares, backs, w_gate, w_up, blocks, slots)
    back_grad = scatter(gradients)
    grad_gate_w, grad_up_w, grad_down = weight_grads(rows_in, rows_up, act, grad_act)
    mixed, gate_grad, put = mix_rows(back_out, cotangent, picks_t, gates_t, halves, blocks)
    token_grad = token_grads(back_grad, put, halves)
    return mixed, token_grad, gate_grad.T[None], grad_gate_w, grad_up_w, grad_down


def solution(mesh):
    rows = P(("dp", "expert"), None)
    lists = P(("dp", "expert"), None, None)
    tall = P("expert", "dp", None)
    wide = P("expert", None, "dp")
    return jax.shard_map(
        functools.partial(body, mesh.shape["dp"]),
        mesh=mesh,
        in_specs=(rows, rows, lists, lists, tall, tall, wide),
        out_specs=(rows, rows, lists, tall, tall, wide),
        check_vma=False,
    )
```

time: 227 us -> 105 us (0.46)
  local copies, waits for them, and re-layouts: 75.5 us -> 12.1 us
  matrix products: 29.7 us -> 0 us
  Pallas kernels: 0 us -> 24.4 us
  blocking collectives: 15.9 us -> 0 us
  starting transfers between devices: 37.6 us -> 23.9 us
  between operations: 14.3 us -> 0.76 us
  waiting for transfers between devices: 50.1 us -> 43.5 us
  other arithmetic: 2.87 us -> 0 us
    all_to_all x11 -> x0, local copies, waits for them, and re-layouts: 30.4 us -> none  [the longest x3 8.91 us: body(): lax.all_to_all(outgoing[1], 'dp', split_axis=2, concat_axis=1, tiled=True)]
    dot_general x11 -> x0, matrix products: 29.7 us -> none  [the longest x3 12.1 us: contract_cols(): lax.dot_general(left, right, (((1,), (1,)), ((), ())), preferred_element_...]
    pallas_call x0 -> x9, Pallas kernels: none -> 24.4 us  [the longest x1 5.77 us: weight_grads(): pl.pallas_call(weights_kernel, grid=(blocks, steps), in_specs=[chunk, chu...]
    ppermute x0 -> x2, waiting for transfers between devices: none -> 19.8 us  [dp_shares(): lax.ppermute(own, 'dp', [(i, (i + shift) % halves) for i in range(halves)])]
    all_to_all x8 -> x4, starting transfers between devices: 37.6 us -> 20.4 us  [scatter(): lax.all_to_all(messages, EVERYONE, split_axis=0, concat_axis=0, tiled=True)]
    unnamed x19 -> x26, local copies, waits for them, and re-layouts: 28.6 us -> 12.1 us
    reduce_scatter x1 -> x0, waiting for transfers between devices: 16 us -> none  [body(): lax.psum_scatter(terms.astype(jnp.bfloat16), 'dp', scatter_dimension=0, t...]
    all_gather x3 -> x0, blocking collectives: 15.9 us -> none  [the longest x1 5.29 us: body(): lax.all_gather(own_grad_up, 'dp', axis=0, tiled=True)]
  transfers between devices with their start and end apart: 9 -> 6, of which waited for: 7 -> 4; matrix products, arithmetic and copies ran while one was open for 31% -> 0% of each run, Pallas kernels for 0% -> 19%
where the time goes in v2:
time: 105 us
  waiting for transfers between devices  43.5 us (41%)
  Pallas kernels  24.4 us (23%)
  starting transfers between devices  23.9 us (23%)
  local copies, waits for them, and re-layouts  12.1 us (12%)
    all_to_all x4, waiting for transfers between devices, scatter(): lax.all_to_all(messages, EVERYONE, split_axis=0, concat_axis=0, tiled=True)  23.6 us
    all_to_all x4, starting transfers between devices, scatter(): lax.all_to_all(messages, EVERYONE, split_axis=0, concat_axis=0, tiled=True)  20.4 us
    ppermute x2, waiting for transfers between devices, dp_shares(): lax.ppermute(own, 'dp', [(i, (i + shift) % halves) for i in range(halves)])  19.8 us
    unnamed x26, local copies, waits for them, and re-layouts  12.1 us
    pallas_call x1, Pallas kernels, weight_grads(): pl.pallas_call(weights_kernel, grid=(blocks, steps), in_specs=[chunk, chu...  5.77 us
    pallas_call x2, Pallas kernels, send_rows(): pl.pallas_call(functools.partial(send_kernel, halves, blocks, len(lists)...  5.68 us
    pallas_call x1, Pallas kernels, grad_rows(): pl.pallas_call(functools.partial(grad_rows_kernel, slots, blocks, len(sha...  3.74 us
    ppermute x2, starting transfers between devices, dp_shares(): lax.ppermute(own, 'dp', [(i, (i + shift) % halves) for i in range(halves)])  3.47 us
  transfers between devices with their start and end apart: 6, of which 4 were waited for; matrix products, arithmetic and copies ran while one was open for 0% of the time, Pallas kernels for 19%

profile of v2, /device:TPU:0, one launch (start us, length us, event | category | flops | bytes accessed | tf_op | source)
XLA Modules:
  0.0 104.6 jit_solution(16030922065139411675)
XLA Ops:
  0.6 2.8 %send_rows.2 = bf16[256,1280]{1,0:T(8,128)(2,1)} custom-call(s32[4,16]{1,0:T(4,128)} %bitcast.21, bf16[128,5120]{1,0:T(8,128)(2,1)} %refs_1_.1), custom_call_target="tpu_custom_call" | custom-call | flops 167772160 | bytes 1966080 | tf_op jit(solution)/shard_map/send_rows/pallas_call | solution.py:128
  3.4 7.3 %all-to-all-start = ((bf16[32,8,1280]{2,1,0:T(8,128)(2,1)}), bf16[32,8,1280]{2,1,0:T(8,128)(2,1)S(1)}, u32[]{:S(2)}, u32[]{:S(2)}) async-start(bf16[32,8,1280]{2,1,0:T(8,128)(2,1)} %bitcast.5), calls=%async_computation | async-start | bytes 1310720 | tf_op jit(solution)/shard_map/all_to_all | solution.py:424
  10.7 2.9 %send_rows.3 = bf16[256,1280]{1,0:T(8,128)(2,1)} custom-call(s32[4,16]{1,0:T(4,128)} %bitcast.22, f32[4,16]{1,0:T(4,128)} %bitcast.24, bf16[128,5120]{1,0:T(8,128)(2,1)} %refs_2_.3), custom_call_target="tpu_custom_call" | custom-call | flops 167772160 | bytes 1966080 | tf_op jit(solution)/shard_map/send_rows/pallas_call | solution.py:128
  13.6 15.8 %all-to-all-done = bf16[32,8,1280]{2,1,0:T(8,128)(2,1)S(1)} async-done(((bf16[32,8,1280]{2,1,0:T(8,128)(2,1)}), bf16[32,8,1280]{2,1,0:T(8,128)(2,1)S(1)}, u32[]{:S(2)}, u32[]{:S(2)}) %all-to-all-start) | async-done | bytes 655392 | tf_op jit(solution)/shard_map/all_to_all | solution.py:424
  29.5 2.6 %all-to-all-start.2 = ((bf16[32,8,1280]{2,1,0:T(8,128)(2,1)}), bf16[32,8,1280]{2,1,0:T(8,128)(2,1)S(1)}, u32[]{:S(2)}, u32[]{:S(2)}) async-start(bf16[32,8,1280]{2,1,0:T(8,128)(2,1)} %bitcast.10), calls=%async_computation.2 | async-start | bytes 1310720 | tf_op jit(solution)/shard_map/all_to_all | solution.py:424
  32.1 2.1 %copy-done.2 = bf16[1,2560,768]{2,1,0:T(8,128)(2,1)S(1)} copy-done((bf16[1,2560,768]{2,1,0:T(8,128)(2,1)S(1)}, bf16[1,2560,768]{2,1,0:T(8,128)(2,1)}, u32[]{:S(2)}) %copy-start.2) | copy-done | bytes 3932184
  34.2 2.1 %copy-done.4 = bf16[1,2560,768]{2,1,0:T(8,128)(2,1)S(1)} copy-done((bf16[1,2560,768]{2,1,0:T(8,128)(2,1)S(1)}, bf16[1,2560,768]{2,1,0:T(8,128)(2,1)}, u32[]{:S(2)}) %copy-start.4) | copy-done | bytes 3932184
  36.3 1.4 %gate_up_sums.1 = (bf16[128,1536]{1,0:T(8,128)(2,1)S(1)}, bf16[2,128,1280]{2,1,0:T(8,128)(2,1)S(1)}) custom-call(bf16[256,1280]{1,0:T(8,128)(2,1)S(1)} %bitcast.17, bf16[1,2560,768]{2,1,0:T(8,128)(2,1)S(1)} %copy-done.2, bf16[1,2560,768]{2,1,0:T(8,128)(2,1)S(1)} %copy-done.4), custom_call_target="tpu_custom_call" | custom-call | flops 1006632960 | bytes 7864320 | tf_op jit(solution)/shard_map/gate_up_sums/pallas_call | solution.py:200
  37.7 1.7 %collective-permute-start = (bf16[128,1536]{1,0:T(8,128)(2,1)S(1)}, bf16[128,1536]{1,0:T(8,128)(2,1)S(1)}, u32[]{:S(2)}, u32[]{:S(2)}) collective-permute-start(bf16[128,1536]{1,0:T(8,128)(2,1)S(1)} %get-tuple-element.20.refs_0_), channel_id=1, source_target_pairs={{0,16},{16,0},{1,17},{17,1},{2,18},{18,2},{3,19},{19,3},{4,20},{20... | collective-permute-start | bytes 1179656 | tf_op jit(solution)/shard_map/ppermute | solution.py:429
  39.4 12.3 %collective-permute-done.refs_1_ = bf16[128,1536]{1,0:T(8,128)(2,1)S(1)} collective-permute-done((bf16[128,1536]{1,0:T(8,128)(2,1)S(1)}, bf16[128,1536]{1,0:T(8,128)(2,1)S(1)}, u32[]{:S(2)}, u32[]{:S(2)}) %collective-permute-start) | collective-permute-done | bytes 393248 | tf_op jit(solution)/shard_map/ppermute | solution.py:429
  51.8 1.8 %output_rows.1 = (bf16[128,768]{1,0:T(8,128)(2,1)S(1)}, bf16[256,1280]{1,0:T(8,128)(2,1)}) custom-call(bf16[128,1536]{1,0:T(8,128)(2,1)S(1)} %get-tuple-element.20.refs_0_, bf16[128,1536]{1,0:T(8,128)(2,1)S(1)} %collective-permute-done.refs_1_, bf16[1,768,2560]{2,1,0:T(8,128)(2,1)S(1)} %copy-done), custom_call_target="tpu_custom_call" | custom-call | flops 503316480 | bytes 3932160 | tf_op jit(solution)/shard_map/output_rows/pallas_call | solution.py:257
  53.6 4.7 %all-to-all-start.1 = ((bf16[32,8,1280]{2,1,0:T(8,128)(2,1)}), bf16[32,8,1280]{2,1,0:T(8,128)(2,1)S(1)}, u32[]{:S(2)}, u32[]{:S(2)}) async-start(bf16[32,8,1280]{2,1,0:T(8,128)(2,1)} %bitcast.7), calls=%async_computation.1 | async-start | bytes 1310720 | tf_op jit(solution)/shard_map/all_to_all | solution.py:424
  58.3 2.1 %copy-done.1 = bf16[1,768,2560]{2,1,0:T(8,128)(2,1)S(1)} copy-done((bf16[1,768,2560]{2,1,0:T(8,128)(2,1)S(1)}, bf16[1,768,2560]{2,1,0:T(8,128)(2,1)}, u32[]{:S(2)}) %copy-start.1) | copy-done | bytes 3932184
  60.4 1.6 %back_sums.1 = (bf16[128,768]{1,0:T(8,128)(2,1)S(1)}, bf16[2,128,1280]{2,1,0:T(8,128)(2,1)S(1)}) custom-call(bf16[256,1280]{1,0:T(8,128)(2,1)S(1)} %bitcast.18, bf16[1,768,2560]{2,1,0:T(8,128)(2,1)S(1)} %copy-done.1), custom_call_target="tpu_custom_call" | custom-call | flops 503316480 | bytes 3932160 | tf_op jit(solution)/shard_map/back_sums/pallas_call | solution.py:224
  62.8 1.8 %collective-permute-start.1 = (bf16[128,768]{1,0:T(8,128)(2,1)S(1)}, bf16[128,768]{1,0:T(8,128)(2,1)S(1)}, u32[]{:S(2)}, u32[]{:S(2)}) collective-permute-start(bf16[128,768]{1,0:T(8,128)(2,1)S(1)} %get-tuple-element.24.refs_2_), channel_id=1, source_target_pairs={{0,16},{16,0},{1,17},{17,1},{2,18},{18,2},{3,19},{19,3},{4,20},{20... | collective-permute-start | bytes 589832 | tf_op jit(solution)/shard_map/ppermute | solution.py:429
  64.6 7.5 %collective-permute-done.1.refs_3_ = bf16[128,768]{1,0:T(8,128)(2,1)S(1)} collective-permute-done((bf16[128,768]{1,0:T(8,128)(2,1)S(1)}, bf16[128,768]{1,0:T(8,128)(2,1)S(1)}, u32[]{:S(2)}, u32[]{:S(2)}) %collective-permute-start.1) | collective-permute-done | bytes 196640 | tf_op jit(solution)/shard_map/ppermute | solution.py:429
  72.1 2.1 %copy-done.5 = bf16[1,2560,768]{2,1,0:T(8,128)(2,1)S(1)} copy-done((bf16[1,2560,768]{2,1,0:T(8,128)(2,1)S(1)}, bf16[1,2560,768]{2,1,0:T(8,128)(2,1)}, u32[]{:S(2)}) %copy-start.5) | copy-done | bytes 3932184
  74.2 3.7 %gradient_rows.1 = (bf16[128,1536]{1,0:T(8,128)(2,1)S(1)}, bf16[256,1280]{1,0:T(8,128)(2,1)}) custom-call(bf16[128,1536]{1,0:T(8,128)(2,1)S(1)} %get-tuple-element.20.refs_0_, bf16[128,1536]{1,0:T(8,128)(2,1)S(1)} %collective-permute-done.refs_1_, bf16[128,768]{1,0:T(8,128)(2,1)S(1)} %get-tuple-element.24.refs_2_, ...), custom_call_target="tpu_custom_call" | custom-call | flops 1006632960 | bytes 7864320 | tf_op jit(solution)/shard_map/gradient_rows/pallas_call | solution.py:290
  78.7 5.8 %all-to-all-start.3 = ((bf16[32,8,1280]{2,1,0:T(8,128)(2,1)}), bf16[32,8,1280]{2,1,0:T(8,128)(2,1)S(1)}, u32[]{:S(2)}, u32[]{:S(2)}) async-start(bf16[32,8,1280]{2,1,0:T(8,128)(2,1)} %bitcast.12), calls=%async_computation.3 | async-start | bytes 1310720 | tf_op jit(solution)/shard_map/all_to_all | solution.py:424
  84.5 1.1 %copy-done.10 = bf16[2,128,1280]{2,1,0:T(8,128)(2,1)S(1)} copy-done((bf16[2,128,1280]{2,1,0:T(8,128)(2,1)S(1)}, bf16[2,128,1280]{2,1,0:T(8,128)(2,1)}, u32[]{:S(2)}) %copy-start.10) | copy-done | bytes 655384
  86.6 5.8 %weight_grads.1 = (bf16[1,2560,768]{2,1,0:T(8,128)(2,1)}, bf16[1,2560,768]{2,1,0:T(8,128)(2,1)}, bf16[1,768,2560]{2,1,0:T(8,128)(2,1)}) custom-call(bf16[2,128,1280]{2,1,0:T(8,128)(2,1)S(1)} %get-tuple-element.27.rows_in_ref, bf16[2,128,1280]{2,1,0:T(8,128)(2,1)S(1)} %copy-done.10, bf16[128,768]{1,0:T(8,128)(2,1)S(1)} %get-tuple-element.29.act_ref, ...), custom_call_target="tpu_custom_call" | custom-call | flops 1509949440 | bytes 11796480 | tf_op jit(solution)/shard_map/weight_grads/pallas_call | solution.py:317
  92.4 3.0 %mixed_rows.1 = (bf16[128,5120]{1,0:T(8,128)(2,1)}, f32[4,16]{1,0:T(4,128)}, bf16[2,128,128]{2,1,0:T(8,128)(2,1)S(1)}) custom-call(s32[4,16]{1,0:T(4,128)S(1)} %bitcast.23, f32[4,16]{1,0:T(4,128)S(1)} %bitcast.25, bf16[128,5120]{1,0:T(8,128)(2,1)S(1)} %copy-done.6, bf16[256,1280]{1,0:T(8,128)(2,1)S(1)} %bitcast.20), custom_call_target="tpu_custom_call" | custom-call | flops 671088640 | bytes 2621440 | tf_op jit(solution)/shard_map/mixed_rows/pallas_call | solution.py:382
  95.4 7.8 %all-to-all-done.3 = bf16[32,8,1280]{2,1,0:T(8,128)(2,1)S(1)} async-done(((bf16[32,8,1280]{2,1,0:T(8,128)(2,1)}), bf16[32,8,1280]{2,1,0:T(8,128)(2,1)S(1)}, u32[]{:S(2)}, u32[]{:S(2)}) %all-to-all-start.3) | async-done | bytes 655392 | tf_op jit(solution)/shard_map/all_to_all | solution.py:424
  103.2 1.3 %token_grads.1 = bf16[128,5120]{1,0:T(8,128)(2,1)} custom-call(bf16[2,128,128]{2,1,0:T(8,128)(2,1)S(1)} %get-tuple-element.23.put_ref, bf16[256,1280]{1,0:T(8,128)(2,1)S(1)} %bitcast.19), custom_call_target="tpu_custom_call" | custom-call | flops 167772160 | bytes 1310720 | tf_op jit(solution)/shard_map/token_grads/pallas_call | solution.py:411
  (23 shorter events, 2.6 us)
Async XLA Ops:
  3.4 26.0 %all-to-all-start = ((bf16[32,8,1280]{2,1,0:T(8,128)(2,1)}), bf16[32,8,1280]{2,1,0:T(8,128)(2,1)S(1)}, u32[]{:S(2)}, u32[]{:S(2)}) async-start(bf16[32,8,1280]{2,1,0:T(8,128)(2,1)} %bitcast.5), calls=%async_computation | async-start | bytes 1310720 | tf_op jit(solution)/shard_map/all_to_all | solution.py:424
  29.5 24.1 %all-to-all-start.2 = ((bf16[32,8,1280]{2,1,0:T(8,128)(2,1)}), bf16[32,8,1280]{2,1,0:T(8,128)(2,1)S(1)}, u32[]{:S(2)}, u32[]{:S(2)}) async-start(bf16[32,8,1280]{2,1,0:T(8,128)(2,1)} %bitcast.10), calls=%async_computation.2 | async-start | bytes 1310720 | tf_op jit(solution)/shard_map/all_to_all | solution.py:424
  32.1 2.1 %copy-start.2 = (bf16[1,2560,768]{2,1,0:T(8,128)(2,1)S(1)}, bf16[1,2560,768]{2,1,0:T(8,128)(2,1)}, u32[]{:S(2)}) copy-start(bf16[1,2560,768]{2,1,0:T(8,128)(2,1)} %refs_4_.1) | copy-start | bytes 11796484
  34.2 2.1 %copy-start.4 = (bf16[1,2560,768]{2,1,0:T(8,128)(2,1)S(1)}, bf16[1,2560,768]{2,1,0:T(8,128)(2,1)}, u32[]{:S(2)}) copy-start(bf16[1,2560,768]{2,1,0:T(8,128)(2,1)} %refs_5_.1) | copy-start | bytes 11796484
  36.3 15.5 %copy-start = (bf16[1,768,2560]{2,1,0:T(8,128)(2,1)S(1)}, bf16[1,768,2560]{2,1,0:T(8,128)(2,1)}, u32[]{:S(2)}) copy-start(bf16[1,768,2560]{2,1,0:T(8,128)(2,1)} %down_ref.1) | copy-start | bytes 11796484
  37.7 14.1 %collective-permute-start = (bf16[128,1536]{1,0:T(8,128)(2,1)S(1)}, bf16[128,1536]{1,0:T(8,128)(2,1)S(1)}, u32[]{:S(2)}, u32[]{:S(2)}) collective-permute-start(bf16[128,1536]{1,0:T(8,128)(2,1)S(1)} %get-tuple-element.20.refs_0_), channel_id=1, source_target_pairs={{0,16},{16,0},{1,17},{17,1},{2,18},{18,2},{3,19},{19,3},{4,20},{20... | collective-permute-start | bytes 1179656 | tf_op jit(solution)/shard_map/ppermute | solution.py:429
  53.6 25.1 %all-to-all-start.1 = ((bf16[32,8,1280]{2,1,0:T(8,128)(2,1)}), bf16[32,8,1280]{2,1,0:T(8,128)(2,1)S(1)}, u32[]{:S(2)}, u32[]{:S(2)}) async-start(bf16[32,8,1280]{2,1,0:T(8,128)(2,1)} %bitcast.7), calls=%async_computation.1 | async-start | bytes 1310720 | tf_op jit(solution)/shard_map/all_to_all | solution.py:424
  58.2 2.1 %copy-start.1 = (bf16[1,768,2560]{2,1,0:T(8,128)(2,1)S(1)}, bf16[1,768,2560]{2,1,0:T(8,128)(2,1)}, u32[]{:S(2)}) copy-start(bf16[1,768,2560]{2,1,0:T(8,128)(2,1)} %down_ref.1) | copy-start | bytes 11796484
  60.4 11.7 %copy-start.3 = (bf16[1,2560,768]{2,1,0:T(8,128)(2,1)S(1)}, bf16[1,2560,768]{2,1,0:T(8,128)(2,1)}, u32[]{:S(2)}) copy-start(bf16[1,2560,768]{2,1,0:T(8,128)(2,1)} %refs_4_.1) | copy-start | bytes 11796484
  62.0 0.8 copy-start.9
  62.8 9.2 %collective-permute-start.1 = (bf16[128,768]{1,0:T(8,128)(2,1)S(1)}, bf16[128,768]{1,0:T(8,128)(2,1)S(1)}, u32[]{:S(2)}, u32[]{:S(2)}) collective-permute-start(bf16[128,768]{1,0:T(8,128)(2,1)S(1)} %get-tuple-element.24.refs_2_), channel_id=1, source_target_pairs={{0,16},{16,0},{1,17},{17,1},{2,18},{18,2},{3,19},{19,3},{4,20},{20... | collective-permute-start | bytes 589832 | tf_op jit(solution)/shard_map/ppermute | solution.py:429
  72.1 2.1 %copy-start.5 = (bf16[1,2560,768]{2,1,0:T(8,128)(2,1)S(1)}, bf16[1,2560,768]{2,1,0:T(8,128)(2,1)}, u32[]{:S(2)}) copy-start(bf16[1,2560,768]{2,1,0:T(8,128)(2,1)} %refs_5_.1) | copy-start | bytes 11796484
  77.9 0.7 copy-start.11
  78.7 13.7 %copy-start.6 = (bf16[128,5120]{1,0:T(8,128)(2,1)S(1)}, bf16[128,5120]{1,0:T(8,128)(2,1)}, u32[]{:S(2)}) copy-start(bf16[128,5120]{1,0:T(8,128)(2,1)} %refs_2_.3) | copy-start | bytes 3932164
  78.7 13.7 %copy-start.7 = (s32[1,16,4]{1,2,0:T(4,128)S(1)}, s32[1,16,4]{1,2,0:T(4,128)}, u32[]{:S(2)}) copy-start(s32[1,16,4]{1,2,0:T(4,128)} %param.9) | copy-start | bytes 772
  78.7 13.7 %copy-start.8 = (f32[1,16,4]{1,2,0:T(4,128)S(1)}, f32[1,16,4]{1,2,0:T(4,128)}, u32[]{:S(2)}) copy-start(f32[1,16,4]{1,2,0:T(4,128)} %param.10) | copy-start | bytes 772
  78.7 24.5 %all-to-all-start.3 = ((bf16[32,8,1280]{2,1,0:T(8,128)(2,1)}), bf16[32,8,1280]{2,1,0:T(8,128)(2,1)S(1)}, u32[]{:S(2)}, u32[]{:S(2)}) async-start(bf16[32,8,1280]{2,1,0:T(8,128)(2,1)} %bitcast.12), calls=%async_computation.3 | async-start | bytes 1310720 | tf_op jit(solution)/shard_map/all_to_all | solution.py:424
  84.5 1.1 %copy-start.10 = (bf16[2,128,1280]{2,1,0:T(8,128)(2,1)S(1)}, bf16[2,128,1280]{2,1,0:T(8,128)(2,1)}, u32[]{:S(2)}) copy-start(bf16[2,128,1280]{2,1,0:T(8,128)(2,1)} %copy-done.9) | copy-start | bytes 1966084
  85.6 1.0 copy-start.12

commit v3 on v2

--- a/solution.py
+++ b/solution.py
@@ -79,11 +79,13 @@
     return jnp.sum(jnp.where(mine, wide, 0.0), axis=0, keepdims=True)
 
 
-def send_kernel(halves, blocks, scaled, *refs):
+def send_kernel(halves, blocks, scaled, extra, *refs):
     count = 2 if scaled else 1
-    lists, source_ref, out_ref = refs[:count], refs[count], refs[count + 1]
-    held_ref, sems, list_sems = refs[count + 2 : count + 5]
-    list_refs = refs[count + 5 :]
+    lists, source_ref, refs = refs[:count], refs[count], refs[count + 1 :]
+    kept, out_ref, refs = refs[:extra], refs[extra], refs[extra + 1 :]
+    kept_refs, refs = refs[:extra], refs[extra:]
+    held_ref, sems, list_sems, kept_sems = refs[:4]
+    list_refs = refs[4:]
     rows, cols = out_ref.shape
     rows = rows // halves
     tokens = source_ref.shape[0]
@@ -104,6 +106,11 @@
                 )
             )
             copies[-1].start()
+    kept_copies = [
+        pltpu.make_async_copy(ref, target, kept_sems.at[i]) for i, (ref, target) in enumerate(zip(kept, kept_refs))
+    ]
+    for copy in kept_copies:
+        copy.start()
     for copy in list_copies:
         copy.wait()
     slots = list_refs[0].shape[0]
@@ -118,28 +125,31 @@
         if scaled:
             picked = picked * scale
         out_ref[half * rows : (half + 1) * rows] = picked.astype(BF16)
-
-
-def send_rows(source, lists, halves, blocks):
+    for copy in kept_copies:
+        copy.wait()
+
+
+def send_rows(source, lists, halves, blocks, kept=()):
     slots, experts = lists[0].shape
     tokens, width = source.shape
     cols = width // (halves * blocks)
     rows = halves * experts * blocks * slots
     return pl.pallas_call(
-        functools.partial(send_kernel, halves, blocks, len(lists) == 2),
-        in_specs=[hbm()] * (len(lists) + 1),
-        out_specs=vmem(),
-        out_shape=shape_of(rows, cols),
+        functools.partial(send_kernel, halves, blocks, len(lists) == 2, len(kept)),
+        in_specs=[hbm()] * (len(lists) + 1 + len(kept)),
+        out_specs=[vmem()] * (1 + len(kept)),
+        out_shape=[shape_of(rows, cols)] + [shape_of(*value.shape) for value in kept],
         scratch_shapes=[
             pltpu.VMEM((halves, blocks * tokens, cols), BF16),
             pltpu.SemaphoreType.DMA((halves, blocks)),
             pltpu.SemaphoreType.DMA((2,)),
+            pltpu.SemaphoreType.DMA((3,)),
         ]
         + [pltpu.VMEM((slots, experts), value.dtype) for value in lists],
-        compiler_params=params(16),
-        cost_estimate=cost(2 * rows * cols * tokens * blocks, 2 * tokens * width + 2 * rows * cols),
+        compiler_params=params(20),
+        cost_estimate=cost(2 * rows * cols * tokens * blocks, 2 * tokens * width + 2 * sum(v.size for v in kept)),
         name="send_rows",
-    )(*[in_hbm(value) for value in lists], in_hbm(source))
+    )(*[in_hbm(value) for value in lists], in_hbm(source), *[in_hbm(value) for value in kept])
 
 
 def sort_matrix(rows, blocks, slots, back):
@@ -436,8 +446,10 @@
     blocks = 2 if tokens.shape[1] // halves % 256 == 0 else 1
     picks_t = picks[0].T
     gates_t = gates[0].T
-    arrived_in = scatter(send_rows(tokens, (picks_t,), halves, blocks))
-    arrived_up = scatter(send_rows(cotangent, (picks_t, gates_t), halves, blocks))
+    arrived_in = scatter(send_rows(tokens, (picks_t,), halves, blocks)[0])
+    weights = (w_gate, w_up, w_down)
+    messages_up, w_gate, w_up, w_down = send_rows(cotangent, (picks_t, gates_t), halves, blocks, weights)
+    arrived_up = scatter(messages_up)
     own_sums, rows_in = in_sums(arrived_in, w_gate, w_up, blocks, slots)
     shares = dp_shares(own_sums, halves)
     act, outputs = out_rows(shares, w_down, blocks, slots)

time: 105 us -> 105 us (level)
  waiting for transfers between devices: 43.5 us -> 34.7 us
  local copies, waits for them, and re-layouts: 12.1 us -> 18 us
  Pallas kernels: 24.4 us -> 27.3 us
    all_to_all x4, waiting for transfers between devices: 23.6 us -> 15 us  [scatter(): lax.all_to_all(messages, EVERYONE, split_axis=0, concat_axis=0, tiled=True)]
    unnamed x26 -> x32, local copies, waits for them, and re-layouts: 12.1 us -> 18 us
    pallas_call x2, Pallas kernels: 5.68 us -> 8.61 us  [send_rows(): pl.pallas_call(functools.partial(send_kernel, halves, blocks, len(lists)...]
  transfers between devices with their start and end apart: 6 -> 6, of which waited for: 4 -> 4; matrix products, arithmetic and copies ran while one was open for 0% -> 0% of each run, Pallas kernels for 19% -> 22%
where the time goes in v3:
time: 105 us
  waiting for transfers between devices  34.7 us (33%)
  Pallas kernels  27.3 us (26%)
  starting transfers between devices  23.9 us (23%)
  local copies, waits for them, and re-layouts  18 us (17%)
    all_to_all x4, starting transfers between devices, scatter(): lax.all_to_all(messages, EVERYONE, split_axis=0, concat_axis=0, tiled=True)  20.5 us
    ppermute x2, waiting for transfers between devices, dp_shares(): lax.ppermute(own, 'dp', [(i, (i + shift) % halves) for i in range(halves)])  19.7 us
    unnamed x32, local copies, waits for them, and re-layouts  18 us
    all_to_all x4, waiting for transfers between devices, scatter(): lax.all_to_all(messages, EVERYONE, split_axis=0, concat_axis=0, tiled=True)  15 us
    pallas_call x2, Pallas kernels, send_rows(): pl.pallas_call(functools.partial(send_kernel, halves, blocks, len(lists)...  8.61 us
    pallas_call x1, Pallas kernels, weight_grads(): pl.pallas_call(weights_kernel, grid=(blocks, steps), in_specs=[chunk, chu...  5.77 us
    pallas_call x1, Pallas kernels, grad_rows(): pl.pallas_call(functools.partial(grad_rows_kernel, slots, blocks, len(sha...  3.75 us
    ppermute x2, starting transfers between devices, dp_shares(): lax.ppermute(own, 'dp', [(i, (i + shift) % halves) for i in range(halves)])  3.47 us
  transfers between devices with their start and end apart: 6, of which 4 were waited for; matrix products, arithmetic and copies ran while one was open for 0% of the time, Pallas kernels for 22%

profile of v3, /device:TPU:0, one launch (start us, length us, event | category | flops | bytes accessed | tf_op | source)
XLA Modules:
  0.0 104.7 jit_solution(12268850511778705728)
XLA Ops:
  0.6 2.8 %send_rows.2 = bf16[256,1280]{1,0:T(8,128)(2,1)} custom-call(s32[4,16]{1,0:T(4,128)} %bitcast.21, bf16[128,5120]{1,0:T(8,128)(2,1)} %refs_1_.1), custom_call_target="tpu_custom_call" | custom-call | flops 167772160 | bytes 1310720 | tf_op jit(solution)/shard_map/send_rows/pallas_call | solution.py:137
  3.5 7.3 %all-to-all-start = ((bf16[32,8,1280]{2,1,0:T(8,128)(2,1)}), bf16[32,8,1280]{2,1,0:T(8,128)(2,1)S(1)}, u32[]{:S(2)}, u32[]{:S(2)}) async-start(bf16[32,8,1280]{2,1,0:T(8,128)(2,1)} %bitcast.5), calls=%async_computation | async-start | bytes 1310720 | tf_op jit(solution)/shard_map/all_to_all | solution.py:434
  10.8 5.8 %send_rows.3 = (bf16[256,1280]{1,0:T(8,128)(2,1)}, bf16[1,2560,768]{2,1,0:T(8,128)(2,1)S(1)}, bf16[1,2560,768]{2,1,0:T(8,128)(2,1)S(1)}, bf16[1,768,2560]{2,1,0:T(8,128)(2,1)S(1)}) custom-call(s32[4,16]{1,0:T(4,128)} %bitcast.22, f32[4,16]{1,0:T(4,128)} %bitcast.24, bf16[128,5120]{1,0:T(8,128)(2,1)} %cot_ref.1, bf16[1,2560,768]{2,1,0:T(8,128)(2,1)} %refs_3_.1, ...), custom_call_target="tpu_custom_call" | custom-call | flops 167772160 | bytes 13107200 | tf_op jit(solution)/shard_map/send_rows/pallas_call | solution.py:137
  16.6 1.9 %copy-done = bf16[1,2560,768]{2,1,0:T(8,128)(2,1)} copy-done((bf16[1,2560,768]{2,1,0:T(8,128)(2,1)}, bf16[1,2560,768]{2,1,0:T(8,128)(2,1)S(1)}, u32[]{:S(2)}) %copy-start) | copy-done | bytes 3932184
  18.5 1.9 %copy-done.3 = bf16[1,2560,768]{2,1,0:T(8,128)(2,1)} copy-done((bf16[1,2560,768]{2,1,0:T(8,128)(2,1)}, bf16[1,2560,768]{2,1,0:T(8,128)(2,1)S(1)}, u32[]{:S(2)}) %copy-start.3) | copy-done | bytes 3932184
  20.4 1.9 %copy-done.6 = bf16[1,768,2560]{2,1,0:T(8,128)(2,1)} copy-done((bf16[1,768,2560]{2,1,0:T(8,128)(2,1)}, bf16[1,768,2560]{2,1,0:T(8,128)(2,1)S(1)}, u32[]{:S(2)}) %copy-start.6) | copy-done | bytes 3932184
  22.3 7.1 %all-to-all-done = bf16[32,8,1280]{2,1,0:T(8,128)(2,1)S(1)} async-done(((bf16[32,8,1280]{2,1,0:T(8,128)(2,1)}), bf16[32,8,1280]{2,1,0:T(8,128)(2,1)S(1)}, u32[]{:S(2)}, u32[]{:S(2)}) %all-to-all-start) | async-done | bytes 655392 | tf_op jit(solution)/shard_map/all_to_all | solution.py:434
  29.5 2.6 %all-to-all-start.2 = ((bf16[32,8,1280]{2,1,0:T(8,128)(2,1)}), bf16[32,8,1280]{2,1,0:T(8,128)(2,1)S(1)}, u32[]{:S(2)}, u32[]{:S(2)}) async-start(bf16[32,8,1280]{2,1,0:T(8,128)(2,1)} %bitcast.10), calls=%async_computation.2 | async-start | bytes 1310720 | tf_op jit(solution)/shard_map/all_to_all | solution.py:434
  32.1 2.1 %copy-done.1 = bf16[1,2560,768]{2,1,0:T(8,128)(2,1)S(1)} copy-done((bf16[1,2560,768]{2,1,0:T(8,128)(2,1)S(1)}, bf16[1,2560,768]{2,1,0:T(8,128)(2,1)}, u32[]{:S(2)}) %copy-start.1) | copy-done | bytes 3932184
  34.2 2.1 %copy-done.4 = bf16[1,2560,768]{2,1,0:T(8,128)(2,1)S(1)} copy-done((bf16[1,2560,768]{2,1,0:T(8,128)(2,1)S(1)}, bf16[1,2560,768]{2,1,0:T(8,128)(2,1)}, u32[]{:S(2)}) %copy-start.4) | copy-done | bytes 3932184
  37.8 1.7 %collective-permute-start = (bf16[128,1536]{1,0:T(8,128)(2,1)S(1)}, bf16[128,1536]{1,0:T(8,128)(2,1)S(1)}, u32[]{:S(2)}, u32[]{:S(2)}) collective-permute-start(bf16[128,1536]{1,0:T(8,128)(2,1)S(1)} %get-tuple-element.26.refs_0_), channel_id=1, source_target_pairs={{0,16},{16,0},{1,17},{17,1},{2,18},{18,2},{3,19},{19,3},{4,20},{20... | collective-permute-start | bytes 1179656 | tf_op jit(solution)/shard_map/ppermute | solution.py:439
  39.5 12.3 %collective-permute-done.refs_1_ = bf16[128,1536]{1,0:T(8,128)(2,1)S(1)} collective-permute-done((bf16[128,1536]{1,0:T(8,128)(2,1)S(1)}, bf16[128,1536]{1,0:T(8,128)(2,1)S(1)}, u32[]{:S(2)}, u32[]{:S(2)}) %collective-permute-start) | collective-permute-done | bytes 393248 | tf_op jit(solution)/shard_map/ppermute | solution.py:439
  51.8 1.8 %output_rows.1 = (bf16[128,768]{1,0:T(8,128)(2,1)S(1)}, bf16[256,1280]{1,0:T(8,128)(2,1)}) custom-call(bf16[128,1536]{1,0:T(8,128)(2,1)S(1)} %get-tuple-element.26.refs_0_, bf16[128,1536]{1,0:T(8,128)(2,1)S(1)} %collective-permute-done.refs_1_, bf16[1,768,2560]{2,1,0:T(8,128)(2,1)S(1)} %copy-done.7), custom_call_target="tpu_custom_call" | custom-call | flops 503316480 | bytes 3932160 | tf_op jit(solution)/shard_map/output_rows/pallas_call | solution.py:267
  53.6 4.7 %all-to-all-start.1 = ((bf16[32,8,1280]{2,1,0:T(8,128)(2,1)}), bf16[32,8,1280]{2,1,0:T(8,128)(2,1)S(1)}, u32[]{:S(2)}, u32[]{:S(2)}) async-start(bf16[32,8,1280]{2,1,0:T(8,128)(2,1)} %bitcast.8), calls=%async_computation.1 | async-start | bytes 1310720 | tf_op jit(solution)/shard_map/all_to_all | solution.py:434
  58.3 2.3 %copy-done.8 = bf16[1,768,2560]{2,1,0:T(8,128)(2,1)S(1)} copy-done((bf16[1,768,2560]{2,1,0:T(8,128)(2,1)S(1)}, bf16[1,768,2560]{2,1,0:T(8,128)(2,1)}, u32[]{:S(2)}) %copy-start.8) | copy-done | bytes 3932184
  60.6 1.6 %back_sums.1 = (bf16[128,768]{1,0:T(8,128)(2,1)S(1)}, bf16[2,128,1280]{2,1,0:T(8,128)(2,1)S(1)}) custom-call(bf16[256,1280]{1,0:T(8,128)(2,1)S(1)} %bitcast.18, bf16[1,768,2560]{2,1,0:T(8,128)(2,1)S(1)} %copy-done.8), custom_call_target="tpu_custom_call" | custom-call | flops 503316480 | bytes 3932160 | tf_op jit(solution)/shard_map/back_sums/pallas_call | solution.py:234
  63.0 1.8 %collective-permute-start.1 = (bf16[128,768]{1,0:T(8,128)(2,1)S(1)}, bf16[128,768]{1,0:T(8,128)(2,1)S(1)}, u32[]{:S(2)}, u32[]{:S(2)}) collective-permute-start(bf16[128,768]{1,0:T(8,128)(2,1)S(1)} %get-tuple-element.32.refs_2_), channel_id=1, source_target_pairs={{0,16},{16,0},{1,17},{17,1},{2,18},{18,2},{3,19},{19,3},{4,20},{20... | collective-permute-start | bytes 589832 | tf_op jit(solution)/shard_map/ppermute | solution.py:439
  64.8 7.4 %collective-permute-done.1.refs_3_ = bf16[128,768]{1,0:T(8,128)(2,1)S(1)} collective-permute-done((bf16[128,768]{1,0:T(8,128)(2,1)S(1)}, bf16[128,768]{1,0:T(8,128)(2,1)S(1)}, u32[]{:S(2)}, u32[]{:S(2)}) %collective-permute-start.1) | collective-permute-done | bytes 196640 | tf_op jit(solution)/shard_map/ppermute | solution.py:439
  72.2 2.1 %copy-done.5 = bf16[1,2560,768]{2,1,0:T(8,128)(2,1)S(1)} copy-done((bf16[1,2560,768]{2,1,0:T(8,128)(2,1)S(1)}, bf16[1,2560,768]{2,1,0:T(8,128)(2,1)}, u32[]{:S(2)}) %copy-start.5) | copy-done | bytes 3932184
  74.3 3.7 %gradient_rows.1 = (bf16[128,1536]{1,0:T(8,128)(2,1)S(1)}, bf16[256,1280]{1,0:T(8,128)(2,1)}) custom-call(bf16[128,1536]{1,0:T(8,128)(2,1)S(1)} %get-tuple-element.26.refs_0_, bf16[128,1536]{1,0:T(8,128)(2,1)S(1)} %collective-permute-done.refs_1_, bf16[128,768]{1,0:T(8,128)(2,1)S(1)} %get-tuple-element.32.refs_2_, ...), custom_call_target="tpu_custom_call" | custom-call | flops 1006632960 | bytes 7864320 | tf_op jit(solution)/shard_map/gradient_rows/pallas_call | solution.py:300
  78.8 5.9 %all-to-all-start.3 = ((bf16[32,8,1280]{2,1,0:T(8,128)(2,1)}), bf16[32,8,1280]{2,1,0:T(8,128)(2,1)S(1)}, u32[]{:S(2)}, u32[]{:S(2)}) async-start(bf16[32,8,1280]{2,1,0:T(8,128)(2,1)} %bitcast.12), calls=%async_computation.3 | async-start | bytes 1310720 | tf_op jit(solution)/shard_map/all_to_all | solution.py:434
  86.7 5.8 %weight_grads.1 = (bf16[1,2560,768]{2,1,0:T(8,128)(2,1)}, bf16[1,2560,768]{2,1,0:T(8,128)(2,1)}, bf16[1,768,2560]{2,1,0:T(8,128)(2,1)}) custom-call(bf16[2,128,1280]{2,1,0:T(8,128)(2,1)S(1)} %get-tuple-element.35.rows_in_ref, bf16[2,128,1280]{2,1,0:T(8,128)(2,1)S(1)} %copy-done.13, bf16[128,768]{1,0:T(8,128)(2,1)S(1)} %get-tuple-element.37.act_ref, ...), custom_call_target="tpu_custom_call" | custom-call | flops 1509949440 | bytes 11796480 | tf_op jit(solution)/shard_map/weight_grads/pallas_call | solution.py:327
  92.5 3.0 %mixed_rows.1 = (bf16[128,5120]{1,0:T(8,128)(2,1)}, f32[4,16]{1,0:T(4,128)}, bf16[2,128,128]{2,1,0:T(8,128)(2,1)S(1)}) custom-call(s32[4,16]{1,0:T(4,128)S(1)} %bitcast.23, f32[4,16]{1,0:T(4,128)S(1)} %bitcast.25, bf16[128,5120]{1,0:T(8,128)(2,1)S(1)} %copy-done.9, bf16[256,1280]{1,0:T(8,128)(2,1)S(1)} %bitcast.20), custom_call_target="tpu_custom_call" | custom-call | flops 671088640 | bytes 2621440 | tf_op jit(solution)/shard_map/mixed_rows/pallas_call | solution.py:392
  95.5 7.8 %all-to-all-done.3 = bf16[32,8,1280]{2,1,0:T(8,128)(2,1)S(1)} async-done(((bf16[32,8,1280]{2,1,0:T(8,128)(2,1)}), bf16[32,8,1280]{2,1,0:T(8,128)(2,1)S(1)}, u32[]{:S(2)}, u32[]{:S(2)}) %all-to-all-start.3) | async-done | bytes 655392 | tf_op jit(solution)/shard_map/all_to_all | solution.py:434
  (29 shorter events, 6.4 us)
Async XLA Ops:
  3.5 26.0 %all-to-all-start = ((bf16[32,8,1280]{2,1,0:T(8,128)(2,1)}), bf16[32,8,1280]{2,1,0:T(8,128)(2,1)S(1)}, u32[]{:S(2)}, u32[]{:S(2)}) async-start(bf16[32,8,1280]{2,1,0:T(8,128)(2,1)} %bitcast.5), calls=%async_computation | async-start | bytes 1310720 | tf_op jit(solution)/shard_map/all_to_all | solution.py:434
  16.6 1.9 %copy-start = (bf16[1,2560,768]{2,1,0:T(8,128)(2,1)}, bf16[1,2560,768]{2,1,0:T(8,128)(2,1)S(1)}, u32[]{:S(2)}) copy-start(bf16[1,2560,768]{2,1,0:T(8,128)(2,1)S(1)} %get-tuple-element.24.gate_ref.refs_4_) | copy-start | bytes 11796484
  18.5 1.9 %copy-start.3 = (bf16[1,2560,768]{2,1,0:T(8,128)(2,1)}, bf16[1,2560,768]{2,1,0:T(8,128)(2,1)S(1)}, u32[]{:S(2)}) copy-start(bf16[1,2560,768]{2,1,0:T(8,128)(2,1)S(1)} %get-tuple-element.25.up_ref.refs_5_) | copy-start | bytes 11796484
  20.4 1.9 %copy-start.6 = (bf16[1,768,2560]{2,1,0:T(8,128)(2,1)}, bf16[1,768,2560]{2,1,0:T(8,128)(2,1)S(1)}, u32[]{:S(2)}) copy-start(bf16[1,768,2560]{2,1,0:T(8,128)(2,1)S(1)} %get-tuple-element.27.refs_2_.down_ref) | copy-start | bytes 11796484
  29.5 24.1 %all-to-all-start.2 = ((bf16[32,8,1280]{2,1,0:T(8,128)(2,1)}), bf16[32,8,1280]{2,1,0:T(8,128)(2,1)S(1)}, u32[]{:S(2)}, u32[]{:S(2)}) async-start(bf16[32,8,1280]{2,1,0:T(8,128)(2,1)} %bitcast.10), calls=%async_computation.2 | async-start | bytes 1310720 | tf_op jit(solution)/shard_map/all_to_all | solution.py:434
  32.1 2.1 %copy-start.1 = (bf16[1,2560,768]{2,1,0:T(8,128)(2,1)S(1)}, bf16[1,2560,768]{2,1,0:T(8,128)(2,1)}, u32[]{:S(2)}) copy-start(bf16[1,2560,768]{2,1,0:T(8,128)(2,1)} %copy-done) | copy-start | bytes 11796484
  34.2 2.1 %copy-start.4 = (bf16[1,2560,768]{2,1,0:T(8,128)(2,1)S(1)}, bf16[1,2560,768]{2,1,0:T(8,128)(2,1)}, u32[]{:S(2)}) copy-start(bf16[1,2560,768]{2,1,0:T(8,128)(2,1)} %copy-done.3) | copy-start | bytes 11796484
  36.3 15.5 %copy-start.7 = (bf16[1,768,2560]{2,1,0:T(8,128)(2,1)S(1)}, bf16[1,768,2560]{2,1,0:T(8,128)(2,1)}, u32[]{:S(2)}) copy-start(bf16[1,768,2560]{2,1,0:T(8,128)(2,1)} %copy-done.6) | copy-start | bytes 11796484
  37.8 14.1 %collective-permute-start = (bf16[128,1536]{1,0:T(8,128)(2,1)S(1)}, bf16[128,1536]{1,0:T(8,128)(2,1)S(1)}, u32[]{:S(2)}, u32[]{:S(2)}) collective-permute-start(bf16[128,1536]{1,0:T(8,128)(2,1)S(1)} %get-tuple-element.26.refs_0_), channel_id=1, source_target_pairs={{0,16},{16,0},{1,17},{17,1},{2,18},{18,2},{3,19},{19,3},{4,20},{20... | collective-permute-start | bytes 1179656 | tf_op jit(solution)/shard_map/ppermute | solution.py:439
  53.6 25.2 %all-to-all-start.1 = ((bf16[32,8,1280]{2,1,0:T(8,128)(2,1)}), bf16[32,8,1280]{2,1,0:T(8,128)(2,1)S(1)}, u32[]{:S(2)}, u32[]{:S(2)}) async-start(bf16[32,8,1280]{2,1,0:T(8,128)(2,1)} %bitcast.8), calls=%async_computation.1 | async-start | bytes 1310720 | tf_op jit(solution)/shard_map/all_to_all | solution.py:434
  58.3 13.9 %copy-start.2 = (bf16[1,2560,768]{2,1,0:T(8,128)(2,1)S(1)}, bf16[1,2560,768]{2,1,0:T(8,128)(2,1)}, u32[]{:S(2)}) copy-start(bf16[1,2560,768]{2,1,0:T(8,128)(2,1)} %copy-done) | copy-start | bytes 11796484
  58.3 2.3 %copy-start.8 = (bf16[1,768,2560]{2,1,0:T(8,128)(2,1)S(1)}, bf16[1,768,2560]{2,1,0:T(8,128)(2,1)}, u32[]{:S(2)}) copy-start(bf16[1,768,2560]{2,1,0:T(8,128)(2,1)} %copy-done.6) | copy-start | bytes 11796484
  62.2 0.8 copy-start.12
  63.0 9.1 %collective-permute-start.1 = (bf16[128,768]{1,0:T(8,128)(2,1)S(1)}, bf16[128,768]{1,0:T(8,128)(2,1)S(1)}, u32[]{:S(2)}, u32[]{:S(2)}) collective-permute-start(bf16[128,768]{1,0:T(8,128)(2,1)S(1)} %get-tuple-element.32.refs_2_), channel_id=1, source_target_pairs={{0,16},{16,0},{1,17},{17,1},{2,18},{18,2},{3,19},{19,3},{4,20},{20... | collective-permute-start | bytes 589832 | tf_op jit(solution)/shard_map/ppermute | solution.py:439
  72.2 2.1 %copy-start.5 = (bf16[1,2560,768]{2,1,0:T(8,128)(2,1)S(1)}, bf16[1,2560,768]{2,1,0:T(8,128)(2,1)}, u32[]{:S(2)}) copy-start(bf16[1,2560,768]{2,1,0:T(8,128)(2,1)} %copy-done.3) | copy-start | bytes 11796484
  78.0 0.7 copy-start.14
  78.8 13.7 %copy-start.9 = (bf16[128,5120]{1,0:T(8,128)(2,1)S(1)}, bf16[128,5120]{1,0:T(8,128)(2,1)}, u32[]{:S(2)}) copy-start(bf16[128,5120]{1,0:T(8,128)(2,1)} %cot_ref.1) | copy-start | bytes 3932164
  78.8 13.7 %copy-start.10 = (s32[1,16,4]{1,2,0:T(4,128)S(1)}, s32[1,16,4]{1,2,0:T(4,128)}, u32[]{:S(2)}) copy-start(s32[1,16,4]{1,2,0:T(4,128)} %param.9) | copy-start | bytes 772
  78.8 13.7 %copy-start.11 = (f32[1,16,4]{1,2,0:T(4,128)S(1)}, f32[1,16,4]{1,2,0:T(4,128)}, u32[]{:S(2)}) copy-start(f32[1,16,4]{1,2,0:T(4,128)} %param.10) | copy-start | bytes 772
  78.8 24.6 %all-to-all-start.3 = ((bf16[32,8,1280]{2,1,0:T(8,128)(2,1)}), bf16[32,8,1280]{2,1,0:T(8,128)(2,1)S(1)}, u32[]{:S(2)}, u32[]{:S(2)}) async-start(bf16[32,8,1280]{2,1,0:T(8,128)(2,1)} %bitcast.12), calls=%async_computation.3 | async-start | bytes 1310720 | tf_op jit(solution)/shard_map/all_to_all | solution.py:434
  84.6 1.1 %copy-start.13 = (bf16[2,128,1280]{2,1,0:T(8,128)(2,1)S(1)}, bf16[2,128,1280]{2,1,0:T(8,128)(2,1)}, u32[]{:S(2)}) copy-start(bf16[2,128,1280]{2,1,0:T(8,128)(2,1)} %copy-done.12) | copy-start | bytes 1966084
  85.7 1.0 copy-start.15

commit v4 on v2

--- a/solution.py
+++ b/solution.py
@@ -25,6 +25,15 @@
     return lax.broadcasted_iota(jnp.int32, shape, axis)
 
 
+def planes_of(experts):
+    return experts // 4 if experts % 4 == 0 else 1
+
+
+def expert_at(place, experts):
+    planes = planes_of(experts)
+    return place % planes * (experts // planes) + place // planes
+
+
 def one_hot(condition):
     return jnp.where(condition, 1.0, 0.0).astype(BF16)
 
@@ -43,6 +52,10 @@
 
 def shape_of(*sizes, dtype=BF16):
     return jax.ShapeDtypeStruct(sizes, dtype)
+
+
+def hbm_shape(*sizes):
+    return pltpu.HBM(sizes, BF16)
 
 
 def params(mib=24):
@@ -64,7 +77,7 @@
 def spread_column(values, blocks):
     slots, experts = values.shape
     rows = experts * blocks * slots
-    owner = (iota((rows, experts), 0) // (blocks * slots) == iota((rows, experts), 1)).astype(F32)
+    owner = (expert_at(iota((rows, experts), 0) // (blocks * slots), experts) == iota((rows, experts), 1)).astype(F32)
     wide = exact_dot(owner, values, ((1,), (1,)))
     mine = iota((rows, slots), 0) % slots == iota((rows, slots), 1)
     return jnp.sum(jnp.where(mine, wide, 0.0), axis=1, keepdims=True)
@@ -73,7 +86,7 @@
 def spread_row(values, blocks):
     slots, experts = values.shape
     rows = experts * blocks * slots
-    owner = (iota((experts, rows), 1) // (blocks * slots) == iota((experts, rows), 0)).astype(F32)
+    owner = (expert_at(iota((experts, rows), 1) // (blocks * slots), experts) == iota((experts, rows), 0)).astype(F32)
     wide = exact_dot(values, owner)
     mine = iota((slots, rows), 1) % slots == iota((slots, rows), 0)
     return jnp.sum(jnp.where(mine, wide, 0.0), axis=0, keepdims=True)
@@ -106,7 +119,8 @@
             copies[-1].start()
     for copy in list_copies:
         copy.wait()
-    slots = list_refs[0].shape[0]
+    slots, experts = list_refs[0].shape
+    run = planes_of(experts) * blocks * slots
     chosen = spread_column(list_refs[0][...].astype(F32), blocks).astype(jnp.int32)
     target = chosen + iota((rows, 1), 0) % (blocks * slots) // slots * tokens
     take = one_hot(target == iota((rows, blocks * tokens), 1))
@@ -117,7 +131,10 @@
         picked = dot(take, held_ref[half])
         if scaled:
             picked = picked * scale
-        out_ref[half * rows : (half + 1) * rows] = picked.astype(BF16)
+        picked = picked.astype(BF16)
+        for place in range(rows // run):
+            start = (place * halves + half) * run
+            out_ref[start : start + run] = picked[place * run : (place + 1) * run]
 
 
 def send_rows(source, lists, halves, blocks):
@@ -163,17 +180,17 @@
             rows_ref[block, part * group : (part + 1) * group] = ordered[block * group : (block + 1) * group]
 
 
-def unsort_rows(made, out_ref, slots):
+def unsort_rows(made, out_ref, slots, span=slice(None)):
     blocks, total = len(made), made[0].shape[0]
     if blocks == 1:
-        out_ref[...] = made[0]
+        out_ref[:, span] = made[0]
         return
     size = min(blocks * total, 256)
     group = size // blocks
     order = sort_matrix(size, blocks, slots, True)
     for part in range(total // group):
         stacked = jnp.concatenate([value[part * group : (part + 1) * group] for value in made], axis=0)
-        out_ref[part * size : (part + 1) * size] = dot(order, stacked).astype(BF16)
+        out_ref[part * size : (part + 1) * size, span] = dot(order, stacked).astype(BF16)
 
 
 def spans(ref, blocks):
@@ -185,51 +202,105 @@
     return functools.reduce(jnp.add, terms)
 
 
-def in_sums_kernel(slots, messages_ref, gate_ref, up_ref, out_ref, rows_ref):
-    blocks = rows_ref.shape[0]
-    part, hidden = gate_ref.shape[1:]
+def pieces_of(width):
+    if width % 256 or width <= 768:
+        return [(0, width)]
+    first = width // 2 // 256 * 256
+    return [(0, first), (first, width - first)]
+
+
+class Stream:
+    def __init__(self, sems):
+        self.sems, self.copies = sems, []
+
+    def start(self, source, target):
+        copy = pltpu.make_async_copy(source, target, self.sems.at[len(self.copies)])
+        copy.start()
+        self.copies.append(copy)
+        return copy
+
+
+def in_sums_kernel(slots, messages_ref, gate_ref, up_ref, out_ref, kept_ref, rows_ref, held_ref, acc_ref, sems):
+    blocks, _, cols = rows_ref.shape
+    hidden = gate_ref.shape[2]
+    stream = Stream(sems)
+    cuts = [(block, start, size) for block in range(blocks) for start, size in pieces_of(cols)]
+    copies = []
+    for block, start, size in cuts:
+        span = slice(block * cols + start, block * cols + start + size)
+        copies += [stream.start(ref.at[0, span], held_ref.at[i, span]) for i, ref in enumerate((gate_ref, up_ref))]
     sort_rows(messages_ref, rows_ref, slots)
-    for place, ref in enumerate((gate_ref, up_ref)):
-        total = added([dot(rows_ref[b], ref[0, span, :]) for b, span in enumerate(spans(part, blocks))])
-        out_ref[:, place * hidden : (place + 1) * hidden] = total.astype(BF16)
+    kept = stream.start(rows_ref, kept_ref)
+    for number, (block, start, size) in enumerate(cuts):
+        span = slice(block * cols + start, block * cols + start + size)
+        for i in range(2):
+            copies[2 * number + i].wait()
+            term = dot(rows_ref[block, :, start : start + size], held_ref[i, span])
+            acc_ref[i] = term if number == 0 else acc_ref[i] + term
+    for i in range(2):
+        out_ref[:, i * hidden : (i + 1) * hidden] = acc_ref[i].astype(BF16)
+    kept.wait()
 
 
 def in_sums(messages, w_gate, w_up, blocks, slots):
     part, hidden = w_gate.shape[1:]
     rows = messages.shape[0] // blocks
+    cols = part // blocks
     return pl.pallas_call(
         functools.partial(in_sums_kernel, slots),
-        in_specs=[vmem()] * 3,
-        out_specs=[vmem()] * 2,
-        out_shape=[shape_of(rows, 2 * hidden), shape_of(blocks, rows, part // blocks)],
+        in_specs=[vmem(), hbm(), hbm()],
+        out_specs=[vmem(), hbm()],
+        out_shape=[shape_of(rows, 2 * hidden), hbm_shape(blocks, rows, cols)],
+        scratch_shapes=[
+            pltpu.VMEM((blocks, rows, cols), BF16),
+            pltpu.VMEM((2, part, hidden), BF16),
+            pltpu.VMEM((2, rows, hidden), F32),
+            pltpu.SemaphoreType.DMA((2 * blocks * len(pieces_of(cols)) + 1,)),
+        ],
         compiler_params=params(),
         cost_estimate=cost(4 * rows * part * hidden, 4 * part * hidden),
         name="gate_up_sums",
-    )(messages, w_gate, w_up)
-
-
-def up_sums_kernel(slots, messages_ref, down_ref, out_ref, rows_ref):
-    blocks = rows_ref.shape[0]
-    part = down_ref.shape[2]
+    )(messages, in_hbm(w_gate), in_hbm(w_up))
+
+
+def up_sums_kernel(slots, messages_ref, down_ref, out_ref, kept_ref, rows_ref, held_ref, acc_ref, sems):
+    blocks, _, cols = rows_ref.shape
+    stream = Stream(sems)
+    cuts = [(block, start, size) for block in range(blocks) for start, size in pieces_of(cols)]
+    copies = []
+    for block, start, size in cuts:
+        span = slice(block * cols + start, block * cols + start + size)
+        copies.append(stream.start(down_ref.at[0, :, span], held_ref.at[:, span]))
     sort_rows(messages_ref, rows_ref, slots)
-    total = added(
-        [dot(rows_ref[b], down_ref[0, :, span], ((1,), (1,))) for b, span in enumerate(spans(part, blocks))]
-    )
-    out_ref[...] = total.astype(BF16)
+    kept = stream.start(rows_ref, kept_ref)
+    for number, (block, start, size) in enumerate(cuts):
+        span = slice(block * cols + start, block * cols + start + size)
+        copies[number].wait()
+        term = dot(rows_ref[block, :, start : start + size], held_ref[:, span], ((1,), (1,)))
+        acc_ref[...] = term if number == 0 else acc_ref[...] + term
+    out_ref[...] = acc_ref[...].astype(BF16)
+    kept.wait()
 
 
 def up_sums(messages, w_down, blocks, slots):
     hidden, part = w_down.shape[1:]
     rows = messages.shape[0] // blocks
+    cols = part // blocks
     return pl.pallas_call(
         functools.partial(up_sums_kernel, slots),
-        in_specs=[vmem()] * 2,
-        out_specs=[vmem()] * 2,
-        out_shape=[shape_of(rows, hidden), shape_of(blocks, rows, part // blocks)],
+        in_specs=[vmem(), hbm()],
+        out_specs=[vmem(), hbm()],
+        out_shape=[shape_of(rows, hidden), hbm_shape(blocks, rows, cols)],
+        scratch_shapes=[
+            pltpu.VMEM((blocks, rows, cols), BF16),
+            pltpu.VMEM((hidden, part), BF16),
+            pltpu.VMEM((rows, hidden), F32),
+            pltpu.SemaphoreType.DMA((blocks * len(pieces_of(cols)) + 1,)),
+        ],
         compiler_params=params(),
         cost_estimate=cost(2 * rows * part * hidden, 2 * part * hidden),
         name="back_sums",
-    )(messages, w_down)
+    )(messages, in_hbm(w_down))
 
 
 def row_parts(total):
@@ -267,8 +338,15 @@
 
 def grad_rows_kernel(slots, blocks, count, *refs):
     shares, backs = refs[:count], refs[count : 2 * count]
-    gate_ref, up_ref, act_ref, out_ref = refs[2 * count :]
+    gate_ref, up_ref, kept_ref, out_ref, act_ref, held_ref, sems = refs[2 * count :]
     part, hidden = gate_ref.shape[1:]
+    cols = part // blocks
+    stream = Stream(sems)
+    cuts = [(start, size, block) for start, size in pieces_of(cols) for block in range(blocks)]
+    copies = []
+    for start, size, block in cuts:
+        span = slice(block * cols + start, block * cols + start + size)
+        copies.append([stream.start(r.at[0, span], held_ref.at[i, span]) for i, r in enumerate((gate_ref, up_ref))])
     for rows in row_parts(act_ref.shape[0]):
         gate_sum = summed(shares, rows, slice(0, hidden))
         up_sum = summed(shares, rows, slice(hidden, 2 * hidden))
@@ -276,26 +354,39 @@
         sig = jax.nn.sigmoid(gate_sum)
         act_ref[rows, :hidden] = (back_sum * up_sum * sig * (1.0 + gate_sum * (1.0 - sig))).astype(BF16)
         act_ref[rows, hidden:] = (back_sum * (gate_sum * sig)).astype(BF16)
+    kept = stream.start(act_ref, kept_ref)
     made = []
-    for span in spans(part, blocks):
-        total = dot(act_ref[:, :hidden], gate_ref[0, span, :], ((1,), (1,)))
-        total = total + dot(act_ref[:, hidden:], up_ref[0, span, :], ((1,), (1,)))
-        made.append(total.astype(BF16))
-    unsort_rows(made, out_ref, slots)
+    for (start, size, block), pair in zip(cuts, copies):
+        span = slice(block * cols + start, block * cols + start + size)
+        terms = []
+        for i in range(2):
+            pair[i].wait()
+            terms.append(dot(act_ref[:, i * hidden : (i + 1) * hidden], held_ref[i, span], ((1,), (1,))))
+        made.append(added(terms).astype(BF16))
+        if block == blocks - 1:
+            unsort_rows(made, out_ref, slots, slice(start, start + size))
+            made = []
+    kept.wait()
 
 
 def grad_rows(shares, backs, w_gate, w_up, blocks, slots):
     part, hidden = w_gate.shape[1:]
     rows = shares[0].shape[0]
+    cols = part // blocks
     return pl.pallas_call(
         functools.partial(grad_rows_kernel, slots, blocks, len(shares)),
-        in_specs=[vmem()] * (2 * len(shares) + 2),
-        out_specs=[vmem()] * 2,
-        out_shape=[shape_of(rows, 2 * hidden), shape_of(blocks * rows, part // blocks)],
-        compiler_params=params(32),
+        in_specs=[vmem()] * (2 * len(shares)) + [hbm()] * 2,
+        out_specs=[hbm(), vmem()],
+        out_shape=[hbm_shape(rows, 2 * hidden), shape_of(blocks * rows, cols)],
+        scratch_shapes=[
+            pltpu.VMEM((rows, 2 * hidden), BF16),
+            pltpu.VMEM((2, part, hidden), BF16),
+            pltpu.SemaphoreType.DMA((2 * blocks * len(pieces_of(cols)) + 1,)),
+        ],
+        compiler_params=params(40),
         cost_estimate=cost(4 * rows * part * hidden, 4 * part * hidden),
         name="gradient_rows",
-    )(*shares, *backs, w_gate, w_up)
+    )(*shares, *backs, in_hbm(w_gate), in_hbm(w_up))
 
 
 def weights_kernel(rows_in_ref, rows_up_ref, act_ref, grad_act_ref, gate_ref, up_ref, down_ref):
@@ -331,6 +422,11 @@
     )(rows_in, rows_up, act, grad_act)
 
 
+def back_rows(back_ref, half, halves, run):
+    total = back_ref.shape[0]
+    return jnp.concatenate([back_ref[start : start + run] for start in range(half * run, total, halves * run)], axis=0)
+
+
 def put_columns(held_ref, target_ref, sems, half, block):
     blocks, _, cols = held_ref.shape[1:]
     place = half * blocks + block
@@ -348,6 +444,8 @@
     hit = spread_row(picks_ref[...].astype(F32), blocks).astype(jnp.int32) == iota((tokens, rows), 0)
     scale = spread_row(gates_ref[...], blocks)
     of_block = iota((tokens, rows), 1) % (blocks * slots) // slots
+    run = planes_of(experts) * blocks * slots
+    backs = [back_rows(back_ref, half, halves, run) for half in range(halves)]
     copies = []
     products = None
     for block in range(blocks):
@@ -359,7 +457,7 @@
             pieces.append(rest.astype(BF16))
             rest = rest - pieces[-1].astype(F32)
         for half in range(halves):
-            back = back_ref[half * rows : (half + 1) * rows]
+            back = backs[half]
             held_ref[half, block] = added([dot(piece, back) for piece in pieces]).astype(BF16)
             copies.append(put_columns(held_ref, mixed_ref, sems, half, block))
             place = half * blocks + block
@@ -368,7 +466,7 @@
             products = product if products is None else products + product
     values = jnp.sum(products, axis=0, keepdims=True)
     mine = iota((slots, rows), 1) % slots == iota((slots, rows), 0)
-    owner = (iota((rows, experts), 0) // (blocks * slots) == iota((rows, experts), 1)).astype(F32)
+    owner = (expert_at(iota((rows, experts), 0) // (blocks * slots), experts) == iota((rows, experts), 1)).astype(F32)
     gate_grad_ref[...] = exact_dot(jnp.where(mine, values, 0.0), owner)
     for copy in copies:
         copy.wait()
@@ -391,25 +489,24 @@
     )(picks, gates, cotangent, back)
 
 
-def token_grad_kernel(put_ref, back_ref, grad_ref, held_ref, sems):
+def token_grad_kernel(run, put_ref, back_ref, grad_ref, held_ref, sems):
     halves, blocks = held_ref.shape[:2]
-    rows = back_ref.shape[0] // halves
     copies = []
     for half in range(halves):
+        back = back_rows(back_ref, half, halves, run)
         for block in range(blocks):
-            back = back_ref[half * rows : (half + 1) * rows]
             held_ref[half, block] = dot(put_ref[block], back).astype(BF16)
             copies.append(put_columns(held_ref, grad_ref, sems, half, block))
     for copy in copies:
         copy.wait()
 
 
-def token_grads(back, put, halves):
+def token_grads(back, put, halves, run):
     blocks, tokens, rows = put.shape
     cols = back.shape[1]
     width = halves * blocks * cols
     return pl.pallas_call(
-        token_grad_kernel,
+        functools.partial(token_grad_kernel, run),
         in_specs=[vmem()] * 2,
         out_specs=hbm(),
         out_shape=shape_of(tokens, width),
@@ -420,8 +517,17 @@
     )(put, back)
 
 
-def scatter(messages):
-    return lax.all_to_all(messages, EVERYONE, split_axis=0, concat_axis=0, tiled=True)
+def to_owners(halves, experts, messages):
+    planes = planes_of(experts)
+    order = [
+        half * experts + plane * (experts // planes) + place
+        for place in range(experts // planes)
+        for half in range(halves)
+        for plane in range(planes)
+    ]
+    return lax.all_to_all(
+        messages, EVERYONE, split_axis=0, concat_axis=0, tiled=True, axis_index_groups=[order]
+    )
 
 
 def dp_shares(own, halves):
@@ -432,7 +538,8 @@
 
 
 def body(halves, tokens, cotangent, picks, gates, w_gate, w_up, w_down):
-    slots = picks.shape[2]
+    experts, slots = picks.shape[1:]
+    scatter = functools.partial(to_owners, halves, experts)
     blocks = 2 if tokens.shape[1] // halves % 256 == 0 else 1
     picks_t = picks[0].T
     gates_t = gates[0].T
@@ -448,7 +555,7 @@
     back_grad = scatter(gradients)
     grad_gate_w, grad_up_w, grad_down = weight_grads(rows_in, rows_up, act, grad_act)
     mixed, gate_grad, put = mix_rows(back_out, cotangent, picks_t, gates_t, halves, blocks)
-    token_grad = token_grads(back_grad, put, halves)
+    token_grad = token_grads(back_grad, put, halves, planes_of(experts) * blocks * slots)
     return mixed, token_grad, gate_grad.T[None], grad_gate_w, grad_up_w, grad_down
 
 

time: 105 us -> 105 us (level)
  local copies, waits for them, and re-layouts: 12.1 us -> 2.11 us
  Pallas kernels: 24.4 us -> 31.7 us
  starting transfers between devices: 23.9 us -> 25.3 us
    unnamed x26 -> x14, local copies, waits for them, and re-layouts: 12.1 us -> 2.11 us
    pallas_call x1, Pallas kernels: 1.4 us -> 4.26 us  [in_sums(): pl.pallas_call(functools.partial(in_sums_kernel, slots), in_specs=[vmem()...]
    pallas_call x1, Pallas kernels: 3.74 us -> 6.47 us  [grad_rows(): pl.pallas_call(functools.partial(grad_rows_kernel, slots, blocks, len(sha...]
    pallas_call x1, Pallas kernels: 1.62 us -> 3.42 us  [up_sums(): pl.pallas_call(functools.partial(up_sums_kernel, slots), in_specs=[vmem()...]
    all_to_all x4, starting transfers between devices: 20.4 us -> 21.8 us  [to_owners(): lax.all_to_all(messages, EVERYONE, split_axis=0, concat_axis=0, tiled=Tru...]
    ppermute x2, waiting for transfers between devices: 19.8 us -> 21.1 us  [dp_shares(): lax.ppermute(own, 'dp', [(i, (i + shift) % halves) for i in range(halves)])]
  transfers between devices with their start and end apart: 6 -> 6, of which waited for: 4 -> 4; matrix products, arithmetic and copies ran while one was open for 0% -> 0% of each run, Pallas kernels for 19% -> 27%
where the time goes in v4:
time: 105 us; the launch traced here: 104 us
  waiting for transfers between devices  44.2 us (42%)
  Pallas kernels  31.7 us (30%)
  starting transfers between devices  25.3 us (24%)
  local copies, waits for them, and re-layouts  2.11 us (2%)
    all_to_all x4, waiting for transfers between devices, to_owners(): lax.all_to_all(messages, EVERYONE, split_axis=0, concat_axis=0, tiled=Tru...  23.2 us
    all_to_all x4, starting transfers between devices, to_owners(): lax.all_to_all(messages, EVERYONE, split_axis=0, concat_axis=0, tiled=Tru...  21.8 us
    ppermute x2, waiting for transfers between devices, dp_shares(): lax.ppermute(own, 'dp', [(i, (i + shift) % halves) for i in range(halves)])  21.1 us
    pallas_call x1, Pallas kernels, grad_rows(): pl.pallas_call(functools.partial(grad_rows_kernel, slots, blocks, len(sha...  6.47 us
    pallas_call x1, Pallas kernels, weight_grads(): pl.pallas_call(weights_kernel, grid=(blocks, steps), in_specs=[chunk, chu...  5.77 us
    pallas_call x2, Pallas kernels, send_rows(): pl.pallas_call(functools.partial(send_kernel, halves, blocks, len(lists)...  5.7 us
    pallas_call x1, Pallas kernels, in_sums(): pl.pallas_call(functools.partial(in_sums_kernel, slots), in_specs=[vmem()...  4.26 us
    ppermute x2, starting transfers between devices, dp_shares(): lax.ppermute(own, 'dp', [(i, (i + shift) % halves) for i in range(halves)])  3.53 us
  transfers between devices with their start and end apart: 6, of which 4 were waited for; matrix products, arithmetic and copies ran while one was open for 0% of the time, Pallas kernels for 27%

profile of v4, /device:TPU:0, one launch (start us, length us, event | category | flops | bytes accessed | tf_op | source)
XLA Modules:
  0.0 104.2 jit_solution(8242174723975893759)
XLA Ops:
  0.6 2.8 %send_rows.2 = bf16[256,1280]{1,0:T(8,128)(2,1)} custom-call(s32[4,16]{1,0:T(4,128)} %bitcast.21, bf16[128,5120]{1,0:T(8,128)(2,1)} %refs_1_.1), custom_call_target="tpu_custom_call" | custom-call | flops 167772160 | bytes 1966080 | tf_op jit(solution)/shard_map/send_rows/pallas_call | solution.py:145
  3.4 7.3 %all-to-all-start = ((bf16[32,8,1280]{2,1,0:T(8,128)(2,1)}), bf16[32,8,1280]{2,1,0:T(8,128)(2,1)S(1)}, u32[]{:S(2)}, u32[]{:S(2)}) async-start(bf16[32,8,1280]{2,1,0:T(8,128)(2,1)} %bitcast.5), calls=%async_computation | async-start | bytes 1310720 | tf_op jit(solution)/shard_map/all_to_all | solution.py:528
  10.7 2.9 %send_rows.3 = bf16[256,1280]{1,0:T(8,128)(2,1)} custom-call(s32[4,16]{1,0:T(4,128)} %bitcast.22, f32[4,16]{1,0:T(4,128)} %bitcast.24, bf16[128,5120]{1,0:T(8,128)(2,1)} %refs_2_.3), custom_call_target="tpu_custom_call" | custom-call | flops 167772160 | bytes 1966080 | tf_op jit(solution)/shard_map/send_rows/pallas_call | solution.py:145
  13.7 15.6 %all-to-all-done = bf16[32,8,1280]{2,1,0:T(8,128)(2,1)S(1)} async-done(((bf16[32,8,1280]{2,1,0:T(8,128)(2,1)}), bf16[32,8,1280]{2,1,0:T(8,128)(2,1)S(1)}, u32[]{:S(2)}, u32[]{:S(2)}) %all-to-all-start) | async-done | bytes 655392 | tf_op jit(solution)/shard_map/all_to_all | solution.py:528
  29.2 2.6 %all-to-all-start.2 = ((bf16[32,8,1280]{2,1,0:T(8,128)(2,1)}), bf16[32,8,1280]{2,1,0:T(8,128)(2,1)S(1)}, u32[]{:S(2)}, u32[]{:S(2)}) async-start(bf16[32,8,1280]{2,1,0:T(8,128)(2,1)} %bitcast.10), calls=%async_computation.2 | async-start | bytes 1310720 | tf_op jit(solution)/shard_map/all_to_all | solution.py:528
  31.9 0.0 copy-start
  31.9 4.3 %gate_up_sums.1 = (bf16[128,1536]{1,0:T(8,128)(2,1)S(1)}, bf16[2,128,1280]{2,1,0:T(8,128)(2,1)}) custom-call(bf16[256,1280]{1,0:T(8,128)(2,1)S(1)} %bitcast.17, bf16[1,2560,768]{2,1,0:T(8,128)(2,1)} %refs_4_.1, bf16[1,2560,768]{2,1,0:T(8,128)(2,1)} %refs_5_.1), custom_call_target="tpu_custom_call" | custom-call | flops 1006632960 | bytes 7864320 | tf_op jit(solution)/shard_map/gate_up_sums/pallas_call | solution.py:249
  36.1 1.7 %collective-permute-start = (bf16[128,1536]{1,0:T(8,128)(2,1)S(1)}, bf16[128,1536]{1,0:T(8,128)(2,1)S(1)}, u32[]{:S(2)}, u32[]{:S(2)}) collective-permute-start(bf16[128,1536]{1,0:T(8,128)(2,1)S(1)} %get-tuple-element.20.refs_0_), channel_id=1, source_target_pairs={{0,16},{16,0},{1,17},{17,1},{2,18},{18,2},{3,19},{19,3},{4,20},{20... | collective-permute-start | bytes 1179656 | tf_op jit(solution)/shard_map/ppermute | solution.py:535
  37.8 13.4 %collective-permute-done.refs_1_ = bf16[128,1536]{1,0:T(8,128)(2,1)S(1)} collective-permute-done((bf16[128,1536]{1,0:T(8,128)(2,1)S(1)}, bf16[128,1536]{1,0:T(8,128)(2,1)S(1)}, u32[]{:S(2)}, u32[]{:S(2)}) %collective-permute-start) | collective-permute-done | bytes 393248 | tf_op jit(solution)/shard_map/ppermute | solution.py:535
  51.2 1.8 %output_rows.1 = (bf16[128,768]{1,0:T(8,128)(2,1)S(1)}, bf16[256,1280]{1,0:T(8,128)(2,1)}) custom-call(bf16[128,1536]{1,0:T(8,128)(2,1)S(1)} %get-tuple-element.20.refs_0_, bf16[128,1536]{1,0:T(8,128)(2,1)S(1)} %collective-permute-done.refs_1_, bf16[1,768,2560]{2,1,0:T(8,128)(2,1)S(1)} %copy-done), custom_call_target="tpu_custom_call" | custom-call | flops 503316480 | bytes 3932160 | tf_op jit(solution)/shard_map/output_rows/pallas_call | solution.py:328
  53.0 4.8 %all-to-all-start.1 = ((bf16[32,8,1280]{2,1,0:T(8,128)(2,1)}), bf16[32,8,1280]{2,1,0:T(8,128)(2,1)S(1)}, u32[]{:S(2)}, u32[]{:S(2)}) async-start(bf16[32,8,1280]{2,1,0:T(8,128)(2,1)} %bitcast.7), calls=%async_computation.1 | async-start | bytes 1310720 | tf_op jit(solution)/shard_map/all_to_all | solution.py:528
  57.8 3.4 %back_sums.1 = (bf16[128,768]{1,0:T(8,128)(2,1)S(1)}, bf16[2,128,1280]{2,1,0:T(8,128)(2,1)}) custom-call(bf16[256,1280]{1,0:T(8,128)(2,1)S(1)} %bitcast.18, bf16[1,768,2560]{2,1,0:T(8,128)(2,1)} %down_ref.1), custom_call_target="tpu_custom_call" | custom-call | flops 503316480 | bytes 3932160 | tf_op jit(solution)/shard_map/back_sums/pallas_call | solution.py:289
  61.3 0.0 copy-start.4
  61.3 1.8 %collective-permute-start.1 = (bf16[128,768]{1,0:T(8,128)(2,1)S(1)}, bf16[128,768]{1,0:T(8,128)(2,1)S(1)}, u32[]{:S(2)}, u32[]{:S(2)}) collective-permute-start(bf16[128,768]{1,0:T(8,128)(2,1)S(1)} %get-tuple-element.24.refs_2_), channel_id=1, source_target_pairs={{0,16},{16,0},{1,17},{17,1},{2,18},{18,2},{3,19},{19,3},{4,20},{20... | collective-permute-start | bytes 589832 | tf_op jit(solution)/shard_map/ppermute | solution.py:535
  63.1 7.7 %collective-permute-done.1.refs_3_ = bf16[128,768]{1,0:T(8,128)(2,1)S(1)} collective-permute-done((bf16[128,768]{1,0:T(8,128)(2,1)S(1)}, bf16[128,768]{1,0:T(8,128)(2,1)S(1)}, u32[]{:S(2)}, u32[]{:S(2)}) %collective-permute-start.1) | collective-permute-done | bytes 196640 | tf_op jit(solution)/shard_map/ppermute | solution.py:535
  70.8 6.5 %gradient_rows.1 = (bf16[128,1536]{1,0:T(8,128)(2,1)}, bf16[256,1280]{1,0:T(8,128)(2,1)}) custom-call(bf16[128,1536]{1,0:T(8,128)(2,1)S(1)} %get-tuple-element.20.refs_0_, bf16[128,1536]{1,0:T(8,128)(2,1)S(1)} %collective-permute-done.refs_1_, bf16[128,768]{1,0:T(8,128)(2,1)S(1)} %get-tuple-element.24.refs_2_, ...), custom_call_target="tpu_custom_call" | custom-call | flops 1006632960 | bytes 7864320 | tf_op jit(solution)/shard_map/gradient_rows/pallas_call | solution.py:376
  77.3 0.0 copy-start.1
  77.3 7.0 %all-to-all-start.3 = ((bf16[32,8,1280]{2,1,0:T(8,128)(2,1)}), bf16[32,8,1280]{2,1,0:T(8,128)(2,1)S(1)}, u32[]{:S(2)}, u32[]{:S(2)}) async-start(bf16[32,8,1280]{2,1,0:T(8,128)(2,1)} %bitcast.12), calls=%async_computation.3 | async-start | bytes 1310720 | tf_op jit(solution)/shard_map/all_to_all | solution.py:528
  84.4 1.1 %copy-done.5 = bf16[2,128,1280]{2,1,0:T(8,128)(2,1)S(1)} copy-done((bf16[2,128,1280]{2,1,0:T(8,128)(2,1)S(1)}, bf16[2,128,1280]{2,1,0:T(8,128)(2,1)}, u32[]{:S(2)}) %copy-start.5) | copy-done | bytes 655384
  85.4 1.0 copy-done.6
  86.4 5.8 %weight_grads.1 = (bf16[1,2560,768]{2,1,0:T(8,128)(2,1)}, bf16[1,2560,768]{2,1,0:T(8,128)(2,1)}, bf16[1,768,2560]{2,1,0:T(8,128)(2,1)}) custom-call(bf16[2,128,1280]{2,1,0:T(8,128)(2,1)S(1)} %copy-done.4, bf16[2,128,1280]{2,1,0:T(8,128)(2,1)S(1)} %copy-done.5, bf16[128,768]{1,0:T(8,128)(2,1)S(1)} %get-tuple-element.29.act_ref, bf16[128,1536]{1,0:T(8,128)(2,1)S(1)} %copy-done.6), custom_call_target="tpu_custom_call" | custom-call | flops 1509949440 | bytes 11796480 | tf_op jit(solution)/shard_map/weight_grads/pallas_call | solution.py:408
  92.2 3.0 %mixed_rows.1 = (bf16[128,5120]{1,0:T(8,128)(2,1)}, f32[4,16]{1,0:T(4,128)}, bf16[2,128,128]{2,1,0:T(8,128)(2,1)S(1)}) custom-call(s32[4,16]{1,0:T(4,128)S(1)} %bitcast.23, f32[4,16]{1,0:T(4,128)S(1)} %bitcast.25, bf16[128,5120]{1,0:T(8,128)(2,1)S(1)} %copy-done.1, bf16[256,1280]{1,0:T(8,128)(2,1)S(1)} %bitcast.20), custom_call_target="tpu_custom_call" | custom-call | flops 671088640 | bytes 2621440 | tf_op jit(solution)/shard_map/mixed_rows/pallas_call | solution.py:480
  95.3 7.6 %all-to-all-done.3 = bf16[32,8,1280]{2,1,0:T(8,128)(2,1)S(1)} async-done(((bf16[32,8,1280]{2,1,0:T(8,128)(2,1)}), bf16[32,8,1280]{2,1,0:T(8,128)(2,1)S(1)}, u32[]{:S(2)}, u32[]{:S(2)}) %all-to-all-start.3) | async-done | bytes 655392 | tf_op jit(solution)/shard_map/all_to_all | solution.py:528
  102.8 1.3 %token_grads.1 = bf16[128,5120]{1,0:T(8,128)(2,1)} custom-call(bf16[2,128,128]{2,1,0:T(8,128)(2,1)S(1)} %get-tuple-element.23.put_ref, bf16[256,1280]{1,0:T(8,128)(2,1)S(1)} %bitcast.19), custom_call_target="tpu_custom_call" | custom-call | flops 167772160 | bytes 1310720 | tf_op jit(solution)/shard_map/token_grads/pallas_call | solution.py:508
  (11 shorter events, 0.0 us)
Async XLA Ops:
  3.4 25.8 %all-to-all-start = ((bf16[32,8,1280]{2,1,0:T(8,128)(2,1)}), bf16[32,8,1280]{2,1,0:T(8,128)(2,1)S(1)}, u32[]{:S(2)}, u32[]{:S(2)}) async-start(bf16[32,8,1280]{2,1,0:T(8,128)(2,1)} %bitcast.5), calls=%async_computation | async-start | bytes 1310720 | tf_op jit(solution)/shard_map/all_to_all | solution.py:528
  29.2 23.8 %all-to-all-start.2 = ((bf16[32,8,1280]{2,1,0:T(8,128)(2,1)}), bf16[32,8,1280]{2,1,0:T(8,128)(2,1)S(1)}, u32[]{:S(2)}, u32[]{:S(2)}) async-start(bf16[32,8,1280]{2,1,0:T(8,128)(2,1)} %bitcast.10), calls=%async_computation.2 | async-start | bytes 1310720 | tf_op jit(solution)/shard_map/all_to_all | solution.py:528
  31.9 19.4 %copy-start = (bf16[1,768,2560]{2,1,0:T(8,128)(2,1)S(1)}, bf16[1,768,2560]{2,1,0:T(8,128)(2,1)}, u32[]{:S(2)}) copy-start(bf16[1,768,2560]{2,1,0:T(8,128)(2,1)} %down_ref.1) | copy-start | bytes 11796484
  36.1 15.1 %collective-permute-start = (bf16[128,1536]{1,0:T(8,128)(2,1)S(1)}, bf16[128,1536]{1,0:T(8,128)(2,1)S(1)}, u32[]{:S(2)}, u32[]{:S(2)}) collective-permute-start(bf16[128,1536]{1,0:T(8,128)(2,1)S(1)} %get-tuple-element.20.refs_0_), channel_id=1, source_target_pairs={{0,16},{16,0},{1,17},{17,1},{2,18},{18,2},{3,19},{19,3},{4,20},{20... | collective-permute-start | bytes 1179656 | tf_op jit(solution)/shard_map/ppermute | solution.py:535
  53.0 24.3 %all-to-all-start.1 = ((bf16[32,8,1280]{2,1,0:T(8,128)(2,1)}), bf16[32,8,1280]{2,1,0:T(8,128)(2,1)S(1)}, u32[]{:S(2)}, u32[]{:S(2)}) async-start(bf16[32,8,1280]{2,1,0:T(8,128)(2,1)} %bitcast.7), calls=%async_computation.1 | async-start | bytes 1310720 | tf_op jit(solution)/shard_map/all_to_all | solution.py:528
  61.3 23.1 %copy-start.4 = (bf16[2,128,1280]{2,1,0:T(8,128)(2,1)S(1)}, bf16[2,128,1280]{2,1,0:T(8,128)(2,1)}, u32[]{:S(2)}) copy-start(bf16[2,128,1280]{2,1,0:T(8,128)(2,1)} %get-tuple-element.27.rows_in_ref) | copy-start | bytes 1966084
  61.3 9.5 %collective-permute-start.1 = (bf16[128,768]{1,0:T(8,128)(2,1)S(1)}, bf16[128,768]{1,0:T(8,128)(2,1)S(1)}, u32[]{:S(2)}, u32[]{:S(2)}) collective-permute-start(bf16[128,768]{1,0:T(8,128)(2,1)S(1)} %get-tuple-element.24.refs_2_), channel_id=1, source_target_pairs={{0,16},{16,0},{1,17},{17,1},{2,18},{18,2},{3,19},{19,3},{4,20},{20... | collective-permute-start | bytes 589832 | tf_op jit(solution)/shard_map/ppermute | solution.py:535
  77.3 15.0 %copy-start.1 = (bf16[128,5120]{1,0:T(8,128)(2,1)S(1)}, bf16[128,5120]{1,0:T(8,128)(2,1)}, u32[]{:S(2)}) copy-start(bf16[128,5120]{1,0:T(8,128)(2,1)} %refs_2_.3) | copy-start | bytes 3932164
  77.3 14.9 %copy-start.2 = (s32[1,16,4]{1,2,0:T(4,128)S(1)}, s32[1,16,4]{1,2,0:T(4,128)}, u32[]{:S(2)}) copy-start(s32[1,16,4]{1,2,0:T(4,128)} %param.9) | copy-start | bytes 772
  77.3 14.9 %copy-start.3 = (f32[1,16,4]{1,2,0:T(4,128)S(1)}, f32[1,16,4]{1,2,0:T(4,128)}, u32[]{:S(2)}) copy-start(f32[1,16,4]{1,2,0:T(4,128)} %param.10) | copy-start | bytes 772
  77.3 25.5 %all-to-all-start.3 = ((bf16[32,8,1280]{2,1,0:T(8,128)(2,1)}), bf16[32,8,1280]{2,1,0:T(8,128)(2,1)S(1)}, u32[]{:S(2)}, u32[]{:S(2)}) async-start(bf16[32,8,1280]{2,1,0:T(8,128)(2,1)} %bitcast.12), calls=%async_computation.3 | async-start | bytes 1310720 | tf_op jit(solution)/shard_map/all_to_all | solution.py:528
  84.3 1.1 %copy-start.5 = (bf16[2,128,1280]{2,1,0:T(8,128)(2,1)S(1)}, bf16[2,128,1280]{2,1,0:T(8,128)(2,1)}, u32[]{:S(2)}) copy-start(bf16[2,128,1280]{2,1,0:T(8,128)(2,1)} %get-tuple-element.28.rows_up_ref) | copy-start | bytes 1966084
  85.4 1.0 copy-start.6

commit v5 on v4

--- a/solution.py
+++ b/solution.py
@@ -92,11 +92,13 @@
     return jnp.sum(jnp.where(mine, wide, 0.0), axis=0, keepdims=True)
 
 
-def send_kernel(halves, blocks, scaled, *refs):
+def send_kernel(halves, blocks, scaled, extra, *refs):
     count = 2 if scaled else 1
-    lists, source_ref, out_ref = refs[:count], refs[count], refs[count + 1]
-    held_ref, sems, list_sems = refs[count + 2 : count + 5]
-    list_refs = refs[count + 5 :]
+    lists, source_ref, refs = refs[:count], refs[count], refs[count + 1 :]
+    kept, out_ref, refs = refs[:extra], refs[extra], refs[extra + 1 :]
+    kept_refs, refs = refs[:extra], refs[extra:]
+    held_ref, sems, list_sems, kept_sems = refs[:4]
+    list_refs = refs[4:]
     rows, cols = out_ref.shape
     rows = rows // halves
     tokens = source_ref.shape[0]
@@ -117,6 +119,11 @@
                 )
             )
             copies[-1].start()
+    kept_copies = [
+        pltpu.make_async_copy(ref, target, kept_sems.at[i]) for i, (ref, target) in enumerate(zip(kept, kept_refs))
+    ]
+    for copy in kept_copies:
+        copy.start()
     for copy in list_copies:
         copy.wait()
     slots, experts = list_refs[0].shape
@@ -135,28 +142,31 @@
         for place in range(rows // run):
             start = (place * halves + half) * run
             out_ref[start : start + run] = picked[place * run : (place + 1) * run]
-
-
-def send_rows(source, lists, halves, blocks):
+    for copy in kept_copies:
+        copy.wait()
+
+
+def send_rows(source, lists, halves, blocks, kept=()):
     slots, experts = lists[0].shape
     tokens, width = source.shape
     cols = width // (halves * blocks)
     rows = halves * experts * blocks * slots
     return pl.pallas_call(
-        functools.partial(send_kernel, halves, blocks, len(lists) == 2),
-        in_specs=[hbm()] * (len(lists) + 1),
-        out_specs=vmem(),
-        out_shape=shape_of(rows, cols),
+        functools.partial(send_kernel, halves, blocks, len(lists) == 2, len(kept)),
+        in_specs=[hbm()] * (len(lists) + 1 + len(kept)),
+        out_specs=[vmem()] * (1 + len(kept)),
+        out_shape=[shape_of(rows, cols)] + [shape_of(*value.shape) for value in kept],
         scratch_shapes=[
             pltpu.VMEM((halves, blocks * tokens, cols), BF16),
             pltpu.SemaphoreType.DMA((halves, blocks)),
             pltpu.SemaphoreType.DMA((2,)),
+            pltpu.SemaphoreType.DMA((2,)),
         ]
         + [pltpu.VMEM((slots, experts), value.dtype) for value in lists],
         compiler_params=params(16),
-        cost_estimate=cost(2 * rows * cols * tokens * blocks, 2 * tokens * width + 2 * rows * cols),
+        cost_estimate=cost(2 * rows * cols * tokens * blocks, 2 * tokens * width + 2 * sum(v.size for v in kept)),
         name="send_rows",
-    )(*[in_hbm(value) for value in lists], in_hbm(source))
+    )(*[in_hbm(value) for value in lists], in_hbm(source), *[in_hbm(value) for value in kept])
 
 
 def sort_matrix(rows, blocks, slots, back):
@@ -220,87 +230,46 @@
         return copy
 
 
-def in_sums_kernel(slots, messages_ref, gate_ref, up_ref, out_ref, kept_ref, rows_ref, held_ref, acc_ref, sems):
+def sums_kernel(slots, back, messages_ref, *refs):
+    count = 1 if back else 2
+    weights, (_, out_ref, kept_ref, _, rows_ref, sem) = refs[:count], refs[count:]
     blocks, _, cols = rows_ref.shape
-    hidden = gate_ref.shape[2]
-    stream = Stream(sems)
-    cuts = [(block, start, size) for block in range(blocks) for start, size in pieces_of(cols)]
-    copies = []
-    for block, start, size in cuts:
-        span = slice(block * cols + start, block * cols + start + size)
-        copies += [stream.start(ref.at[0, span], held_ref.at[i, span]) for i, ref in enumerate((gate_ref, up_ref))]
+    hidden = out_ref.shape[1] // count
     sort_rows(messages_ref, rows_ref, slots)
-    kept = stream.start(rows_ref, kept_ref)
-    for number, (block, start, size) in enumerate(cuts):
-        span = slice(block * cols + start, block * cols + start + size)
-        for i in range(2):
-            copies[2 * number + i].wait()
-            term = dot(rows_ref[block, :, start : start + size], held_ref[i, span])
-            acc_ref[i] = term if number == 0 else acc_ref[i] + term
-    for i in range(2):
-        out_ref[:, i * hidden : (i + 1) * hidden] = acc_ref[i].astype(BF16)
+    kept = pltpu.make_async_copy(rows_ref, kept_ref, sem)
+    kept.start()
+    for place, ref in enumerate(weights):
+        terms = []
+        for block, span in enumerate(spans(blocks * cols, blocks)):
+            if back:
+                terms.append(dot(rows_ref[block], ref[0, :, span], ((1,), (1,))))
+            else:
+                terms.append(dot(rows_ref[block], ref[0, span, :]))
+        out_ref[:, place * hidden : (place + 1) * hidden] = added(terms).astype(BF16)
     kept.wait()
 
 
-def in_sums(messages, w_gate, w_up, blocks, slots):
-    part, hidden = w_gate.shape[1:]
+def column_sums(messages, weights, following, hidden, blocks, slots):
     rows = messages.shape[0] // blocks
-    cols = part // blocks
-    return pl.pallas_call(
-        functools.partial(in_sums_kernel, slots),
-        in_specs=[vmem(), hbm(), hbm()],
-        out_specs=[vmem(), hbm()],
-        out_shape=[shape_of(rows, 2 * hidden), hbm_shape(blocks, rows, cols)],
-        scratch_shapes=[
-            pltpu.VMEM((blocks, rows, cols), BF16),
-            pltpu.VMEM((2, part, hidden), BF16),
-            pltpu.VMEM((2, rows, hidden), F32),
-            pltpu.SemaphoreType.DMA((2 * blocks * len(pieces_of(cols)) + 1,)),
+    cols = messages.shape[1]
+    back = len(weights) == 1
+    return pl.pallas_call(
+        functools.partial(sums_kernel, slots, back),
+        in_specs=[vmem()] * (1 + len(weights)) + [hbm()],
+        out_specs=[vmem(), hbm(), hbm()],
+        out_shape=[
+            shape_of(rows, len(weights) * hidden),
+            hbm_shape(blocks, rows, cols),
+            hbm_shape(*following.shape),
         ],
+        scratch_shapes=[pltpu.VMEM((blocks, rows, cols), BF16), pltpu.SemaphoreType.DMA],
+        input_output_aliases={1 + len(weights): 2},
         compiler_params=params(),
-        cost_estimate=cost(4 * rows * part * hidden, 4 * part * hidden),
-        name="gate_up_sums",
-    )(messages, in_hbm(w_gate), in_hbm(w_up))
-
-
-def up_sums_kernel(slots, messages_ref, down_ref, out_ref, kept_ref, rows_ref, held_ref, acc_ref, sems):
-    blocks, _, cols = rows_ref.shape
-    stream = Stream(sems)
-    cuts = [(block, start, size) for block in range(blocks) for start, size in pieces_of(cols)]
-    copies = []
-    for block, start, size in cuts:
-        span = slice(block * cols + start, block * cols + start + size)
-        copies.append(stream.start(down_ref.at[0, :, span], held_ref.at[:, span]))
-    sort_rows(messages_ref, rows_ref, slots)
-    kept = stream.start(rows_ref, kept_ref)
-    for number, (block, start, size) in enumerate(cuts):
-        span = slice(block * cols + start, block * cols + start + size)
-        copies[number].wait()
-        term = dot(rows_ref[block, :, start : start + size], held_ref[:, span], ((1,), (1,)))
-        acc_ref[...] = term if number == 0 else acc_ref[...] + term
-    out_ref[...] = acc_ref[...].astype(BF16)
-    kept.wait()
-
-
-def up_sums(messages, w_down, blocks, slots):
-    hidden, part = w_down.shape[1:]
-    rows = messages.shape[0] // blocks
-    cols = part // blocks
-    return pl.pallas_call(
-        functools.partial(up_sums_kernel, slots),
-        in_specs=[vmem(), hbm()],
-        out_specs=[vmem(), hbm()],
-        out_shape=[shape_of(rows, hidden), hbm_shape(blocks, rows, cols)],
-        scratch_shapes=[
-            pltpu.VMEM((blocks, rows, cols), BF16),
-            pltpu.VMEM((hidden, part), BF16),
-            pltpu.VMEM((rows, hidden), F32),
-            pltpu.SemaphoreType.DMA((blocks * len(pieces_of(cols)) + 1,)),
-        ],
-        compiler_params=params(),
-        cost_estimate=cost(2 * rows * part * hidden, 2 * part * hidden),
-        name="back_sums",
-    )(messages, in_hbm(w_down))
+        cost_estimate=cost(
+            2 * len(weights) * rows * blocks * cols * hidden, 2 * len(weights) * blocks * cols * hidden
+        ),
+        name="back_sums" if back else "gate_up_sums",
+    )(messages, *weights, in_hbm(following))
 
 
 def row_parts(total):
@@ -543,14 +512,16 @@
     blocks = 2 if tokens.shape[1] // halves % 256 == 0 else 1
     picks_t = picks[0].T
     gates_t = gates[0].T
-    arrived_in = scatter(send_rows(tokens, (picks_t,), halves, blocks))
-    arrived_up = scatter(send_rows(cotangent, (picks_t, gates_t), halves, blocks))
-    own_sums, rows_in = in_sums(arrived_in, w_gate, w_up, blocks, slots)
+    hidden = w_gate.shape[2]
+    arrived_in = scatter(send_rows(tokens, (picks_t,), halves, blocks)[0])
+    messages_up, near_gate, near_up = send_rows(cotangent, (picks_t, gates_t), halves, blocks, (w_gate, w_up))
+    own_sums, rows_in, messages_up = column_sums(arrived_in, (near_gate, near_up), messages_up, hidden, blocks, slots)
     shares = dp_shares(own_sums, halves)
+    arrived_up = scatter(messages_up)
     act, outputs = out_rows(shares, w_down, blocks, slots)
+    own_back, rows_up, outputs = column_sums(arrived_up, (w_down,), outputs, hidden, blocks, slots)
+    backs = dp_shares(own_back, halves)
     back_out = scatter(outputs)
-    own_back, rows_up = up_sums(arrived_up, w_down, blocks, slots)
-    backs = dp_shares(own_back, halves)
     grad_act, gradients = grad_rows(shares, backs, w_gate, w_up, blocks, slots)
     back_grad = scatter(gradients)
     grad_gate_w, grad_up_w, grad_down = weight_grads(rows_in, rows_up, act, grad_act)

time: 105 us -> 114 us (1.086)
  local copies, waits for them, and re-layouts: 2.11 us -> 16.1 us
  Pallas kernels: 31.7 us -> 27.8 us
    unnamed x14 -> x28, local copies, waits for them, and re-layouts: 2.11 us -> 16.1 us
    ppermute x2, waiting for transfers between devices: 21.1 us -> 26.8 us  [dp_shares(): lax.ppermute(own, 'dp', [(i, (i + shift) % halves) for i in range(halves)])]
    all_to_all x4, waiting for transfers between devices: 23.2 us -> 17.5 us  [to_owners(): lax.all_to_all(messages, EVERYONE, split_axis=0, concat_axis=0, tiled=Tru...]
    pallas_call x2, Pallas kernels: 7.67 us -> 3.69 us  [column_sums(): pl.pallas_call(functools.partial(sums_kernel, slots, back), in_specs=[vme...]
  transfers between devices with their start and end apart: 6 -> 6, of which waited for: 4 -> 4; matrix products, arithmetic and copies ran while one was open for 0% -> 0% of each run, Pallas kernels for 27% -> 18%
where the time goes in v5:
time: 114 us
  waiting for transfers between devices  44.3 us (39%)
  Pallas kernels  27.8 us (24%)
  starting transfers between devices  24.7 us (22%)
  local copies, waits for them, and re-layouts  16.1 us (14%)
    ppermute x2, waiting for transfers between devices, dp_shares(): lax.ppermute(own, 'dp', [(i, (i + shift) % halves) for i in range(halves)])  26.8 us
    all_to_all x4, starting transfers between devices, to_owners(): lax.all_to_all(messages, EVERYONE, split_axis=0, concat_axis=0, tiled=Tru...  21.1 us
    all_to_all x4, waiting for transfers between devices, to_owners(): lax.all_to_all(messages, EVERYONE, split_axis=0, concat_axis=0, tiled=Tru...  17.5 us
    unnamed x28, local copies, waits for them, and re-layouts  16.1 us
    pallas_call x2, Pallas kernels, send_rows(): pl.pallas_call(functools.partial(send_kernel, halves, blocks, len(lists)...  6.64 us
    pallas_call x1, Pallas kernels, grad_rows(): pl.pallas_call(functools.partial(grad_rows_kernel, slots, blocks, len(sha...  6.44 us
    pallas_call x1, Pallas kernels, weight_grads(): pl.pallas_call(weights_kernel, grid=(blocks, steps), in_specs=[chunk, chu...  5.77 us
    pallas_call x2, Pallas kernels, column_sums(): pl.pallas_call(functools.partial(sums_kernel, slots, back), in_specs=[vme...  3.69 us
  transfers between devices with their start and end apart: 6, of which 4 were waited for; matrix products, arithmetic and copies ran while one was open for 0% of the time, Pallas kernels for 18%

profile of v5, /device:TPU:0, one launch (start us, length us, event | category | flops | bytes accessed | tf_op | source)
XLA Modules:
  0.0 113.7 jit_solution(6582615007454902177)
XLA Ops:
  0.6 2.8 %send_rows.2 = bf16[256,1280]{1,0:T(8,128)(2,1)} custom-call(s32[4,16]{1,0:T(4,128)} %bitcast.23, bf16[128,5120]{1,0:T(8,128)(2,1)} %refs_1_.1), custom_call_target="tpu_custom_call" | custom-call | flops 167772160 | bytes 1310720 | tf_op jit(solution)/shard_map/send_rows/pallas_call | solution.py:154
  3.5 7.3 %all-to-all-start = ((bf16[32,8,1280]{2,1,0:T(8,128)(2,1)}), bf16[32,8,1280]{2,1,0:T(8,128)(2,1)S(1)}, u32[]{:S(2)}, u32[]{:S(2)}) async-start(bf16[32,8,1280]{2,1,0:T(8,128)(2,1)} %bitcast.5), calls=%async_computation | async-start | bytes 1310720 | tf_op jit(solution)/shard_map/all_to_all | solution.py:497
  10.8 3.8 %send_rows.3 = (bf16[256,1280]{1,0:T(8,128)(2,1)S(1)}, bf16[1,2560,768]{2,1,0:T(8,128)(2,1)S(1)}, bf16[1,2560,768]{2,1,0:T(8,128)(2,1)S(1)}) custom-call(s32[4,16]{1,0:T(4,128)} %bitcast.24, f32[4,16]{1,0:T(4,128)} %bitcast.26, bf16[128,5120]{1,0:T(8,128)(2,1)} %cot_ref.1, bf16[1,2560,768]{2,1,0:T(8,128)(2,1)} %refs_4_.3, bf16[1,2560,768]{2,1,0:T(8,128)(2,1)} %refs_5_.1), custom_call_target="tpu_custom_call" | custom-call | flops 167772160 | bytes 9175040 | tf_op jit(solution)/shard_map/send_rows/pallas_call | solution.py:154
  14.6 1.9 %copy-done.2 = bf16[1,2560,768]{2,1,0:T(8,128)(2,1)} copy-done((bf16[1,2560,768]{2,1,0:T(8,128)(2,1)}, bf16[1,2560,768]{2,1,0:T(8,128)(2,1)S(1)}, u32[]{:S(2)}) %copy-start.2) | copy-done | bytes 3932184
  16.5 1.9 %copy-done.4 = bf16[1,2560,768]{2,1,0:T(8,128)(2,1)} copy-done((bf16[1,2560,768]{2,1,0:T(8,128)(2,1)}, bf16[1,2560,768]{2,1,0:T(8,128)(2,1)S(1)}, u32[]{:S(2)}) %copy-start.4) | copy-done | bytes 3932184
  19.3 10.0 %all-to-all-done = bf16[32,8,1280]{2,1,0:T(8,128)(2,1)S(1)} async-done(((bf16[32,8,1280]{2,1,0:T(8,128)(2,1)}), bf16[32,8,1280]{2,1,0:T(8,128)(2,1)S(1)}, u32[]{:S(2)}, u32[]{:S(2)}) %all-to-all-start) | async-done | bytes 655392 | tf_op jit(solution)/shard_map/all_to_all | solution.py:497
  29.3 2.1 %copy-done.3 = bf16[1,2560,768]{2,1,0:T(8,128)(2,1)S(1)} copy-done((bf16[1,2560,768]{2,1,0:T(8,128)(2,1)S(1)}, bf16[1,2560,768]{2,1,0:T(8,128)(2,1)}, u32[]{:S(2)}) %copy-start.3) | copy-done | bytes 3932184
  31.4 2.1 %copy-done.5 = bf16[1,2560,768]{2,1,0:T(8,128)(2,1)S(1)} copy-done((bf16[1,2560,768]{2,1,0:T(8,128)(2,1)S(1)}, bf16[1,2560,768]{2,1,0:T(8,128)(2,1)}, u32[]{:S(2)}) %copy-start.5) | copy-done | bytes 3932184
  33.5 2.0 %gate_up_sums.1 = (bf16[128,1536]{1,0:T(8,128)(2,1)S(1)}, bf16[2,128,1280]{2,1,0:T(8,128)(2,1)}, bf16[256,1280]{1,0:T(8,128)(2,1)}) custom-call(bf16[256,1280]{1,0:T(8,128)(2,1)S(1)} %bitcast.17, bf16[1,2560,768]{2,1,0:T(8,128)(2,1)S(1)} %copy-done.3, bf16[1,2560,768]{2,1,0:T(8,128)(2,1)S(1)} %copy-done.5, ...), custom_call_target="tpu_custom_call", output_to_operand_aliasing={{2}: (3, {})} | custom-call | flops 1006632960 | bytes 7864320 | tf_op jit(solution)/shard_map/gate_up_sums/pallas_call | solution.py:256
  35.5 2.6 %all-to-all-start.1 = ((bf16[32,8,1280]{2,1,0:T(8,128)(2,1)}), bf16[32,8,1280]{2,1,0:T(8,128)(2,1)S(1)}, u32[]{:S(2)}, u32[]{:S(2)}) async-start(bf16[32,8,1280]{2,1,0:T(8,128)(2,1)} %bitcast.18), calls=%async_computation.1 | async-start | bytes 1310720 | tf_op jit(solution)/shard_map/all_to_all | solution.py:497
  38.2 1.7 %collective-permute-start = (bf16[128,1536]{1,0:T(8,128)(2,1)S(1)}, bf16[128,1536]{1,0:T(8,128)(2,1)S(1)}, u32[]{:S(2)}, u32[]{:S(2)}) collective-permute-start(bf16[128,1536]{1,0:T(8,128)(2,1)S(1)} %get-tuple-element.29.refs_0_), channel_id=1, source_target_pairs={{0,16},{16,0},{1,17},{17,1},{2,18},{18,2},{3,19},{19,3},{4,20},{20... | collective-permute-start | bytes 1179656 | tf_op jit(solution)/shard_map/ppermute | solution.py:504
  39.9 16.3 %collective-permute-done.refs_1_ = bf16[128,1536]{1,0:T(8,128)(2,1)S(1)} collective-permute-done((bf16[128,1536]{1,0:T(8,128)(2,1)S(1)}, bf16[128,1536]{1,0:T(8,128)(2,1)S(1)}, u32[]{:S(2)}, u32[]{:S(2)}) %collective-permute-start) | collective-permute-done | bytes 393248 | tf_op jit(solution)/shard_map/ppermute | solution.py:504
  56.1 2.1 %copy-done = bf16[1,768,2560]{2,1,0:T(8,128)(2,1)S(1)} copy-done((bf16[1,768,2560]{2,1,0:T(8,128)(2,1)S(1)}, bf16[1,768,2560]{2,1,0:T(8,128)(2,1)}, u32[]{:S(2)}) %copy-start) | copy-done | bytes 3932184
  60.0 2.1 %copy-done.1 = bf16[1,768,2560]{2,1,0:T(8,128)(2,1)S(1)} copy-done((bf16[1,768,2560]{2,1,0:T(8,128)(2,1)S(1)}, bf16[1,768,2560]{2,1,0:T(8,128)(2,1)}, u32[]{:S(2)}) %copy-start.1) | copy-done | bytes 3932184
  62.2 1.6 %back_sums.1 = (bf16[128,768]{1,0:T(8,128)(2,1)S(1)}, bf16[2,128,1280]{2,1,0:T(8,128)(2,1)}, bf16[256,1280]{1,0:T(8,128)(2,1)}) custom-call(bf16[256,1280]{1,0:T(8,128)(2,1)S(1)} %bitcast.19, bf16[1,768,2560]{2,1,0:T(8,128)(2,1)S(1)} %copy-done.1, bf16[256,1280]{1,0:T(8,128)(2,1)} %copy-done.7), custom_call_target="tpu_custom_call", output_to_operand_aliasing={{2}: (2, {})} | custom-call | flops 503316480 | bytes 3932160 | tf_op jit(solution)/shard_map/back_sums/pallas_call | solution.py:256
  63.8 4.9 %all-to-all-start.2 = ((bf16[32,8,1280]{2,1,0:T(8,128)(2,1)}), bf16[32,8,1280]{2,1,0:T(8,128)(2,1)S(1)}, u32[]{:S(2)}, u32[]{:S(2)}) async-start(bf16[32,8,1280]{2,1,0:T(8,128)(2,1)} %bitcast.20), calls=%async_computation.2 | async-start | bytes 1310720 | tf_op jit(solution)/shard_map/all_to_all | solution.py:497
  68.7 1.8 %collective-permute-start.1 = (bf16[128,768]{1,0:T(8,128)(2,1)S(1)}, bf16[128,768]{1,0:T(8,128)(2,1)S(1)}, u32[]{:S(2)}, u32[]{:S(2)}) collective-permute-start(bf16[128,768]{1,0:T(8,128)(2,1)S(1)} %get-tuple-element.34.refs_2_), channel_id=1, source_target_pairs={{0,16},{16,0},{1,17},{17,1},{2,18},{18,2},{3,19},{19,3},{4,20},{20... | collective-permute-start | bytes 589832 | tf_op jit(solution)/shard_map/ppermute | solution.py:504
  70.6 10.5 %collective-permute-done.1.refs_3_ = bf16[128,768]{1,0:T(8,128)(2,1)S(1)} collective-permute-done((bf16[128,768]{1,0:T(8,128)(2,1)S(1)}, bf16[128,768]{1,0:T(8,128)(2,1)S(1)}, u32[]{:S(2)}, u32[]{:S(2)}) %collective-permute-start.1) | collective-permute-done | bytes 196640 | tf_op jit(solution)/shard_map/ppermute | solution.py:504
  81.1 6.4 %gradient_rows.1 = (bf16[128,1536]{1,0:T(8,128)(2,1)}, bf16[256,1280]{1,0:T(8,128)(2,1)}) custom-call(bf16[128,1536]{1,0:T(8,128)(2,1)S(1)} %get-tuple-element.29.refs_0_, bf16[128,1536]{1,0:T(8,128)(2,1)S(1)} %collective-permute-done.refs_1_, bf16[128,768]{1,0:T(8,128)(2,1)S(1)} %get-tuple-element.34.refs_2_, ...), custom_call_target="tpu_custom_call" | custom-call | flops 1006632960 | bytes 7864320 | tf_op jit(solution)/shard_map/gradient_rows/pallas_call | solution.py:345
  87.6 6.3 %all-to-all-start.3 = ((bf16[32,8,1280]{2,1,0:T(8,128)(2,1)}), bf16[32,8,1280]{2,1,0:T(8,128)(2,1)S(1)}, u32[]{:S(2)}, u32[]{:S(2)}) async-start(bf16[32,8,1280]{2,1,0:T(8,128)(2,1)} %bitcast.12), calls=%async_computation.3 | async-start | bytes 1310720 | tf_op jit(solution)/shard_map/all_to_all | solution.py:497
  96.0 5.8 %weight_grads.1 = (bf16[1,2560,768]{2,1,0:T(8,128)(2,1)}, bf16[1,2560,768]{2,1,0:T(8,128)(2,1)}, bf16[1,768,2560]{2,1,0:T(8,128)(2,1)}) custom-call(bf16[2,128,1280]{2,1,0:T(8,128)(2,1)S(1)} %copy-done.11, bf16[2,128,1280]{2,1,0:T(8,128)(2,1)S(1)} %copy-done.12, bf16[128,768]{1,0:T(8,128)(2,1)S(1)} %get-tuple-element.39.act_ref, bf16[128,1536]{1,0:T(8,128)(2,1)S(1)} %copy-done.13), custom_call_target="tpu_custom_call" | custom-call | flops 1509949440 | bytes 11796480 | tf_op jit(solution)/shard_map/weight_grads/pallas_call | solution.py:377
  101.8 3.0 %mixed_rows.1 = (bf16[128,5120]{1,0:T(8,128)(2,1)}, f32[4,16]{1,0:T(4,128)}, bf16[2,128,128]{2,1,0:T(8,128)(2,1)S(1)}) custom-call(s32[4,16]{1,0:T(4,128)S(1)} %bitcast.25, f32[4,16]{1,0:T(4,128)S(1)} %bitcast.27, bf16[128,5120]{1,0:T(8,128)(2,1)S(1)} %copy-done.8, bf16[256,1280]{1,0:T(8,128)(2,1)S(1)} %bitcast.22), custom_call_target="tpu_custom_call" | custom-call | flops 671088640 | bytes 2621440 | tf_op jit(solution)/shard_map/mixed_rows/pallas_call | solution.py:449
  104.8 7.6 %all-to-all-done.3 = bf16[32,8,1280]{2,1,0:T(8,128)(2,1)S(1)} async-done(((bf16[32,8,1280]{2,1,0:T(8,128)(2,1)}), bf16[32,8,1280]{2,1,0:T(8,128)(2,1)S(1)}, u32[]{:S(2)}, u32[]{:S(2)}) %all-to-all-start.3) | async-done | bytes 655392 | tf_op jit(solution)/shard_map/all_to_all | solution.py:497
  112.4 1.3 %token_grads.1 = bf16[128,5120]{1,0:T(8,128)(2,1)} custom-call(bf16[2,128,128]{2,1,0:T(8,128)(2,1)S(1)} %get-tuple-element.33.put_ref, bf16[256,1280]{1,0:T(8,128)(2,1)S(1)} %bitcast.21), custom_call_target="tpu_custom_call" | custom-call | flops 167772160 | bytes 1310720 | tf_op jit(solution)/shard_map/token_grads/pallas_call | solution.py:477
  (25 shorter events, 4.7 us)
Async XLA Ops:
  3.5 25.8 %all-to-all-start = ((bf16[32,8,1280]{2,1,0:T(8,128)(2,1)}), bf16[32,8,1280]{2,1,0:T(8,128)(2,1)S(1)}, u32[]{:S(2)}, u32[]{:S(2)}) async-start(bf16[32,8,1280]{2,1,0:T(8,128)(2,1)} %bitcast.5), calls=%async_computation | async-start | bytes 1310720 | tf_op jit(solution)/shard_map/all_to_all | solution.py:497
  14.6 1.9 %copy-start.2 = (bf16[1,2560,768]{2,1,0:T(8,128)(2,1)}, bf16[1,2560,768]{2,1,0:T(8,128)(2,1)S(1)}, u32[]{:S(2)}) copy-start(bf16[1,2560,768]{2,1,0:T(8,128)(2,1)S(1)} %get-tuple-element.25.refs_0_) | copy-start | bytes 11796484
  16.5 1.9 %copy-start.4 = (bf16[1,2560,768]{2,1,0:T(8,128)(2,1)}, bf16[1,2560,768]{2,1,0:T(8,128)(2,1)S(1)}, u32[]{:S(2)}) copy-start(bf16[1,2560,768]{2,1,0:T(8,128)(2,1)S(1)} %get-tuple-element.26.refs_1_) | copy-start | bytes 11796484
  18.4 0.8 copy-start.6
  29.3 2.1 %copy-start.3 = (bf16[1,2560,768]{2,1,0:T(8,128)(2,1)S(1)}, bf16[1,2560,768]{2,1,0:T(8,128)(2,1)}, u32[]{:S(2)}) copy-start(bf16[1,2560,768]{2,1,0:T(8,128)(2,1)} %copy-done.2) | copy-start | bytes 11796484
  31.4 2.1 %copy-start.5 = (bf16[1,2560,768]{2,1,0:T(8,128)(2,1)S(1)}, bf16[1,2560,768]{2,1,0:T(8,128)(2,1)}, u32[]{:S(2)}) copy-start(bf16[1,2560,768]{2,1,0:T(8,128)(2,1)} %copy-done.4) | copy-start | bytes 11796484
  35.5 24.5 %all-to-all-start.1 = ((bf16[32,8,1280]{2,1,0:T(8,128)(2,1)}), bf16[32,8,1280]{2,1,0:T(8,128)(2,1)S(1)}, u32[]{:S(2)}, u32[]{:S(2)}) async-start(bf16[32,8,1280]{2,1,0:T(8,128)(2,1)} %bitcast.18), calls=%async_computation.1 | async-start | bytes 1310720 | tf_op jit(solution)/shard_map/all_to_all | solution.py:497
  38.2 18.0 %collective-permute-start = (bf16[128,1536]{1,0:T(8,128)(2,1)S(1)}, bf16[128,1536]{1,0:T(8,128)(2,1)S(1)}, u32[]{:S(2)}, u32[]{:S(2)}) collective-permute-start(bf16[128,1536]{1,0:T(8,128)(2,1)S(1)} %get-tuple-element.29.refs_0_), channel_id=1, source_target_pairs={{0,16},{16,0},{1,17},{17,1},{2,18},{18,2},{3,19},{19,3},{4,20},{20... | collective-permute-start | bytes 1179656 | tf_op jit(solution)/shard_map/ppermute | solution.py:504
  56.1 2.1 %copy-start = (bf16[1,768,2560]{2,1,0:T(8,128)(2,1)S(1)}, bf16[1,768,2560]{2,1,0:T(8,128)(2,1)}, u32[]{:S(2)}) copy-start(bf16[1,768,2560]{2,1,0:T(8,128)(2,1)} %refs_0_.1) | copy-start | bytes 11796484
  59.2 0.8 copy-start.7
  60.0 2.1 %copy-start.1 = (bf16[1,768,2560]{2,1,0:T(8,128)(2,1)S(1)}, bf16[1,768,2560]{2,1,0:T(8,128)(2,1)}, u32[]{:S(2)}) copy-start(bf16[1,768,2560]{2,1,0:T(8,128)(2,1)} %refs_0_.1) | copy-start | bytes 11796484
  63.8 23.8 %all-to-all-start.2 = ((bf16[32,8,1280]{2,1,0:T(8,128)(2,1)}), bf16[32,8,1280]{2,1,0:T(8,128)(2,1)S(1)}, u32[]{:S(2)}, u32[]{:S(2)}) async-start(bf16[32,8,1280]{2,1,0:T(8,128)(2,1)} %bitcast.20), calls=%async_computation.2 | async-start | bytes 1310720 | tf_op jit(solution)/shard_map/all_to_all | solution.py:497
  68.7 25.2 %copy-start.11 = (bf16[2,128,1280]{2,1,0:T(8,128)(2,1)S(1)}, bf16[2,128,1280]{2,1,0:T(8,128)(2,1)}, u32[]{:S(2)}) copy-start(bf16[2,128,1280]{2,1,0:T(8,128)(2,1)} %get-tuple-element.37.rows_in_ref) | copy-start | bytes 1966084
  68.7 12.4 %collective-permute-start.1 = (bf16[128,768]{1,0:T(8,128)(2,1)S(1)}, bf16[128,768]{1,0:T(8,128)(2,1)S(1)}, u32[]{:S(2)}, u32[]{:S(2)}) collective-permute-start(bf16[128,768]{1,0:T(8,128)(2,1)S(1)} %get-tuple-element.34.refs_2_), channel_id=1, source_target_pairs={{0,16},{16,0},{1,17},{17,1},{2,18},{18,2},{3,19},{19,3},{4,20},{20... | collective-permute-start | bytes 589832 | tf_op jit(solution)/shard_map/ppermute | solution.py:504
  87.5 14.2 %copy-start.8 = (bf16[128,5120]{1,0:T(8,128)(2,1)S(1)}, bf16[128,5120]{1,0:T(8,128)(2,1)}, u32[]{:S(2)}) copy-start(bf16[128,5120]{1,0:T(8,128)(2,1)} %cot_ref.1) | copy-start | bytes 3932164
  87.6 14.2 %copy-start.9 = (s32[1,16,4]{1,2,0:T(4,128)S(1)}, s32[1,16,4]{1,2,0:T(4,128)}, u32[]{:S(2)}) copy-start(s32[1,16,4]{1,2,0:T(4,128)} %param.9) | copy-start | bytes 772
  87.6 14.2 %copy-start.10 = (f32[1,16,4]{1,2,0:T(4,128)S(1)}, f32[1,16,4]{1,2,0:T(4,128)}, u32[]{:S(2)}) copy-start(f32[1,16,4]{1,2,0:T(4,128)} %param.10) | copy-start | bytes 772
  87.6 24.8 %all-to-all-start.3 = ((bf16[32,8,1280]{2,1,0:T(8,128)(2,1)}), bf16[32,8,1280]{2,1,0:T(8,128)(2,1)S(1)}, u32[]{:S(2)}, u32[]{:S(2)}) async-start(bf16[32,8,1280]{2,1,0:T(8,128)(2,1)} %bitcast.12), calls=%async_computation.3 | async-start | bytes 1310720 | tf_op jit(solution)/shard_map/all_to_all | solution.py:497
  93.9 1.1 copy-start.12
  95.0 1.0 copy-start.13

commit v6 on v4

--- a/solution.py
+++ b/solution.py
@@ -209,6 +209,11 @@
     return [(0, first), (first, width - first)]
 
 
+def thirds_of(height):
+    size = height // 3 if height % 384 == 0 else height
+    return [(start, size) for start in range(0, height, size)]
+
+
 class Stream:
     def __init__(self, sems):
         self.sems, self.copies = sems, []
@@ -220,82 +225,83 @@
         return copy
 
 
-def in_sums_kernel(slots, messages_ref, gate_ref, up_ref, out_ref, kept_ref, rows_ref, held_ref, acc_ref, sems):
+def in_sums_kernel(slots, sort, source_ref, weight_ref, out_ref, *refs):
+    held_ref, acc_ref, sems = refs[-3:]
+    part, hidden = weight_ref.shape[1:]
+    stream = Stream(sems)
+    if sort:
+        rows_ref, kept_ref = refs[:2]
+    else:
+        rows_ref = source_ref
     blocks, _, cols = rows_ref.shape
-    hidden = gate_ref.shape[2]
+    cuts = [(block, start, size) for block in range(blocks) for start, size in pieces_of(cols)]
+    spots = [slice(block * cols + start, block * cols + start + size) for block, start, size in cuts]
+    copies = [stream.start(weight_ref.at[0, spot], held_ref.at[spot]) for spot in spots]
+    if sort:
+        sort_rows(source_ref, rows_ref, slots)
+        kept = stream.start(rows_ref, kept_ref)
+    for number, (block, start, size) in enumerate(cuts):
+        copies[number].wait()
+        term = dot(rows_ref[block, :, start : start + size], held_ref[spots[number]])
+        if number < len(cuts) - 1:
+            acc_ref[...] = term if number == 0 else acc_ref[...] + term
+        else:
+            out_ref[...] = (term if number == 0 else acc_ref[...] + term).astype(BF16)
+    if sort:
+        kept.wait()
+
+
+def in_sums(source, weight, blocks, slots):
+    part, hidden = weight.shape[1:]
+    cols = part // blocks
+    sort = len(source.shape) == 2
+    rows = source.shape[0] // blocks if sort else source.shape[1]
+    more = [shape_of(blocks, rows, cols), hbm_shape(blocks, rows, cols)] if sort else []
+    return pl.pallas_call(
+        functools.partial(in_sums_kernel, slots, sort),
+        in_specs=[vmem(), hbm()],
+        out_specs=[vmem()] + ([vmem(), hbm()] if sort else []),
+        out_shape=[shape_of(rows, hidden)] + more,
+        scratch_shapes=[
+            pltpu.VMEM((part, hidden), BF16),
+            pltpu.VMEM((rows, hidden), F32),
+            pltpu.SemaphoreType.DMA((blocks * len(pieces_of(cols)) + 1,)),
+        ],
+        compiler_params=params(),
+        cost_estimate=cost(2 * rows * part * hidden, 2 * part * hidden),
+        name="gate_sums" if sort else "up_sums",
+    )(source, in_hbm(weight))
+
+
+def back_sums_kernel(slots, messages_ref, down_ref, out_ref, kept_ref, rows_ref, held_ref, sems):
+    blocks, _, cols = rows_ref.shape
     stream = Stream(sems)
-    cuts = [(block, start, size) for block in range(blocks) for start, size in pieces_of(cols)]
-    copies = []
-    for block, start, size in cuts:
-        span = slice(block * cols + start, block * cols + start + size)
-        copies += [stream.start(ref.at[0, span], held_ref.at[i, span]) for i, ref in enumerate((gate_ref, up_ref))]
+    spots = [slice(start, start + size) for start, size in thirds_of(down_ref.shape[1])]
+    copies = [stream.start(down_ref.at[0, spot], held_ref.at[spot]) for spot in spots]
     sort_rows(messages_ref, rows_ref, slots)
     kept = stream.start(rows_ref, kept_ref)
-    for number, (block, start, size) in enumerate(cuts):
-        span = slice(block * cols + start, block * cols + start + size)
-        for i in range(2):
-            copies[2 * number + i].wait()
-            term = dot(rows_ref[block, :, start : start + size], held_ref[i, span])
-            acc_ref[i] = term if number == 0 else acc_ref[i] + term
-    for i in range(2):
-        out_ref[:, i * hidden : (i + 1) * hidden] = acc_ref[i].astype(BF16)
+    for spot, copy in zip(spots, copies):
+        copy.wait()
+        terms = [
+            dot(rows_ref[b], held_ref[spot, span], ((1,), (1,))) for b, span in enumerate(spans(blocks * cols, blocks))
+        ]
+        out_ref[:, spot] = added(terms).astype(BF16)
     kept.wait()
 
 
-def in_sums(messages, w_gate, w_up, blocks, slots):
-    part, hidden = w_gate.shape[1:]
-    rows = messages.shape[0] // blocks
-    cols = part // blocks
-    return pl.pallas_call(
-        functools.partial(in_sums_kernel, slots),
-        in_specs=[vmem(), hbm(), hbm()],
-        out_specs=[vmem(), hbm()],
-        out_shape=[shape_of(rows, 2 * hidden), hbm_shape(blocks, rows, cols)],
-        scratch_shapes=[
-            pltpu.VMEM((blocks, rows, cols), BF16),
-            pltpu.VMEM((2, part, hidden), BF16),
-            pltpu.VMEM((2, rows, hidden), F32),
-            pltpu.SemaphoreType.DMA((2 * blocks * len(pieces_of(cols)) + 1,)),
-        ],
-        compiler_params=params(),
-        cost_estimate=cost(4 * rows * part * hidden, 4 * part * hidden),
-        name="gate_up_sums",
-    )(messages, in_hbm(w_gate), in_hbm(w_up))
-
-
-def up_sums_kernel(slots, messages_ref, down_ref, out_ref, kept_ref, rows_ref, held_ref, acc_ref, sems):
-    blocks, _, cols = rows_ref.shape
-    stream = Stream(sems)
-    cuts = [(block, start, size) for block in range(blocks) for start, size in pieces_of(cols)]
-    copies = []
-    for block, start, size in cuts:
-        span = slice(block * cols + start, block * cols + start + size)
-        copies.append(stream.start(down_ref.at[0, :, span], held_ref.at[:, span]))
-    sort_rows(messages_ref, rows_ref, slots)
-    kept = stream.start(rows_ref, kept_ref)
-    for number, (block, start, size) in enumerate(cuts):
-        span = slice(block * cols + start, block * cols + start + size)
-        copies[number].wait()
-        term = dot(rows_ref[block, :, start : start + size], held_ref[:, span], ((1,), (1,)))
-        acc_ref[...] = term if number == 0 else acc_ref[...] + term
-    out_ref[...] = acc_ref[...].astype(BF16)
-    kept.wait()
-
-
-def up_sums(messages, w_down, blocks, slots):
+def back_sums(messages, w_down, blocks, slots):
     hidden, part = w_down.shape[1:]
     rows = messages.shape[0] // blocks
     cols = part // blocks
     return pl.pallas_call(
-        functools.partial(up_sums_kernel, slots),
+        functools.partial(back_sums_kernel, slots),
         in_specs=[vmem(), hbm()],
         out_specs=[vmem(), hbm()],
         out_shape=[shape_of(rows, hidden), hbm_shape(blocks, rows, cols)],
         scratch_shapes=[
             pltpu.VMEM((blocks, rows, cols), BF16),
             pltpu.VMEM((hidden, part), BF16),
-            pltpu.VMEM((rows, hidden), F32),
-            pltpu.SemaphoreType.DMA((blocks * len(pieces_of(cols)) + 1,)),
+            pltpu.SemaphoreType.DMA((len(thirds_of(hidden)) + 1,)),
         ],
         compiler_params=params(),
         cost_estimate=cost(2 * rows * part * hidden, 2 * part * hidden),
@@ -303,90 +309,97 @@
     )(messages, in_hbm(w_down))
 
 
+def bring_kernel(count, *refs):
+    sources, targets, sems = refs[1 : count + 1], refs[count + 1 : 2 * count + 1], refs[-1]
+    copies = [pltpu.make_async_copy(s, t, sems.at[i]) for i, (s, t) in enumerate(zip(sources, targets))]
+    for copy in copies:
+        copy.start()
+    for copy in copies:
+        copy.wait()
+
+
+def bring(values, after):
+    return pl.pallas_call(
+        functools.partial(bring_kernel, len(values)),
+        in_specs=[pl.BlockSpec(memory_space=pl.ANY)] + [hbm()] * len(values),
+        out_specs=[vmem()] * len(values),
+        out_shape=[shape_of(*value.shape) for value in values],
+        scratch_shapes=[pltpu.SemaphoreType.DMA((len(values),))],
+        compiler_params=params(16),
+        cost_estimate=cost(0, 2 * sum(value.size for value in values)),
+        name="bring_weights",
+    )(after, *[in_hbm(value) for value in values])
+
+
 def row_parts(total):
     size = min(total, 128)
     return [slice(start, start + size) for start in range(0, total, size)]
 
 
-def summed(refs, rows, span):
-    return added([ref[rows, span].astype(F32) for ref in refs])
+def summed(refs, rows):
+    return added([ref[rows].astype(F32) for ref in refs])
 
 
 def out_rows_kernel(slots, blocks, count, *refs):
-    shares, (down_ref, act_ref, out_ref) = refs[:count], refs[count:]
-    hidden, part = down_ref.shape[1:]
+    gates, ups, (down_ref, act_ref, out_ref) = refs[:count], refs[count : 2 * count], refs[2 * count :]
+    part = down_ref.shape[2]
     for rows in row_parts(act_ref.shape[0]):
-        gate_sum = summed(shares, rows, slice(0, hidden))
-        up_sum = summed(shares, rows, slice(hidden, 2 * hidden))
-        act_ref[rows] = (gate_sum * jax.nn.sigmoid(gate_sum) * up_sum).astype(BF16)
+        gate_sum = summed(gates, rows)
+        act_ref[rows] = (gate_sum * jax.nn.sigmoid(gate_sum) * summed(ups, rows)).astype(BF16)
     unsort_rows([dot(act_ref[...], down_ref[0, :, span]).astype(BF16) for span in spans(part, blocks)], out_ref, slots)
 
 
-def out_rows(shares, w_down, blocks, slots):
+def out_rows(gates, ups, w_down, blocks, slots):
     hidden, part = w_down.shape[1:]
-    rows = shares[0].shape[0]
-    return pl.pallas_call(
-        functools.partial(out_rows_kernel, slots, blocks, len(shares)),
-        in_specs=[vmem()] * (len(shares) + 1),
+    rows = gates[0].shape[0]
+    return pl.pallas_call(
+        functools.partial(out_rows_kernel, slots, blocks, len(gates)),
+        in_specs=[vmem()] * (2 * len(gates) + 1),
         out_specs=[vmem()] * 2,
         out_shape=[shape_of(rows, hidden), shape_of(blocks * rows, part // blocks)],
         compiler_params=params(),
         cost_estimate=cost(2 * rows * part * hidden, 2 * part * hidden),
         name="output_rows",
-    )(*shares, w_down)
+    )(*gates, *ups, w_down)
 
 
 def grad_rows_kernel(slots, blocks, count, *refs):
-    shares, backs = refs[:count], refs[count : 2 * count]
-    gate_ref, up_ref, kept_ref, out_ref, act_ref, held_ref, sems = refs[2 * count :]
+    gates, ups, backs = refs[:count], refs[count : 2 * count], refs[2 * count : 3 * count]
+    gate_ref, up_ref, kept_ref, out_ref, act_ref, sem = refs[3 * count :]
     part, hidden = gate_ref.shape[1:]
     cols = part // blocks
-    stream = Stream(sems)
-    cuts = [(start, size, block) for start, size in pieces_of(cols) for block in range(blocks)]
-    copies = []
-    for start, size, block in cuts:
-        span = slice(block * cols + start, block * cols + start + size)
-        copies.append([stream.start(r.at[0, span], held_ref.at[i, span]) for i, r in enumerate((gate_ref, up_ref))])
     for rows in row_parts(act_ref.shape[0]):
-        gate_sum = summed(shares, rows, slice(0, hidden))
-        up_sum = summed(shares, rows, slice(hidden, 2 * hidden))
-        back_sum = summed(backs, rows, slice(0, hidden))
+        gate_sum, up_sum, back_sum = summed(gates, rows), summed(ups, rows), summed(backs, rows)
         sig = jax.nn.sigmoid(gate_sum)
         act_ref[rows, :hidden] = (back_sum * up_sum * sig * (1.0 + gate_sum * (1.0 - sig))).astype(BF16)
         act_ref[rows, hidden:] = (back_sum * (gate_sum * sig)).astype(BF16)
-    kept = stream.start(act_ref, kept_ref)
-    made = []
-    for (start, size, block), pair in zip(cuts, copies):
-        span = slice(block * cols + start, block * cols + start + size)
-        terms = []
-        for i in range(2):
-            pair[i].wait()
-            terms.append(dot(act_ref[:, i * hidden : (i + 1) * hidden], held_ref[i, span], ((1,), (1,))))
-        made.append(added(terms).astype(BF16))
-        if block == blocks - 1:
-            unsort_rows(made, out_ref, slots, slice(start, start + size))
-            made = []
+    kept = pltpu.make_async_copy(act_ref, kept_ref, sem)
+    kept.start()
+    for start, size in pieces_of(cols):
+        made = []
+        for block in range(blocks):
+            span = slice(block * cols + start, block * cols + start + size)
+            total = dot(act_ref[:, :hidden], gate_ref[0, span, :], ((1,), (1,)))
+            total = total + dot(act_ref[:, hidden:], up_ref[0, span, :], ((1,), (1,)))
+            made.append(total.astype(BF16))
+        unsort_rows(made, out_ref, slots, slice(start, start + size))
     kept.wait()
 
 
-def grad_rows(shares, backs, w_gate, w_up, blocks, slots):
+def grad_rows(gates, ups, backs, w_gate, w_up, blocks, slots):
     part, hidden = w_gate.shape[1:]
-    rows = shares[0].shape[0]
+    rows = gates[0].shape[0]
     cols = part // blocks
     return pl.pallas_call(
-        functools.partial(grad_rows_kernel, slots, blocks, len(shares)),
-        in_specs=[vmem()] * (2 * len(shares)) + [hbm()] * 2,
+        functools.partial(grad_rows_kernel, slots, blocks, len(gates)),
+        in_specs=[vmem()] * (3 * len(gates) + 2),
         out_specs=[hbm(), vmem()],
         out_shape=[hbm_shape(rows, 2 * hidden), shape_of(blocks * rows, cols)],
-        scratch_shapes=[
-            pltpu.VMEM((rows, 2 * hidden), BF16),
-            pltpu.VMEM((2, part, hidden), BF16),
-            pltpu.SemaphoreType.DMA((2 * blocks * len(pieces_of(cols)) + 1,)),
-        ],
-        compiler_params=params(40),
+        scratch_shapes=[pltpu.VMEM((rows, 2 * hidden), BF16), pltpu.SemaphoreType.DMA],
+        compiler_params=params(32),
         cost_estimate=cost(4 * rows * part * hidden, 4 * part * hidden),
         name="gradient_rows",
-    )(*shares, *backs, in_hbm(w_gate), in_hbm(w_up))
+    )(*gates, *ups, *backs, w_gate, w_up)
 
 
 def weights_kernel(rows_in_ref, rows_up_ref, act_ref, grad_act_ref, gate_ref, up_ref, down_ref):
@@ -545,13 +558,16 @@
     gates_t = gates[0].T
     arrived_in = scatter(send_rows(tokens, (picks_t,), halves, blocks))
     arrived_up = scatter(send_rows(cotangent, (picks_t, gates_t), halves, blocks))
-    own_sums, rows_in = in_sums(arrived_in, w_gate, w_up, blocks, slots)
-    shares = dp_shares(own_sums, halves)
-    act, outputs = out_rows(shares, w_down, blocks, slots)
+    own_gate, near_rows, rows_in = in_sums(arrived_in, w_gate, blocks, slots)
+    gates_sum = dp_shares(own_gate, halves)
+    (own_up,) = in_sums(near_rows, w_up, blocks, slots)
+    ups_sum = dp_shares(own_up, halves)
+    act, outputs = out_rows(gates_sum, ups_sum, w_down, blocks, slots)
     back_out = scatter(outputs)
-    own_back, rows_up = up_sums(arrived_up, w_down, blocks, slots)
-    backs = dp_shares(own_back, halves)
-    grad_act, gradients = grad_rows(shares, backs, w_gate, w_up, blocks, slots)
+    own_back, rows_up = back_sums(arrived_up, w_down, blocks, slots)
+    backs_sum = dp_shares(own_back, halves)
+    near_gate, near_up = bring((w_gate, w_up), own_back)
+    grad_act, gradients = grad_rows(gates_sum, ups_sum, backs_sum, near_gate, near_up, blocks, slots)
     back_grad = scatter(gradients)
     grad_gate_w, grad_up_w, grad_down = weight_grads(rows_in, rows_up, act, grad_act)
     mixed, gate_grad, put = mix_rows(back_out, cotangent, picks_t, gates_t, halves, blocks)

time: 105 us -> 103 us (0.981)
  waiting for transfers between devices: 44.2 us -> 40.6 us
  Pallas kernels: 31.7 us -> 34.8 us
  starting transfers between devices: 25.3 us -> 23.8 us
    ppermute x2 -> x3, waiting for transfers between devices: 21.1 us -> 16.9 us  [dp_shares(): lax.ppermute(own, 'dp', [(i, (i + shift) % halves) for i in range(halves)])]
    pallas_call x4 -> x6, Pallas kernels: 15.9 us -> 18.9 us  [the longest x2 5.47 us: in_sums(): pl.pallas_call(functools.partial(in_sums_kernel, slots, sort), in_specs=[...]
    all_to_all x4, starting transfers between devices: 21.8 us -> 19.9 us  [to_owners(): lax.all_to_all(messages, EVERYONE, split_axis=0, concat_axis=0, tiled=Tru...]
    ppermute x2 -> x3, starting transfers between devices: 3.53 us -> 3.92 us  [dp_shares(): lax.ppermute(own, 'dp', [(i, (i + shift) % halves) for i in range(halves)])]
  transfers between devices with their start and end apart: 6 -> 7, of which waited for: 4 -> 6; matrix products, arithmetic and copies ran while one was open for 0% -> 0% of each run, Pallas kernels for 27% -> 30%
where the time goes in v6:
time: 103 us; the launch traced here: 102 us
  waiting for transfers between devices  40.6 us (39%)
  Pallas kernels  34.8 us (34%)
  starting transfers between devices  23.8 us (23%)
  local copies, waits for them, and re-layouts  2.11 us (2%)
    all_to_all x4, waiting for transfers between devices, to_owners(): lax.all_to_all(messages, EVERYONE, split_axis=0, concat_axis=0, tiled=Tru...  23.8 us
    all_to_all x4, starting transfers between devices, to_owners(): lax.all_to_all(messages, EVERYONE, split_axis=0, concat_axis=0, tiled=Tru...  19.9 us
    ppermute x3, waiting for transfers between devices, dp_shares(): lax.ppermute(own, 'dp', [(i, (i + shift) % halves) for i in range(halves)])  16.9 us
    pallas_call x1, Pallas kernels, weight_grads(): pl.pallas_call(weights_kernel, grid=(blocks, steps), in_specs=[chunk, chu...  5.77 us
    pallas_call x2, Pallas kernels, send_rows(): pl.pallas_call(functools.partial(send_kernel, halves, blocks, len(lists)...  5.7 us
    pallas_call x2, Pallas kernels, in_sums(): pl.pallas_call(functools.partial(in_sums_kernel, slots, sort), in_specs=[...  5.47 us
    pallas_call x1, Pallas kernels, grad_rows(): pl.pallas_call(functools.partial(grad_rows_kernel, slots, blocks, len(gat...  4.24 us
    pallas_call x1, Pallas kernels, back_sums(): pl.pallas_call(functools.partial(back_sums_kernel, slots), in_specs=[vmem...  4.11 us
  transfers between devices with their start and end apart: 7, of which 6 were waited for; matrix products, arithmetic and copies ran while one was open for 0% of the time, Pallas kernels for 30%

profile of v6, /device:TPU:0, one launch (start us, length us, event | category | flops | bytes accessed | tf_op | source)
XLA Modules:
  0.0 102.1 jit_solution(16692756119251501982)
XLA Ops:
  0.6 2.8 %send_rows.2 = bf16[256,1280]{1,0:T(8,128)(2,1)} custom-call(s32[4,16]{1,0:T(4,128)} %bitcast.21, bf16[128,5120]{1,0:T(8,128)(2,1)} %refs_1_.2), custom_call_target="tpu_custom_call" | custom-call | flops 167772160 | bytes 1966080 | tf_op jit(solution)/shard_map/send_rows/pallas_call | solution.py:145
  3.4 7.3 %all-to-all-start = ((bf16[32,8,1280]{2,1,0:T(8,128)(2,1)}), bf16[32,8,1280]{2,1,0:T(8,128)(2,1)S(1)}, u32[]{:S(2)}, u32[]{:S(2)}) async-start(bf16[32,8,1280]{2,1,0:T(8,128)(2,1)} %bitcast.5), calls=%async_computation | async-start | bytes 1310720 | tf_op jit(solution)/shard_map/all_to_all | solution.py:541
  10.7 2.9 %send_rows.3 = bf16[256,1280]{1,0:T(8,128)(2,1)} custom-call(s32[4,16]{1,0:T(4,128)} %bitcast.22, f32[4,16]{1,0:T(4,128)} %bitcast.24, bf16[128,5120]{1,0:T(8,128)(2,1)} %refs_2_.2), custom_call_target="tpu_custom_call" | custom-call | flops 167772160 | bytes 1966080 | tf_op jit(solution)/shard_map/send_rows/pallas_call | solution.py:145
  13.7 15.6 %all-to-all-done = bf16[32,8,1280]{2,1,0:T(8,128)(2,1)S(1)} async-done(((bf16[32,8,1280]{2,1,0:T(8,128)(2,1)}), bf16[32,8,1280]{2,1,0:T(8,128)(2,1)S(1)}, u32[]{:S(2)}, u32[]{:S(2)}) %all-to-all-start) | async-done | bytes 655392 | tf_op jit(solution)/shard_map/all_to_all | solution.py:541
  29.2 2.6 %all-to-all-start.2 = ((bf16[32,8,1280]{2,1,0:T(8,128)(2,1)}), bf16[32,8,1280]{2,1,0:T(8,128)(2,1)S(1)}, u32[]{:S(2)}, u32[]{:S(2)}) async-start(bf16[32,8,1280]{2,1,0:T(8,128)(2,1)} %bitcast.10), calls=%async_computation.2 | async-start | bytes 1310720 | tf_op jit(solution)/shard_map/all_to_all | solution.py:541
  31.9 2.9 %gate_sums.1 = (bf16[128,768]{1,0:T(8,128)(2,1)S(1)}, bf16[2,128,1280]{2,1,0:T(8,128)(2,1)S(1)}, bf16[2,128,1280]{2,1,0:T(8,128)(2,1)}) custom-call(bf16[256,1280]{1,0:T(8,128)(2,1)S(1)} %bitcast.18, bf16[1,2560,768]{2,1,0:T(8,128)(2,1)} %refs_1_.3), custom_call_target="tpu_custom_call" | custom-call | flops 503316480 | bytes 3932160 | tf_op jit(solution)/shard_map/gate_sums/pallas_call | solution.py:260
  34.8 2.5 %up_sums.1.refs_2_ = bf16[128,768]{1,0:T(8,128)(2,1)S(1)} custom-call(bf16[2,128,1280]{2,1,0:T(8,128)(2,1)S(1)} %get-tuple-element.24.source_ref, bf16[1,2560,768]{2,1,0:T(8,128)(2,1)} %refs_2_.3), custom_call_target="tpu_custom_call" | custom-call | flops 503316480 | bytes 3932160 | tf_op jit(solution)/shard_map/up_sums/pallas_call | solution.py:260
  37.4 1.7 %collective-permute-start.1 = (bf16[128,768]{1,0:T(8,128)(2,1)S(1)}, bf16[128,768]{1,0:T(8,128)(2,1)S(1)}, u32[]{:S(2)}, u32[]{:S(2)}) collective-permute-start(bf16[128,768]{1,0:T(8,128)(2,1)S(1)} %up_sums.1.refs_2_), channel_id=1, source_target_pairs={{0,16},{16,0},{1,17},{17,1},{2,18},{18,2},{3,19},{19,3},{4,20},{20... | collective-permute-start | bytes 589832 | tf_op jit(solution)/shard_map/ppermute | solution.py:548
  39.5 7.3 %collective-permute-done.1.refs_3_ = bf16[128,768]{1,0:T(8,128)(2,1)S(1)} collective-permute-done((bf16[128,768]{1,0:T(8,128)(2,1)S(1)}, bf16[128,768]{1,0:T(8,128)(2,1)S(1)}, u32[]{:S(2)}, u32[]{:S(2)}) %collective-permute-start.1) | collective-permute-done | bytes 196640 | tf_op jit(solution)/shard_map/ppermute | solution.py:548
  46.8 5.2 %collective-permute-done.refs_1_ = bf16[128,768]{1,0:T(8,128)(2,1)S(1)} collective-permute-done((bf16[128,768]{1,0:T(8,128)(2,1)S(1)}, bf16[128,768]{1,0:T(8,128)(2,1)S(1)}, u32[]{:S(2)}, u32[]{:S(2)}) %collective-permute-start) | collective-permute-done | bytes 196640 | tf_op jit(solution)/shard_map/ppermute | solution.py:548
  52.0 1.8 %output_rows.1 = (bf16[128,768]{1,0:T(8,128)(2,1)S(1)}, bf16[256,1280]{1,0:T(8,128)(2,1)}) custom-call(bf16[128,768]{1,0:T(8,128)(2,1)S(1)} %get-tuple-element.23.refs_0_, bf16[128,768]{1,0:T(8,128)(2,1)S(1)} %collective-permute-done.refs_1_, bf16[128,768]{1,0:T(8,128)(2,1)S(1)} %up_sums.1.refs_2_, bf16[128,768]{1,0:T(8,128)(2,1)S(1)} %collective-permute-done.1.refs_3_, ...), custom_call_target="tpu_custom_call" | custom-call | flops 503316480 | bytes 3932160 | tf_op jit(solution)/shard_map/output_rows/pallas_call | solution.py:355
  53.8 4.2 %all-to-all-start.1 = ((bf16[32,8,1280]{2,1,0:T(8,128)(2,1)}), bf16[32,8,1280]{2,1,0:T(8,128)(2,1)S(1)}, u32[]{:S(2)}, u32[]{:S(2)}) async-start(bf16[32,8,1280]{2,1,0:T(8,128)(2,1)} %bitcast.7), calls=%async_computation.1 | async-start | bytes 1310720 | tf_op jit(solution)/shard_map/all_to_all | solution.py:541
  58.0 4.1 %back_sums.1 = (bf16[128,768]{1,0:T(8,128)(2,1)S(1)}, bf16[2,128,1280]{2,1,0:T(8,128)(2,1)}) custom-call(bf16[256,1280]{1,0:T(8,128)(2,1)S(1)} %bitcast.17, bf16[1,768,2560]{2,1,0:T(8,128)(2,1)} %down_ref.1), custom_call_target="tpu_custom_call" | custom-call | flops 503316480 | bytes 3932160 | tf_op jit(solution)/shard_map/back_sums/pallas_call | solution.py:296
  62.1 1.8 %collective-permute-start.2 = (bf16[128,768]{1,0:T(8,128)(2,1)S(1)}, bf16[128,768]{1,0:T(8,128)(2,1)S(1)}, u32[]{:S(2)}, u32[]{:S(2)}) collective-permute-start(bf16[128,768]{1,0:T(8,128)(2,1)S(1)} %get-tuple-element.28.refs_0_.refs_4_), channel_id=1, source_target_pairs={{0,16},{16,0},{1,17},{17,1},{2,18},{18,2},{3,19},{19,3},{4,20},{20... | collective-permute-start | bytes 589832 | tf_op jit(solution)/shard_map/ppermute | solution.py:548
  64.0 3.3 %bring_weights.1 = (bf16[1,2560,768]{2,1,0:T(8,128)(2,1)S(1)}, bf16[1,2560,768]{2,1,0:T(8,128)(2,1)S(1)}) custom-call(bf16[128,768]{1,0:T(8,128)(2,1)S(1)} %get-tuple-element.28.refs_0_.refs_4_, bf16[1,2560,768]{2,1,0:T(8,128)(2,1)} %refs_1_.3, bf16[1,2560,768]{2,1,0:T(8,128)(2,1)} %refs_2_.3), custom_call_target="tpu_custom_call" | custom-call | bytes 7864320 | tf_op jit(solution)/shard_map/bring_weights/pallas_call | solution.py:322
  67.3 4.3 %collective-permute-done.2.refs_5_ = bf16[128,768]{1,0:T(8,128)(2,1)S(1)} collective-permute-done((bf16[128,768]{1,0:T(8,128)(2,1)S(1)}, bf16[128,768]{1,0:T(8,128)(2,1)S(1)}, u32[]{:S(2)}, u32[]{:S(2)}) %collective-permute-start.2) | collective-permute-done | bytes 196640 | tf_op jit(solution)/shard_map/ppermute | solution.py:548
  71.6 4.2 %gradient_rows.1 = (bf16[128,1536]{1,0:T(8,128)(2,1)}, bf16[256,1280]{1,0:T(8,128)(2,1)}) custom-call(bf16[128,768]{1,0:T(8,128)(2,1)S(1)} %get-tuple-element.23.refs_0_, bf16[128,768]{1,0:T(8,128)(2,1)S(1)} %collective-permute-done.refs_1_, bf16[128,768]{1,0:T(8,128)(2,1)S(1)} %up_sums.1.refs_2_, bf16[128,768]{1,0:T(8,128)(2,1)S(1)} %collective-permute-done.1.refs_3_, ...), custom_call_target="tpu_custom_call" | custom-call | flops 1006632960 | bytes 7864320 | tf_op jit(solution)/shard_map/gradient_rows/pallas_call | solution.py:393
  76.5 5.8 %all-to-all-start.3 = ((bf16[32,8,1280]{2,1,0:T(8,128)(2,1)}), bf16[32,8,1280]{2,1,0:T(8,128)(2,1)S(1)}, u32[]{:S(2)}, u32[]{:S(2)}) async-start(bf16[32,8,1280]{2,1,0:T(8,128)(2,1)} %bitcast.12), calls=%async_computation.3 | async-start | bytes 1310720 | tf_op jit(solution)/shard_map/all_to_all | solution.py:541
  82.3 1.1 %copy-done.5 = bf16[2,128,1280]{2,1,0:T(8,128)(2,1)S(1)} copy-done((bf16[2,128,1280]{2,1,0:T(8,128)(2,1)S(1)}, bf16[2,128,1280]{2,1,0:T(8,128)(2,1)}, u32[]{:S(2)}) %copy-start.5) | copy-done | bytes 655384
  83.4 1.0 copy-done.6
  84.4 5.8 %weight_grads.1 = (bf16[1,2560,768]{2,1,0:T(8,128)(2,1)}, bf16[1,2560,768]{2,1,0:T(8,128)(2,1)}, bf16[1,768,2560]{2,1,0:T(8,128)(2,1)}) custom-call(bf16[2,128,1280]{2,1,0:T(8,128)(2,1)S(1)} %copy-done.4, bf16[2,128,1280]{2,1,0:T(8,128)(2,1)S(1)} %copy-done.5, bf16[128,768]{1,0:T(8,128)(2,1)S(1)} %get-tuple-element.35.act_ref, bf16[128,1536]{1,0:T(8,128)(2,1)S(1)} %copy-done.6), custom_call_target="tpu_custom_call" | custom-call | flops 1509949440 | bytes 11796480 | tf_op jit(solution)/shard_map/weight_grads/pallas_call | solution.py:421
  90.1 3.0 %mixed_rows.1 = (bf16[128,5120]{1,0:T(8,128)(2,1)}, f32[4,16]{1,0:T(4,128)}, bf16[2,128,128]{2,1,0:T(8,128)(2,1)S(1)}) custom-call(s32[4,16]{1,0:T(4,128)S(1)} %bitcast.23, f32[4,16]{1,0:T(4,128)S(1)} %bitcast.25, bf16[128,5120]{1,0:T(8,128)(2,1)S(1)} %copy-done.1, bf16[256,1280]{1,0:T(8,128)(2,1)S(1)} %bitcast.20), custom_call_target="tpu_custom_call" | custom-call | flops 671088640 | bytes 2621440 | tf_op jit(solution)/shard_map/mixed_rows/pallas_call | solution.py:493
  93.2 7.6 %all-to-all-done.3 = bf16[32,8,1280]{2,1,0:T(8,128)(2,1)S(1)} async-done(((bf16[32,8,1280]{2,1,0:T(8,128)(2,1)}), bf16[32,8,1280]{2,1,0:T(8,128)(2,1)S(1)}, u32[]{:S(2)}, u32[]{:S(2)}) %all-to-all-start.3) | async-done | bytes 655392 | tf_op jit(solution)/shard_map/all_to_all | solution.py:541
  100.8 1.3 %token_grads.1 = bf16[128,5120]{1,0:T(8,128)(2,1)} custom-call(bf16[2,128,128]{2,1,0:T(8,128)(2,1)S(1)} %get-tuple-element.27.put_ref, bf16[256,1280]{1,0:T(8,128)(2,1)S(1)} %bitcast.19), custom_call_target="tpu_custom_call" | custom-call | flops 167772160 | bytes 1310720 | tf_op jit(solution)/shard_map/token_grads/pallas_call | solution.py:521
  (15 shorter events, 1.0 us)
Async XLA Ops:
  3.4 25.8 %all-to-all-start = ((bf16[32,8,1280]{2,1,0:T(8,128)(2,1)}), bf16[32,8,1280]{2,1,0:T(8,128)(2,1)S(1)}, u32[]{:S(2)}, u32[]{:S(2)}) async-start(bf16[32,8,1280]{2,1,0:T(8,128)(2,1)} %bitcast.5), calls=%async_computation | async-start | bytes 1310720 | tf_op jit(solution)/shard_map/all_to_all | solution.py:541
  29.2 24.5 %all-to-all-start.2 = ((bf16[32,8,1280]{2,1,0:T(8,128)(2,1)}), bf16[32,8,1280]{2,1,0:T(8,128)(2,1)S(1)}, u32[]{:S(2)}, u32[]{:S(2)}) async-start(bf16[32,8,1280]{2,1,0:T(8,128)(2,1)} %bitcast.10), calls=%async_computation.2 | async-start | bytes 1310720 | tf_op jit(solution)/shard_map/all_to_all | solution.py:541
  31.9 20.1 %copy-start = (bf16[1,768,2560]{2,1,0:T(8,128)(2,1)S(1)}, bf16[1,768,2560]{2,1,0:T(8,128)(2,1)}, u32[]{:S(2)}) copy-start(bf16[1,768,2560]{2,1,0:T(8,128)(2,1)} %down_ref.1) | copy-start | bytes 11796484
  37.4 9.4 %collective-permute-start.1 = (bf16[128,768]{1,0:T(8,128)(2,1)S(1)}, bf16[128,768]{1,0:T(8,128)(2,1)S(1)}, u32[]{:S(2)}, u32[]{:S(2)}) collective-permute-start(bf16[128,768]{1,0:T(8,128)(2,1)S(1)} %up_sums.1.refs_2_), channel_id=1, source_target_pairs={{0,16},{16,0},{1,17},{17,1},{2,18},{18,2},{3,19},{19,3},{4,20},{20... | collective-permute-start | bytes 589832 | tf_op jit(solution)/shard_map/ppermute | solution.py:548
  39.1 12.9 %collective-permute-start = (bf16[128,768]{1,0:T(8,128)(2,1)S(1)}, bf16[128,768]{1,0:T(8,128)(2,1)S(1)}, u32[]{:S(2)}, u32[]{:S(2)}) collective-permute-start(bf16[128,768]{1,0:T(8,128)(2,1)S(1)} %get-tuple-element.23.refs_0_), channel_id=1, source_target_pairs={{0,16},{16,0},{1,17},{17,1},{2,18},{18,2},{3,19},{19,3},{4,20},{20... | collective-permute-start | bytes 589832 | tf_op jit(solution)/shard_map/ppermute | solution.py:548
  53.8 22.7 %all-to-all-start.1 = ((bf16[32,8,1280]{2,1,0:T(8,128)(2,1)}), bf16[32,8,1280]{2,1,0:T(8,128)(2,1)S(1)}, u32[]{:S(2)}, u32[]{:S(2)}) async-start(bf16[32,8,1280]{2,1,0:T(8,128)(2,1)} %bitcast.7), calls=%async_computation.1 | async-start | bytes 1310720 | tf_op jit(solution)/shard_map/all_to_all | solution.py:541
  62.1 9.5 %collective-permute-start.2 = (bf16[128,768]{1,0:T(8,128)(2,1)S(1)}, bf16[128,768]{1,0:T(8,128)(2,1)S(1)}, u32[]{:S(2)}, u32[]{:S(2)}) collective-permute-start(bf16[128,768]{1,0:T(8,128)(2,1)S(1)} %get-tuple-element.28.refs_0_.refs_4_), channel_id=1, source_target_pairs={{0,16},{16,0},{1,17},{17,1},{2,18},{18,2},{3,19},{19,3},{4,20},{20... | collective-permute-start | bytes 589832 | tf_op jit(solution)/shard_map/ppermute | solution.py:548
  71.6 10.7 %copy-start.4 = (bf16[2,128,1280]{2,1,0:T(8,128)(2,1)S(1)}, bf16[2,128,1280]{2,1,0:T(8,128)(2,1)}, u32[]{:S(2)}) copy-start(bf16[2,128,1280]{2,1,0:T(8,128)(2,1)} %get-tuple-element.33.rows_in_ref) | copy-start | bytes 1966084
  75.8 14.3 %copy-start.1 = (bf16[128,5120]{1,0:T(8,128)(2,1)S(1)}, bf16[128,5120]{1,0:T(8,128)(2,1)}, u32[]{:S(2)}) copy-start(bf16[128,5120]{1,0:T(8,128)(2,1)} %refs_2_.2) | copy-start | bytes 3932164
  75.9 14.3 %copy-start.2 = (s32[1,16,4]{1,2,0:T(4,128)S(1)}, s32[1,16,4]{1,2,0:T(4,128)}, u32[]{:S(2)}) copy-start(s32[1,16,4]{1,2,0:T(4,128)} %param.9) | copy-start | bytes 772
  75.9 14.3 %copy-start.3 = (f32[1,16,4]{1,2,0:T(4,128)S(1)}, f32[1,16,4]{1,2,0:T(4,128)}, u32[]{:S(2)}) copy-start(f32[1,16,4]{1,2,0:T(4,128)} %param.10) | copy-start | bytes 772
  76.5 24.3 %all-to-all-start.3 = ((bf16[32,8,1280]{2,1,0:T(8,128)(2,1)}), bf16[32,8,1280]{2,1,0:T(8,128)(2,1)S(1)}, u32[]{:S(2)}, u32[]{:S(2)}) async-start(bf16[32,8,1280]{2,1,0:T(8,128)(2,1)} %bitcast.12), calls=%async_computation.3 | async-start | bytes 1310720 | tf_op jit(solution)/shard_map/all_to_all | solution.py:541
  82.3 1.1 %copy-start.5 = (bf16[2,128,1280]{2,1,0:T(8,128)(2,1)S(1)}, bf16[2,128,1280]{2,1,0:T(8,128)(2,1)}, u32[]{:S(2)}) copy-start(bf16[2,128,1280]{2,1,0:T(8,128)(2,1)} %get-tuple-element.34.rows_up_ref) | copy-start | bytes 1966084
  83.4 1.0 copy-start.6

commit v7 on v6

--- a/solution.py
+++ b/solution.py
@@ -32,6 +32,10 @@
 def expert_at(place, experts):
     planes = planes_of(experts)
     return place % planes * (experts // planes) + place // planes
+
+
+def split_place(place, halves, planes):
+    return (place // (halves * planes) * planes + place % planes) * halves + place // planes % halves
 
 
 def one_hot(condition):
@@ -137,6 +141,78 @@
             out_ref[start : start + run] = picked[place * run : (place + 1) * run]
 
 
+def pair_kernel(blocks, _, picks_ref, gates_ref, source_ref, own_ref, other_ref, held_ref, sems):
+    slots, experts = picks_ref.shape
+    tokens = source_ref.shape[0]
+    rows, cols = own_ref.shape
+    half = lax.axis_index("dp")
+    copies = []
+    for far in range(2):
+        for block in range(blocks):
+            start = (jnp.bitwise_xor(half, far) * blocks + block) * cols
+            copies.append(
+                pltpu.make_async_copy(
+                    source_ref.at[:, pl.ds(pl.multiple_of(start, 128), cols)],
+                    held_ref.at[far, block * tokens : (block + 1) * tokens],
+                    sems.at[far, block],
+                )
+            )
+            copies[-1].start()
+    chosen = spread_column(picks_ref[...].astype(F32), blocks).astype(jnp.int32)
+    target = chosen + iota((rows, 1), 0) % (blocks * slots) // slots * tokens
+    take = one_hot(target == iota((rows, blocks * tokens), 1))
+    scale = spread_column(gates_ref[...], blocks)
+    for far, out_ref in enumerate((own_ref, other_ref)):
+        for block in range(blocks):
+            copies[far * blocks + block].wait()
+        out_ref[...] = (dot(take, held_ref[far]) * scale).astype(BF16)
+
+
+def pair_rows(source, picks, gates, blocks, after):
+    slots, experts = picks.shape
+    tokens, width = source.shape
+    cols = width // (2 * blocks)
+    rows = experts * blocks * slots
+    return pl.pallas_call(
+        functools.partial(pair_kernel, blocks),
+        in_specs=[pl.BlockSpec(memory_space=pl.ANY), vmem(), vmem(), hbm()],
+        out_specs=[vmem()] * 2,
+        out_shape=[shape_of(rows, cols)] * 2,
+        scratch_shapes=[pltpu.VMEM((2, blocks * tokens, cols), BF16), pltpu.SemaphoreType.DMA((2, blocks))],
+        compiler_params=params(16),
+        cost_estimate=cost(4 * rows * cols * tokens * blocks, 2 * tokens * width),
+        name="pair_rows",
+    )(after, picks, gates, in_hbm(source))
+
+
+def join_kernel(own_ref, other_ref, out_ref, sems):
+    half = lax.axis_index("dp")
+    copies = [
+        pltpu.make_async_copy(own_ref, out_ref.at[:, half], sems.at[0]),
+        pltpu.make_async_copy(other_ref, out_ref.at[:, 1 - half], sems.at[1]),
+    ]
+    for copy in copies:
+        copy.start()
+    for copy in copies:
+        copy.wait()
+
+
+def join_rows(own, other, experts):
+    rows, cols = own.shape
+    shape = (experts, rows // experts, cols)
+    joined = pl.pallas_call(
+        join_kernel,
+        in_specs=[pl.BlockSpec(memory_space=pl.ANY)] * 2,
+        out_specs=hbm(),
+        out_shape=hbm_shape(experts, 2, *shape[1:]),
+        scratch_shapes=[pltpu.SemaphoreType.DMA((2,))],
+        compiler_params=params(16),
+        cost_estimate=cost(0, 8 * rows * cols),
+        name="join_rows",
+    )(own.reshape(shape), other.reshape(shape))
+    return joined.reshape(2 * rows, cols)
+
+
 def send_rows(source, lists, halves, blocks):
     slots, experts = lists[0].shape
     tokens, width = source.shape
@@ -159,21 +235,21 @@
     )(*[in_hbm(value) for value in lists], in_hbm(source))
 
 
-def sort_matrix(rows, blocks, slots, back):
+def sort_matrix(rows, blocks, slots, back, place=lambda device: device):
     a = iota((rows, rows), 1 if back else 0)
     b = iota((rows, rows), 0 if back else 1)
     group = rows // blocks
-    return one_hot(a % group // slots * (blocks * slots) + a // group * slots + a % slots == b)
-
-
-def sort_rows(messages_ref, rows_ref, slots):
+    return one_hot(place(a % group // slots) * (blocks * slots) + a // group * slots + a % slots == b)
+
+
+def sort_rows(messages_ref, rows_ref, slots, place=None):
     blocks, total = rows_ref.shape[:2]
-    if blocks == 1:
+    if blocks == 1 and place is None:
         rows_ref[0] = messages_ref[...]
         return
     size = min(blocks * total, 256)
     group = size // blocks
-    order = sort_matrix(size, blocks, slots, False)
+    order = sort_matrix(size, blocks, slots, False, place or (lambda device: device))
     for part in range(total // group):
         ordered = dot(order, messages_ref[part * size : (part + 1) * size]).astype(BF16)
         for block in range(blocks):
@@ -273,12 +349,12 @@
     )(source, in_hbm(weight))
 
 
-def back_sums_kernel(slots, messages_ref, down_ref, out_ref, kept_ref, rows_ref, held_ref, sems):
+def back_sums_kernel(slots, place, messages_ref, down_ref, out_ref, kept_ref, rows_ref, held_ref, sems):
     blocks, _, cols = rows_ref.shape
     stream = Stream(sems)
     spots = [slice(start, start + size) for start, size in thirds_of(down_ref.shape[1])]
     copies = [stream.start(down_ref.at[0, spot], held_ref.at[spot]) for spot in spots]
-    sort_rows(messages_ref, rows_ref, slots)
+    sort_rows(messages_ref, rows_ref, slots, place)
     kept = stream.start(rows_ref, kept_ref)
     for spot, copy in zip(spots, copies):
         copy.wait()
@@ -289,12 +365,12 @@
     kept.wait()
 
 
-def back_sums(messages, w_down, blocks, slots):
+def back_sums(messages, w_down, blocks, slots, place):
     hidden, part = w_down.shape[1:]
     rows = messages.shape[0] // blocks
     cols = part // blocks
     return pl.pallas_call(
-        functools.partial(back_sums_kernel, slots),
+        functools.partial(back_sums_kernel, slots, place),
         in_specs=[vmem(), hbm()],
         out_specs=[vmem(), hbm()],
         out_shape=[shape_of(rows, hidden), hbm_shape(blocks, rows, cols)],
@@ -543,6 +619,11 @@
     )
 
 
+def to_experts(experts, messages):
+    order = [expert_at(place, experts) for place in range(experts)]
+    return lax.all_to_all(messages, "expert", split_axis=0, concat_axis=0, tiled=True, axis_index_groups=[order])
+
+
 def dp_shares(own, halves):
     shares = [own] + [
         lax.ppermute(own, "dp", [(i, (i + shift) % halves) for i in range(halves)]) for shift in range(1, halves)
@@ -556,15 +637,23 @@
     blocks = 2 if tokens.shape[1] // halves % 256 == 0 else 1
     picks_t = picks[0].T
     gates_t = gates[0].T
-    arrived_in = scatter(send_rows(tokens, (picks_t,), halves, blocks))
-    arrived_up = scatter(send_rows(cotangent, (picks_t, gates_t), halves, blocks))
+    messages_in = send_rows(tokens, (picks_t,), halves, blocks)
+    arrived_in = scatter(messages_in)
+    if halves == 2:
+        own, other = pair_rows(cotangent, picks_t, gates_t, blocks, messages_in)
+        other = lax.ppermute(other, "dp", [(0, 1), (1, 0)])
+        arrived_up = to_experts(experts, join_rows(own, other, experts))
+        place = functools.partial(split_place, halves=halves, planes=planes_of(experts))
+    else:
+        arrived_up = scatter(send_rows(cotangent, (picks_t, gates_t), halves, blocks))
+        place = None
     own_gate, near_rows, rows_in = in_sums(arrived_in, w_gate, blocks, slots)
     gates_sum = dp_shares(own_gate, halves)
     (own_up,) = in_sums(near_rows, w_up, blocks, slots)
     ups_sum = dp_shares(own_up, halves)
     act, outputs = out_rows(gates_sum, ups_sum, w_down, blocks, slots)
     back_out = scatter(outputs)
-    own_back, rows_up = back_sums(arrived_up, w_down, blocks, slots)
+    own_back, rows_up = back_sums(arrived_up, w_down, blocks, slots, place)
     backs_sum = dp_shares(own_back, halves)
     near_gate, near_up = bring((w_gate, w_up), own_back)
     grad_act, gradients = grad_rows(gates_sum, ups_sum, backs_sum, near_gate, near_up, blocks, slots)

time: 103 us -> 104 us (level)
  waiting for transfers between devices: 40.6 us -> 34.6 us
  starting transfers between devices: 23.8 us -> 29.6 us
  local copies, waits for them, and re-layouts: 2.11 us -> 3.46 us
    all_to_all x4 -> x3, waiting for transfers between devices: 23.8 us -> 9.98 us  [to_owners(): lax.all_to_all(messages, EVERYONE, split_axis=0, concat_axis=0, tiled=Tru...]
    ppermute x0 -> x1, waiting for transfers between devices: none -> 10.9 us  [body(): other = lax.ppermute(other, 'dp', [(0, 1), (1, 0)])]
    all_to_all x0 -> x1, starting transfers between devices: none -> 5.58 us  [to_experts(): lax.all_to_all(messages, 'expert', split_axis=0, concat_axis=0, tiled=Tru...]
    ppermute x3, waiting for transfers between devices: 16.9 us -> 13.7 us  [dp_shares(): lax.ppermute(own, 'dp', [(i, (i + shift) % halves) for i in range(halves)])]
    pallas_call x2 -> x1, Pallas kernels: 5.7 us -> 2.8 us  [send_rows(): pl.pallas_call(functools.partial(send_kernel, halves, blocks, len(lists)...]
    pallas_call x1 -> x3, Pallas kernels: 4.11 us -> 6.69 us  [the longest x1 4.18 us: back_sums(): pl.pallas_call(functools.partial(back_sums_kernel, slots, place), in_spec...]
    ppermute x0 -> x1, starting transfers between devices: none -> 1.83 us  [body(): other = lax.ppermute(other, 'dp', [(0, 1), (1, 0)])]
    all_to_all x4 -> x3, starting transfers between devices: 19.9 us -> 18.3 us  [to_owners(): lax.all_to_all(messages, EVERYONE, split_axis=0, concat_axis=0, tiled=Tru...]
  transfers between devices with their start and end apart: 7 -> 8, of which waited for: 6 -> 7; matrix products, arithmetic and copies ran while one was open for 0% -> 0% of each run, Pallas kernels for 30% -> 29%
where the time goes in v7:
time: 104 us; the launch traced here: 103 us
  waiting for transfers between devices  34.6 us (33%)
  Pallas kernels  34.4 us (33%)
  starting transfers between devices  29.6 us (28%)
  local copies, waits for them, and re-layouts  3.46 us (3%)
    all_to_all x3, starting transfers between devices, to_owners(): lax.all_to_all(messages, EVERYONE, split_axis=0, concat_axis=0, tiled=Tru...  18.3 us
    ppermute x3, waiting for transfers between devices, dp_shares(): lax.ppermute(own, 'dp', [(i, (i + shift) % halves) for i in range(halves)])  13.7 us
    ppermute x1, waiting for transfers between devices, body(): other = lax.ppermute(other, 'dp', [(0, 1), (1, 0)])  10.9 us
    all_to_all x3, waiting for transfers between devices, to_owners(): lax.all_to_all(messages, EVERYONE, split_axis=0, concat_axis=0, tiled=Tru...  9.98 us
    pallas_call x1, Pallas kernels, weight_grads(): pl.pallas_call(weights_kernel, grid=(blocks, steps), in_specs=[chunk, chu...  5.77 us
    all_to_all x1, starting transfers between devices, to_experts(): lax.all_to_all(messages, 'expert', split_axis=0, concat_axis=0, tiled=Tru...  5.58 us
    pallas_call x2, Pallas kernels, in_sums(): pl.pallas_call(functools.partial(in_sums_kernel, slots, sort), in_specs=[...  5.47 us
    pallas_call x1, Pallas kernels, grad_rows(): pl.pallas_call(functools.partial(grad_rows_kernel, slots, blocks, len(gat...  4.22 us
  transfers between devices with their start and end apart: 8, of which 7 were waited for; matrix products, arithmetic and copies ran while one was open for 0% of the time, Pallas kernels for 29%

profile of v7, /device:TPU:0, one launch (start us, length us, event | category | flops | bytes accessed | tf_op | source)
XLA Modules:
  0.0 102.9 jit_solution(7193119003209280643)
XLA Ops:
  0.6 2.8 %send_rows.1._ = bf16[256,1280]{1,0:T(8,128)(2,1)} custom-call(s32[4,16]{1,0:T(4,128)} %bitcast.25, bf16[128,5120]{1,0:T(8,128)(2,1)} %refs_1_.2), custom_call_target="tpu_custom_call" | custom-call | flops 167772160 | bytes 1966080 | tf_op jit(solution)/shard_map/send_rows/pallas_call | solution.py:221
  3.4 7.3 %all-to-all-start = ((bf16[32,8,1280]{2,1,0:T(8,128)(2,1)}), bf16[32,8,1280]{2,1,0:T(8,128)(2,1)S(1)}, u32[]{:S(2)}, u32[]{:S(2)}) async-start(bf16[32,8,1280]{2,1,0:T(8,128)(2,1)} %bitcast.5), calls=%async_computation | async-start | bytes 1310720 | tf_op jit(solution)/shard_map/all_to_all | solution.py:617
  12.1 1.7 %pair_rows.1 = (bf16[128,1280]{1,0:T(8,128)(2,1)S(1)}, bf16[128,1280]{1,0:T(8,128)(2,1)S(1)}) custom-call(bf16[256,1280]{1,0:T(8,128)(2,1)} %send_rows.1._, s32[4,16]{1,0:T(4,128)S(1)} %bitcast.26, f32[4,16]{1,0:T(4,128)S(1)} %bitcast.28, bf16[128,5120]{1,0:T(8,128)(2,1)} %source_ref.1), custom_call_target="tpu_custom_call" | custom-call | flops 167772160 | bytes 1310720 | tf_op jit(solution)/shard_map/pair_rows/pallas_call | solution.py:176
  13.8 1.8 %collective-permute-start.2 = (bf16[128,1280]{1,0:T(8,128)(2,1)S(1)}, bf16[128,1280]{1,0:T(8,128)(2,1)S(1)}, u32[]{:S(2)}, u32[]{:S(2)}) collective-permute-start(bf16[128,1280]{1,0:T(8,128)(2,1)S(1)} %get-tuple-element.31), channel_id=1, source_target_pairs={{0,16},{16,0},{1,17},{17,1},{2,18},{18,2},{3,19},{19,3},{4,20},{20... | collective-permute-start | bytes 983048 | tf_op jit(solution)/shard_map/ppermute | solution.py:644
  15.6 10.9 %collective-permute-done.2 = bf16[128,1280]{1,0:T(8,128)(2,1)S(1)} collective-permute-done((bf16[128,1280]{1,0:T(8,128)(2,1)S(1)}, bf16[128,1280]{1,0:T(8,128)(2,1)S(1)}, u32[]{:S(2)}, u32[]{:S(2)}) %collective-permute-start.2) | collective-permute-done | bytes 327712 | tf_op jit(solution)/shard_map/ppermute | solution.py:644
  27.4 1.8 %all-to-all-done = bf16[32,8,1280]{2,1,0:T(8,128)(2,1)S(1)} async-done(((bf16[32,8,1280]{2,1,0:T(8,128)(2,1)}), bf16[32,8,1280]{2,1,0:T(8,128)(2,1)S(1)}, u32[]{:S(2)}, u32[]{:S(2)}) %all-to-all-start) | async-done | bytes 655392 | tf_op jit(solution)/shard_map/all_to_all | solution.py:617
  29.2 5.6 %all-to-all-start.2 = ((bf16[16,16,1280]{2,1,0:T(8,128)(2,1)}), bf16[16,16,1280]{2,1,0:T(8,128)(2,1)S(1)}, u32[]{:S(2)}, u32[]{:S(2)}) async-start(bf16[16,16,1280]{2,1,0:T(8,128)(2,1)} %bitcast.30), calls=%async_computation.2 | async-start | bytes 1310720 | tf_op jit(solution)/shard_map/all_to_all | solution.py:624
  34.8 2.9 %gate_sums.1 = (bf16[128,768]{1,0:T(8,128)(2,1)S(1)}, bf16[2,128,1280]{2,1,0:T(8,128)(2,1)S(1)}, bf16[2,128,1280]{2,1,0:T(8,128)(2,1)}) custom-call(bf16[256,1280]{1,0:T(8,128)(2,1)S(1)} %bitcast.20, bf16[1,2560,768]{2,1,0:T(8,128)(2,1)} %refs_1_.3), custom_call_target="tpu_custom_call" | custom-call | flops 503316480 | bytes 3932160 | tf_op jit(solution)/shard_map/gate_sums/pallas_call | solution.py:336
  37.8 2.5 %up_sums.1.refs_2_ = bf16[128,768]{1,0:T(8,128)(2,1)S(1)} custom-call(bf16[2,128,1280]{2,1,0:T(8,128)(2,1)S(1)} %get-tuple-element.26.source_ref, bf16[1,2560,768]{2,1,0:T(8,128)(2,1)} %refs_2_.1), custom_call_target="tpu_custom_call" | custom-call | flops 503316480 | bytes 3932160 | tf_op jit(solution)/shard_map/up_sums/pallas_call | solution.py:336
  40.3 1.1 %collective-permute-start.1 = (bf16[128,768]{1,0:T(8,128)(2,1)S(1)}, bf16[128,768]{1,0:T(8,128)(2,1)S(1)}, u32[]{:S(2)}, u32[]{:S(2)}) collective-permute-start(bf16[128,768]{1,0:T(8,128)(2,1)S(1)} %up_sums.1.refs_2_), channel_id=1, source_target_pairs={{0,16},{16,0},{1,17},{17,1},{2,18},{18,2},{3,19},{19,3},{4,20},{20... | collective-permute-start | bytes 589832 | tf_op jit(solution)/shard_map/ppermute | solution.py:629
  42.4 5.7 %collective-permute-done.1.refs_3_ = bf16[128,768]{1,0:T(8,128)(2,1)S(1)} collective-permute-done((bf16[128,768]{1,0:T(8,128)(2,1)S(1)}, bf16[128,768]{1,0:T(8,128)(2,1)S(1)}, u32[]{:S(2)}, u32[]{:S(2)}) %collective-permute-start.1) | collective-permute-done | bytes 196640 | tf_op jit(solution)/shard_map/ppermute | solution.py:629
  48.1 3.7 %collective-permute-done.refs_1_ = bf16[128,768]{1,0:T(8,128)(2,1)S(1)} collective-permute-done((bf16[128,768]{1,0:T(8,128)(2,1)S(1)}, bf16[128,768]{1,0:T(8,128)(2,1)S(1)}, u32[]{:S(2)}, u32[]{:S(2)}) %collective-permute-start) | collective-permute-done | bytes 196640 | tf_op jit(solution)/shard_map/ppermute | solution.py:629
  51.8 1.8 %output_rows.1 = (bf16[128,768]{1,0:T(8,128)(2,1)S(1)}, bf16[256,1280]{1,0:T(8,128)(2,1)}) custom-call(bf16[128,768]{1,0:T(8,128)(2,1)S(1)} %get-tuple-element.25.refs_0_, bf16[128,768]{1,0:T(8,128)(2,1)S(1)} %collective-permute-done.refs_1_, bf16[128,768]{1,0:T(8,128)(2,1)S(1)} %up_sums.1.refs_2_, bf16[128,768]{1,0:T(8,128)(2,1)S(1)} %collective-permute-done.1.refs_3_, ...), custom_call_target="tpu_custom_call" | custom-call | flops 503316480 | bytes 3932160 | tf_op jit(solution)/shard_map/output_rows/pallas_call | solution.py:431
  53.6 5.2 %all-to-all-start.1 = ((bf16[32,8,1280]{2,1,0:T(8,128)(2,1)}), bf16[32,8,1280]{2,1,0:T(8,128)(2,1)S(1)}, u32[]{:S(2)}, u32[]{:S(2)}) async-start(bf16[32,8,1280]{2,1,0:T(8,128)(2,1)} %bitcast.7), calls=%async_computation.1 | async-start | bytes 1310720 | tf_op jit(solution)/shard_map/all_to_all | solution.py:617
  58.8 4.2 %back_sums.1 = (bf16[128,768]{1,0:T(8,128)(2,1)S(1)}, bf16[2,128,1280]{2,1,0:T(8,128)(2,1)}) custom-call(bf16[256,1280]{1,0:T(8,128)(2,1)S(1)} %bitcast.19, bf16[1,768,2560]{2,1,0:T(8,128)(2,1)} %down_ref.1), custom_call_target="tpu_custom_call" | custom-call | flops 503316480 | bytes 3932160 | tf_op jit(solution)/shard_map/back_sums/pallas_call | solution.py:372
  63.0 1.8 %collective-permute-start.3 = (bf16[128,768]{1,0:T(8,128)(2,1)S(1)}, bf16[128,768]{1,0:T(8,128)(2,1)S(1)}, u32[]{:S(2)}, u32[]{:S(2)}) collective-permute-start(bf16[128,768]{1,0:T(8,128)(2,1)S(1)} %get-tuple-element.32.refs_0_.refs_4_), channel_id=1, source_target_pairs={{0,16},{16,0},{1,17},{17,1},{2,18},{18,2},{3,19},{19,3},{4,20},{20... | collective-permute-start | bytes 589832 | tf_op jit(solution)/shard_map/ppermute | solution.py:629
  64.8 3.3 %bring_weights.1 = (bf16[1,2560,768]{2,1,0:T(8,128)(2,1)S(1)}, bf16[1,2560,768]{2,1,0:T(8,128)(2,1)S(1)}) custom-call(bf16[128,768]{1,0:T(8,128)(2,1)S(1)} %get-tuple-element.32.refs_0_.refs_4_, bf16[1,2560,768]{2,1,0:T(8,128)(2,1)} %refs_1_.3, bf16[1,2560,768]{2,1,0:T(8,128)(2,1)} %refs_2_.1), custom_call_target="tpu_custom_call" | custom-call | bytes 7864320 | tf_op jit(solution)/shard_map/bring_weights/pallas_call | solution.py:398
  68.2 4.3 %collective-permute-done.3.refs_5_ = bf16[128,768]{1,0:T(8,128)(2,1)S(1)} collective-permute-done((bf16[128,768]{1,0:T(8,128)(2,1)S(1)}, bf16[128,768]{1,0:T(8,128)(2,1)S(1)}, u32[]{:S(2)}, u32[]{:S(2)}) %collective-permute-start.3) | collective-permute-done | bytes 196640 | tf_op jit(solution)/shard_map/ppermute | solution.py:629
  72.5 4.2 %gradient_rows.1 = (bf16[128,1536]{1,0:T(8,128)(2,1)}, bf16[256,1280]{1,0:T(8,128)(2,1)}) custom-call(bf16[128,768]{1,0:T(8,128)(2,1)S(1)} %get-tuple-element.25.refs_0_, bf16[128,768]{1,0:T(8,128)(2,1)S(1)} %collective-permute-done.refs_1_, bf16[128,768]{1,0:T(8,128)(2,1)S(1)} %up_sums.1.refs_2_, bf16[128,768]{1,0:T(8,128)(2,1)S(1)} %collective-permute-done.1.refs_3_, ...), custom_call_target="tpu_custom_call" | custom-call | flops 1006632960 | bytes 7864320 | tf_op jit(solution)/shard_map/gradient_rows/pallas_call | solution.py:469
  77.3 5.8 %all-to-all-start.3 = ((bf16[32,8,1280]{2,1,0:T(8,128)(2,1)}), bf16[32,8,1280]{2,1,0:T(8,128)(2,1)S(1)}, u32[]{:S(2)}, u32[]{:S(2)}) async-start(bf16[32,8,1280]{2,1,0:T(8,128)(2,1)} %bitcast.14), calls=%async_computation.3 | async-start | bytes 1310720 | tf_op jit(solution)/shard_map/all_to_all | solution.py:617
  85.2 5.8 %weight_grads.1 = (bf16[1,2560,768]{2,1,0:T(8,128)(2,1)}, bf16[1,2560,768]{2,1,0:T(8,128)(2,1)}, bf16[1,768,2560]{2,1,0:T(8,128)(2,1)}) custom-call(bf16[2,128,1280]{2,1,0:T(8,128)(2,1)S(1)} %copy-done.6, bf16[2,128,1280]{2,1,0:T(8,128)(2,1)S(1)} %copy-done.7, bf16[128,768]{1,0:T(8,128)(2,1)S(1)} %get-tuple-element.39.act_ref, bf16[128,1536]{1,0:T(8,128)(2,1)S(1)} %copy-done.8), custom_call_target="tpu_custom_call" | custom-call | flops 1509949440 | bytes 11796480 | tf_op jit(solution)/shard_map/weight_grads/pallas_call | solution.py:497
  91.0 3.0 %mixed_rows.1 = (bf16[128,5120]{1,0:T(8,128)(2,1)}, f32[4,16]{1,0:T(4,128)}, bf16[2,128,128]{2,1,0:T(8,128)(2,1)S(1)}) custom-call(s32[4,16]{1,0:T(4,128)S(1)} %bitcast.27, f32[4,16]{1,0:T(4,128)S(1)} %bitcast.29, bf16[128,5120]{1,0:T(8,128)(2,1)S(1)} %copy-done.1, bf16[256,1280]{1,0:T(8,128)(2,1)S(1)} %bitcast.22), custom_call_target="tpu_custom_call" | custom-call | flops 671088640 | bytes 2621440 | tf_op jit(solution)/shard_map/mixed_rows/pallas_call | solution.py:569
  94.0 7.6 %all-to-all-done.3 = bf16[32,8,1280]{2,1,0:T(8,128)(2,1)S(1)} async-done(((bf16[32,8,1280]{2,1,0:T(8,128)(2,1)}), bf16[32,8,1280]{2,1,0:T(8,128)(2,1)S(1)}, u32[]{:S(2)}, u32[]{:S(2)}) %all-to-all-start.3) | async-done | bytes 655392 | tf_op jit(solution)/shard_map/all_to_all | solution.py:617
  101.6 1.3 %token_grads.1 = bf16[128,5120]{1,0:T(8,128)(2,1)} custom-call(bf16[2,128,128]{2,1,0:T(8,128)(2,1)S(1)} %get-tuple-element.29.put_ref, bf16[256,1280]{1,0:T(8,128)(2,1)S(1)} %bitcast.21), custom_call_target="tpu_custom_call" | custom-call | flops 167772160 | bytes 1310720 | tf_op jit(solution)/shard_map/token_grads/pallas_call | solution.py:597
  (22 shorter events, 5.9 us)
Async XLA Ops:
  3.4 25.8 %all-to-all-start = ((bf16[32,8,1280]{2,1,0:T(8,128)(2,1)}), bf16[32,8,1280]{2,1,0:T(8,128)(2,1)S(1)}, u32[]{:S(2)}, u32[]{:S(2)}) async-start(bf16[32,8,1280]{2,1,0:T(8,128)(2,1)} %bitcast.5), calls=%async_computation | async-start | bytes 1310720 | tf_op jit(solution)/shard_map/all_to_all | solution.py:617
  10.7 0.7 copy-start.2
  11.4 0.7 copy-start.4
  13.8 12.8 %collective-permute-start.2 = (bf16[128,1280]{1,0:T(8,128)(2,1)S(1)}, bf16[128,1280]{1,0:T(8,128)(2,1)S(1)}, u32[]{:S(2)}, u32[]{:S(2)}) collective-permute-start(bf16[128,1280]{1,0:T(8,128)(2,1)S(1)} %get-tuple-element.31), channel_id=1, source_target_pairs={{0,16},{16,0},{1,17},{17,1},{2,18},{18,2},{3,19},{19,3},{4,20},{20... | collective-permute-start | bytes 983048 | tf_op jit(solution)/shard_map/ppermute | solution.py:644
  29.2 24.4 %all-to-all-start.2 = ((bf16[16,16,1280]{2,1,0:T(8,128)(2,1)}), bf16[16,16,1280]{2,1,0:T(8,128)(2,1)S(1)}, u32[]{:S(2)}, u32[]{:S(2)}) async-start(bf16[16,16,1280]{2,1,0:T(8,128)(2,1)} %bitcast.30), calls=%async_computation.2 | async-start | bytes 1310720 | tf_op jit(solution)/shard_map/all_to_all | solution.py:624
  34.8 17.0 %copy-start = (bf16[1,768,2560]{2,1,0:T(8,128)(2,1)S(1)}, bf16[1,768,2560]{2,1,0:T(8,128)(2,1)}, u32[]{:S(2)}) copy-start(bf16[1,768,2560]{2,1,0:T(8,128)(2,1)} %down_ref.1) | copy-start | bytes 11796484
  40.3 7.8 %collective-permute-start.1 = (bf16[128,768]{1,0:T(8,128)(2,1)S(1)}, bf16[128,768]{1,0:T(8,128)(2,1)S(1)}, u32[]{:S(2)}, u32[]{:S(2)}) collective-permute-start(bf16[128,768]{1,0:T(8,128)(2,1)S(1)} %up_sums.1.refs_2_), channel_id=1, source_target_pairs={{0,16},{16,0},{1,17},{17,1},{2,18},{18,2},{3,19},{19,3},{4,20},{20... | collective-permute-start | bytes 589832 | tf_op jit(solution)/shard_map/ppermute | solution.py:629
  41.5 10.4 %collective-permute-start = (bf16[128,768]{1,0:T(8,128)(2,1)S(1)}, bf16[128,768]{1,0:T(8,128)(2,1)S(1)}, u32[]{:S(2)}, u32[]{:S(2)}) collective-permute-start(bf16[128,768]{1,0:T(8,128)(2,1)S(1)} %get-tuple-element.25.refs_0_), channel_id=1, source_target_pairs={{0,16},{16,0},{1,17},{17,1},{2,18},{18,2},{3,19},{19,3},{4,20},{20... | collective-permute-start | bytes 589832 | tf_op jit(solution)/shard_map/ppermute | solution.py:629
  53.6 23.7 %all-to-all-start.1 = ((bf16[32,8,1280]{2,1,0:T(8,128)(2,1)}), bf16[32,8,1280]{2,1,0:T(8,128)(2,1)S(1)}, u32[]{:S(2)}, u32[]{:S(2)}) async-start(bf16[32,8,1280]{2,1,0:T(8,128)(2,1)} %bitcast.7), calls=%async_computation.1 | async-start | bytes 1310720 | tf_op jit(solution)/shard_map/all_to_all | solution.py:617
  63.0 9.4 %collective-permute-start.3 = (bf16[128,768]{1,0:T(8,128)(2,1)S(1)}, bf16[128,768]{1,0:T(8,128)(2,1)S(1)}, u32[]{:S(2)}, u32[]{:S(2)}) collective-permute-start(bf16[128,768]{1,0:T(8,128)(2,1)S(1)} %get-tuple-element.32.refs_0_.refs_4_), channel_id=1, source_target_pairs={{0,16},{16,0},{1,17},{17,1},{2,18},{18,2},{3,19},{19,3},{4,20},{20... | collective-permute-start | bytes 589832 | tf_op jit(solution)/shard_map/ppermute | solution.py:629
  72.5 10.6 %copy-start.6 = (bf16[2,128,1280]{2,1,0:T(8,128)(2,1)S(1)}, bf16[2,128,1280]{2,1,0:T(8,128)(2,1)}, u32[]{:S(2)}) copy-start(bf16[2,128,1280]{2,1,0:T(8,128)(2,1)} %get-tuple-element.37.rows_in_ref) | copy-start | bytes 1966084
  76.7 14.3 %copy-start.1 = (bf16[128,5120]{1,0:T(8,128)(2,1)S(1)}, bf16[128,5120]{1,0:T(8,128)(2,1)}, u32[]{:S(2)}) copy-start(bf16[128,5120]{1,0:T(8,128)(2,1)} %source_ref.1) | copy-start | bytes 3932164
  76.7 14.3 %copy-start.3 = (s32[1,16,4]{1,2,0:T(4,128)S(1)}, s32[1,16,4]{1,2,0:T(4,128)}, u32[]{:S(2)}) copy-start(s32[1,16,4]{1,2,0:T(4,128)} %param.9) | copy-start | bytes 772
  76.7 14.3 %copy-start.5 = (f32[1,16,4]{1,2,0:T(4,128)S(1)}, f32[1,16,4]{1,2,0:T(4,128)}, u32[]{:S(2)}) copy-start(f32[1,16,4]{1,2,0:T(4,128)} %param.10) | copy-start | bytes 772
  77.3 24.3 %all-to-all-start.3 = ((bf16[32,8,1280]{2,1,0:T(8,128)(2,1)}), bf16[32,8,1280]{2,1,0:T(8,128)(2,1)S(1)}, u32[]{:S(2)}, u32[]{:S(2)}) async-start(bf16[32,8,1280]{2,1,0:T(8,128)(2,1)} %bitcast.14), calls=%async_computation.3 | async-start | bytes 1310720 | tf_op jit(solution)/shard_map/all_to_all | solution.py:617
  83.1 1.1 %copy-start.7 = (bf16[2,128,1280]{2,1,0:T(8,128)(2,1)S(1)}, bf16[2,128,1280]{2,1,0:T(8,128)(2,1)}, u32[]{:S(2)}) copy-start(bf16[2,128,1280]{2,1,0:T(8,128)(2,1)} %get-tuple-element.38.rows_up_ref) | copy-start | bytes 1966084
  84.2 1.0 copy-start.8

commit v8 on v4

--- a/solution.py
+++ b/solution.py
@@ -32,6 +32,10 @@
 def expert_at(place, experts):
     planes = planes_of(experts)
     return place % planes * (experts // planes) + place // planes
+
+
+def split_place(place, halves, planes):
+    return (place // (halves * planes) * planes + place % planes) * halves + place // planes % halves
 
 
 def one_hot(condition):
@@ -159,11 +163,15 @@
     )(*[in_hbm(value) for value in lists], in_hbm(source))
 
 
-def sort_matrix(rows, blocks, slots, back):
+def same_place(device):
+    return device
+
+
+def sort_matrix(rows, blocks, slots, back, place=same_place):
     a = iota((rows, rows), 1 if back else 0)
     b = iota((rows, rows), 0 if back else 1)
     group = rows // blocks
-    return one_hot(a % group // slots * (blocks * slots) + a // group * slots + a % slots == b)
+    return one_hot(place(a % group // slots) * (blocks * slots) + a // group * slots + a % slots == b)
 
 
 def sort_rows(messages_ref, rows_ref, slots):
@@ -180,14 +188,14 @@
             rows_ref[block, part * group : (part + 1) * group] = ordered[block * group : (block + 1) * group]
 
 
-def unsort_rows(made, out_ref, slots, span=slice(None)):
+def unsort_rows(made, out_ref, slots, span=slice(None), place=same_place):
     blocks, total = len(made), made[0].shape[0]
-    if blocks == 1:
+    if blocks == 1 and place is same_place:
         out_ref[:, span] = made[0]
         return
     size = min(blocks * total, 256)
     group = size // blocks
-    order = sort_matrix(size, blocks, slots, True)
+    order = sort_matrix(size, blocks, slots, True, place)
     for part in range(total // group):
         stacked = jnp.concatenate([value[part * group : (part + 1) * group] for value in made], axis=0)
         out_ref[part * size : (part + 1) * size, span] = dot(order, stacked).astype(BF16)
@@ -207,6 +215,11 @@
         return [(0, width)]
     first = width // 2 // 256 * 256
     return [(0, first), (first, width - first)]
+
+
+def thirds_of(height):
+    size = height // 3 if height % 384 == 0 else height
+    return [(start, size) for start in range(0, height, size)]
 
 
 class Stream:
@@ -263,39 +276,35 @@
     )(messages, in_hbm(w_gate), in_hbm(w_up))
 
 
-def up_sums_kernel(slots, messages_ref, down_ref, out_ref, kept_ref, rows_ref, held_ref, acc_ref, sems):
+def back_sums_kernel(slots, messages_ref, down_ref, out_ref, kept_ref, rows_ref, held_ref, sems):
     blocks, _, cols = rows_ref.shape
     stream = Stream(sems)
-    cuts = [(block, start, size) for block in range(blocks) for start, size in pieces_of(cols)]
-    copies = []
-    for block, start, size in cuts:
-        span = slice(block * cols + start, block * cols + start + size)
-        copies.append(stream.start(down_ref.at[0, :, span], held_ref.at[:, span]))
+    spots = [slice(start, start + size) for start, size in thirds_of(down_ref.shape[1])]
+    copies = [stream.start(down_ref.at[0, spot], held_ref.at[spot]) for spot in spots]
     sort_rows(messages_ref, rows_ref, slots)
     kept = stream.start(rows_ref, kept_ref)
-    for number, (block, start, size) in enumerate(cuts):
-        span = slice(block * cols + start, block * cols + start + size)
-        copies[number].wait()
-        term = dot(rows_ref[block, :, start : start + size], held_ref[:, span], ((1,), (1,)))
-        acc_ref[...] = term if number == 0 else acc_ref[...] + term
-    out_ref[...] = acc_ref[...].astype(BF16)
+    for spot, copy in zip(spots, copies):
+        copy.wait()
+        terms = [
+            dot(rows_ref[b], held_ref[spot, span], ((1,), (1,))) for b, span in enumerate(spans(blocks * cols, blocks))
+        ]
+        out_ref[:, spot] = added(terms).astype(BF16)
     kept.wait()
 
 
-def up_sums(messages, w_down, blocks, slots):
+def back_sums(messages, w_down, blocks, slots):
     hidden, part = w_down.shape[1:]
     rows = messages.shape[0] // blocks
     cols = part // blocks
     return pl.pallas_call(
-        functools.partial(up_sums_kernel, slots),
+        functools.partial(back_sums_kernel, slots),
         in_specs=[vmem(), hbm()],
         out_specs=[vmem(), hbm()],
         out_shape=[shape_of(rows, hidden), hbm_shape(blocks, rows, cols)],
         scratch_shapes=[
             pltpu.VMEM((blocks, rows, cols), BF16),
             pltpu.VMEM((hidden, part), BF16),
-            pltpu.VMEM((rows, hidden), F32),
-            pltpu.SemaphoreType.DMA((blocks * len(pieces_of(cols)) + 1,)),
+            pltpu.SemaphoreType.DMA((len(thirds_of(hidden)) + 1,)),
         ],
         compiler_params=params(),
         cost_estimate=cost(2 * rows * part * hidden, 2 * part * hidden),
@@ -303,6 +312,28 @@
     )(messages, in_hbm(w_down))
 
 
+def bring_kernel(count, *refs):
+    sources, targets, sems = refs[1 : count + 1], refs[count + 1 : 2 * count + 1], refs[-1]
+    copies = [pltpu.make_async_copy(s, t, sems.at[i]) for i, (s, t) in enumerate(zip(sources, targets))]
+    for copy in copies:
+        copy.start()
+    for copy in copies:
+        copy.wait()
+
+
+def bring(values, after):
+    return pl.pallas_call(
+        functools.partial(bring_kernel, len(values)),
+        in_specs=[pl.BlockSpec(memory_space=pl.ANY)] + [hbm()] * len(values),
+        out_specs=[vmem()] * len(values),
+        out_shape=[shape_of(*value.shape) for value in values],
+        scratch_shapes=[pltpu.SemaphoreType.DMA((len(values),))],
+        compiler_params=params(16),
+        cost_estimate=cost(0, 2 * sum(value.size for value in values)),
+        name="bring_weights",
+    )(after, *[in_hbm(value) for value in values])
+
+
 def row_parts(total):
     size = min(total, 128)
     return [slice(start, start + size) for start in range(0, total, size)]
@@ -312,21 +343,22 @@
     return added([ref[rows, span].astype(F32) for ref in refs])
 
 
-def out_rows_kernel(slots, blocks, count, *refs):
+def out_rows_kernel(slots, blocks, place, count, *refs):
     shares, (down_ref, act_ref, out_ref) = refs[:count], refs[count:]
     hidden, part = down_ref.shape[1:]
     for rows in row_parts(act_ref.shape[0]):
         gate_sum = summed(shares, rows, slice(0, hidden))
         up_sum = summed(shares, rows, slice(hidden, 2 * hidden))
         act_ref[rows] = (gate_sum * jax.nn.sigmoid(gate_sum) * up_sum).astype(BF16)
-    unsort_rows([dot(act_ref[...], down_ref[0, :, span]).astype(BF16) for span in spans(part, blocks)], out_ref, slots)
-
-
-def out_rows(shares, w_down, blocks, slots):
+    made = [dot(act_ref[...], down_ref[0, :, span]).astype(BF16) for span in spans(part, blocks)]
+    unsort_rows(made, out_ref, slots, place=place)
+
+
+def out_rows(shares, w_down, blocks, slots, place):
     hidden, part = w_down.shape[1:]
     rows = shares[0].shape[0]
     return pl.pallas_call(
-        functools.partial(out_rows_kernel, slots, blocks, len(shares)),
+        functools.partial(out_rows_kernel, slots, blocks, place, len(shares)),
         in_specs=[vmem()] * (len(shares) + 1),
         out_specs=[vmem()] * 2,
         out_shape=[shape_of(rows, hidden), shape_of(blocks * rows, part // blocks)],
@@ -338,15 +370,9 @@
 
 def grad_rows_kernel(slots, blocks, count, *refs):
     shares, backs = refs[:count], refs[count : 2 * count]
-    gate_ref, up_ref, kept_ref, out_ref, act_ref, held_ref, sems = refs[2 * count :]
+    gate_ref, up_ref, kept_ref, out_ref, act_ref, sem = refs[2 * count :]
     part, hidden = gate_ref.shape[1:]
     cols = part // blocks
-    stream = Stream(sems)
-    cuts = [(start, size, block) for start, size in pieces_of(cols) for block in range(blocks)]
-    copies = []
-    for start, size, block in cuts:
-        span = slice(block * cols + start, block * cols + start + size)
-        copies.append([stream.start(r.at[0, span], held_ref.at[i, span]) for i, r in enumerate((gate_ref, up_ref))])
     for rows in row_parts(act_ref.shape[0]):
         gate_sum = summed(shares, rows, slice(0, hidden))
         up_sum = summed(shares, rows, slice(hidden, 2 * hidden))
@@ -354,18 +380,16 @@
         sig = jax.nn.sigmoid(gate_sum)
         act_ref[rows, :hidden] = (back_sum * up_sum * sig * (1.0 + gate_sum * (1.0 - sig))).astype(BF16)
         act_ref[rows, hidden:] = (back_sum * (gate_sum * sig)).astype(BF16)
-    kept = stream.start(act_ref, kept_ref)
-    made = []
-    for (start, size, block), pair in zip(cuts, copies):
-        span = slice(block * cols + start, block * cols + start + size)
-        terms = []
-        for i in range(2):
-            pair[i].wait()
-            terms.append(dot(act_ref[:, i * hidden : (i + 1) * hidden], held_ref[i, span], ((1,), (1,))))
-        made.append(added(terms).astype(BF16))
-        if block == blocks - 1:
-            unsort_rows(made, out_ref, slots, slice(start, start + size))
-            made = []
+    kept = pltpu.make_async_copy(act_ref, kept_ref, sem)
+    kept.start()
+    for start, size in pieces_of(cols):
+        made = []
+        for block in range(blocks):
+            span = slice(block * cols + start, block * cols + start + size)
+            total = dot(act_ref[:, :hidden], gate_ref[0, span, :], ((1,), (1,)))
+            total = total + dot(act_ref[:, hidden:], up_ref[0, span, :], ((1,), (1,)))
+            made.append(total.astype(BF16))
+        unsort_rows(made, out_ref, slots, slice(start, start + size))
     kept.wait()
 
 
@@ -375,18 +399,14 @@
     cols = part // blocks
     return pl.pallas_call(
         functools.partial(grad_rows_kernel, slots, blocks, len(shares)),
-        in_specs=[vmem()] * (2 * len(shares)) + [hbm()] * 2,
+        in_specs=[vmem()] * (2 * len(shares) + 2),
         out_specs=[hbm(), vmem()],
         out_shape=[hbm_shape(rows, 2 * hidden), shape_of(blocks * rows, cols)],
-        scratch_shapes=[
-            pltpu.VMEM((rows, 2 * hidden), BF16),
-            pltpu.VMEM((2, part, hidden), BF16),
-            pltpu.SemaphoreType.DMA((2 * blocks * len(pieces_of(cols)) + 1,)),
-        ],
-        compiler_params=params(40),
+        scratch_shapes=[pltpu.VMEM((rows, 2 * hidden), BF16), pltpu.SemaphoreType.DMA],
+        compiler_params=params(32),
         cost_estimate=cost(4 * rows * part * hidden, 4 * part * hidden),
         name="gradient_rows",
-    )(*shares, *backs, in_hbm(w_gate), in_hbm(w_up))
+    )(*shares, *backs, w_gate, w_up)
 
 
 def weights_kernel(rows_in_ref, rows_up_ref, act_ref, grad_act_ref, gate_ref, up_ref, down_ref):
@@ -427,25 +447,30 @@
     return jnp.concatenate([back_ref[start : start + run] for start in range(half * run, total, halves * run)], axis=0)
 
 
-def put_columns(held_ref, target_ref, sems, half, block):
+def put_columns(held_ref, target_ref, sems, half, block, start=None):
     blocks, _, cols = held_ref.shape[1:]
-    place = half * blocks + block
-    copy = pltpu.make_async_copy(
-        held_ref.at[half, block], target_ref.at[:, place * cols : (place + 1) * cols], sems.at[half, block]
-    )
+    start = (half * blocks + block) * cols if start is None else start
+    copy = pltpu.make_async_copy(held_ref.at[half, block], target_ref.at[:, pl.ds(start, cols)], sems.at[half, block])
     copy.start()
     return copy
 
 
-def mixed_kernel(picks_ref, gates_ref, cot_ref, back_ref, mixed_ref, gate_grad_ref, put_ref, held_ref, sems):
+def mixed_kernel(crossed, picks_ref, gates_ref, cot_ref, *refs):
+    back_refs, (mixed_ref, gate_grad_ref, put_ref, held_ref, sems) = refs[:-5], refs[-5:]
     slots, experts = picks_ref.shape
     halves, blocks, tokens, cols = held_ref.shape
     rows = experts * blocks * slots
     hit = spread_row(picks_ref[...].astype(F32), blocks).astype(jnp.int32) == iota((tokens, rows), 0)
     scale = spread_row(gates_ref[...], blocks)
     of_block = iota((tokens, rows), 1) % (blocks * slots) // slots
-    run = planes_of(experts) * blocks * slots
-    backs = [back_rows(back_ref, half, halves, run) for half in range(halves)]
+    if crossed:
+        backs = [ref[...] for ref in back_refs]
+        own = lax.axis_index("dp")
+        places = [own, 1 - own]
+    else:
+        run = planes_of(experts) * blocks * slots
+        backs = [back_rows(back_refs[0], half, halves, run) for half in range(halves)]
+        places = list(range(halves))
     copies = []
     products = None
     for block in range(blocks):
@@ -458,10 +483,10 @@
             rest = rest - pieces[-1].astype(F32)
         for half in range(halves):
             back = backs[half]
+            start = pl.multiple_of((places[half] * blocks + block) * cols, 128)
             held_ref[half, block] = added([dot(piece, back) for piece in pieces]).astype(BF16)
-            copies.append(put_columns(held_ref, mixed_ref, sems, half, block))
-            place = half * blocks + block
-            product = dot(cot_ref[:, place * cols : (place + 1) * cols], back, ((1,), (1,)))
+            copies.append(put_columns(held_ref, mixed_ref, sems, half, block, start))
+            product = dot(cot_ref[:, pl.ds(start, cols)], back, ((1,), (1,)))
             product = jnp.where(inside, product, 0.0)
             products = product if products is None else products + product
     values = jnp.sum(products, axis=0, keepdims=True)
@@ -472,21 +497,49 @@
         copy.wait()
 
 
-def mix_rows(back, cotangent, picks, gates, halves, blocks):
+def mix_rows(backs, cotangent, picks, gates, halves, blocks):
     slots, experts = picks.shape
     tokens, width = cotangent.shape
     cols = width // (halves * blocks)
     rows = experts * blocks * slots
     return pl.pallas_call(
-        mixed_kernel,
-        in_specs=[vmem()] * 4,
+        functools.partial(mixed_kernel, len(backs) == 2),
+        in_specs=[vmem()] * (3 + len(backs)),
         out_specs=[hbm(), vmem(), vmem()],
         out_shape=[shape_of(tokens, width), shape_of(slots, experts, dtype=F32), shape_of(blocks, tokens, rows)],
         scratch_shapes=[pltpu.VMEM((halves, blocks, tokens, cols), BF16), pltpu.SemaphoreType.DMA((halves, blocks))],
         compiler_params=params(16),
         cost_estimate=cost(8 * rows * tokens * width, 4 * tokens * width),
         name="mixed_rows",
-    )(picks, gates, cotangent, back)
+    )(picks, gates, cotangent, *backs)
+
+
+def part_kernel(joined_ref, own_ref, other_ref, sems):
+    half = lax.axis_index("dp")
+    copies = [
+        pltpu.make_async_copy(joined_ref.at[:, half], own_ref, sems.at[0]),
+        pltpu.make_async_copy(joined_ref.at[:, 1 - half], other_ref, sems.at[1]),
+    ]
+    for copy in copies:
+        copy.start()
+    for copy in copies:
+        copy.wait()
+
+
+def part_rows(joined, experts):
+    rows, cols = joined.shape
+    shape = (experts, rows // (2 * experts), cols)
+    parted = pl.pallas_call(
+        part_kernel,
+        in_specs=[pl.BlockSpec(memory_space=pl.ANY)],
+        out_specs=[pl.BlockSpec(memory_space=pl.ANY)] * 2,
+        out_shape=[shape_of(*shape)] * 2,
+        scratch_shapes=[pltpu.SemaphoreType.DMA((2,))],
+        compiler_params=params(16),
+        cost_estimate=cost(0, 4 * rows * cols),
+        name="part_rows",
+    )(joined.reshape(experts, 2, *shape[1:]))
+    return [value.reshape(rows // 2, cols) for value in parted]
 
 
 def token_grad_kernel(run, put_ref, back_ref, grad_ref, held_ref, sems):
@@ -530,6 +583,11 @@
     )
 
 
+def to_experts(experts, messages):
+    order = [expert_at(place, experts) for place in range(experts)]
+    return lax.all_to_all(messages, "expert", split_axis=0, concat_axis=0, tiled=True, axis_index_groups=[order])
+
+
 def dp_shares(own, halves):
     shares = [own] + [
         lax.ppermute(own, "dp", [(i, (i + shift) % halves) for i in range(halves)]) for shift in range(1, halves)
@@ -547,14 +605,20 @@
     arrived_up = scatter(send_rows(cotangent, (picks_t, gates_t), halves, blocks))
     own_sums, rows_in = in_sums(arrived_in, w_gate, w_up, blocks, slots)
     shares = dp_shares(own_sums, halves)
-    act, outputs = out_rows(shares, w_down, blocks, slots)
-    back_out = scatter(outputs)
-    own_back, rows_up = up_sums(arrived_up, w_down, blocks, slots)
+    place = functools.partial(split_place, halves=2, planes=planes_of(experts)) if halves == 2 else same_place
+    act, outputs = out_rows(shares, w_down, blocks, slots, place)
+    back_out = to_experts(experts, outputs) if halves == 2 else scatter(outputs)
+    own_back, rows_up = back_sums(arrived_up, w_down, blocks, slots)
     backs = dp_shares(own_back, halves)
-    grad_act, gradients = grad_rows(shares, backs, w_gate, w_up, blocks, slots)
+    near_gate, near_up = bring((w_gate, w_up), own_back)
+    grad_act, gradients = grad_rows(shares, backs, near_gate, near_up, blocks, slots)
     back_grad = scatter(gradients)
     grad_gate_w, grad_up_w, grad_down = weight_grads(rows_in, rows_up, act, grad_act)
-    mixed, gate_grad, put = mix_rows(back_out, cotangent, picks_t, gates_t, halves, blocks)
+    returned = [back_out]
+    if halves == 2:
+        own_out, other_out = part_rows(back_out, experts)
+        returned = [own_out, lax.ppermute(other_out, "dp", [(0, 1), (1, 0)])]
+    mixed, gate_grad, put = mix_rows(returned, cotangent, picks_t, gates_t, halves, blocks)
     token_grad = token_grads(back_grad, put, halves, planes_of(experts) * blocks * slots)
     return mixed, token_grad, gate_grad.T[None], grad_gate_w, grad_up_w, grad_down
 

time: 105 us -> 100 us (0.952)
  waiting for transfers between devices: 44.2 us -> 40.9 us
  starting transfers between devices: 25.3 us -> 22.4 us
  Pallas kernels: 31.7 us -> 33.6 us
    all_to_all x4 -> x3, starting transfers between devices: 21.8 us -> 12.5 us  [to_owners(): lax.all_to_all(messages, EVERYONE, split_axis=0, concat_axis=0, tiled=Tru...]
    all_to_all x4 -> x3, waiting for transfers between devices: 23.2 us -> 15.6 us  [to_owners(): lax.all_to_all(messages, EVERYONE, split_axis=0, concat_axis=0, tiled=Tru...]
    all_to_all x0 -> x1, starting transfers between devices: none -> 5.85 us  [to_experts(): lax.all_to_all(messages, 'expert', split_axis=0, concat_axis=0, tiled=Tru...]
    ppermute x0 -> x1, waiting for transfers between devices: none -> 5.76 us  [body(): returned = [own_out, lax.ppermute(other_out, 'dp', [(0, 1), (1, 0)])]]
    ppermute x2, waiting for transfers between devices: 21.1 us -> 16.7 us  [dp_shares(): lax.ppermute(own, 'dp', [(i, (i + shift) % halves) for i in range(halves)])]
    pallas_call x3 -> x5, Pallas kernels: 8.22 us -> 12.3 us  [the longest x1 4.11 us: back_sums(): pl.pallas_call(functools.partial(back_sums_kernel, slots), in_specs=[vmem...]
    all_to_all x0 -> x1, waiting for transfers between devices: none -> 2.79 us  [to_experts(): lax.all_to_all(messages, 'expert', split_axis=0, concat_axis=0, tiled=Tru...]
    pallas_call x1, Pallas kernels: 6.47 us -> 4.23 us  [grad_rows(): pl.pallas_call(functools.partial(grad_rows_kernel, slots, blocks, len(sha...]
  transfers between devices with their start and end apart: 6 -> 7, of which waited for: 4 -> 5; matrix products, arithmetic and copies ran while one was open for 0% -> 0% of each run, Pallas kernels for 27% -> 30%
where the time goes in v8:
time: 100 us; the launch traced here: 99.8 us
  waiting for transfers between devices  40.9 us (41%)
  Pallas kernels  33.6 us (34%)
  starting transfers between devices  22.4 us (22%)
  local copies, waits for them, and re-layouts  2.11 us (2%)
    ppermute x2, waiting for transfers between devices, dp_shares(): lax.ppermute(own, 'dp', [(i, (i + shift) % halves) for i in range(halves)])  16.7 us
    all_to_all x3, waiting for transfers between devices, to_owners(): lax.all_to_all(messages, EVERYONE, split_axis=0, concat_axis=0, tiled=Tru...  15.6 us
    all_to_all x3, starting transfers between devices, to_owners(): lax.all_to_all(messages, EVERYONE, split_axis=0, concat_axis=0, tiled=Tru...  12.5 us
    all_to_all x1, starting transfers between devices, to_experts(): lax.all_to_all(messages, 'expert', split_axis=0, concat_axis=0, tiled=Tru...  5.85 us
    pallas_call x1, Pallas kernels, weight_grads(): pl.pallas_call(weights_kernel, grid=(blocks, steps), in_specs=[chunk, chu...  5.77 us
    ppermute x1, waiting for transfers between devices, body(): returned = [own_out, lax.ppermute(other_out, 'dp', [(0, 1), (1, 0)])]  5.76 us
    pallas_call x2, Pallas kernels, send_rows(): pl.pallas_call(functools.partial(send_kernel, halves, blocks, len(lists)...  5.7 us
    pallas_call x1, Pallas kernels, in_sums(): pl.pallas_call(functools.partial(in_sums_kernel, slots), in_specs=[vmem()...  4.26 us
  transfers between devices with their start and end apart: 7, of which 5 were waited for; matrix products, arithmetic and copies ran while one was open for 0% of the time, Pallas kernels for 30%

profile of v8, /device:TPU:0, one launch (start us, length us, event | category | flops | bytes accessed | tf_op | source)
XLA Modules:
  0.0 99.8 jit_solution(11901344710778344942)
XLA Ops:
  0.6 2.8 %send_rows.2 = bf16[256,1280]{1,0:T(8,128)(2,1)} custom-call(s32[4,16]{1,0:T(4,128)} %bitcast.23, bf16[128,5120]{1,0:T(8,128)(2,1)} %refs_1_.2), custom_call_target="tpu_custom_call" | custom-call | flops 167772160 | bytes 1966080 | tf_op jit(solution)/shard_map/send_rows/pallas_call | solution.py:149
  3.4 7.3 %all-to-all-start = ((bf16[32,8,1280]{2,1,0:T(8,128)(2,1)}), bf16[32,8,1280]{2,1,0:T(8,128)(2,1)S(1)}, u32[]{:S(2)}, u32[]{:S(2)}) async-start(bf16[32,8,1280]{2,1,0:T(8,128)(2,1)} %bitcast.5), calls=%async_computation | async-start | bytes 1310720 | tf_op jit(solution)/shard_map/all_to_all | solution.py:581
  10.7 2.9 %send_rows.3 = bf16[256,1280]{1,0:T(8,128)(2,1)} custom-call(s32[4,16]{1,0:T(4,128)} %bitcast.24, f32[4,16]{1,0:T(4,128)} %bitcast.26, bf16[128,5120]{1,0:T(8,128)(2,1)} %refs_2_.4), custom_call_target="tpu_custom_call" | custom-call | flops 167772160 | bytes 1966080 | tf_op jit(solution)/shard_map/send_rows/pallas_call | solution.py:149
  13.7 15.6 %all-to-all-done = bf16[32,8,1280]{2,1,0:T(8,128)(2,1)S(1)} async-done(((bf16[32,8,1280]{2,1,0:T(8,128)(2,1)}), bf16[32,8,1280]{2,1,0:T(8,128)(2,1)S(1)}, u32[]{:S(2)}, u32[]{:S(2)}) %all-to-all-start) | async-done | bytes 655392 | tf_op jit(solution)/shard_map/all_to_all | solution.py:581
  29.2 2.6 %all-to-all-start.2 = ((bf16[32,8,1280]{2,1,0:T(8,128)(2,1)}), bf16[32,8,1280]{2,1,0:T(8,128)(2,1)S(1)}, u32[]{:S(2)}, u32[]{:S(2)}) async-start(bf16[32,8,1280]{2,1,0:T(8,128)(2,1)} %bitcast.12), calls=%async_computation.2 | async-start | bytes 1310720 | tf_op jit(solution)/shard_map/all_to_all | solution.py:581
  31.9 4.3 %gate_up_sums.1 = (bf16[128,1536]{1,0:T(8,128)(2,1)S(1)}, bf16[2,128,1280]{2,1,0:T(8,128)(2,1)}) custom-call(bf16[256,1280]{1,0:T(8,128)(2,1)S(1)} %bitcast.19, bf16[1,2560,768]{2,1,0:T(8,128)(2,1)} %refs_1_.3, bf16[1,2560,768]{2,1,0:T(8,128)(2,1)} %refs_2_.5), custom_call_target="tpu_custom_call" | custom-call | flops 1006632960 | bytes 7864320 | tf_op jit(solution)/shard_map/gate_up_sums/pallas_call | solution.py:262
  36.1 1.7 %collective-permute-start = (bf16[128,1536]{1,0:T(8,128)(2,1)S(1)}, bf16[128,1536]{1,0:T(8,128)(2,1)S(1)}, u32[]{:S(2)}, u32[]{:S(2)}) collective-permute-start(bf16[128,1536]{1,0:T(8,128)(2,1)S(1)} %get-tuple-element.24.refs_0_), channel_id=1, source_target_pairs={{0,16},{16,0},{1,17},{17,1},{2,18},{18,2},{3,19},{19,3},{4,20},{20... | collective-permute-start | bytes 1179656 | tf_op jit(solution)/shard_map/ppermute | solution.py:593
  37.8 13.4 %collective-permute-done.refs_1_ = bf16[128,1536]{1,0:T(8,128)(2,1)S(1)} collective-permute-done((bf16[128,1536]{1,0:T(8,128)(2,1)S(1)}, bf16[128,1536]{1,0:T(8,128)(2,1)S(1)}, u32[]{:S(2)}, u32[]{:S(2)}) %collective-permute-start) | collective-permute-done | bytes 393248 | tf_op jit(solution)/shard_map/ppermute | solution.py:593
  51.2 1.8 %output_rows.1 = (bf16[128,768]{1,0:T(8,128)(2,1)S(1)}, bf16[256,1280]{1,0:T(8,128)(2,1)}) custom-call(bf16[128,1536]{1,0:T(8,128)(2,1)S(1)} %get-tuple-element.24.refs_0_, bf16[128,1536]{1,0:T(8,128)(2,1)S(1)} %collective-permute-done.refs_1_, bf16[1,768,2560]{2,1,0:T(8,128)(2,1)S(1)} %copy-done), custom_call_target="tpu_custom_call" | custom-call | flops 503316480 | bytes 3932160 | tf_op jit(solution)/shard_map/output_rows/pallas_call | solution.py:360
  53.0 5.8 %all-to-all-start.1 = ((bf16[16,16,1280]{2,1,0:T(8,128)(2,1)}), bf16[16,16,1280]{2,1,0:T(8,128)(2,1)S(1)}, u32[]{:S(2)}, u32[]{:S(2)}) async-start(bf16[16,16,1280]{2,1,0:T(8,128)(2,1)} %bitcast.7), calls=%async_computation.1 | async-start | bytes 1310720 | tf_op jit(solution)/shard_map/all_to_all | solution.py:588
  58.9 4.1 %back_sums.1 = (bf16[128,768]{1,0:T(8,128)(2,1)S(1)}, bf16[2,128,1280]{2,1,0:T(8,128)(2,1)}) custom-call(bf16[256,1280]{1,0:T(8,128)(2,1)S(1)} %bitcast.20, bf16[1,768,2560]{2,1,0:T(8,128)(2,1)} %down_ref.1), custom_call_target="tpu_custom_call" | custom-call | flops 503316480 | bytes 3932160 | tf_op jit(solution)/shard_map/back_sums/pallas_call | solution.py:299
  63.0 0.6 collective-permute-start.2
  63.6 3.3 %bring_weights.1 = (bf16[1,2560,768]{2,1,0:T(8,128)(2,1)S(1)}, bf16[1,2560,768]{2,1,0:T(8,128)(2,1)S(1)}) custom-call(bf16[128,768]{1,0:T(8,128)(2,1)S(1)} %get-tuple-element.30.refs_0_.refs_2_, bf16[1,2560,768]{2,1,0:T(8,128)(2,1)} %refs_1_.3, bf16[1,2560,768]{2,1,0:T(8,128)(2,1)} %refs_2_.5), custom_call_target="tpu_custom_call" | custom-call | bytes 7864320 | tf_op jit(solution)/shard_map/bring_weights/pallas_call | solution.py:325
  66.9 3.4 %collective-permute-done.2.refs_3_ = bf16[128,768]{1,0:T(8,128)(2,1)S(1)} collective-permute-done((bf16[128,768]{1,0:T(8,128)(2,1)S(1)}, bf16[128,768]{1,0:T(8,128)(2,1)S(1)}, u32[]{:S(2)}, u32[]{:S(2)}) %collective-permute-start.2) | collective-permute-done | bytes 196640 | tf_op jit(solution)/shard_map/ppermute | solution.py:593
  70.3 4.2 %gradient_rows.1 = (bf16[128,1536]{1,0:T(8,128)(2,1)}, bf16[256,1280]{1,0:T(8,128)(2,1)}) custom-call(bf16[128,1536]{1,0:T(8,128)(2,1)S(1)} %get-tuple-element.24.refs_0_, bf16[128,1536]{1,0:T(8,128)(2,1)S(1)} %collective-permute-done.refs_1_, bf16[128,768]{1,0:T(8,128)(2,1)S(1)} %get-tuple-element.30.refs_0_.refs_2_, ...), custom_call_target="tpu_custom_call" | custom-call | flops 1006632960 | bytes 7864320 | tf_op jit(solution)/shard_map/gradient_rows/pallas_call | solution.py:400
  74.6 2.8 %all-to-all-done.1 = bf16[16,16,1280]{2,1,0:T(8,128)(2,1)S(1)} async-done(((bf16[16,16,1280]{2,1,0:T(8,128)(2,1)}), bf16[16,16,1280]{2,1,0:T(8,128)(2,1)S(1)}, u32[]{:S(2)}, u32[]{:S(2)}) %all-to-all-start.1) | async-done | bytes 655392 | tf_op jit(solution)/shard_map/all_to_all | solution.py:588
  77.3 2.6 %all-to-all-start.3 = ((bf16[32,8,1280]{2,1,0:T(8,128)(2,1)}), bf16[32,8,1280]{2,1,0:T(8,128)(2,1)S(1)}, u32[]{:S(2)}, u32[]{:S(2)}) async-start(bf16[32,8,1280]{2,1,0:T(8,128)(2,1)} %bitcast.14), calls=%async_computation.3 | async-start | bytes 1310720 | tf_op jit(solution)/shard_map/all_to_all | solution.py:581
  80.1 1.7 %collective-permute-start.1 = (bf16[128,1280]{1,0:T(8,128)(2,1)S(1)}, bf16[128,1280]{1,0:T(8,128)(2,1)S(1)}, u32[]{:S(2)}, u32[]{:S(2)}) collective-permute-start(bf16[128,1280]{1,0:T(8,128)(2,1)S(1)} %bitcast.29), channel_id=1, source_target_pairs={{0,16},{16,0},{1,17},{17,1},{2,18},{18,2},{3,19},{19,3},{4,20},{20... | collective-permute-start | bytes 983048 | tf_op jit(solution)/shard_map/ppermute | solution.py:620
  81.8 1.1 %copy-done.5 = bf16[2,128,1280]{2,1,0:T(8,128)(2,1)S(1)} copy-done((bf16[2,128,1280]{2,1,0:T(8,128)(2,1)S(1)}, bf16[2,128,1280]{2,1,0:T(8,128)(2,1)}, u32[]{:S(2)}) %copy-start.5) | copy-done | bytes 655384
  82.9 1.0 copy-done.6
  83.9 5.8 %weight_grads.1 = (bf16[1,2560,768]{2,1,0:T(8,128)(2,1)}, bf16[1,2560,768]{2,1,0:T(8,128)(2,1)}, bf16[1,768,2560]{2,1,0:T(8,128)(2,1)}) custom-call(bf16[2,128,1280]{2,1,0:T(8,128)(2,1)S(1)} %copy-done.4, bf16[2,128,1280]{2,1,0:T(8,128)(2,1)S(1)} %copy-done.5, bf16[128,768]{1,0:T(8,128)(2,1)S(1)} %get-tuple-element.37.act_ref, bf16[128,1536]{1,0:T(8,128)(2,1)S(1)} %copy-done.6), custom_call_target="tpu_custom_call" | custom-call | flops 1509949440 | bytes 11796480 | tf_op jit(solution)/shard_map/weight_grads/pallas_call | solution.py:428
  89.6 5.8 %collective-permute-done.1.refs_1_ = bf16[128,1280]{1,0:T(8,128)(2,1)S(1)} collective-permute-done((bf16[128,1280]{1,0:T(8,128)(2,1)S(1)}, bf16[128,1280]{1,0:T(8,128)(2,1)S(1)}, u32[]{:S(2)}, u32[]{:S(2)}) %collective-permute-start.1) | collective-permute-done | bytes 327712 | tf_op jit(solution)/shard_map/ppermute | solution.py:620
  95.4 3.0 %mixed_rows.1 = (bf16[128,5120]{1,0:T(8,128)(2,1)}, f32[4,16]{1,0:T(4,128)}, bf16[2,128,128]{2,1,0:T(8,128)(2,1)S(1)}) custom-call(s32[4,16]{1,0:T(4,128)S(1)} %bitcast.25, f32[4,16]{1,0:T(4,128)S(1)} %bitcast.27, bf16[128,5120]{1,0:T(8,128)(2,1)S(1)} %copy-done.1, bf16[128,1280]{1,0:T(8,128)(2,1)S(1)} %bitcast.28, ...), custom_call_target="tpu_custom_call" | custom-call | flops 671088640 | bytes 2621440 | tf_op jit(solution)/shard_map/mixed_rows/pallas_call | solution.py:505
  98.5 1.3 %token_grads.1 = bf16[128,5120]{1,0:T(8,128)(2,1)} custom-call(bf16[2,128,128]{2,1,0:T(8,128)(2,1)S(1)} %get-tuple-element.29.put_ref, bf16[256,1280]{1,0:T(8,128)(2,1)S(1)} %bitcast.22), custom_call_target="tpu_custom_call" | custom-call | flops 167772160 | bytes 1310720 | tf_op jit(solution)/shard_map/token_grads/pallas_call | solution.py:561
  (15 shorter events, 0.1 us)
Async XLA Ops:
  3.4 25.8 %all-to-all-start = ((bf16[32,8,1280]{2,1,0:T(8,128)(2,1)}), bf16[32,8,1280]{2,1,0:T(8,128)(2,1)S(1)}, u32[]{:S(2)}, u32[]{:S(2)}) async-start(bf16[32,8,1280]{2,1,0:T(8,128)(2,1)} %bitcast.5), calls=%async_computation | async-start | bytes 1310720 | tf_op jit(solution)/shard_map/all_to_all | solution.py:581
  29.2 23.8 %all-to-all-start.2 = ((bf16[32,8,1280]{2,1,0:T(8,128)(2,1)}), bf16[32,8,1280]{2,1,0:T(8,128)(2,1)S(1)}, u32[]{:S(2)}, u32[]{:S(2)}) async-start(bf16[32,8,1280]{2,1,0:T(8,128)(2,1)} %bitcast.12), calls=%async_computation.2 | async-start | bytes 1310720 | tf_op jit(solution)/shard_map/all_to_all | solution.py:581
  31.9 19.4 %copy-start = (bf16[1,768,2560]{2,1,0:T(8,128)(2,1)S(1)}, bf16[1,768,2560]{2,1,0:T(8,128)(2,1)}, u32[]{:S(2)}) copy-start(bf16[1,768,2560]{2,1,0:T(8,128)(2,1)} %down_ref.1) | copy-start | bytes 11796484
  36.1 15.1 %collective-permute-start = (bf16[128,1536]{1,0:T(8,128)(2,1)S(1)}, bf16[128,1536]{1,0:T(8,128)(2,1)S(1)}, u32[]{:S(2)}, u32[]{:S(2)}) collective-permute-start(bf16[128,1536]{1,0:T(8,128)(2,1)S(1)} %get-tuple-element.24.refs_0_), channel_id=1, source_target_pairs={{0,16},{16,0},{1,17},{17,1},{2,18},{18,2},{3,19},{19,3},{4,20},{20... | collective-permute-start | bytes 1179656 | tf_op jit(solution)/shard_map/ppermute | solution.py:593
  53.0 24.4 %all-to-all-start.1 = ((bf16[16,16,1280]{2,1,0:T(8,128)(2,1)}), bf16[16,16,1280]{2,1,0:T(8,128)(2,1)S(1)}, u32[]{:S(2)}, u32[]{:S(2)}) async-start(bf16[16,16,1280]{2,1,0:T(8,128)(2,1)} %bitcast.7), calls=%async_computation.1 | async-start | bytes 1310720 | tf_op jit(solution)/shard_map/all_to_all | solution.py:588
  63.0 7.3 %collective-permute-start.2 = (bf16[128,768]{1,0:T(8,128)(2,1)S(1)}, bf16[128,768]{1,0:T(8,128)(2,1)S(1)}, u32[]{:S(2)}, u32[]{:S(2)}) collective-permute-start(bf16[128,768]{1,0:T(8,128)(2,1)S(1)} %get-tuple-element.30.refs_0_.refs_2_), channel_id=1, source_target_pairs={{0,16},{16,0},{1,17},{17,1},{2,18},{18,2},{3,19},{19,3},{4,20},{20... | collective-permute-start | bytes 589832 | tf_op jit(solution)/shard_map/ppermute | solution.py:593
  70.3 11.5 %copy-start.4 = (bf16[2,128,1280]{2,1,0:T(8,128)(2,1)S(1)}, bf16[2,128,1280]{2,1,0:T(8,128)(2,1)}, u32[]{:S(2)}) copy-start(bf16[2,128,1280]{2,1,0:T(8,128)(2,1)} %get-tuple-element.35.rows_in_ref) | copy-start | bytes 1966084
  74.5 20.9 %copy-start.1 = (bf16[128,5120]{1,0:T(8,128)(2,1)S(1)}, bf16[128,5120]{1,0:T(8,128)(2,1)}, u32[]{:S(2)}) copy-start(bf16[128,5120]{1,0:T(8,128)(2,1)} %refs_2_.4) | copy-start | bytes 3932164
  74.5 20.9 %copy-start.2 = (s32[1,16,4]{1,2,0:T(4,128)S(1)}, s32[1,16,4]{1,2,0:T(4,128)}, u32[]{:S(2)}) copy-start(s32[1,16,4]{1,2,0:T(4,128)} %param.9) | copy-start | bytes 772
  74.5 20.8 %copy-start.3 = (f32[1,16,4]{1,2,0:T(4,128)S(1)}, f32[1,16,4]{1,2,0:T(4,128)}, u32[]{:S(2)}) copy-start(f32[1,16,4]{1,2,0:T(4,128)} %param.10) | copy-start | bytes 772
  77.3 21.1 %all-to-all-start.3 = ((bf16[32,8,1280]{2,1,0:T(8,128)(2,1)}), bf16[32,8,1280]{2,1,0:T(8,128)(2,1)S(1)}, u32[]{:S(2)}, u32[]{:S(2)}) async-start(bf16[32,8,1280]{2,1,0:T(8,128)(2,1)} %bitcast.14), calls=%async_computation.3 | async-start | bytes 1310720 | tf_op jit(solution)/shard_map/all_to_all | solution.py:581
  80.1 15.3 %collective-permute-start.1 = (bf16[128,1280]{1,0:T(8,128)(2,1)S(1)}, bf16[128,1280]{1,0:T(8,128)(2,1)S(1)}, u32[]{:S(2)}, u32[]{:S(2)}) collective-permute-start(bf16[128,1280]{1,0:T(8,128)(2,1)S(1)} %bitcast.29), channel_id=1, source_target_pairs={{0,16},{16,0},{1,17},{17,1},{2,18},{18,2},{3,19},{19,3},{4,20},{20... | collective-permute-start | bytes 983048 | tf_op jit(solution)/shard_map/ppermute | solution.py:620
  81.8 1.1 %copy-start.5 = (bf16[2,128,1280]{2,1,0:T(8,128)(2,1)S(1)}, bf16[2,128,1280]{2,1,0:T(8,128)(2,1)}, u32[]{:S(2)}) copy-start(bf16[2,128,1280]{2,1,0:T(8,128)(2,1)} %get-tuple-element.36.rows_up_ref) | copy-start | bytes 1966084
  82.9 1.0 copy-start.6

commit v9 on v8

--- a/solution.py
+++ b/solution.py
@@ -99,8 +99,8 @@
 def send_kernel(halves, blocks, scaled, *refs):
     count = 2 if scaled else 1
     lists, source_ref, out_ref = refs[:count], refs[count], refs[count + 1]
-    held_ref, sems, list_sems = refs[count + 2 : count + 5]
-    list_refs = refs[count + 5 :]
+    held_ref, made_ref, sems, list_sems, out_sems = refs[count + 2 : count + 7]
+    list_refs = refs[count + 7 :]
     rows, cols = out_ref.shape
     rows = rows // halves
     tokens = source_ref.shape[0]
@@ -129,6 +129,7 @@
     target = chosen + iota((rows, 1), 0) % (blocks * slots) // slots * tokens
     take = one_hot(target == iota((rows, blocks * tokens), 1))
     scale = spread_column(list_refs[1][...], blocks) if scaled else None
+    out_copies = []
     for half in range(halves):
         for block in range(blocks):
             copies[half * blocks + block].wait()
@@ -138,7 +139,101 @@
         picked = picked.astype(BF16)
         for place in range(rows // run):
             start = (place * halves + half) * run
-            out_ref[start : start + run] = picked[place * run : (place + 1) * run]
+            made_ref[start : start + run] = picked[place * run : (place + 1) * run]
+            out_copies.append(
+                pltpu.make_async_copy(
+                    made_ref.at[start : start + run], out_ref.at[start : start + run], out_sems.at[half, place]
+                )
+            )
+            out_copies[-1].start()
+    for copy in out_copies:
+        copy.wait()
+
+
+def pair_kernel(blocks, _, picks_ref, gates_ref, source_ref, own_ref, other_ref, held_ref, sems, list_sems, *list_refs):
+    slots = picks_ref.shape[0]
+    tokens = source_ref.shape[0]
+    rows, cols = own_ref.shape
+    half = lax.axis_index("dp")
+    list_copies = [
+        pltpu.make_async_copy(ref, target, list_sems.at[i])
+        for i, (ref, target) in enumerate(zip((picks_ref, gates_ref), list_refs))
+    ]
+    for copy in list_copies:
+        copy.start()
+    copies = []
+    for far in range(2):
+        for block in range(blocks):
+            start = (jnp.bitwise_xor(half, far) * blocks + block) * cols
+            copies.append(
+                pltpu.make_async_copy(
+                    source_ref.at[:, pl.ds(pl.multiple_of(start, 128), cols)],
+                    held_ref.at[far, block * tokens : (block + 1) * tokens],
+                    sems.at[far, block],
+                )
+            )
+            copies[-1].start()
+    for copy in list_copies:
+        copy.wait()
+    chosen = spread_column(list_refs[0][...].astype(F32), blocks).astype(jnp.int32)
+    target = chosen + iota((rows, 1), 0) % (blocks * slots) // slots * tokens
+    take = one_hot(target == iota((rows, blocks * tokens), 1))
+    scale = spread_column(list_refs[1][...], blocks)
+    for far, out_ref in enumerate((own_ref, other_ref)):
+        for block in range(blocks):
+            copies[far * blocks + block].wait()
+        out_ref[...] = (dot(take, held_ref[far]) * scale).astype(BF16)
+
+
+def pair_rows(source, picks, gates, blocks, after):
+    slots, experts = picks.shape
+    tokens, width = source.shape
+    cols = width // (2 * blocks)
+    rows = experts * blocks * slots
+    return pl.pallas_call(
+        functools.partial(pair_kernel, blocks),
+        in_specs=[hbm()] * 4,
+        out_specs=[vmem()] * 2,
+        out_shape=[shape_of(rows, cols)] * 2,
+        scratch_shapes=[
+            pltpu.VMEM((2, blocks * tokens, cols), BF16),
+            pltpu.SemaphoreType.DMA((2, blocks)),
+            pltpu.SemaphoreType.DMA((2,)),
+            pltpu.VMEM((slots, experts), picks.dtype),
+            pltpu.VMEM((slots, experts), gates.dtype),
+        ],
+        compiler_params=params(16),
+        cost_estimate=cost(4 * rows * cols * tokens * blocks, 2 * tokens * width),
+        name="pair_rows",
+    )(in_hbm(after), in_hbm(picks), in_hbm(gates), in_hbm(source))
+
+
+def join_kernel(own_ref, other_ref, out_ref, sems):
+    half = lax.axis_index("dp")
+    copies = [
+        pltpu.make_async_copy(own_ref, out_ref.at[:, half], sems.at[0]),
+        pltpu.make_async_copy(other_ref, out_ref.at[:, 1 - half], sems.at[1]),
+    ]
+    for copy in copies:
+        copy.start()
+    for copy in copies:
+        copy.wait()
+
+
+def join_rows(own, other, experts):
+    rows, cols = own.shape
+    shape = (experts, rows // experts, cols)
+    joined = pl.pallas_call(
+        join_kernel,
+        in_specs=[pl.BlockSpec(memory_space=pl.ANY)] * 2,
+        out_specs=hbm(),
+        out_shape=hbm_shape(experts, 2, *shape[1:]),
+        scratch_shapes=[pltpu.SemaphoreType.DMA((2,))],
+        compiler_params=params(16),
+        cost_estimate=cost(0, 8 * rows * cols),
+        name="join_rows",
+    )(own.reshape(shape), other.reshape(shape))
+    return joined.reshape(2 * rows, cols)
 
 
 def send_rows(source, lists, halves, blocks):
@@ -149,12 +244,14 @@
     return pl.pallas_call(
         functools.partial(send_kernel, halves, blocks, len(lists) == 2),
         in_specs=[hbm()] * (len(lists) + 1),
-        out_specs=vmem(),
-        out_shape=shape_of(rows, cols),
+        out_specs=hbm(),
+        out_shape=hbm_shape(rows, cols),
         scratch_shapes=[
             pltpu.VMEM((halves, blocks * tokens, cols), BF16),
+            pltpu.VMEM((rows, cols), BF16),
             pltpu.SemaphoreType.DMA((halves, blocks)),
             pltpu.SemaphoreType.DMA((2,)),
+            pltpu.SemaphoreType.DMA((halves, experts // planes_of(experts))),
         ]
         + [pltpu.VMEM((slots, experts), value.dtype) for value in lists],
         compiler_params=params(16),
@@ -174,14 +271,14 @@
     return one_hot(place(a % group // slots) * (blocks * slots) + a // group * slots + a % slots == b)
 
 
-def sort_rows(messages_ref, rows_ref, slots):
+def sort_rows(messages_ref, rows_ref, slots, place=same_place):
     blocks, total = rows_ref.shape[:2]
-    if blocks == 1:
+    if blocks == 1 and place is same_place:
         rows_ref[0] = messages_ref[...]
         return
     size = min(blocks * total, 256)
     group = size // blocks
-    order = sort_matrix(size, blocks, slots, False)
+    order = sort_matrix(size, blocks, slots, False, place)
     for part in range(total // group):
         ordered = dot(order, messages_ref[part * size : (part + 1) * size]).astype(BF16)
         for block in range(blocks):
@@ -276,12 +373,12 @@
     )(messages, in_hbm(w_gate), in_hbm(w_up))
 
 
-def back_sums_kernel(slots, messages_ref, down_ref, out_ref, kept_ref, rows_ref, held_ref, sems):
+def back_sums_kernel(slots, place, messages_ref, down_ref, out_ref, kept_ref, rows_ref, held_ref, sems):
     blocks, _, cols = rows_ref.shape
     stream = Stream(sems)
     spots = [slice(start, start + size) for start, size in thirds_of(down_ref.shape[1])]
     copies = [stream.start(down_ref.at[0, spot], held_ref.at[spot]) for spot in spots]
-    sort_rows(messages_ref, rows_ref, slots)
+    sort_rows(messages_ref, rows_ref, slots, place)
     kept = stream.start(rows_ref, kept_ref)
     for spot, copy in zip(spots, copies):
         copy.wait()
@@ -292,12 +389,12 @@
     kept.wait()
 
 
-def back_sums(messages, w_down, blocks, slots):
+def back_sums(messages, w_down, blocks, slots, place):
     hidden, part = w_down.shape[1:]
     rows = messages.shape[0] // blocks
     cols = part // blocks
     return pl.pallas_call(
-        functools.partial(back_sums_kernel, slots),
+        functools.partial(back_sums_kernel, slots, place),
         in_specs=[vmem(), hbm()],
         out_specs=[vmem(), hbm()],
         out_shape=[shape_of(rows, hidden), hbm_shape(blocks, rows, cols)],
@@ -439,7 +536,7 @@
         compiler_params=params(),
         cost_estimate=cost(6 * total * part * hidden, 6 * part * hidden),
         name="weight_grads",
-    )(rows_in, rows_up, act, grad_act)
+    )(*[in_hbm(value) for value in (rows_in, rows_up, act, grad_act)])
 
 
 def back_rows(back_ref, half, halves, run):
@@ -455,22 +552,15 @@
     return copy
 
 
-def mixed_kernel(crossed, picks_ref, gates_ref, cot_ref, *refs):
-    back_refs, (mixed_ref, gate_grad_ref, put_ref, held_ref, sems) = refs[:-5], refs[-5:]
+def mixed_kernel(picks_ref, gates_ref, cot_ref, back_ref, mixed_ref, gate_grad_ref, put_ref, held_ref, sems):
     slots, experts = picks_ref.shape
     halves, blocks, tokens, cols = held_ref.shape
     rows = experts * blocks * slots
     hit = spread_row(picks_ref[...].astype(F32), blocks).astype(jnp.int32) == iota((tokens, rows), 0)
     scale = spread_row(gates_ref[...], blocks)
     of_block = iota((tokens, rows), 1) % (blocks * slots) // slots
-    if crossed:
-        backs = [ref[...] for ref in back_refs]
-        own = lax.axis_index("dp")
-        places = [own, 1 - own]
-    else:
-        run = planes_of(experts) * blocks * slots
-        backs = [back_rows(back_refs[0], half, halves, run) for half in range(halves)]
-        places = list(range(halves))
+    run = planes_of(experts) * blocks * slots
+    backs = [back_rows(back_ref, half, halves, run) for half in range(halves)]
     copies = []
     products = None
     for block in range(blocks):
@@ -483,10 +573,10 @@
             rest = rest - pieces[-1].astype(F32)
         for half in range(halves):
             back = backs[half]
-            start = pl.multiple_of((places[half] * blocks + block) * cols, 128)
             held_ref[half, block] = added([dot(piece, back) for piece in pieces]).astype(BF16)
-            copies.append(put_columns(held_ref, mixed_ref, sems, half, block, start))
-            product = dot(cot_ref[:, pl.ds(start, cols)], back, ((1,), (1,)))
+            copies.append(put_columns(held_ref, mixed_ref, sems, half, block))
+            place = half * blocks + block
+            product = dot(cot_ref[:, place * cols : (place + 1) * cols], back, ((1,), (1,)))
             product = jnp.where(inside, product, 0.0)
             products = product if products is None else products + product
     values = jnp.sum(products, axis=0, keepdims=True)
@@ -497,21 +587,106 @@
         copy.wait()
 
 
-def mix_rows(backs, cotangent, picks, gates, halves, blocks):
+def mix_rows(back, cotangent, picks, gates, halves, blocks):
     slots, experts = picks.shape
     tokens, width = cotangent.shape
     cols = width // (halves * blocks)
     rows = experts * blocks * slots
     return pl.pallas_call(
-        functools.partial(mixed_kernel, len(backs) == 2),
-        in_specs=[vmem()] * (3 + len(backs)),
+        mixed_kernel,
+        in_specs=[vmem()] * 4,
         out_specs=[hbm(), vmem(), vmem()],
         out_shape=[shape_of(tokens, width), shape_of(slots, experts, dtype=F32), shape_of(blocks, tokens, rows)],
         scratch_shapes=[pltpu.VMEM((halves, blocks, tokens, cols), BF16), pltpu.SemaphoreType.DMA((halves, blocks))],
         compiler_params=params(16),
         cost_estimate=cost(8 * rows * tokens * width, 4 * tokens * width),
         name="mixed_rows",
-    )(picks, gates, cotangent, *backs)
+    )(picks, gates, cotangent, back)
+
+
+def mix_half(half, put_ref, pieces_ref, cot_ref, back_ref, target_ref, held_ref, sems):
+    blocks, tokens, cols = held_ref.shape
+    back = back_ref[...]
+    copies = []
+    products = None
+    for block in range(blocks):
+        start = pl.multiple_of((half * blocks + block) * cols, 128)
+        held_ref[block] = added([dot(pieces_ref[block, i], back) for i in range(3)]).astype(BF16)
+        copies.append(pltpu.make_async_copy(held_ref.at[block], target_ref.at[:, pl.ds(start, cols)], sems.at[block]))
+        copies[-1].start()
+        product = dot(cot_ref[:, pl.ds(start, cols)], back, ((1,), (1,))) * put_ref[block].astype(F32)
+        products = product if products is None else products + product
+    return jnp.sum(products, axis=0, keepdims=True), copies
+
+
+def near_kernel(picks_ref, gates_ref, cot_ref, back_ref, mixed_ref, put_ref, pieces_ref, sums_ref, held_ref, sems):
+    slots = picks_ref.shape[0]
+    blocks, tokens, rows = put_ref.shape
+    hit = spread_row(picks_ref[...].astype(F32), blocks).astype(jnp.int32) == iota((tokens, rows), 0)
+    scale = spread_row(gates_ref[...], blocks)
+    of_block = iota((tokens, rows), 1) % (blocks * slots) // slots
+    for block in range(blocks):
+        inside = hit & (of_block == block)
+        put_ref[block] = one_hot(inside)
+        rest = jnp.where(inside, scale, 0.0)
+        for i in range(3):
+            piece = rest.astype(BF16)
+            pieces_ref[block, i] = piece
+            rest = rest - piece.astype(F32)
+    half = lax.axis_index("dp")
+    sums_ref[...], copies = mix_half(half, put_ref, pieces_ref, cot_ref, back_ref, mixed_ref, held_ref, sems)
+    for copy in copies:
+        copy.wait()
+
+
+def far_kernel(
+    slots, put_ref, pieces_ref, sums_ref, cot_ref, back_ref, _, mixed_ref, gate_grad_ref, held_ref, sems
+):
+    blocks, _, rows = put_ref.shape
+    experts = gate_grad_ref.shape[1]
+    half = 1 - lax.axis_index("dp")
+    values, copies = mix_half(half, put_ref, pieces_ref, cot_ref, back_ref, mixed_ref, held_ref, sems)
+    values = values + sums_ref[...]
+    mine = iota((slots, rows), 1) % slots == iota((slots, rows), 0)
+    owner = (expert_at(iota((rows, experts), 0) // (blocks * slots), experts) == iota((rows, experts), 1)).astype(F32)
+    gate_grad_ref[...] = exact_dot(jnp.where(mine, values, 0.0), owner)
+    for copy in copies:
+        copy.wait()
+
+
+def mix_halves(own, other, cotangent, picks, gates, blocks):
+    slots, experts = picks.shape
+    tokens, width = cotangent.shape
+    rows, cols = own.shape
+    scratch = [pltpu.VMEM((blocks, tokens, cols), BF16), pltpu.SemaphoreType.DMA((blocks,))]
+    work = cost(4 * rows * tokens * width, 2 * tokens * width)
+    mixed, put, pieces, sums = pl.pallas_call(
+        near_kernel,
+        in_specs=[vmem()] * 4,
+        out_specs=[hbm()] + [vmem()] * 3,
+        out_shape=[
+            hbm_shape(tokens, width),
+            shape_of(blocks, tokens, rows),
+            shape_of(blocks, 3, tokens, rows),
+            shape_of(1, rows, dtype=F32),
+        ],
+        scratch_shapes=scratch,
+        compiler_params=params(16),
+        cost_estimate=work,
+        name="mixed_near",
+    )(picks, gates, cotangent, own)
+    mixed, gate_grad = pl.pallas_call(
+        functools.partial(far_kernel, slots),
+        in_specs=[vmem()] * 5 + [hbm()],
+        out_specs=[hbm(), vmem()],
+        out_shape=[hbm_shape(tokens, width), shape_of(slots, experts, dtype=F32)],
+        scratch_shapes=scratch,
+        input_output_aliases={5: 0},
+        compiler_params=params(16),
+        cost_estimate=work,
+        name="mixed_far",
+    )(put, pieces, sums, cotangent, other, in_hbm(mixed))
+    return mixed, gate_grad, put
 
 
 def part_kernel(joined_ref, own_ref, other_ref, sems):
@@ -601,24 +776,31 @@
     blocks = 2 if tokens.shape[1] // halves % 256 == 0 else 1
     picks_t = picks[0].T
     gates_t = gates[0].T
-    arrived_in = scatter(send_rows(tokens, (picks_t,), halves, blocks))
-    arrived_up = scatter(send_rows(cotangent, (picks_t, gates_t), halves, blocks))
+    messages_in = send_rows(tokens, (picks_t,), halves, blocks)
+    arrived_in = scatter(messages_in)
+    if halves == 2:
+        own, other = pair_rows(cotangent, picks_t, gates_t, blocks, messages_in)
+        other = lax.ppermute(other, "dp", [(0, 1), (1, 0)])
+        arrived_up = to_experts(experts, join_rows(own, other, experts))
+    else:
+        arrived_up = scatter(send_rows(cotangent, (picks_t, gates_t), halves, blocks))
     own_sums, rows_in = in_sums(arrived_in, w_gate, w_up, blocks, slots)
     shares = dp_shares(own_sums, halves)
     place = functools.partial(split_place, halves=2, planes=planes_of(experts)) if halves == 2 else same_place
     act, outputs = out_rows(shares, w_down, blocks, slots, place)
     back_out = to_experts(experts, outputs) if halves == 2 else scatter(outputs)
-    own_back, rows_up = back_sums(arrived_up, w_down, blocks, slots)
+    own_back, rows_up = back_sums(arrived_up, w_down, blocks, slots, place)
     backs = dp_shares(own_back, halves)
     near_gate, near_up = bring((w_gate, w_up), own_back)
     grad_act, gradients = grad_rows(shares, backs, near_gate, near_up, blocks, slots)
     back_grad = scatter(gradients)
     grad_gate_w, grad_up_w, grad_down = weight_grads(rows_in, rows_up, act, grad_act)
-    returned = [back_out]
     if halves == 2:
         own_out, other_out = part_rows(back_out, experts)
-        returned = [own_out, lax.ppermute(other_out, "dp", [(0, 1), (1, 0)])]
-    mixed, gate_grad, put = mix_rows(returned, cotangent, picks_t, gates_t, halves, blocks)
+        other_out = lax.ppermute(other_out, "dp", [(0, 1), (1, 0)])
+        mixed, gate_grad, put = mix_halves(own_out, other_out, cotangent, picks_t, gates_t, blocks)
+    else:
+        mixed, gate_grad, put = mix_rows(back_out, cotangent, picks_t, gates_t, halves, blocks)
     token_grad = token_grads(back_grad, put, halves, planes_of(experts) * blocks * slots)
     return mixed, token_grad, gate_grad.T[None], grad_gate_w, grad_up_w, grad_down
 

time: 100 us -> 101 us (1.010)
  starting transfers between devices: 22.4 us -> 25.2 us
  Pallas kernels: 33.6 us -> 35.7 us
  waiting for transfers between devices: 40.9 us -> 38.8 us
  local copies, waits for them, and re-layouts: 2.11 us -> 0.03 us
    ppermute x1 -> x2, waiting for transfers between devices: 5.76 us -> 12.1 us  [the longest x1 12.1 us: body(): other = lax.ppermute(other, 'dp', [(0, 1), (1, 0)])]
    all_to_all x3 -> x2, waiting for transfers between devices: 15.6 us -> 9.47 us  [to_owners(): lax.all_to_all(messages, EVERYONE, split_axis=0, concat_axis=0, tiled=Tru...]
    all_to_all x1 -> x2, starting transfers between devices: 5.85 us -> 9.67 us  [to_experts(): lax.all_to_all(messages, 'expert', split_axis=0, concat_axis=0, tiled=Tru...]
    pallas_call x2 -> x5, Pallas kernels: 7.16 us -> 10.7 us  [the longest x1 4.18 us: back_sums(): pl.pallas_call(functools.partial(back_sums_kernel, slots, place), in_spec...]
    ppermute x2, waiting for transfers between devices: 16.7 us -> 13.5 us  [dp_shares(): lax.ppermute(own, 'dp', [(i, (i + shift) % halves) for i in range(halves)])]
    pallas_call x2 -> x1, Pallas kernels: 5.7 us -> 2.73 us  [send_rows(): pl.pallas_call(functools.partial(send_kernel, halves, blocks, len(lists)...]
    all_to_all x3 -> x2, starting transfers between devices: 12.5 us -> 9.98 us  [to_owners(): lax.all_to_all(messages, EVERYONE, split_axis=0, concat_axis=0, tiled=Tru...]
    unnamed x14 -> x10, local copies, waits for them, and re-layouts: 2.11 us -> 0.03 us
  transfers between devices with their start and end apart: 7 -> 8, of which waited for: 5 -> 7; matrix products, arithmetic and copies ran while one was open for 0% -> 0% of each run, Pallas kernels for 30% -> 31%
where the time goes in v9:
time: 101 us
  waiting for transfers between devices  38.8 us (38%)
  Pallas kernels  35.7 us (35%)
  starting transfers between devices  25.2 us (25%)
    ppermute x2, waiting for transfers between devices, dp_shares(): lax.ppermute(own, 'dp', [(i, (i + shift) % halves) for i in range(halves)])  13.5 us
    ppermute x1, waiting for transfers between devices, body(): other = lax.ppermute(other, 'dp', [(0, 1), (1, 0)])  12.1 us
    all_to_all x2, starting transfers between devices, to_owners(): lax.all_to_all(messages, EVERYONE, split_axis=0, concat_axis=0, tiled=Tru...  9.98 us
    all_to_all x2, starting transfers between devices, to_experts(): lax.all_to_all(messages, 'expert', split_axis=0, concat_axis=0, tiled=Tru...  9.67 us
    all_to_all x2, waiting for transfers between devices, to_owners(): lax.all_to_all(messages, EVERYONE, split_axis=0, concat_axis=0, tiled=Tru...  9.47 us
    pallas_call x1, Pallas kernels, weight_grads(): pl.pallas_call(weights_kernel, grid=(blocks, steps), in_specs=[chunk, chu...  7.28 us
    pallas_call x1, Pallas kernels, in_sums(): pl.pallas_call(functools.partial(in_sums_kernel, slots), in_specs=[vmem()...  4.25 us
    pallas_call x1, Pallas kernels, grad_rows(): pl.pallas_call(functools.partial(grad_rows_kernel, slots, blocks, len(sha...  4.25 us
  transfers between devices with their start and end apart: 8, of which 7 were waited for; matrix products, arithmetic and copies ran while one was open for 0% of the time, Pallas kernels for 31%

profile of v9, /device:TPU:0, one launch (start us, length us, event | category | flops | bytes accessed | tf_op | source)
XLA Modules:
  0.0 100.6 jit_solution(9125636455345533880)
XLA Ops:
  0.6 2.7 %send_rows.1._ = bf16[256,1280]{1,0:T(8,128)(2,1)} custom-call(s32[4,16]{1,0:T(4,128)} %bitcast.28, bf16[128,5120]{1,0:T(8,128)(2,1)} %refs_1_.2), custom_call_target="tpu_custom_call" | custom-call | flops 167772160 | bytes 1966080 | tf_op jit(solution)/shard_map/send_rows/pallas_call | solution.py:244
  3.4 7.3 %all-to-all-start = ((bf16[32,8,1280]{2,1,0:T(8,128)(2,1)}), bf16[32,8,1280]{2,1,0:T(8,128)(2,1)S(1)}, u32[]{:S(2)}, u32[]{:S(2)}) async-start(bf16[32,8,1280]{2,1,0:T(8,128)(2,1)} %bitcast.34), calls=%async_computation | async-start | bytes 1310720 | tf_op jit(solution)/shard_map/all_to_all | solution.py:756
  10.7 1.7 %pair_rows.1 = (bf16[128,1280]{1,0:T(8,128)(2,1)S(1)}, bf16[128,1280]{1,0:T(8,128)(2,1)S(1)}) custom-call(bf16[256,1280]{1,0:T(8,128)(2,1)} %send_rows.1._, s32[4,16]{1,0:T(4,128)} %bitcast.29, f32[4,16]{1,0:T(4,128)} %bitcast.31, bf16[128,5120]{1,0:T(8,128)(2,1)} %source_ref.1), custom_call_target="tpu_custom_call" | custom-call | flops 167772160 | bytes 1310720 | tf_op jit(solution)/shard_map/pair_rows/pallas_call | solution.py:193
  12.4 1.8 %collective-permute-start.2 = (bf16[128,1280]{1,0:T(8,128)(2,1)S(1)}, bf16[128,1280]{1,0:T(8,128)(2,1)S(1)}, u32[]{:S(2)}, u32[]{:S(2)}) collective-permute-start(bf16[128,1280]{1,0:T(8,128)(2,1)S(1)} %get-tuple-element.39), channel_id=1, source_target_pairs={{0,16},{16,0},{1,17},{17,1},{2,18},{18,2},{3,19},{19,3},{4,20},{20... | collective-permute-start | bytes 983048 | tf_op jit(solution)/shard_map/ppermute | solution.py:783
  14.2 12.1 %collective-permute-done.2 = bf16[128,1280]{1,0:T(8,128)(2,1)S(1)} collective-permute-done((bf16[128,1280]{1,0:T(8,128)(2,1)S(1)}, bf16[128,1280]{1,0:T(8,128)(2,1)S(1)}, u32[]{:S(2)}, u32[]{:S(2)}) %collective-permute-start.2) | collective-permute-done | bytes 327712 | tf_op jit(solution)/shard_map/ppermute | solution.py:783
  27.2 2.0 %all-to-all-done = bf16[32,8,1280]{2,1,0:T(8,128)(2,1)S(1)} async-done(((bf16[32,8,1280]{2,1,0:T(8,128)(2,1)}), bf16[32,8,1280]{2,1,0:T(8,128)(2,1)S(1)}, u32[]{:S(2)}, u32[]{:S(2)}) %all-to-all-start) | async-done | bytes 655392 | tf_op jit(solution)/shard_map/all_to_all | solution.py:756
  29.2 4.9 %all-to-all-start.2 = ((bf16[16,16,1280]{2,1,0:T(8,128)(2,1)}), bf16[16,16,1280]{2,1,0:T(8,128)(2,1)S(1)}, u32[]{:S(2)}, u32[]{:S(2)}) async-start(bf16[16,16,1280]{2,1,0:T(8,128)(2,1)} %bitcast.35), calls=%async_computation.2 | async-start | bytes 1310720 | tf_op jit(solution)/shard_map/all_to_all | solution.py:763
  34.1 4.2 %gate_up_sums.1 = (bf16[128,1536]{1,0:T(8,128)(2,1)S(1)}, bf16[2,128,1280]{2,1,0:T(8,128)(2,1)}) custom-call(bf16[256,1280]{1,0:T(8,128)(2,1)S(1)} %bitcast.21, bf16[1,2560,768]{2,1,0:T(8,128)(2,1)} %refs_1_.3, bf16[1,2560,768]{2,1,0:T(8,128)(2,1)} %refs_2_.3), custom_call_target="tpu_custom_call" | custom-call | flops 1006632960 | bytes 7864320 | tf_op jit(solution)/shard_map/gate_up_sums/pallas_call | solution.py:359
  38.3 1.0 collective-permute-start
  39.3 10.5 %collective-permute-done.refs_1_ = bf16[128,1536]{1,0:T(8,128)(2,1)S(1)} collective-permute-done((bf16[128,1536]{1,0:T(8,128)(2,1)S(1)}, bf16[128,1536]{1,0:T(8,128)(2,1)S(1)}, u32[]{:S(2)}, u32[]{:S(2)}) %collective-permute-start) | collective-permute-done | bytes 393248 | tf_op jit(solution)/shard_map/ppermute | solution.py:768
  49.8 1.8 %output_rows.1 = (bf16[128,768]{1,0:T(8,128)(2,1)S(1)}, bf16[256,1280]{1,0:T(8,128)(2,1)}) custom-call(bf16[128,1536]{1,0:T(8,128)(2,1)S(1)} %get-tuple-element.29.refs_0_, bf16[128,1536]{1,0:T(8,128)(2,1)S(1)} %collective-permute-done.refs_1_, bf16[1,768,2560]{2,1,0:T(8,128)(2,1)S(1)} %copy-done), custom_call_target="tpu_custom_call" | custom-call | flops 503316480 | bytes 3932160 | tf_op jit(solution)/shard_map/output_rows/pallas_call | solution.py:457
  52.5 4.8 %all-to-all-start.1 = ((bf16[16,16,1280]{2,1,0:T(8,128)(2,1)}), bf16[16,16,1280]{2,1,0:T(8,128)(2,1)S(1)}, u32[]{:S(2)}, u32[]{:S(2)}) async-start(bf16[16,16,1280]{2,1,0:T(8,128)(2,1)} %bitcast.7), calls=%async_computation.1 | async-start | bytes 1310720 | tf_op jit(solution)/shard_map/all_to_all | solution.py:763
  57.4 4.2 %back_sums.1 = (bf16[128,768]{1,0:T(8,128)(2,1)S(1)}, bf16[2,128,1280]{2,1,0:T(8,128)(2,1)}) custom-call(bf16[256,1280]{1,0:T(8,128)(2,1)S(1)} %bitcast.22, bf16[1,768,2560]{2,1,0:T(8,128)(2,1)} %down_ref.1), custom_call_target="tpu_custom_call" | custom-call | flops 503316480 | bytes 3932160 | tf_op jit(solution)/shard_map/back_sums/pallas_call | solution.py:396
  62.5 3.3 %bring_weights.1 = (bf16[1,2560,768]{2,1,0:T(8,128)(2,1)S(1)}, bf16[1,2560,768]{2,1,0:T(8,128)(2,1)S(1)}) custom-call(bf16[128,768]{1,0:T(8,128)(2,1)S(1)} %get-tuple-element.40.refs_0_.refs_2_, bf16[1,2560,768]{2,1,0:T(8,128)(2,1)} %refs_1_.3, bf16[1,2560,768]{2,1,0:T(8,128)(2,1)} %refs_2_.3), custom_call_target="tpu_custom_call" | custom-call | bytes 7864320 | tf_op jit(solution)/shard_map/bring_weights/pallas_call | solution.py:422
  65.8 3.0 %collective-permute-done.3.refs_3_ = bf16[128,768]{1,0:T(8,128)(2,1)S(1)} collective-permute-done((bf16[128,768]{1,0:T(8,128)(2,1)S(1)}, bf16[128,768]{1,0:T(8,128)(2,1)S(1)}, u32[]{:S(2)}, u32[]{:S(2)}) %collective-permute-start.3) | collective-permute-done | bytes 196640 | tf_op jit(solution)/shard_map/ppermute | solution.py:768
  68.8 4.2 %gradient_rows.1 = (bf16[128,1536]{1,0:T(8,128)(2,1)}, bf16[256,1280]{1,0:T(8,128)(2,1)}) custom-call(bf16[128,1536]{1,0:T(8,128)(2,1)S(1)} %get-tuple-element.29.refs_0_, bf16[128,1536]{1,0:T(8,128)(2,1)S(1)} %collective-permute-done.refs_1_, bf16[128,768]{1,0:T(8,128)(2,1)S(1)} %get-tuple-element.40.refs_0_.refs_2_, ...), custom_call_target="tpu_custom_call" | custom-call | flops 1006632960 | bytes 7864320 | tf_op jit(solution)/shard_map/gradient_rows/pallas_call | solution.py:497
  73.1 2.7 %all-to-all-done.1 = bf16[16,16,1280]{2,1,0:T(8,128)(2,1)S(1)} async-done(((bf16[16,16,1280]{2,1,0:T(8,128)(2,1)}), bf16[16,16,1280]{2,1,0:T(8,128)(2,1)S(1)}, u32[]{:S(2)}, u32[]{:S(2)}) %all-to-all-start.1) | async-done | bytes 655392 | tf_op jit(solution)/shard_map/all_to_all | solution.py:763
  75.8 2.7 %all-to-all-start.3 = ((bf16[32,8,1280]{2,1,0:T(8,128)(2,1)}), bf16[32,8,1280]{2,1,0:T(8,128)(2,1)S(1)}, u32[]{:S(2)}, u32[]{:S(2)}) async-start(bf16[32,8,1280]{2,1,0:T(8,128)(2,1)} %bitcast.16), calls=%async_computation.3 | async-start | bytes 1310720 | tf_op jit(solution)/shard_map/all_to_all | solution.py:756
  78.6 1.8 %collective-permute-start.1 = (bf16[128,1280]{1,0:T(8,128)(2,1)S(1)}, bf16[128,1280]{1,0:T(8,128)(2,1)S(1)}, u32[]{:S(2)}, u32[]{:S(2)}) collective-permute-start(bf16[128,1280]{1,0:T(8,128)(2,1)S(1)} %bitcast.33), channel_id=1, source_target_pairs={{0,16},{16,0},{1,17},{17,1},{2,18},{18,2},{3,19},{19,3},{4,20},{20... | collective-permute-start | bytes 983048 | tf_op jit(solution)/shard_map/ppermute | solution.py:800
  80.5 7.3 %weight_grads.1 = (bf16[1,2560,768]{2,1,0:T(8,128)(2,1)}, bf16[1,2560,768]{2,1,0:T(8,128)(2,1)}, bf16[1,768,2560]{2,1,0:T(8,128)(2,1)}) custom-call(bf16[2,128,1280]{2,1,0:T(8,128)(2,1)} %get-tuple-element.45.rows_in_ref, bf16[2,128,1280]{2,1,0:T(8,128)(2,1)} %get-tuple-element.46.rows_up_ref, bf16[128,768]{1,0:T(8,128)(2,1)} %copy-done.4, ...), custom_call_target="tpu_custom_call" | custom-call | flops 1509949440 | bytes 11796480 | tf_op jit(solution)/shard_map/weight_grads/pallas_call | solution.py:525
  87.8 1.8 %mixed_near.1 = (bf16[128,5120]{1,0:T(8,128)(2,1)}, bf16[2,128,128]{2,1,0:T(8,128)(2,1)S(1)}, bf16[2,3,128,128]{3,2,1,0:T(8,128)(2,1)S(1)}, f32[1,128]{1,0:T(1,128)S(1)}) custom-call(s32[4,16]{1,0:T(4,128)S(1)} %bitcast.30, f32[4,16]{1,0:T(4,128)S(1)} %bitcast.32, bf16[128,5120]{1,0:T(8,128)(2,1)S(1)} %copy-done.1, bf16[128,1280]{1,0:T(8,128)(2,1)S(1)} %bitcast.27), custom_call_target="tpu_custom_call" | custom-call | flops 335544320 | bytes 1310720 | tf_op jit(solution)/shard_map/mixed_near/pallas_call | solution.py:663
  89.5 7.5 %all-to-all-done.3 = bf16[32,8,1280]{2,1,0:T(8,128)(2,1)S(1)} async-done(((bf16[32,8,1280]{2,1,0:T(8,128)(2,1)}), bf16[32,8,1280]{2,1,0:T(8,128)(2,1)S(1)}, u32[]{:S(2)}, u32[]{:S(2)}) %all-to-all-start.3) | async-done | bytes 655392 | tf_op jit(solution)/shard_map/all_to_all | solution.py:756
  97.0 1.3 %token_grads.1 = bf16[128,5120]{1,0:T(8,128)(2,1)} custom-call(bf16[2,128,128]{2,1,0:T(8,128)(2,1)S(1)} %get-tuple-element.32.put_ref, bf16[256,1280]{1,0:T(8,128)(2,1)S(1)} %bitcast.24), custom_call_target="tpu_custom_call" | custom-call | flops 167772160 | bytes 1310720 | tf_op jit(solution)/shard_map/token_grads/pallas_call | solution.py:736
  98.4 2.2 %mixed_far.1 = (bf16[128,5120]{1,0:T(8,128)(2,1)}, f32[4,16]{1,0:T(4,128)}) custom-call(bf16[2,128,128]{2,1,0:T(8,128)(2,1)S(1)} %get-tuple-element.32.put_ref, bf16[2,3,128,128]{3,2,1,0:T(8,128)(2,1)S(1)} %get-tuple-element.33.pieces_ref, f32[1,128]{1,0:T(1,128)S(1)} %get-tuple-element.34.sums_ref, ...), custom_call_target="tpu_custom_call", output_to_operand_aliasing={{0}: (5, {})} | custom-call | flops 335544320 | bytes 1310720 | tf_op jit(solution)/shard_map/mixed_far/pallas_call | solution.py:678
  (15 shorter events, 2.9 us)
Async XLA Ops:
  3.4 25.8 %all-to-all-start = ((bf16[32,8,1280]{2,1,0:T(8,128)(2,1)}), bf16[32,8,1280]{2,1,0:T(8,128)(2,1)S(1)}, u32[]{:S(2)}, u32[]{:S(2)}) async-start(bf16[32,8,1280]{2,1,0:T(8,128)(2,1)} %bitcast.34), calls=%async_computation | async-start | bytes 1310720 | tf_op jit(solution)/shard_map/all_to_all | solution.py:756
  12.4 13.9 %collective-permute-start.2 = (bf16[128,1280]{1,0:T(8,128)(2,1)S(1)}, bf16[128,1280]{1,0:T(8,128)(2,1)S(1)}, u32[]{:S(2)}, u32[]{:S(2)}) collective-permute-start(bf16[128,1280]{1,0:T(8,128)(2,1)S(1)} %get-tuple-element.39), channel_id=1, source_target_pairs={{0,16},{16,0},{1,17},{17,1},{2,18},{18,2},{3,19},{19,3},{4,20},{20... | collective-permute-start | bytes 983048 | tf_op jit(solution)/shard_map/ppermute | solution.py:783
  29.2 23.4 %all-to-all-start.2 = ((bf16[16,16,1280]{2,1,0:T(8,128)(2,1)}), bf16[16,16,1280]{2,1,0:T(8,128)(2,1)S(1)}, u32[]{:S(2)}, u32[]{:S(2)}) async-start(bf16[16,16,1280]{2,1,0:T(8,128)(2,1)} %bitcast.35), calls=%async_computation.2 | async-start | bytes 1310720 | tf_op jit(solution)/shard_map/all_to_all | solution.py:763
  34.0 15.8 %copy-start = (bf16[1,768,2560]{2,1,0:T(8,128)(2,1)S(1)}, bf16[1,768,2560]{2,1,0:T(8,128)(2,1)}, u32[]{:S(2)}) copy-start(bf16[1,768,2560]{2,1,0:T(8,128)(2,1)} %down_ref.1) | copy-start | bytes 11796484
  38.3 11.5 %collective-permute-start = (bf16[128,1536]{1,0:T(8,128)(2,1)S(1)}, bf16[128,1536]{1,0:T(8,128)(2,1)S(1)}, u32[]{:S(2)}, u32[]{:S(2)}) collective-permute-start(bf16[128,1536]{1,0:T(8,128)(2,1)S(1)} %get-tuple-element.29.refs_0_), channel_id=1, source_target_pairs={{0,16},{16,0},{1,17},{17,1},{2,18},{18,2},{3,19},{19,3},{4,20},{20... | collective-permute-start | bytes 1179656 | tf_op jit(solution)/shard_map/ppermute | solution.py:768
  51.6 5.8 %copy-start.4 = (bf16[128,768]{1,0:T(8,128)(2,1)}, bf16[128,768]{1,0:T(8,128)(2,1)S(1)}, u32[]{:S(2)}) copy-start(bf16[128,768]{1,0:T(8,128)(2,1)S(1)} %get-tuple-element.47.act_ref) | copy-start | bytes 589828
  52.5 23.3 %all-to-all-start.1 = ((bf16[16,16,1280]{2,1,0:T(8,128)(2,1)}), bf16[16,16,1280]{2,1,0:T(8,128)(2,1)S(1)}, u32[]{:S(2)}, u32[]{:S(2)}) async-start(bf16[16,16,1280]{2,1,0:T(8,128)(2,1)} %bitcast.7), calls=%async_computation.1 | async-start | bytes 1310720 | tf_op jit(solution)/shard_map/all_to_all | solution.py:763
  61.5 7.3 %collective-permute-start.3 = (bf16[128,768]{1,0:T(8,128)(2,1)S(1)}, bf16[128,768]{1,0:T(8,128)(2,1)S(1)}, u32[]{:S(2)}, u32[]{:S(2)}) collective-permute-start(bf16[128,768]{1,0:T(8,128)(2,1)S(1)} %get-tuple-element.40.refs_0_.refs_2_), channel_id=1, source_target_pairs={{0,16},{16,0},{1,17},{17,1},{2,18},{18,2},{3,19},{19,3},{4,20},{20... | collective-permute-start | bytes 589832 | tf_op jit(solution)/shard_map/ppermute | solution.py:768
  73.1 14.6 %copy-start.1 = (bf16[128,5120]{1,0:T(8,128)(2,1)S(1)}, bf16[128,5120]{1,0:T(8,128)(2,1)}, u32[]{:S(2)}) copy-start(bf16[128,5120]{1,0:T(8,128)(2,1)} %source_ref.1) | copy-start | bytes 3932164
  73.1 14.6 %copy-start.2 = (s32[1,16,4]{1,2,0:T(4,128)S(1)}, s32[1,16,4]{1,2,0:T(4,128)}, u32[]{:S(2)}) copy-start(s32[1,16,4]{1,2,0:T(4,128)} %param.9) | copy-start | bytes 772
  73.1 14.6 %copy-start.3 = (f32[1,16,4]{1,2,0:T(4,128)S(1)}, f32[1,16,4]{1,2,0:T(4,128)}, u32[]{:S(2)}) copy-start(f32[1,16,4]{1,2,0:T(4,128)} %param.10) | copy-start | bytes 772
  75.8 21.2 %all-to-all-start.3 = ((bf16[32,8,1280]{2,1,0:T(8,128)(2,1)}), bf16[32,8,1280]{2,1,0:T(8,128)(2,1)S(1)}, u32[]{:S(2)}, u32[]{:S(2)}) async-start(bf16[32,8,1280]{2,1,0:T(8,128)(2,1)} %bitcast.16), calls=%async_computation.3 | async-start | bytes 1310720 | tf_op jit(solution)/shard_map/all_to_all | solution.py:756
  78.6 19.7 %collective-permute-start.1 = (bf16[128,1280]{1,0:T(8,128)(2,1)S(1)}, bf16[128,1280]{1,0:T(8,128)(2,1)S(1)}, u32[]{:S(2)}, u32[]{:S(2)}) collective-permute-start(bf16[128,1280]{1,0:T(8,128)(2,1)S(1)} %bitcast.33), channel_id=1, source_target_pairs={{0,16},{16,0},{1,17},{17,1},{2,18},{18,2},{3,19},{19,3},{4,20},{20... | collective-permute-start | bytes 983048 | tf_op jit(solution)/shard_map/ppermute | solution.py:800

commit v10 on v9

--- a/solution.py
+++ b/solution.py
@@ -314,11 +314,6 @@
     return [(0, first), (first, width - first)]
 
 
-def thirds_of(height):
-    size = height // 3 if height % 384 == 0 else height
-    return [(start, size) for start in range(0, height, size)]
-
-
 class Stream:
     def __init__(self, sems):
         self.sems, self.copies = sems, []
@@ -373,19 +368,22 @@
     )(messages, in_hbm(w_gate), in_hbm(w_up))
 
 
-def back_sums_kernel(slots, place, messages_ref, down_ref, out_ref, kept_ref, rows_ref, held_ref, sems):
+def back_sums_kernel(slots, place, messages_ref, down_ref, out_ref, kept_ref, rows_ref, held_ref, acc_ref, sems):
     blocks, _, cols = rows_ref.shape
     stream = Stream(sems)
-    spots = [slice(start, start + size) for start, size in thirds_of(down_ref.shape[1])]
-    copies = [stream.start(down_ref.at[0, spot], held_ref.at[spot]) for spot in spots]
+    cuts = [(block, start, size) for block in range(blocks) for start, size in pieces_of(cols)]
+    copies = []
+    for block, start, size in cuts:
+        span = slice(block * cols + start, block * cols + start + size)
+        copies.append(stream.start(down_ref.at[0, :, span], held_ref.at[:, span]))
     sort_rows(messages_ref, rows_ref, slots, place)
     kept = stream.start(rows_ref, kept_ref)
-    for spot, copy in zip(spots, copies):
-        copy.wait()
-        terms = [
-            dot(rows_ref[b], held_ref[spot, span], ((1,), (1,))) for b, span in enumerate(spans(blocks * cols, blocks))
-        ]
-        out_ref[:, spot] = added(terms).astype(BF16)
+    for number, (block, start, size) in enumerate(cuts):
+        span = slice(block * cols + start, block * cols + start + size)
+        copies[number].wait()
+        term = dot(rows_ref[block, :, start : start + size], held_ref[:, span], ((1,), (1,)))
+        acc_ref[...] = term if number == 0 else acc_ref[...] + term
+    out_ref[...] = acc_ref[...].astype(BF16)
     kept.wait()
 
 
@@ -401,7 +399,8 @@
         scratch_shapes=[
             pltpu.VMEM((blocks, rows, cols), BF16),
             pltpu.VMEM((hidden, part), BF16),
-            pltpu.SemaphoreType.DMA((len(thirds_of(hidden)) + 1,)),
+            pltpu.VMEM((rows, hidden), F32),
+            pltpu.SemaphoreType.DMA((blocks * len(pieces_of(cols)) + 1,)),
         ],
         compiler_params=params(),
         cost_estimate=cost(2 * rows * part * hidden, 2 * part * hidden),
@@ -717,7 +716,7 @@
     return [value.reshape(rows // 2, cols) for value in parted]
 
 
-def token_grad_kernel(run, put_ref, back_ref, grad_ref, held_ref, sems):
+def token_grad_kernel(run, _, put_ref, back_ref, grad_ref, held_ref, sems):
     halves, blocks = held_ref.shape[:2]
     copies = []
     for half in range(halves):
@@ -729,20 +728,20 @@
         copy.wait()
 
 
-def token_grads(back, put, halves, run):
+def token_grads(back, put, halves, run, after):
     blocks, tokens, rows = put.shape
     cols = back.shape[1]
     width = halves * blocks * cols
     return pl.pallas_call(
         functools.partial(token_grad_kernel, run),
-        in_specs=[vmem()] * 2,
+        in_specs=[pl.BlockSpec(memory_space=pl.ANY)] + [vmem()] * 2,
         out_specs=hbm(),
         out_shape=shape_of(tokens, width),
         scratch_shapes=[pltpu.VMEM((halves, blocks, tokens, cols), BF16), pltpu.SemaphoreType.DMA((halves, blocks))],
         compiler_params=params(16),
         cost_estimate=cost(2 * rows * tokens * width, 2 * tokens * width),
         name="token_grads",
-    )(put, back)
+    )(after, put, back)
 
 
 def to_owners(halves, experts, messages):
@@ -801,7 +800,7 @@
         mixed, gate_grad, put = mix_halves(own_out, other_out, cotangent, picks_t, gates_t, blocks)
     else:
         mixed, gate_grad, put = mix_rows(back_out, cotangent, picks_t, gates_t, halves, blocks)
-    token_grad = token_grads(back_grad, put, halves, planes_of(experts) * blocks * slots)
+    token_grad = token_grads(back_grad, put, halves, planes_of(experts) * blocks * slots, gate_grad)
     return mixed, token_grad, gate_grad.T[None], grad_gate_w, grad_up_w, grad_down
 
 

time: 101 us -> 99.7 us (0.987)
  waiting for transfers between devices: 38.8 us -> 37.3 us
    all_to_all x2, waiting for transfers between devices: 9.47 us -> 2.6 us  [to_owners(): lax.all_to_all(messages, EVERYONE, split_axis=0, concat_axis=0, tiled=Tru...]
    ppermute x1, waiting for transfers between devices: 0.01 us -> 4.68 us  [body(): other_out = lax.ppermute(other_out, 'dp', [(0, 1), (1, 0)])]
  transfers between devices with their start and end apart: 8 -> 8, of which waited for: 7 -> 8; matrix products, arithmetic and copies ran while one was open for 0% -> 0% of each run, Pallas kernels for 31% -> 31%
where the time goes in v10:
time: 99.7 us; the launch traced here: 99 us
  waiting for transfers between devices  37.3 us (37%)
  Pallas kernels  35 us (35%)
  starting transfers between devices  25.2 us (25%)
    ppermute x2, waiting for transfers between devices, dp_shares(): lax.ppermute(own, 'dp', [(i, (i + shift) % halves) for i in range(halves)])  13.6 us
    ppermute x1, waiting for transfers between devices, body(): other = lax.ppermute(other, 'dp', [(0, 1), (1, 0)])  12.1 us
    all_to_all x2, starting transfers between devices, to_owners(): lax.all_to_all(messages, EVERYONE, split_axis=0, concat_axis=0, tiled=Tru...  9.98 us
    all_to_all x2, starting transfers between devices, to_experts(): lax.all_to_all(messages, 'expert', split_axis=0, concat_axis=0, tiled=Tru...  9.67 us
    pallas_call x1, Pallas kernels, weight_grads(): pl.pallas_call(weights_kernel, grid=(blocks, steps), in_specs=[chunk, chu...  7.28 us
    ppermute x1, waiting for transfers between devices, body(): other_out = lax.ppermute(other_out, 'dp', [(0, 1), (1, 0)])  4.68 us
    all_to_all x2, waiting for transfers between devices, to_experts(): lax.all_to_all(messages, 'expert', split_axis=0, concat_axis=0, tiled=Tru...  4.36 us
    pallas_call x1, Pallas kernels, in_sums(): pl.pallas_call(functools.partial(in_sums_kernel, slots), in_specs=[vmem()...  4.25 us
  transfers between devices with their start and end apart: 8, of which 8 were waited for; matrix products, arithmetic and copies ran while one was open for 0% of the time, Pallas kernels for 31%

profile of v10, /device:TPU:0, one launch (start us, length us, event | category | flops | bytes accessed | tf_op | source)
XLA Modules:
  0.0 99.0 jit_solution(9529778535383009589)
XLA Ops:
  0.6 2.7 %send_rows.1._ = bf16[256,1280]{1,0:T(8,128)(2,1)} custom-call(s32[4,16]{1,0:T(4,128)} %bitcast.28, bf16[128,5120]{1,0:T(8,128)(2,1)} %refs_1_.2), custom_call_target="tpu_custom_call" | custom-call | flops 167772160 | bytes 1966080 | tf_op jit(solution)/shard_map/send_rows/pallas_call | solution.py:244
  3.4 7.3 %all-to-all-start = ((bf16[32,8,1280]{2,1,0:T(8,128)(2,1)}), bf16[32,8,1280]{2,1,0:T(8,128)(2,1)S(1)}, u32[]{:S(2)}, u32[]{:S(2)}) async-start(bf16[32,8,1280]{2,1,0:T(8,128)(2,1)} %bitcast.35), calls=%async_computation | async-start | bytes 1310720 | tf_op jit(solution)/shard_map/all_to_all | solution.py:755
  10.7 1.7 %pair_rows.1 = (bf16[128,1280]{1,0:T(8,128)(2,1)S(1)}, bf16[128,1280]{1,0:T(8,128)(2,1)S(1)}) custom-call(bf16[256,1280]{1,0:T(8,128)(2,1)} %send_rows.1._, s32[4,16]{1,0:T(4,128)} %bitcast.29, f32[4,16]{1,0:T(4,128)} %bitcast.31, bf16[128,5120]{1,0:T(8,128)(2,1)} %source_ref.1), custom_call_target="tpu_custom_call" | custom-call | flops 167772160 | bytes 1310720 | tf_op jit(solution)/shard_map/pair_rows/pallas_call | solution.py:193
  12.4 1.8 %collective-permute-start.2 = (bf16[128,1280]{1,0:T(8,128)(2,1)S(1)}, bf16[128,1280]{1,0:T(8,128)(2,1)S(1)}, u32[]{:S(2)}, u32[]{:S(2)}) collective-permute-start(bf16[128,1280]{1,0:T(8,128)(2,1)S(1)} %get-tuple-element.40), channel_id=1, source_target_pairs={{0,16},{16,0},{1,17},{17,1},{2,18},{18,2},{3,19},{19,3},{4,20},{20... | collective-permute-start | bytes 983048 | tf_op jit(solution)/shard_map/ppermute | solution.py:782
  14.2 12.1 %collective-permute-done.2 = bf16[128,1280]{1,0:T(8,128)(2,1)S(1)} collective-permute-done((bf16[128,1280]{1,0:T(8,128)(2,1)S(1)}, bf16[128,1280]{1,0:T(8,128)(2,1)S(1)}, u32[]{:S(2)}, u32[]{:S(2)}) %collective-permute-start.2) | collective-permute-done | bytes 327712 | tf_op jit(solution)/shard_map/ppermute | solution.py:782
  27.2 2.0 %all-to-all-done = bf16[32,8,1280]{2,1,0:T(8,128)(2,1)S(1)} async-done(((bf16[32,8,1280]{2,1,0:T(8,128)(2,1)}), bf16[32,8,1280]{2,1,0:T(8,128)(2,1)S(1)}, u32[]{:S(2)}, u32[]{:S(2)}) %all-to-all-start) | async-done | bytes 655392 | tf_op jit(solution)/shard_map/all_to_all | solution.py:755
  29.2 4.9 %all-to-all-start.2 = ((bf16[16,16,1280]{2,1,0:T(8,128)(2,1)}), bf16[16,16,1280]{2,1,0:T(8,128)(2,1)S(1)}, u32[]{:S(2)}, u32[]{:S(2)}) async-start(bf16[16,16,1280]{2,1,0:T(8,128)(2,1)} %bitcast.36), calls=%async_computation.2 | async-start | bytes 1310720 | tf_op jit(solution)/shard_map/all_to_all | solution.py:762
  34.1 4.2 %gate_up_sums.1 = (bf16[128,1536]{1,0:T(8,128)(2,1)S(1)}, bf16[2,128,1280]{2,1,0:T(8,128)(2,1)}) custom-call(bf16[256,1280]{1,0:T(8,128)(2,1)S(1)} %bitcast.21, bf16[1,2560,768]{2,1,0:T(8,128)(2,1)} %refs_1_.3, bf16[1,2560,768]{2,1,0:T(8,128)(2,1)} %refs_2_.3), custom_call_target="tpu_custom_call" | custom-call | flops 1006632960 | bytes 7864320 | tf_op jit(solution)/shard_map/gate_up_sums/pallas_call | solution.py:354
  38.3 1.0 collective-permute-start
  39.3 10.5 %collective-permute-done.refs_1_ = bf16[128,1536]{1,0:T(8,128)(2,1)S(1)} collective-permute-done((bf16[128,1536]{1,0:T(8,128)(2,1)S(1)}, bf16[128,1536]{1,0:T(8,128)(2,1)S(1)}, u32[]{:S(2)}, u32[]{:S(2)}) %collective-permute-start) | collective-permute-done | bytes 393248 | tf_op jit(solution)/shard_map/ppermute | solution.py:767
  49.8 1.8 %output_rows.1 = (bf16[128,768]{1,0:T(8,128)(2,1)S(1)}, bf16[256,1280]{1,0:T(8,128)(2,1)}) custom-call(bf16[128,1536]{1,0:T(8,128)(2,1)S(1)} %get-tuple-element.29.refs_0_, bf16[128,1536]{1,0:T(8,128)(2,1)S(1)} %collective-permute-done.refs_1_, bf16[1,768,2560]{2,1,0:T(8,128)(2,1)S(1)} %copy-done), custom_call_target="tpu_custom_call" | custom-call | flops 503316480 | bytes 3932160 | tf_op jit(solution)/shard_map/output_rows/pallas_call | solution.py:456
  52.5 4.8 %all-to-all-start.1 = ((bf16[16,16,1280]{2,1,0:T(8,128)(2,1)}), bf16[16,16,1280]{2,1,0:T(8,128)(2,1)S(1)}, u32[]{:S(2)}, u32[]{:S(2)}) async-start(bf16[16,16,1280]{2,1,0:T(8,128)(2,1)} %bitcast.7), calls=%async_computation.1 | async-start | bytes 1310720 | tf_op jit(solution)/shard_map/all_to_all | solution.py:762
  57.4 3.5 %back_sums.1 = (bf16[128,768]{1,0:T(8,128)(2,1)S(1)}, bf16[2,128,1280]{2,1,0:T(8,128)(2,1)}) custom-call(bf16[256,1280]{1,0:T(8,128)(2,1)S(1)} %bitcast.23, bf16[1,768,2560]{2,1,0:T(8,128)(2,1)} %down_ref.1), custom_call_target="tpu_custom_call" | custom-call | flops 503316480 | bytes 3932160 | tf_op jit(solution)/shard_map/back_sums/pallas_call | solution.py:394
  61.8 3.3 %bring_weights.1 = (bf16[1,2560,768]{2,1,0:T(8,128)(2,1)S(1)}, bf16[1,2560,768]{2,1,0:T(8,128)(2,1)S(1)}) custom-call(bf16[128,768]{1,0:T(8,128)(2,1)S(1)} %get-tuple-element.41.refs_0_.refs_2_, bf16[1,2560,768]{2,1,0:T(8,128)(2,1)} %refs_1_.3, bf16[1,2560,768]{2,1,0:T(8,128)(2,1)} %refs_2_.3), custom_call_target="tpu_custom_call" | custom-call | bytes 7864320 | tf_op jit(solution)/shard_map/bring_weights/pallas_call | solution.py:421
  65.1 3.0 %collective-permute-done.3.refs_3_ = bf16[128,768]{1,0:T(8,128)(2,1)S(1)} collective-permute-done((bf16[128,768]{1,0:T(8,128)(2,1)S(1)}, bf16[128,768]{1,0:T(8,128)(2,1)S(1)}, u32[]{:S(2)}, u32[]{:S(2)}) %collective-permute-start.3) | collective-permute-done | bytes 196640 | tf_op jit(solution)/shard_map/ppermute | solution.py:767
  68.1 4.2 %gradient_rows.1 = (bf16[128,1536]{1,0:T(8,128)(2,1)}, bf16[256,1280]{1,0:T(8,128)(2,1)}) custom-call(bf16[128,1536]{1,0:T(8,128)(2,1)S(1)} %get-tuple-element.29.refs_0_, bf16[128,1536]{1,0:T(8,128)(2,1)S(1)} %collective-permute-done.refs_1_, bf16[128,768]{1,0:T(8,128)(2,1)S(1)} %get-tuple-element.41.refs_0_.refs_2_, ...), custom_call_target="tpu_custom_call" | custom-call | flops 1006632960 | bytes 7864320 | tf_op jit(solution)/shard_map/gradient_rows/pallas_call | solution.py:496
  72.4 3.4 %all-to-all-done.1 = bf16[16,16,1280]{2,1,0:T(8,128)(2,1)S(1)} async-done(((bf16[16,16,1280]{2,1,0:T(8,128)(2,1)}), bf16[16,16,1280]{2,1,0:T(8,128)(2,1)S(1)}, u32[]{:S(2)}, u32[]{:S(2)}) %all-to-all-start.1) | async-done | bytes 655392 | tf_op jit(solution)/shard_map/all_to_all | solution.py:762
  75.8 2.7 %all-to-all-start.3 = ((bf16[32,8,1280]{2,1,0:T(8,128)(2,1)}), bf16[32,8,1280]{2,1,0:T(8,128)(2,1)S(1)}, u32[]{:S(2)}, u32[]{:S(2)}) async-start(bf16[32,8,1280]{2,1,0:T(8,128)(2,1)} %bitcast.16), calls=%async_computation.3 | async-start | bytes 1310720 | tf_op jit(solution)/shard_map/all_to_all | solution.py:755
  78.6 1.8 %collective-permute-start.1 = (bf16[128,1280]{1,0:T(8,128)(2,1)S(1)}, bf16[128,1280]{1,0:T(8,128)(2,1)S(1)}, u32[]{:S(2)}, u32[]{:S(2)}) collective-permute-start(bf16[128,1280]{1,0:T(8,128)(2,1)S(1)} %bitcast.34), channel_id=1, source_target_pairs={{0,16},{16,0},{1,17},{17,1},{2,18},{18,2},{3,19},{19,3},{4,20},{20... | collective-permute-start | bytes 983048 | tf_op jit(solution)/shard_map/ppermute | solution.py:799
  80.5 7.3 %weight_grads.1 = (bf16[1,2560,768]{2,1,0:T(8,128)(2,1)}, bf16[1,2560,768]{2,1,0:T(8,128)(2,1)}, bf16[1,768,2560]{2,1,0:T(8,128)(2,1)}) custom-call(bf16[2,128,1280]{2,1,0:T(8,128)(2,1)} %get-tuple-element.45.rows_in_ref, bf16[2,128,1280]{2,1,0:T(8,128)(2,1)} %get-tuple-element.46.rows_up_ref, bf16[128,768]{1,0:T(8,128)(2,1)} %copy-done.5, ...), custom_call_target="tpu_custom_call" | custom-call | flops 1509949440 | bytes 11796480 | tf_op jit(solution)/shard_map/weight_grads/pallas_call | solution.py:524
  87.8 1.8 %mixed_near.1 = (bf16[128,5120]{1,0:T(8,128)(2,1)}, bf16[2,128,128]{2,1,0:T(8,128)(2,1)S(1)}, bf16[2,3,128,128]{3,2,1,0:T(8,128)(2,1)S(1)}, f32[1,128]{1,0:T(1,128)S(1)}) custom-call(s32[4,16]{1,0:T(4,128)S(1)} %bitcast.30, f32[4,16]{1,0:T(4,128)S(1)} %bitcast.32, bf16[128,5120]{1,0:T(8,128)(2,1)S(1)} %copy-done.1, bf16[128,1280]{1,0:T(8,128)(2,1)S(1)} %bitcast.27), custom_call_target="tpu_custom_call" | custom-call | flops 335544320 | bytes 1310720 | tf_op jit(solution)/shard_map/mixed_near/pallas_call | solution.py:662
  89.5 4.7 %collective-permute-done.1.back_ref = bf16[128,1280]{1,0:T(8,128)(2,1)S(1)} collective-permute-done((bf16[128,1280]{1,0:T(8,128)(2,1)S(1)}, bf16[128,1280]{1,0:T(8,128)(2,1)S(1)}, u32[]{:S(2)}, u32[]{:S(2)}) %collective-permute-start.1) | collective-permute-done | bytes 327712 | tf_op jit(solution)/shard_map/ppermute | solution.py:799
  94.2 2.2 %mixed_far.1 = (bf16[128,5120]{1,0:T(8,128)(2,1)}, f32[4,16]{1,0:T(4,128)}) custom-call(bf16[2,128,128]{2,1,0:T(8,128)(2,1)S(1)} %get-tuple-element.32.put_ref, bf16[2,3,128,128]{3,2,1,0:T(8,128)(2,1)S(1)} %get-tuple-element.33.pieces_ref, f32[1,128]{1,0:T(1,128)S(1)} %get-tuple-element.34.sums_ref, ...), custom_call_target="tpu_custom_call", output_to_operand_aliasing={{0}: (5, {})} | custom-call | flops 335544320 | bytes 1310720 | tf_op jit(solution)/shard_map/mixed_far/pallas_call | solution.py:677
  97.7 1.3 %token_grads.1 = bf16[128,5120]{1,0:T(8,128)(2,1)} custom-call(f32[4,16]{1,0:T(4,128)S(1)} %copy-done.4, bf16[2,128,128]{2,1,0:T(8,128)(2,1)S(1)} %get-tuple-element.32.put_ref, bf16[256,1280]{1,0:T(8,128)(2,1)S(1)} %bitcast.22), custom_call_target="tpu_custom_call" | custom-call | flops 167772160 | bytes 1310720 | tf_op jit(solution)/shard_map/token_grads/pallas_call | solution.py:735
  (17 shorter events, 4.2 us)
Async XLA Ops:
  3.4 25.8 %all-to-all-start = ((bf16[32,8,1280]{2,1,0:T(8,128)(2,1)}), bf16[32,8,1280]{2,1,0:T(8,128)(2,1)S(1)}, u32[]{:S(2)}, u32[]{:S(2)}) async-start(bf16[32,8,1280]{2,1,0:T(8,128)(2,1)} %bitcast.35), calls=%async_computation | async-start | bytes 1310720 | tf_op jit(solution)/shard_map/all_to_all | solution.py:755
  12.4 13.9 %collective-permute-start.2 = (bf16[128,1280]{1,0:T(8,128)(2,1)S(1)}, bf16[128,1280]{1,0:T(8,128)(2,1)S(1)}, u32[]{:S(2)}, u32[]{:S(2)}) collective-permute-start(bf16[128,1280]{1,0:T(8,128)(2,1)S(1)} %get-tuple-element.40), channel_id=1, source_target_pairs={{0,16},{16,0},{1,17},{17,1},{2,18},{18,2},{3,19},{19,3},{4,20},{20... | collective-permute-start | bytes 983048 | tf_op jit(solution)/shard_map/ppermute | solution.py:782
  29.2 23.4 %all-to-all-start.2 = ((bf16[16,16,1280]{2,1,0:T(8,128)(2,1)}), bf16[16,16,1280]{2,1,0:T(8,128)(2,1)S(1)}, u32[]{:S(2)}, u32[]{:S(2)}) async-start(bf16[16,16,1280]{2,1,0:T(8,128)(2,1)} %bitcast.36), calls=%async_computation.2 | async-start | bytes 1310720 | tf_op jit(solution)/shard_map/all_to_all | solution.py:762
  34.0 15.8 %copy-start = (bf16[1,768,2560]{2,1,0:T(8,128)(2,1)S(1)}, bf16[1,768,2560]{2,1,0:T(8,128)(2,1)}, u32[]{:S(2)}) copy-start(bf16[1,768,2560]{2,1,0:T(8,128)(2,1)} %down_ref.1) | copy-start | bytes 11796484
  38.3 11.5 %collective-permute-start = (bf16[128,1536]{1,0:T(8,128)(2,1)S(1)}, bf16[128,1536]{1,0:T(8,128)(2,1)S(1)}, u32[]{:S(2)}, u32[]{:S(2)}) collective-permute-start(bf16[128,1536]{1,0:T(8,128)(2,1)S(1)} %get-tuple-element.29.refs_0_), channel_id=1, source_target_pairs={{0,16},{16,0},{1,17},{17,1},{2,18},{18,2},{3,19},{19,3},{4,20},{20... | collective-permute-start | bytes 1179656 | tf_op jit(solution)/shard_map/ppermute | solution.py:767
  51.6 5.8 %copy-start.5 = (bf16[128,768]{1,0:T(8,128)(2,1)}, bf16[128,768]{1,0:T(8,128)(2,1)S(1)}, u32[]{:S(2)}) copy-start(bf16[128,768]{1,0:T(8,128)(2,1)S(1)} %get-tuple-element.47.act_ref) | copy-start | bytes 589828
  52.5 23.3 %all-to-all-start.1 = ((bf16[16,16,1280]{2,1,0:T(8,128)(2,1)}), bf16[16,16,1280]{2,1,0:T(8,128)(2,1)S(1)}, u32[]{:S(2)}, u32[]{:S(2)}) async-start(bf16[16,16,1280]{2,1,0:T(8,128)(2,1)} %bitcast.7), calls=%async_computation.1 | async-start | bytes 1310720 | tf_op jit(solution)/shard_map/all_to_all | solution.py:762
  60.8 7.3 %collective-permute-start.3 = (bf16[128,768]{1,0:T(8,128)(2,1)S(1)}, bf16[128,768]{1,0:T(8,128)(2,1)S(1)}, u32[]{:S(2)}, u32[]{:S(2)}) collective-permute-start(bf16[128,768]{1,0:T(8,128)(2,1)S(1)} %get-tuple-element.41.refs_0_.refs_2_), channel_id=1, source_target_pairs={{0,16},{16,0},{1,17},{17,1},{2,18},{18,2},{3,19},{19,3},{4,20},{20... | collective-permute-start | bytes 589832 | tf_op jit(solution)/shard_map/ppermute | solution.py:767
  72.4 15.4 %copy-start.1 = (bf16[128,5120]{1,0:T(8,128)(2,1)S(1)}, bf16[128,5120]{1,0:T(8,128)(2,1)}, u32[]{:S(2)}) copy-start(bf16[128,5120]{1,0:T(8,128)(2,1)} %source_ref.1) | copy-start | bytes 3932164
  72.4 15.3 %copy-start.2 = (s32[1,16,4]{1,2,0:T(4,128)S(1)}, s32[1,16,4]{1,2,0:T(4,128)}, u32[]{:S(2)}) copy-start(s32[1,16,4]{1,2,0:T(4,128)} %param.9) | copy-start | bytes 772
  72.4 15.3 %copy-start.3 = (f32[1,16,4]{1,2,0:T(4,128)S(1)}, f32[1,16,4]{1,2,0:T(4,128)}, u32[]{:S(2)}) copy-start(f32[1,16,4]{1,2,0:T(4,128)} %param.10) | copy-start | bytes 772
  75.8 21.2 %all-to-all-start.3 = ((bf16[32,8,1280]{2,1,0:T(8,128)(2,1)}), bf16[32,8,1280]{2,1,0:T(8,128)(2,1)S(1)}, u32[]{:S(2)}, u32[]{:S(2)}) async-start(bf16[32,8,1280]{2,1,0:T(8,128)(2,1)} %bitcast.16), calls=%async_computation.3 | async-start | bytes 1310720 | tf_op jit(solution)/shard_map/all_to_all | solution.py:755
  78.6 15.6 %collective-permute-start.1 = (bf16[128,1280]{1,0:T(8,128)(2,1)S(1)}, bf16[128,1280]{1,0:T(8,128)(2,1)S(1)}, u32[]{:S(2)}, u32[]{:S(2)}) collective-permute-start(bf16[128,1280]{1,0:T(8,128)(2,1)S(1)} %bitcast.34), channel_id=1, source_target_pairs={{0,16},{16,0},{1,17},{17,1},{2,18},{18,2},{3,19},{19,3},{4,20},{20... | collective-permute-start | bytes 983048 | tf_op jit(solution)/shard_map/ppermute | solution.py:799
  97.0 0.7 copy-start.4

commit v11 on v10

--- a/solution.py
+++ b/solution.py
@@ -78,11 +78,14 @@
     return best
 
 
-def spread_column(values, blocks):
+def spread_column(values, blocks, plain=False):
     slots, experts = values.shape
     rows = experts * blocks * slots
     owner = (expert_at(iota((rows, experts), 0) // (blocks * slots), experts) == iota((rows, experts), 1)).astype(F32)
-    wide = exact_dot(owner, values, ((1,), (1,)))
+    if plain:
+        wide = dot(owner.astype(BF16), values.astype(BF16), ((1,), (1,)))
+    else:
+        wide = exact_dot(owner, values, ((1,), (1,)))
     mine = iota((rows, slots), 0) % slots == iota((rows, slots), 1)
     return jnp.sum(jnp.where(mine, wide, 0.0), axis=1, keepdims=True)
 
@@ -125,7 +128,7 @@
         copy.wait()
     slots, experts = list_refs[0].shape
     run = planes_of(experts) * blocks * slots
-    chosen = spread_column(list_refs[0][...].astype(F32), blocks).astype(jnp.int32)
+    chosen = spread_column(list_refs[0][...].astype(F32), blocks, tokens <= 256).astype(jnp.int32)
     target = chosen + iota((rows, 1), 0) % (blocks * slots) // slots * tokens
     take = one_hot(target == iota((rows, blocks * tokens), 1))
     scale = spread_column(list_refs[1][...], blocks) if scaled else None
@@ -175,7 +178,7 @@
             copies[-1].start()
     for copy in list_copies:
         copy.wait()
-    chosen = spread_column(list_refs[0][...].astype(F32), blocks).astype(jnp.int32)
+    chosen = spread_column(list_refs[0][...].astype(F32), blocks, tokens <= 256).astype(jnp.int32)
     target = chosen + iota((rows, 1), 0) % (blocks * slots) // slots * tokens
     take = one_hot(target == iota((rows, blocks * tokens), 1))
     scale = spread_column(list_refs[1][...], blocks)
@@ -734,14 +737,14 @@
     width = halves * blocks * cols
     return pl.pallas_call(
         functools.partial(token_grad_kernel, run),
-        in_specs=[pl.BlockSpec(memory_space=pl.ANY)] + [vmem()] * 2,
+        in_specs=[hbm()] + [vmem()] * 2,
         out_specs=hbm(),
         out_shape=shape_of(tokens, width),
         scratch_shapes=[pltpu.VMEM((halves, blocks, tokens, cols), BF16), pltpu.SemaphoreType.DMA((halves, blocks))],
         compiler_params=params(16),
         cost_estimate=cost(2 * rows * tokens * width, 2 * tokens * width),
         name="token_grads",
-    )(after, put, back)
+    )(in_hbm(after), put, back)
 
 
 def to_owners(halves, experts, messages):

time: 99.7 us -> 98.9 us (level)
  no operation moved by 1% of the time
where the time goes in v11:
time: 98.9 us; the launch traced here: 98.3 us
  waiting for transfers between devices  37.2 us (38%)
  Pallas kernels  34.9 us (35%)
  starting transfers between devices  25.3 us (26%)
    ppermute x2, waiting for transfers between devices, dp_shares(): lax.ppermute(own, 'dp', [(i, (i + shift) % halves) for i in range(halves)])  13.5 us
    ppermute x1, waiting for transfers between devices, body(): other = lax.ppermute(other, 'dp', [(0, 1), (1, 0)])  12.1 us
    all_to_all x2, starting transfers between devices, to_owners(): lax.all_to_all(messages, EVERYONE, split_axis=0, concat_axis=0, tiled=Tru...  10 us
    all_to_all x2, starting transfers between devices, to_experts(): lax.all_to_all(messages, 'expert', split_axis=0, concat_axis=0, tiled=Tru...  9.66 us
    pallas_call x1, Pallas kernels, weight_grads(): pl.pallas_call(weights_kernel, grid=(blocks, steps), in_specs=[chunk, chu...  7.28 us
    ppermute x1, waiting for transfers between devices, body(): other_out = lax.ppermute(other_out, 'dp', [(0, 1), (1, 0)])  4.68 us
    all_to_all x2, waiting for transfers between devices, to_experts(): lax.all_to_all(messages, 'expert', split_axis=0, concat_axis=0, tiled=Tru...  4.36 us
    pallas_call x1, Pallas kernels, in_sums(): pl.pallas_call(functools.partial(in_sums_kernel, slots), in_specs=[vmem()...  4.25 us
  transfers between devices with their start and end apart: 8, of which 8 were waited for; matrix products, arithmetic and copies ran while one was open for 0% of the time, Pallas kernels for 31%

profile of v11, /device:TPU:0, one launch (start us, length us, event | category | flops | bytes accessed | tf_op | source)
XLA Modules:
  0.0 98.3 jit_solution(7649056825011217237)
XLA Ops:
  0.6 2.6 %send_rows.1._ = bf16[256,1280]{1,0:T(8,128)(2,1)} custom-call(s32[4,16]{1,0:T(4,128)} %bitcast.28, bf16[128,5120]{1,0:T(8,128)(2,1)} %refs_1_.2), custom_call_target="tpu_custom_call" | custom-call | flops 167772160 | bytes 1966080 | tf_op jit(solution)/shard_map/send_rows/pallas_call | solution.py:247
  3.3 7.3 %all-to-all-start = ((bf16[32,8,1280]{2,1,0:T(8,128)(2,1)}), bf16[32,8,1280]{2,1,0:T(8,128)(2,1)S(1)}, u32[]{:S(2)}, u32[]{:S(2)}) async-start(bf16[32,8,1280]{2,1,0:T(8,128)(2,1)} %bitcast.34), calls=%async_computation | async-start | bytes 1310720 | tf_op jit(solution)/shard_map/all_to_all | solution.py:758
  10.6 1.7 %pair_rows.1 = (bf16[128,1280]{1,0:T(8,128)(2,1)S(1)}, bf16[128,1280]{1,0:T(8,128)(2,1)S(1)}) custom-call(bf16[256,1280]{1,0:T(8,128)(2,1)} %send_rows.1._, s32[4,16]{1,0:T(4,128)} %bitcast.29, f32[4,16]{1,0:T(4,128)} %bitcast.31, bf16[128,5120]{1,0:T(8,128)(2,1)} %source_ref.1), custom_call_target="tpu_custom_call" | custom-call | flops 167772160 | bytes 1310720 | tf_op jit(solution)/shard_map/pair_rows/pallas_call | solution.py:196
  12.3 1.8 %collective-permute-start.2 = (bf16[128,1280]{1,0:T(8,128)(2,1)S(1)}, bf16[128,1280]{1,0:T(8,128)(2,1)S(1)}, u32[]{:S(2)}, u32[]{:S(2)}) collective-permute-start(bf16[128,1280]{1,0:T(8,128)(2,1)S(1)} %get-tuple-element.40), channel_id=1, source_target_pairs={{0,16},{16,0},{1,17},{17,1},{2,18},{18,2},{3,19},{19,3},{4,20},{20... | collective-permute-start | bytes 983048 | tf_op jit(solution)/shard_map/ppermute | solution.py:785
  14.1 12.1 %collective-permute-done.2 = bf16[128,1280]{1,0:T(8,128)(2,1)S(1)} collective-permute-done((bf16[128,1280]{1,0:T(8,128)(2,1)S(1)}, bf16[128,1280]{1,0:T(8,128)(2,1)S(1)}, u32[]{:S(2)}, u32[]{:S(2)}) %collective-permute-start.2) | collective-permute-done | bytes 327712 | tf_op jit(solution)/shard_map/ppermute | solution.py:785
  27.1 2.0 %all-to-all-done = bf16[32,8,1280]{2,1,0:T(8,128)(2,1)S(1)} async-done(((bf16[32,8,1280]{2,1,0:T(8,128)(2,1)}), bf16[32,8,1280]{2,1,0:T(8,128)(2,1)S(1)}, u32[]{:S(2)}, u32[]{:S(2)}) %all-to-all-start) | async-done | bytes 655392 | tf_op jit(solution)/shard_map/all_to_all | solution.py:758
  29.1 4.9 %all-to-all-start.2 = ((bf16[16,16,1280]{2,1,0:T(8,128)(2,1)}), bf16[16,16,1280]{2,1,0:T(8,128)(2,1)S(1)}, u32[]{:S(2)}, u32[]{:S(2)}) async-start(bf16[16,16,1280]{2,1,0:T(8,128)(2,1)} %bitcast.35), calls=%async_computation.2 | async-start | bytes 1310720 | tf_op jit(solution)/shard_map/all_to_all | solution.py:765
  34.0 4.2 %gate_up_sums.1 = (bf16[128,1536]{1,0:T(8,128)(2,1)S(1)}, bf16[2,128,1280]{2,1,0:T(8,128)(2,1)}) custom-call(bf16[256,1280]{1,0:T(8,128)(2,1)S(1)} %bitcast.21, bf16[1,2560,768]{2,1,0:T(8,128)(2,1)} %refs_1_.3, bf16[1,2560,768]{2,1,0:T(8,128)(2,1)} %refs_2_.3), custom_call_target="tpu_custom_call" | custom-call | flops 1006632960 | bytes 7864320 | tf_op jit(solution)/shard_map/gate_up_sums/pallas_call | solution.py:357
  38.2 1.0 %collective-permute-start = (bf16[128,1536]{1,0:T(8,128)(2,1)S(1)}, bf16[128,1536]{1,0:T(8,128)(2,1)S(1)}, u32[]{:S(2)}, u32[]{:S(2)}) collective-permute-start(bf16[128,1536]{1,0:T(8,128)(2,1)S(1)} %get-tuple-element.29.refs_0_), channel_id=1, source_target_pairs={{0,16},{16,0},{1,17},{17,1},{2,18},{18,2},{3,19},{19,3},{4,20},{20... | collective-permute-start | bytes 1179656 | tf_op jit(solution)/shard_map/ppermute | solution.py:770
  39.2 10.5 %collective-permute-done.refs_1_ = bf16[128,1536]{1,0:T(8,128)(2,1)S(1)} collective-permute-done((bf16[128,1536]{1,0:T(8,128)(2,1)S(1)}, bf16[128,1536]{1,0:T(8,128)(2,1)S(1)}, u32[]{:S(2)}, u32[]{:S(2)}) %collective-permute-start) | collective-permute-done | bytes 393248 | tf_op jit(solution)/shard_map/ppermute | solution.py:770
  49.7 1.8 %output_rows.1 = (bf16[128,768]{1,0:T(8,128)(2,1)S(1)}, bf16[256,1280]{1,0:T(8,128)(2,1)}) custom-call(bf16[128,1536]{1,0:T(8,128)(2,1)S(1)} %get-tuple-element.29.refs_0_, bf16[128,1536]{1,0:T(8,128)(2,1)S(1)} %collective-permute-done.refs_1_, bf16[1,768,2560]{2,1,0:T(8,128)(2,1)S(1)} %copy-done), custom_call_target="tpu_custom_call" | custom-call | flops 503316480 | bytes 3932160 | tf_op jit(solution)/shard_map/output_rows/pallas_call | solution.py:459
  52.4 4.8 %all-to-all-start.1 = ((bf16[16,16,1280]{2,1,0:T(8,128)(2,1)}), bf16[16,16,1280]{2,1,0:T(8,128)(2,1)S(1)}, u32[]{:S(2)}, u32[]{:S(2)}) async-start(bf16[16,16,1280]{2,1,0:T(8,128)(2,1)} %bitcast.7), calls=%async_computation.1 | async-start | bytes 1310720 | tf_op jit(solution)/shard_map/all_to_all | solution.py:765
  57.3 3.5 %back_sums.1 = (bf16[128,768]{1,0:T(8,128)(2,1)S(1)}, bf16[2,128,1280]{2,1,0:T(8,128)(2,1)}) custom-call(bf16[256,1280]{1,0:T(8,128)(2,1)S(1)} %bitcast.23, bf16[1,768,2560]{2,1,0:T(8,128)(2,1)} %down_ref.1), custom_call_target="tpu_custom_call" | custom-call | flops 503316480 | bytes 3932160 | tf_op jit(solution)/shard_map/back_sums/pallas_call | solution.py:397
  61.7 3.3 %bring_weights.1 = (bf16[1,2560,768]{2,1,0:T(8,128)(2,1)S(1)}, bf16[1,2560,768]{2,1,0:T(8,128)(2,1)S(1)}) custom-call(bf16[128,768]{1,0:T(8,128)(2,1)S(1)} %get-tuple-element.41.refs_0_.refs_2_, bf16[1,2560,768]{2,1,0:T(8,128)(2,1)} %refs_1_.3, bf16[1,2560,768]{2,1,0:T(8,128)(2,1)} %refs_2_.3), custom_call_target="tpu_custom_call" | custom-call | bytes 7864320 | tf_op jit(solution)/shard_map/bring_weights/pallas_call | solution.py:424
  65.0 3.0 %collective-permute-done.3.refs_3_ = bf16[128,768]{1,0:T(8,128)(2,1)S(1)} collective-permute-done((bf16[128,768]{1,0:T(8,128)(2,1)S(1)}, bf16[128,768]{1,0:T(8,128)(2,1)S(1)}, u32[]{:S(2)}, u32[]{:S(2)}) %collective-permute-start.3) | collective-permute-done | bytes 196640 | tf_op jit(solution)/shard_map/ppermute | solution.py:770
  68.0 4.2 %gradient_rows.1 = (bf16[128,1536]{1,0:T(8,128)(2,1)}, bf16[256,1280]{1,0:T(8,128)(2,1)}) custom-call(bf16[128,1536]{1,0:T(8,128)(2,1)S(1)} %get-tuple-element.29.refs_0_, bf16[128,1536]{1,0:T(8,128)(2,1)S(1)} %collective-permute-done.refs_1_, bf16[128,768]{1,0:T(8,128)(2,1)S(1)} %get-tuple-element.41.refs_0_.refs_2_, ...), custom_call_target="tpu_custom_call" | custom-call | flops 1006632960 | bytes 7864320 | tf_op jit(solution)/shard_map/gradient_rows/pallas_call | solution.py:499
  72.3 3.4 %all-to-all-done.1 = bf16[16,16,1280]{2,1,0:T(8,128)(2,1)S(1)} async-done(((bf16[16,16,1280]{2,1,0:T(8,128)(2,1)}), bf16[16,16,1280]{2,1,0:T(8,128)(2,1)S(1)}, u32[]{:S(2)}, u32[]{:S(2)}) %all-to-all-start.1) | async-done | bytes 655392 | tf_op jit(solution)/shard_map/all_to_all | solution.py:765
  75.7 2.7 %all-to-all-start.3 = ((bf16[32,8,1280]{2,1,0:T(8,128)(2,1)}), bf16[32,8,1280]{2,1,0:T(8,128)(2,1)S(1)}, u32[]{:S(2)}, u32[]{:S(2)}) async-start(bf16[32,8,1280]{2,1,0:T(8,128)(2,1)} %bitcast.16), calls=%async_computation.3 | async-start | bytes 1310720 | tf_op jit(solution)/shard_map/all_to_all | solution.py:758
  78.5 1.8 %collective-permute-start.1 = (bf16[128,1280]{1,0:T(8,128)(2,1)S(1)}, bf16[128,1280]{1,0:T(8,128)(2,1)S(1)}, u32[]{:S(2)}, u32[]{:S(2)}) collective-permute-start(bf16[128,1280]{1,0:T(8,128)(2,1)S(1)} %bitcast.33), channel_id=1, source_target_pairs={{0,16},{16,0},{1,17},{17,1},{2,18},{18,2},{3,19},{19,3},{4,20},{20... | collective-permute-start | bytes 983048 | tf_op jit(solution)/shard_map/ppermute | solution.py:802
  80.4 7.3 %weight_grads.1 = (bf16[1,2560,768]{2,1,0:T(8,128)(2,1)}, bf16[1,2560,768]{2,1,0:T(8,128)(2,1)}, bf16[1,768,2560]{2,1,0:T(8,128)(2,1)}) custom-call(bf16[2,128,1280]{2,1,0:T(8,128)(2,1)} %get-tuple-element.45.rows_in_ref, bf16[2,128,1280]{2,1,0:T(8,128)(2,1)} %get-tuple-element.46.rows_up_ref, bf16[128,768]{1,0:T(8,128)(2,1)} %copy-done.4, ...), custom_call_target="tpu_custom_call" | custom-call | flops 1509949440 | bytes 11796480 | tf_op jit(solution)/shard_map/weight_grads/pallas_call | solution.py:527
  87.7 1.8 %mixed_near.1 = (bf16[128,5120]{1,0:T(8,128)(2,1)}, bf16[2,128,128]{2,1,0:T(8,128)(2,1)S(1)}, bf16[2,3,128,128]{3,2,1,0:T(8,128)(2,1)S(1)}, f32[1,128]{1,0:T(1,128)S(1)}) custom-call(s32[4,16]{1,0:T(4,128)S(1)} %bitcast.30, f32[4,16]{1,0:T(4,128)S(1)} %bitcast.32, bf16[128,5120]{1,0:T(8,128)(2,1)S(1)} %copy-done.1, bf16[128,1280]{1,0:T(8,128)(2,1)S(1)} %bitcast.27), custom_call_target="tpu_custom_call" | custom-call | flops 335544320 | bytes 1310720 | tf_op jit(solution)/shard_map/mixed_near/pallas_call | solution.py:665
  89.4 4.7 %collective-permute-done.1.back_ref = bf16[128,1280]{1,0:T(8,128)(2,1)S(1)} collective-permute-done((bf16[128,1280]{1,0:T(8,128)(2,1)S(1)}, bf16[128,1280]{1,0:T(8,128)(2,1)S(1)}, u32[]{:S(2)}, u32[]{:S(2)}) %collective-permute-start.1) | collective-permute-done | bytes 327712 | tf_op jit(solution)/shard_map/ppermute | solution.py:802
  94.1 2.2 %mixed_far.1 = (bf16[128,5120]{1,0:T(8,128)(2,1)}, f32[4,16]{1,0:T(4,128)}) custom-call(bf16[2,128,128]{2,1,0:T(8,128)(2,1)S(1)} %get-tuple-element.32.put_ref, bf16[2,3,128,128]{3,2,1,0:T(8,128)(2,1)S(1)} %get-tuple-element.33.pieces_ref, f32[1,128]{1,0:T(1,128)S(1)} %get-tuple-element.34.sums_ref, ...), custom_call_target="tpu_custom_call", output_to_operand_aliasing={{0}: (5, {})} | custom-call | flops 335544320 | bytes 1310720 | tf_op jit(solution)/shard_map/mixed_far/pallas_call | solution.py:680
  96.9 1.3 %token_grads.1 = bf16[128,5120]{1,0:T(8,128)(2,1)} custom-call(f32[4,16]{1,0:T(4,128)} %get-tuple-element.38._, bf16[2,128,128]{2,1,0:T(8,128)(2,1)S(1)} %get-tuple-element.32.put_ref, bf16[256,1280]{1,0:T(8,128)(2,1)S(1)} %bitcast.22), custom_call_target="tpu_custom_call" | custom-call | flops 167772160 | bytes 1310720 | tf_op jit(solution)/shard_map/token_grads/pallas_call | solution.py:738
  (15 shorter events, 3.5 us)
Async XLA Ops:
  3.3 25.8 %all-to-all-start = ((bf16[32,8,1280]{2,1,0:T(8,128)(2,1)}), bf16[32,8,1280]{2,1,0:T(8,128)(2,1)S(1)}, u32[]{:S(2)}, u32[]{:S(2)}) async-start(bf16[32,8,1280]{2,1,0:T(8,128)(2,1)} %bitcast.34), calls=%async_computation | async-start | bytes 1310720 | tf_op jit(solution)/shard_map/all_to_all | solution.py:758
  12.3 13.9 %collective-permute-start.2 = (bf16[128,1280]{1,0:T(8,128)(2,1)S(1)}, bf16[128,1280]{1,0:T(8,128)(2,1)S(1)}, u32[]{:S(2)}, u32[]{:S(2)}) collective-permute-start(bf16[128,1280]{1,0:T(8,128)(2,1)S(1)} %get-tuple-element.40), channel_id=1, source_target_pairs={{0,16},{16,0},{1,17},{17,1},{2,18},{18,2},{3,19},{19,3},{4,20},{20... | collective-permute-start | bytes 983048 | tf_op jit(solution)/shard_map/ppermute | solution.py:785
  29.1 23.4 %all-to-all-start.2 = ((bf16[16,16,1280]{2,1,0:T(8,128)(2,1)}), bf16[16,16,1280]{2,1,0:T(8,128)(2,1)S(1)}, u32[]{:S(2)}, u32[]{:S(2)}) async-start(bf16[16,16,1280]{2,1,0:T(8,128)(2,1)} %bitcast.35), calls=%async_computation.2 | async-start | bytes 1310720 | tf_op jit(solution)/shard_map/all_to_all | solution.py:765
  33.9 15.8 %copy-start = (bf16[1,768,2560]{2,1,0:T(8,128)(2,1)S(1)}, bf16[1,768,2560]{2,1,0:T(8,128)(2,1)}, u32[]{:S(2)}) copy-start(bf16[1,768,2560]{2,1,0:T(8,128)(2,1)} %down_ref.1) | copy-start | bytes 11796484
  38.2 11.5 %collective-permute-start = (bf16[128,1536]{1,0:T(8,128)(2,1)S(1)}, bf16[128,1536]{1,0:T(8,128)(2,1)S(1)}, u32[]{:S(2)}, u32[]{:S(2)}) collective-permute-start(bf16[128,1536]{1,0:T(8,128)(2,1)S(1)} %get-tuple-element.29.refs_0_), channel_id=1, source_target_pairs={{0,16},{16,0},{1,17},{17,1},{2,18},{18,2},{3,19},{19,3},{4,20},{20... | collective-permute-start | bytes 1179656 | tf_op jit(solution)/shard_map/ppermute | solution.py:770
  51.5 5.7 %copy-start.4 = (bf16[128,768]{1,0:T(8,128)(2,1)}, bf16[128,768]{1,0:T(8,128)(2,1)S(1)}, u32[]{:S(2)}) copy-start(bf16[128,768]{1,0:T(8,128)(2,1)S(1)} %get-tuple-element.47.act_ref) | copy-start | bytes 589828
  52.4 23.3 %all-to-all-start.1 = ((bf16[16,16,1280]{2,1,0:T(8,128)(2,1)}), bf16[16,16,1280]{2,1,0:T(8,128)(2,1)S(1)}, u32[]{:S(2)}, u32[]{:S(2)}) async-start(bf16[16,16,1280]{2,1,0:T(8,128)(2,1)} %bitcast.7), calls=%async_computation.1 | async-start | bytes 1310720 | tf_op jit(solution)/shard_map/all_to_all | solution.py:765
  60.7 7.3 %collective-permute-start.3 = (bf16[128,768]{1,0:T(8,128)(2,1)S(1)}, bf16[128,768]{1,0:T(8,128)(2,1)S(1)}, u32[]{:S(2)}, u32[]{:S(2)}) collective-permute-start(bf16[128,768]{1,0:T(8,128)(2,1)S(1)} %get-tuple-element.41.refs_0_.refs_2_), channel_id=1, source_target_pairs={{0,16},{16,0},{1,17},{17,1},{2,18},{18,2},{3,19},{19,3},{4,20},{20... | collective-permute-start | bytes 589832 | tf_op jit(solution)/shard_map/ppermute | solution.py:770
  72.3 15.4 %copy-start.1 = (bf16[128,5120]{1,0:T(8,128)(2,1)S(1)}, bf16[128,5120]{1,0:T(8,128)(2,1)}, u32[]{:S(2)}) copy-start(bf16[128,5120]{1,0:T(8,128)(2,1)} %source_ref.1) | copy-start | bytes 3932164
  72.3 15.4 %copy-start.2 = (s32[1,16,4]{1,2,0:T(4,128)S(1)}, s32[1,16,4]{1,2,0:T(4,128)}, u32[]{:S(2)}) copy-start(s32[1,16,4]{1,2,0:T(4,128)} %param.9) | copy-start | bytes 772
  72.3 15.4 %copy-start.3 = (f32[1,16,4]{1,2,0:T(4,128)S(1)}, f32[1,16,4]{1,2,0:T(4,128)}, u32[]{:S(2)}) copy-start(f32[1,16,4]{1,2,0:T(4,128)} %param.10) | copy-start | bytes 772
  75.7 21.2 %all-to-all-start.3 = ((bf16[32,8,1280]{2,1,0:T(8,128)(2,1)}), bf16[32,8,1280]{2,1,0:T(8,128)(2,1)S(1)}, u32[]{:S(2)}, u32[]{:S(2)}) async-start(bf16[32,8,1280]{2,1,0:T(8,128)(2,1)} %bitcast.16), calls=%async_computation.3 | async-start | bytes 1310720 | tf_op jit(solution)/shard_map/all_to_all | solution.py:758
  78.5 15.6 %collective-permute-start.1 = (bf16[128,1280]{1,0:T(8,128)(2,1)S(1)}, bf16[128,1280]{1,0:T(8,128)(2,1)S(1)}, u32[]{:S(2)}, u32[]{:S(2)}) collective-permute-start(bf16[128,1280]{1,0:T(8,128)(2,1)S(1)} %bitcast.33), channel_id=1, source_target_pairs={{0,16},{16,0},{1,17},{17,1},{2,18},{18,2},{3,19},{19,3},{4,20},{20... | collective-permute-start | bytes 983048 | tf_op jit(solution)/shard_map/ppermute | solution.py:802

commit v12 on v11

--- a/solution.py
+++ b/solution.py
@@ -153,10 +153,10 @@
         copy.wait()
 
 
-def pair_kernel(blocks, _, picks_ref, gates_ref, source_ref, own_ref, other_ref, held_ref, sems, list_sems, *list_refs):
+def side_kernel(blocks, far, _, picks_ref, gates_ref, source_ref, out_ref, held_ref, sems, list_sems, *list_refs):
     slots = picks_ref.shape[0]
     tokens = source_ref.shape[0]
-    rows, cols = own_ref.shape
+    rows, cols = out_ref.shape
     half = lax.axis_index("dp")
     list_copies = [
         pltpu.make_async_copy(ref, target, list_sems.at[i])
@@ -165,49 +165,47 @@
     for copy in list_copies:
         copy.start()
     copies = []
-    for far in range(2):
-        for block in range(blocks):
-            start = (jnp.bitwise_xor(half, far) * blocks + block) * cols
-            copies.append(
-                pltpu.make_async_copy(
-                    source_ref.at[:, pl.ds(pl.multiple_of(start, 128), cols)],
-                    held_ref.at[far, block * tokens : (block + 1) * tokens],
-                    sems.at[far, block],
-                )
+    for block in range(blocks):
+        start = (jnp.bitwise_xor(half, far) * blocks + block) * cols
+        copies.append(
+            pltpu.make_async_copy(
+                source_ref.at[:, pl.ds(pl.multiple_of(start, 128), cols)],
+                held_ref.at[block * tokens : (block + 1) * tokens],
+                sems.at[block],
             )
-            copies[-1].start()
+        )
+        copies[-1].start()
     for copy in list_copies:
         copy.wait()
     chosen = spread_column(list_refs[0][...].astype(F32), blocks, tokens <= 256).astype(jnp.int32)
     target = chosen + iota((rows, 1), 0) % (blocks * slots) // slots * tokens
     take = one_hot(target == iota((rows, blocks * tokens), 1))
     scale = spread_column(list_refs[1][...], blocks)
-    for far, out_ref in enumerate((own_ref, other_ref)):
-        for block in range(blocks):
-            copies[far * blocks + block].wait()
-        out_ref[...] = (dot(take, held_ref[far]) * scale).astype(BF16)
-
-
-def pair_rows(source, picks, gates, blocks, after):
+    for copy in copies:
+        copy.wait()
+    out_ref[...] = (dot(take, held_ref[...]) * scale).astype(BF16)
+
+
+def side_rows(source, picks, gates, blocks, far, after):
     slots, experts = picks.shape
     tokens, width = source.shape
     cols = width // (2 * blocks)
     rows = experts * blocks * slots
     return pl.pallas_call(
-        functools.partial(pair_kernel, blocks),
+        functools.partial(side_kernel, blocks, far),
         in_specs=[hbm()] * 4,
-        out_specs=[vmem()] * 2,
-        out_shape=[shape_of(rows, cols)] * 2,
+        out_specs=vmem(),
+        out_shape=shape_of(rows, cols),
         scratch_shapes=[
-            pltpu.VMEM((2, blocks * tokens, cols), BF16),
-            pltpu.SemaphoreType.DMA((2, blocks)),
+            pltpu.VMEM((blocks * tokens, cols), BF16),
+            pltpu.SemaphoreType.DMA((blocks,)),
             pltpu.SemaphoreType.DMA((2,)),
             pltpu.VMEM((slots, experts), picks.dtype),
             pltpu.VMEM((slots, experts), gates.dtype),
         ],
         compiler_params=params(16),
-        cost_estimate=cost(4 * rows * cols * tokens * blocks, 2 * tokens * width),
-        name="pair_rows",
+        cost_estimate=cost(2 * rows * cols * tokens * blocks, tokens * width),
+        name="side_rows",
     )(in_hbm(after), in_hbm(picks), in_hbm(gates), in_hbm(source))
 
 
@@ -781,8 +779,9 @@
     messages_in = send_rows(tokens, (picks_t,), halves, blocks)
     arrived_in = scatter(messages_in)
     if halves == 2:
-        own, other = pair_rows(cotangent, picks_t, gates_t, blocks, messages_in)
-        other = lax.ppermute(other, "dp", [(0, 1), (1, 0)])
+        leaving = side_rows(cotangent, picks_t, gates_t, blocks, 1, messages_in)
+        other = lax.ppermute(leaving, "dp", [(0, 1), (1, 0)])
+        own = side_rows(cotangent, picks_t, gates_t, blocks, 0, messages_in)
         arrived_up = to_experts(experts, join_rows(own, other, experts))
     else:
         arrived_up = scatter(send_rows(cotangent, (picks_t, gates_t), halves, blocks))

time: 98.9 us -> 98.8 us (level)
  Pallas kernels: 34.9 us -> 36 us
    ppermute x1, waiting for transfers between devices: 12.1 us -> 11 us  [body(): other = lax.ppermute(leaving, 'dp', [(0, 1), (1, 0)])]
    pallas_call x1 -> x2, Pallas kernels: 1.73 us -> 2.85 us  [side_rows(): pl.pallas_call(functools.partial(side_kernel, blocks, far), in_specs=[hbm...]
  transfers between devices with their start and end apart: 8 -> 8, of which waited for: 8 -> 8; matrix products, arithmetic and copies ran while one was open for 0% -> 0% of each run, Pallas kernels for 31% -> 33%
where the time goes in v12:
time: 98.8 us; the launch traced here: 98.2 us
  waiting for transfers between devices  36.6 us (37%)
  Pallas kernels  36 us (36%)
  starting transfers between devices  24.7 us (25%)
    ppermute x2, waiting for transfers between devices, dp_shares(): lax.ppermute(own, 'dp', [(i, (i + shift) % halves) for i in range(halves)])  13.9 us
    ppermute x1, waiting for transfers between devices, body(): other = lax.ppermute(leaving, 'dp', [(0, 1), (1, 0)])  11 us
    all_to_all x2, starting transfers between devices, to_owners(): lax.all_to_all(messages, EVERYONE, split_axis=0, concat_axis=0, tiled=Tru...  9.92 us
    all_to_all x2, starting transfers between devices, to_experts(): lax.all_to_all(messages, 'expert', split_axis=0, concat_axis=0, tiled=Tru...  9.66 us
    pallas_call x1, Pallas kernels, weight_grads(): pl.pallas_call(weights_kernel, grid=(blocks, steps), in_specs=[chunk, chu...  7.28 us
    ppermute x1, waiting for transfers between devices, body(): other_out = lax.ppermute(other_out, 'dp', [(0, 1), (1, 0)])  4.58 us
    all_to_all x2, waiting for transfers between devices, to_experts(): lax.all_to_all(messages, 'expert', split_axis=0, concat_axis=0, tiled=Tru...  4.37 us
    pallas_call x1, Pallas kernels, in_sums(): pl.pallas_call(functools.partial(in_sums_kernel, slots), in_specs=[vmem()...  4.25 us
  transfers between devices with their start and end apart: 8, of which 8 were waited for; matrix products, arithmetic and copies ran while one was open for 0% of the time, Pallas kernels for 33%

profile of v12, /device:TPU:0, one launch (start us, length us, event | category | flops | bytes accessed | tf_op | source)
XLA Modules:
  0.0 98.2 jit_solution(9976883750578895089)
XLA Ops:
  0.6 2.6 %send_rows.1._ = bf16[256,1280]{1,0:T(8,128)(2,1)} custom-call(s32[4,16]{1,0:T(4,128)} %bitcast.28, bf16[128,5120]{1,0:T(8,128)(2,1)} %refs_1_.2), custom_call_target="tpu_custom_call" | custom-call | flops 167772160 | bytes 1966080 | tf_op jit(solution)/shard_map/send_rows/pallas_call | solution.py:245
  3.3 7.3 %all-to-all-start = ((bf16[32,8,1280]{2,1,0:T(8,128)(2,1)}), bf16[32,8,1280]{2,1,0:T(8,128)(2,1)S(1)}, u32[]{:S(2)}, u32[]{:S(2)}) async-start(bf16[32,8,1280]{2,1,0:T(8,128)(2,1)} %bitcast.36), calls=%async_computation | async-start | bytes 1310720 | tf_op jit(solution)/shard_map/all_to_all | solution.py:756
  10.6 1.4 %side_rows.3 = bf16[128,1280]{1,0:T(8,128)(2,1)S(1)} custom-call(bf16[256,1280]{1,0:T(8,128)(2,1)} %send_rows.1._, s32[4,16]{1,0:T(4,128)} %bitcast.29, f32[4,16]{1,0:T(4,128)} %bitcast.32, bf16[128,5120]{1,0:T(8,128)(2,1)} %source_ref.3), custom_call_target="tpu_custom_call" | custom-call | flops 83886080 | bytes 655360 | tf_op jit(solution)/shard_map/side_rows/pallas_call | solution.py:194
  12.0 1.8 %collective-permute-start.2 = (bf16[128,1280]{1,0:T(8,128)(2,1)S(1)}, bf16[128,1280]{1,0:T(8,128)(2,1)S(1)}, u32[]{:S(2)}, u32[]{:S(2)}) collective-permute-start(bf16[128,1280]{1,0:T(8,128)(2,1)S(1)} %side_rows.3), channel_id=1, source_target_pairs={{0,16},{16,0},{1,17},{17,1},{2,18},{18,2},{3,19},{19,3},{4,20},{20... | collective-permute-start | bytes 983048 | tf_op jit(solution)/shard_map/ppermute | solution.py:783
  13.8 1.4 %side_rows.2 = bf16[128,1280]{1,0:T(8,128)(2,1)S(1)} custom-call(bf16[256,1280]{1,0:T(8,128)(2,1)} %send_rows.1._, s32[4,16]{1,0:T(4,128)} %bitcast.30, f32[4,16]{1,0:T(4,128)} %bitcast.33, bf16[128,5120]{1,0:T(8,128)(2,1)} %source_ref.3), custom_call_target="tpu_custom_call" | custom-call | flops 83886080 | bytes 655360 | tf_op jit(solution)/shard_map/side_rows/pallas_call | solution.py:194
  15.3 11.0 %collective-permute-done.2 = bf16[128,1280]{1,0:T(8,128)(2,1)S(1)} collective-permute-done((bf16[128,1280]{1,0:T(8,128)(2,1)S(1)}, bf16[128,1280]{1,0:T(8,128)(2,1)S(1)}, u32[]{:S(2)}, u32[]{:S(2)}) %collective-permute-start.2) | collective-permute-done | bytes 327712 | tf_op jit(solution)/shard_map/ppermute | solution.py:783
  27.1 2.0 %all-to-all-done = bf16[32,8,1280]{2,1,0:T(8,128)(2,1)S(1)} async-done(((bf16[32,8,1280]{2,1,0:T(8,128)(2,1)}), bf16[32,8,1280]{2,1,0:T(8,128)(2,1)S(1)}, u32[]{:S(2)}, u32[]{:S(2)}) %all-to-all-start) | async-done | bytes 655392 | tf_op jit(solution)/shard_map/all_to_all | solution.py:756
  29.1 4.9 %all-to-all-start.2 = ((bf16[16,16,1280]{2,1,0:T(8,128)(2,1)}), bf16[16,16,1280]{2,1,0:T(8,128)(2,1)S(1)}, u32[]{:S(2)}, u32[]{:S(2)}) async-start(bf16[16,16,1280]{2,1,0:T(8,128)(2,1)} %bitcast.37), calls=%async_computation.2 | async-start | bytes 1310720 | tf_op jit(solution)/shard_map/all_to_all | solution.py:763
  34.0 4.2 %gate_up_sums.1 = (bf16[128,1536]{1,0:T(8,128)(2,1)S(1)}, bf16[2,128,1280]{2,1,0:T(8,128)(2,1)}) custom-call(bf16[256,1280]{1,0:T(8,128)(2,1)S(1)} %bitcast.21, bf16[1,2560,768]{2,1,0:T(8,128)(2,1)} %refs_1_.3, bf16[1,2560,768]{2,1,0:T(8,128)(2,1)} %refs_2_.3), custom_call_target="tpu_custom_call" | custom-call | flops 1006632960 | bytes 7864320 | tf_op jit(solution)/shard_map/gate_up_sums/pallas_call | solution.py:355
  39.0 10.7 %collective-permute-done.refs_1_ = bf16[128,1536]{1,0:T(8,128)(2,1)S(1)} collective-permute-done((bf16[128,1536]{1,0:T(8,128)(2,1)S(1)}, bf16[128,1536]{1,0:T(8,128)(2,1)S(1)}, u32[]{:S(2)}, u32[]{:S(2)}) %collective-permute-start) | collective-permute-done | bytes 393248 | tf_op jit(solution)/shard_map/ppermute | solution.py:768
  49.7 1.8 %output_rows.1 = (bf16[128,768]{1,0:T(8,128)(2,1)S(1)}, bf16[256,1280]{1,0:T(8,128)(2,1)}) custom-call(bf16[128,1536]{1,0:T(8,128)(2,1)S(1)} %get-tuple-element.27.refs_0_, bf16[128,1536]{1,0:T(8,128)(2,1)S(1)} %collective-permute-done.refs_1_, bf16[1,768,2560]{2,1,0:T(8,128)(2,1)S(1)} %copy-done.1), custom_call_target="tpu_custom_call" | custom-call | flops 503316480 | bytes 3932160 | tf_op jit(solution)/shard_map/output_rows/pallas_call | solution.py:457
  52.4 4.8 %all-to-all-start.1 = ((bf16[16,16,1280]{2,1,0:T(8,128)(2,1)}), bf16[16,16,1280]{2,1,0:T(8,128)(2,1)S(1)}, u32[]{:S(2)}, u32[]{:S(2)}) async-start(bf16[16,16,1280]{2,1,0:T(8,128)(2,1)} %bitcast.7), calls=%async_computation.1 | async-start | bytes 1310720 | tf_op jit(solution)/shard_map/all_to_all | solution.py:763
  57.3 3.5 %back_sums.1 = (bf16[128,768]{1,0:T(8,128)(2,1)S(1)}, bf16[2,128,1280]{2,1,0:T(8,128)(2,1)}) custom-call(bf16[256,1280]{1,0:T(8,128)(2,1)S(1)} %bitcast.23, bf16[1,768,2560]{2,1,0:T(8,128)(2,1)} %down_ref.1), custom_call_target="tpu_custom_call" | custom-call | flops 503316480 | bytes 3932160 | tf_op jit(solution)/shard_map/back_sums/pallas_call | solution.py:395
  61.5 3.3 %bring_weights.1 = (bf16[1,2560,768]{2,1,0:T(8,128)(2,1)S(1)}, bf16[1,2560,768]{2,1,0:T(8,128)(2,1)S(1)}) custom-call(bf16[128,768]{1,0:T(8,128)(2,1)S(1)} %get-tuple-element.37.refs_0_.refs_2_, bf16[1,2560,768]{2,1,0:T(8,128)(2,1)} %refs_1_.3, bf16[1,2560,768]{2,1,0:T(8,128)(2,1)} %refs_2_.3), custom_call_target="tpu_custom_call" | custom-call | bytes 7864320 | tf_op jit(solution)/shard_map/bring_weights/pallas_call | solution.py:422
  64.8 3.2 %collective-permute-done.3.refs_3_ = bf16[128,768]{1,0:T(8,128)(2,1)S(1)} collective-permute-done((bf16[128,768]{1,0:T(8,128)(2,1)S(1)}, bf16[128,768]{1,0:T(8,128)(2,1)S(1)}, u32[]{:S(2)}, u32[]{:S(2)}) %collective-permute-start.3) | collective-permute-done | bytes 196640 | tf_op jit(solution)/shard_map/ppermute | solution.py:768
  68.0 4.2 %gradient_rows.1 = (bf16[128,1536]{1,0:T(8,128)(2,1)}, bf16[256,1280]{1,0:T(8,128)(2,1)}) custom-call(bf16[128,1536]{1,0:T(8,128)(2,1)S(1)} %get-tuple-element.27.refs_0_, bf16[128,1536]{1,0:T(8,128)(2,1)S(1)} %collective-permute-done.refs_1_, bf16[128,768]{1,0:T(8,128)(2,1)S(1)} %get-tuple-element.37.refs_0_.refs_2_, ...), custom_call_target="tpu_custom_call" | custom-call | flops 1006632960 | bytes 7864320 | tf_op jit(solution)/shard_map/gradient_rows/pallas_call | solution.py:497
  72.3 3.4 %all-to-all-done.1 = bf16[16,16,1280]{2,1,0:T(8,128)(2,1)S(1)} async-done(((bf16[16,16,1280]{2,1,0:T(8,128)(2,1)}), bf16[16,16,1280]{2,1,0:T(8,128)(2,1)S(1)}, u32[]{:S(2)}, u32[]{:S(2)}) %all-to-all-start.1) | async-done | bytes 655392 | tf_op jit(solution)/shard_map/all_to_all | solution.py:763
  75.7 2.6 %all-to-all-start.3 = ((bf16[32,8,1280]{2,1,0:T(8,128)(2,1)}), bf16[32,8,1280]{2,1,0:T(8,128)(2,1)S(1)}, u32[]{:S(2)}, u32[]{:S(2)}) async-start(bf16[32,8,1280]{2,1,0:T(8,128)(2,1)} %bitcast.16), calls=%async_computation.3 | async-start | bytes 1310720 | tf_op jit(solution)/shard_map/all_to_all | solution.py:756
  78.5 1.7 %collective-permute-start.1 = (bf16[128,1280]{1,0:T(8,128)(2,1)S(1)}, bf16[128,1280]{1,0:T(8,128)(2,1)S(1)}, u32[]{:S(2)}, u32[]{:S(2)}) collective-permute-start(bf16[128,1280]{1,0:T(8,128)(2,1)S(1)} %bitcast.35), channel_id=1, source_target_pairs={{0,16},{16,0},{1,17},{17,1},{2,18},{18,2},{3,19},{19,3},{4,20},{20... | collective-permute-start | bytes 983048 | tf_op jit(solution)/shard_map/ppermute | solution.py:801
  80.2 7.3 %weight_grads.1 = (bf16[1,2560,768]{2,1,0:T(8,128)(2,1)}, bf16[1,2560,768]{2,1,0:T(8,128)(2,1)}, bf16[1,768,2560]{2,1,0:T(8,128)(2,1)}) custom-call(bf16[2,128,1280]{2,1,0:T(8,128)(2,1)} %get-tuple-element.41.rows_in_ref, bf16[2,128,1280]{2,1,0:T(8,128)(2,1)} %get-tuple-element.42.rows_up_ref, bf16[128,768]{1,0:T(8,128)(2,1)} %copy-done.4, ...), custom_call_target="tpu_custom_call" | custom-call | flops 1509949440 | bytes 11796480 | tf_op jit(solution)/shard_map/weight_grads/pallas_call | solution.py:525
  87.5 1.8 %mixed_near.1 = (bf16[128,5120]{1,0:T(8,128)(2,1)}, bf16[2,128,128]{2,1,0:T(8,128)(2,1)S(1)}, bf16[2,3,128,128]{3,2,1,0:T(8,128)(2,1)S(1)}, f32[1,128]{1,0:T(1,128)S(1)}) custom-call(s32[4,16]{1,0:T(4,128)S(1)} %bitcast.31, f32[4,16]{1,0:T(4,128)S(1)} %bitcast.34, bf16[128,5120]{1,0:T(8,128)(2,1)S(1)} %copy-done, bf16[128,1280]{1,0:T(8,128)(2,1)S(1)} %bitcast.27), custom_call_target="tpu_custom_call" | custom-call | flops 335544320 | bytes 1310720 | tf_op jit(solution)/shard_map/mixed_near/pallas_call | solution.py:663
  89.2 4.6 %collective-permute-done.1.back_ref = bf16[128,1280]{1,0:T(8,128)(2,1)S(1)} collective-permute-done((bf16[128,1280]{1,0:T(8,128)(2,1)S(1)}, bf16[128,1280]{1,0:T(8,128)(2,1)S(1)}, u32[]{:S(2)}, u32[]{:S(2)}) %collective-permute-start.1) | collective-permute-done | bytes 327712 | tf_op jit(solution)/shard_map/ppermute | solution.py:801
  93.8 2.2 %mixed_far.1 = (bf16[128,5120]{1,0:T(8,128)(2,1)}, f32[4,16]{1,0:T(4,128)}) custom-call(bf16[2,128,128]{2,1,0:T(8,128)(2,1)S(1)} %get-tuple-element.30.put_ref, bf16[2,3,128,128]{3,2,1,0:T(8,128)(2,1)S(1)} %get-tuple-element.31.pieces_ref, f32[1,128]{1,0:T(1,128)S(1)} %get-tuple-element.32.sums_ref, ...), custom_call_target="tpu_custom_call", output_to_operand_aliasing={{0}: (5, {})} | custom-call | flops 335544320 | bytes 1310720 | tf_op jit(solution)/shard_map/mixed_far/pallas_call | solution.py:678
  96.8 1.3 %token_grads.1 = bf16[128,5120]{1,0:T(8,128)(2,1)} custom-call(f32[4,16]{1,0:T(4,128)} %get-tuple-element.36._, bf16[2,128,128]{2,1,0:T(8,128)(2,1)S(1)} %get-tuple-element.30.put_ref, bf16[256,1280]{1,0:T(8,128)(2,1)S(1)} %bitcast.22), custom_call_target="tpu_custom_call" | custom-call | flops 167772160 | bytes 1310720 | tf_op jit(solution)/shard_map/token_grads/pallas_call | solution.py:736
  (16 shorter events, 4.3 us)
Async XLA Ops:
  3.3 25.8 %all-to-all-start = ((bf16[32,8,1280]{2,1,0:T(8,128)(2,1)}), bf16[32,8,1280]{2,1,0:T(8,128)(2,1)S(1)}, u32[]{:S(2)}, u32[]{:S(2)}) async-start(bf16[32,8,1280]{2,1,0:T(8,128)(2,1)} %bitcast.36), calls=%async_computation | async-start | bytes 1310720 | tf_op jit(solution)/shard_map/all_to_all | solution.py:756
  12.0 14.2 %collective-permute-start.2 = (bf16[128,1280]{1,0:T(8,128)(2,1)S(1)}, bf16[128,1280]{1,0:T(8,128)(2,1)S(1)}, u32[]{:S(2)}, u32[]{:S(2)}) collective-permute-start(bf16[128,1280]{1,0:T(8,128)(2,1)S(1)} %side_rows.3), channel_id=1, source_target_pairs={{0,16},{16,0},{1,17},{17,1},{2,18},{18,2},{3,19},{19,3},{4,20},{20... | collective-permute-start | bytes 983048 | tf_op jit(solution)/shard_map/ppermute | solution.py:783
  29.1 23.4 %all-to-all-start.2 = ((bf16[16,16,1280]{2,1,0:T(8,128)(2,1)}), bf16[16,16,1280]{2,1,0:T(8,128)(2,1)S(1)}, u32[]{:S(2)}, u32[]{:S(2)}) async-start(bf16[16,16,1280]{2,1,0:T(8,128)(2,1)} %bitcast.37), calls=%async_computation.2 | async-start | bytes 1310720 | tf_op jit(solution)/shard_map/all_to_all | solution.py:763
  33.9 15.8 %copy-start.1 = (bf16[1,768,2560]{2,1,0:T(8,128)(2,1)S(1)}, bf16[1,768,2560]{2,1,0:T(8,128)(2,1)}, u32[]{:S(2)}) copy-start(bf16[1,768,2560]{2,1,0:T(8,128)(2,1)} %down_ref.1) | copy-start | bytes 11796484
  38.2 11.5 %collective-permute-start = (bf16[128,1536]{1,0:T(8,128)(2,1)S(1)}, bf16[128,1536]{1,0:T(8,128)(2,1)S(1)}, u32[]{:S(2)}, u32[]{:S(2)}) collective-permute-start(bf16[128,1536]{1,0:T(8,128)(2,1)S(1)} %get-tuple-element.27.refs_0_), channel_id=1, source_target_pairs={{0,16},{16,0},{1,17},{17,1},{2,18},{18,2},{3,19},{19,3},{4,20},{20... | collective-permute-start | bytes 1179656 | tf_op jit(solution)/shard_map/ppermute | solution.py:768
  51.5 5.7 %copy-start.4 = (bf16[128,768]{1,0:T(8,128)(2,1)}, bf16[128,768]{1,0:T(8,128)(2,1)S(1)}, u32[]{:S(2)}) copy-start(bf16[128,768]{1,0:T(8,128)(2,1)S(1)} %get-tuple-element.43.act_ref) | copy-start | bytes 589828
  52.4 23.3 %all-to-all-start.1 = ((bf16[16,16,1280]{2,1,0:T(8,128)(2,1)}), bf16[16,16,1280]{2,1,0:T(8,128)(2,1)S(1)}, u32[]{:S(2)}, u32[]{:S(2)}) async-start(bf16[16,16,1280]{2,1,0:T(8,128)(2,1)} %bitcast.7), calls=%async_computation.1 | async-start | bytes 1310720 | tf_op jit(solution)/shard_map/all_to_all | solution.py:763
  60.7 7.3 %collective-permute-start.3 = (bf16[128,768]{1,0:T(8,128)(2,1)S(1)}, bf16[128,768]{1,0:T(8,128)(2,1)S(1)}, u32[]{:S(2)}, u32[]{:S(2)}) collective-permute-start(bf16[128,768]{1,0:T(8,128)(2,1)S(1)} %get-tuple-element.37.refs_0_.refs_2_), channel_id=1, source_target_pairs={{0,16},{16,0},{1,17},{17,1},{2,18},{18,2},{3,19},{19,3},{4,20},{20... | collective-permute-start | bytes 589832 | tf_op jit(solution)/shard_map/ppermute | solution.py:768
  72.3 15.2 %copy-start = (bf16[128,5120]{1,0:T(8,128)(2,1)S(1)}, bf16[128,5120]{1,0:T(8,128)(2,1)}, u32[]{:S(2)}) copy-start(bf16[128,5120]{1,0:T(8,128)(2,1)} %source_ref.3) | copy-start | bytes 3932164
  72.3 15.2 %copy-start.2 = (s32[1,16,4]{1,2,0:T(4,128)S(1)}, s32[1,16,4]{1,2,0:T(4,128)}, u32[]{:S(2)}) copy-start(s32[1,16,4]{1,2,0:T(4,128)} %param.9) | copy-start | bytes 772
  72.3 15.2 %copy-start.3 = (f32[1,16,4]{1,2,0:T(4,128)S(1)}, f32[1,16,4]{1,2,0:T(4,128)}, u32[]{:S(2)}) copy-start(f32[1,16,4]{1,2,0:T(4,128)} %param.10) | copy-start | bytes 772
  75.7 21.1 %all-to-all-start.3 = ((bf16[32,8,1280]{2,1,0:T(8,128)(2,1)}), bf16[32,8,1280]{2,1,0:T(8,128)(2,1)S(1)}, u32[]{:S(2)}, u32[]{:S(2)}) async-start(bf16[32,8,1280]{2,1,0:T(8,128)(2,1)} %bitcast.16), calls=%async_computation.3 | async-start | bytes 1310720 | tf_op jit(solution)/shard_map/all_to_all | solution.py:756
  78.5 15.4 %collective-permute-start.1 = (bf16[128,1280]{1,0:T(8,128)(2,1)S(1)}, bf16[128,1280]{1,0:T(8,128)(2,1)S(1)}, u32[]{:S(2)}, u32[]{:S(2)}) collective-permute-start(bf16[128,1280]{1,0:T(8,128)(2,1)S(1)} %bitcast.35), channel_id=1, source_target_pairs={{0,16},{16,0},{1,17},{17,1},{2,18},{18,2},{3,19},{19,3},{4,20},{20... | collective-permute-start | bytes 983048 | tf_op jit(solution)/shard_map/ppermute | solution.py:801
